TPU v7x, 256 devices: a whole 4x4x8 slice. The times are simulated.
256 devices in a mesh: ctx: 16 (over x, y_hi, core), tp: 16 (over y_lo, z).
Axes of the slice: x: 4, y: 4 (y_hi: 2, y_lo: 2; y = y_hi * 2 + y_lo), z: 8, core: 2. Of those that a mesh axis runs over, the one named last changes fastest.
Arguments:
- queries: bfloat16 [8192, 8192], P('ctx', 'tp'), may hold values from -5 to 5
- keys_values: bfloat16 [2, 8192, 1024], P(None, 'ctx'), may hold values from -5 to 5
- block_list: int32 [64, 16], P('ctx'), may hold values from -1 to 63, as said below
- out_weight: bfloat16 [8192, 8192], P('tp'), may hold values from -0.0625 to 0.0625
Outputs:
- projected: bfloat16 [8192, 8192], P('ctx', 'tp')
Inputs may be any that keep to these rules, and one draw needn't show every extreme that they name: Row r of block_list names distinct key blocks, r first; after the listed blocks the remaining slots hold -1; the number listed tends to grow with r, and the last row lists 16.
All inputs are finite; a program needn't handle non-finite values.
Results may differ from a plain program's by a relative error of at most 0.023.
Values may be sent and summed in bfloat16 or wider, within the bound.
No kernel may reach another device: no remote copies, remote signals or barrier semaphores. Data moves between devices by JAX's collectives and lax.ppermute only.
A program may use at most 128 MiB of HBM per device.

v0:
```python
import math

import jax
import jax.numpy as jnp
from jax import lax
from jax.sharding import PartitionSpec as P

HEADS = 64
KVH = 8
HD = 128
BLOCK = 128


def shifted(array, axis, by):
    count = lax.axis_size(axis)
    return lax.ppermute(array, axis, [(i, (i + by) % count) for i in range(count)])


def shards(queries, keys_values, block_list, out_weight):
    tok = queries.shape[0]
    n_ctx = lax.axis_size("ctx")
    n_tp = lax.axis_size("tp")
    heads_here = HEADS // n_tp
    group = HEADS // KVH
    group_here = min(heads_here, group)
    kv_here = max(1, heads_here // group)
    scale = HD ** (-0.5)
    tp_index = lax.axis_index("tp")
    ctx_index = lax.axis_index("ctx")
    first_kv = tp_index * heads_here // group
    kv_mine = lax.dynamic_slice_in_dim(keys_values, first_kv * HD, kv_here * HD, 2)
    q_heads = queries.reshape(tok, kv_here, group_here, HD)
    nblk = tok * n_ctx // BLOCK
    blocks_here = tok // BLOCK
    allowed = jnp.any(
        block_list[:, :, None] == jnp.arange(nblk, dtype=jnp.int32)[None, None, :], axis=1
    )

    def slice_update(state, kv_slice, first_block):
        top, total, summed = state
        width = kv_slice.shape[1]
        sub_blocks = width // BLOCK
        keys = kv_slice[0].reshape(width, kv_here, HD)
        vals = kv_slice[1].reshape(width, kv_here, HD)
        column = lax.dynamic_slice_in_dim(allowed, first_block, sub_blocks, 1)
        mask = jnp.broadcast_to(
            column[:, None, :, None], (blocks_here, BLOCK, sub_blocks, BLOCK)
        ).reshape(tok, width)
        scores = (
            jnp.einsum("tkgd,ukd->kgtu", q_heads, keys, preferred_element_type=jnp.float32) * scale
        )
        scores = jnp.where(mask[None, None], scores, -1e30)
        new_top = jnp.maximum(top, jnp.max(scores, axis=-1))
        weights = jnp.where(mask[None, None], jnp.exp(scores - new_top[..., None]), 0.0)
        factor = jnp.exp(top - new_top)
        total = total * factor + jnp.sum(weights, axis=-1)
        product = jnp.einsum(
            "kgtu,ukd->kgtd", weights.astype(jnp.bfloat16), vals, preferred_element_type=jnp.float32
        )
        summed = summed * factor[..., None] + product
        return (new_top, total, summed)

    def update(state, piece, start):
        count = piece.shape[1]
        step = math.gcd(count, 4 * BLOCK)
        first_block = start // BLOCK

        def one_slice(j, inner):
            return slice_update(inner, piece, first_block + j * (step // BLOCK))

        return lax.fori_loop(0, count // step, one_slice, state)

    def attend(state, piece, start):
        return update(state, piece, start)

    state = (
        jnp.full((kv_here, group_here, tok), -1e30, jnp.float32),
        jnp.zeros((kv_here, group_here, tok), jnp.float32),
        jnp.zeros((kv_here, group_here, tok, HD), jnp.float32),
    )
    state = attend(state, kv_mine, ctx_index * tok)

    def cycle_step(step, carry):
        inner, moving = carry
        moving = shifted(moving, "ctx", 1)
        source = (ctx_index - step) % n_ctx
        return (attend(inner, moving, source * tok), moving)

    state, _ = lax.fori_loop(1, n_ctx, cycle_step, (state, kv_mine))
    _, total, summed = state
    attended = (summed / total[..., None]).astype(jnp.bfloat16)
    attended = jnp.transpose(attended, (2, 0, 1, 3)).reshape(tok, heads_here * HD)
    partial_value = jnp.dot(attended, out_weight, preferred_element_type=jnp.float32)
    result = lax.psum_scatter(
        partial_value.astype(jnp.bfloat16), "tp", scatter_dimension=1, tiled=True
    )
    return result


def solution(mesh):
    in_specs = (P("ctx", "tp"), P(None, "ctx", None), P("ctx", None), P("tp", None))
    out_specs = P("ctx", "tp")
    return jax.shard_map(shards, mesh=mesh, in_specs=in_specs, out_specs=out_specs, check_vma=False)
```

profile of v0, /device:TPU:6, one launch (start us, length us, event | category | flops | bytes accessed | tf_op | source)
XLA Modules:
  0.0 349.0 jit_solution(12282820409788915279)
XLA Ops:
  9.6 1.9 fusion.19
  12.7 2.5 fusion.29
  15.2 196.8 %while.28 = (s32[]{:T(128)}, f32[1,4,512]{2,1,0:T(4,128)S(1)}, f32[1,4,512]{2,1,0:T(4,128)S(1)}, f32[1,4,512,128]{3,2,1,0:T(8,128)}, bf16[2,512,128]{2,1,0:T(8,1...) while((s32[]{:T(128)}, f32[1,4,512]{2,1,0:T(4,128)S(1)}, ...), condition=%wide.region_6.7_spmd, body=%wide.region_3.0_spmd.sunk | while | flops 551032832 | bytes 27132556 | solution.py:89
  15.7 7.7 %collective-permute-done = bf16[2,512,128]{2,1,0:T(8,128)(2,1)S(1)} collective-permute-done((bf16[2,512,128]{2,1,0:T(8,128)(2,1)S(1)}, bf16[2,512,128]{2,1,0:T(8,128)(2,1)S(1)}, u32[]{:S(2)}, u32[]{:S(2)}) %collective-permute-start) | collective-permute-done | bytes 262176 | tf_op jit(solution)/shard_map/while/body/eval_jaxpr/ppermute | solution.py:16
  28.9 7.7 %collective-permute-done = bf16[2,512,128]{2,1,0:T(8,128)(2,1)S(1)} collective-permute-done((bf16[2,512,128]{2,1,0:T(8,128)(2,1)S(1)}, bf16[2,512,128]{2,1,0:T(8,128)(2,1)S(1)}, u32[]{:S(2)}, u32[]{:S(2)}) %collective-permute-start) | collective-permute-done | bytes 262176 | tf_op jit(solution)/shard_map/while/body/eval_jaxpr/ppermute | solution.py:16
  38.5 1.9 fusion.54
  42.0 7.7 %collective-permute-done = bf16[2,512,128]{2,1,0:T(8,128)(2,1)S(1)} collective-permute-done((bf16[2,512,128]{2,1,0:T(8,128)(2,1)S(1)}, bf16[2,512,128]{2,1,0:T(8,128)(2,1)S(1)}, u32[]{:S(2)}, u32[]{:S(2)}) %collective-permute-start) | collective-permute-done | bytes 262176 | tf_op jit(solution)/shard_map/while/body/eval_jaxpr/ppermute | solution.py:16
  51.6 1.9 fusion.54
  55.1 7.7 %collective-permute-done = bf16[2,512,128]{2,1,0:T(8,128)(2,1)S(1)} collective-permute-done((bf16[2,512,128]{2,1,0:T(8,128)(2,1)S(1)}, bf16[2,512,128]{2,1,0:T(8,128)(2,1)S(1)}, u32[]{:S(2)}, u32[]{:S(2)}) %collective-permute-start) | collective-permute-done | bytes 262176 | tf_op jit(solution)/shard_map/while/body/eval_jaxpr/ppermute | solution.py:16
  64.8 1.9 fusion.54
  68.2 7.7 %collective-permute-done = bf16[2,512,128]{2,1,0:T(8,128)(2,1)S(1)} collective-permute-done((bf16[2,512,128]{2,1,0:T(8,128)(2,1)S(1)}, bf16[2,512,128]{2,1,0:T(8,128)(2,1)S(1)}, u32[]{:S(2)}, u32[]{:S(2)}) %collective-permute-start) | collective-permute-done | bytes 262176 | tf_op jit(solution)/shard_map/while/body/eval_jaxpr/ppermute | solution.py:16
  77.9 1.9 fusion.54
  81.3 7.7 %collective-permute-done = bf16[2,512,128]{2,1,0:T(8,128)(2,1)S(1)} collective-permute-done((bf16[2,512,128]{2,1,0:T(8,128)(2,1)S(1)}, bf16[2,512,128]{2,1,0:T(8,128)(2,1)S(1)}, u32[]{:S(2)}, u32[]{:S(2)}) %collective-permute-start) | collective-permute-done | bytes 262176 | tf_op jit(solution)/shard_map/while/body/eval_jaxpr/ppermute | solution.py:16
  91.0 1.9 fusion.54
  94.5 7.7 %collective-permute-done = bf16[2,512,128]{2,1,0:T(8,128)(2,1)S(1)} collective-permute-done((bf16[2,512,128]{2,1,0:T(8,128)(2,1)S(1)}, bf16[2,512,128]{2,1,0:T(8,128)(2,1)S(1)}, u32[]{:S(2)}, u32[]{:S(2)}) %collective-permute-start) | collective-permute-done | bytes 262176 | tf_op jit(solution)/shard_map/while/body/eval_jaxpr/ppermute | solution.py:16
  104.1 1.9 fusion.54
  107.6 7.7 %collective-permute-done = bf16[2,512,128]{2,1,0:T(8,128)(2,1)S(1)} collective-permute-done((bf16[2,512,128]{2,1,0:T(8,128)(2,1)S(1)}, bf16[2,512,128]{2,1,0:T(8,128)(2,1)S(1)}, u32[]{:S(2)}, u32[]{:S(2)}) %collective-permute-start) | collective-permute-done | bytes 262176 | tf_op jit(solution)/shard_map/while/body/eval_jaxpr/ppermute | solution.py:16
  117.2 1.9 fusion.54
  120.7 7.7 %collective-permute-done = bf16[2,512,128]{2,1,0:T(8,128)(2,1)S(1)} collective-permute-done((bf16[2,512,128]{2,1,0:T(8,128)(2,1)S(1)}, bf16[2,512,128]{2,1,0:T(8,128)(2,1)S(1)}, u32[]{:S(2)}, u32[]{:S(2)}) %collective-permute-start) | collective-permute-done | bytes 262176 | tf_op jit(solution)/shard_map/while/body/eval_jaxpr/ppermute | solution.py:16
  130.4 1.9 fusion.54
  133.8 7.7 %collective-permute-done = bf16[2,512,128]{2,1,0:T(8,128)(2,1)S(1)} collective-permute-done((bf16[2,512,128]{2,1,0:T(8,128)(2,1)S(1)}, bf16[2,512,128]{2,1,0:T(8,128)(2,1)S(1)}, u32[]{:S(2)}, u32[]{:S(2)}) %collective-permute-start) | collective-permute-done | bytes 262176 | tf_op jit(solution)/shard_map/while/body/eval_jaxpr/ppermute | solution.py:16
  143.5 1.9 fusion.54
  146.9 7.7 %collective-permute-done = bf16[2,512,128]{2,1,0:T(8,128)(2,1)S(1)} collective-permute-done((bf16[2,512,128]{2,1,0:T(8,128)(2,1)S(1)}, bf16[2,512,128]{2,1,0:T(8,128)(2,1)S(1)}, u32[]{:S(2)}, u32[]{:S(2)}) %collective-permute-start) | collective-permute-done | bytes 262176 | tf_op jit(solution)/shard_map/while/body/eval_jaxpr/ppermute | solution.py:16
  156.6 1.9 fusion.54
  160.1 7.7 %collective-permute-done = bf16[2,512,128]{2,1,0:T(8,128)(2,1)S(1)} collective-permute-done((bf16[2,512,128]{2,1,0:T(8,128)(2,1)S(1)}, bf16[2,512,128]{2,1,0:T(8,128)(2,1)S(1)}, u32[]{:S(2)}, u32[]{:S(2)}) %collective-permute-start) | collective-permute-done | bytes 262176 | tf_op jit(solution)/shard_map/while/body/eval_jaxpr/ppermute | solution.py:16
  169.7 1.9 fusion.54
  173.2 7.7 %collective-permute-done = bf16[2,512,128]{2,1,0:T(8,128)(2,1)S(1)} collective-permute-done((bf16[2,512,128]{2,1,0:T(8,128)(2,1)S(1)}, bf16[2,512,128]{2,1,0:T(8,128)(2,1)S(1)}, u32[]{:S(2)}, u32[]{:S(2)}) %collective-permute-start) | collective-permute-done | bytes 262176 | tf_op jit(solution)/shard_map/while/body/eval_jaxpr/ppermute | solution.py:16
  187.0 6.9 %collective-permute-done = bf16[2,512,128]{2,1,0:T(8,128)(2,1)S(1)} collective-permute-done((bf16[2,512,128]{2,1,0:T(8,128)(2,1)S(1)}, bf16[2,512,128]{2,1,0:T(8,128)(2,1)S(1)}, u32[]{:S(2)}, u32[]{:S(2)}) %collective-permute-start) | collective-permute-done | bytes 262176 | tf_op jit(solution)/shard_map/while/body/eval_jaxpr/ppermute | solution.py:16
  198.9 1.9 collective-permute-start
  201.4 5.7 %collective-permute-done = bf16[2,512,128]{2,1,0:T(8,128)(2,1)S(1)} collective-permute-done((bf16[2,512,128]{2,1,0:T(8,128)(2,1)S(1)}, bf16[2,512,128]{2,1,0:T(8,128)(2,1)S(1)}, u32[]{:S(2)}, u32[]{:S(2)}) %collective-permute-start) | collective-permute-done | bytes 262176 | tf_op jit(solution)/shard_map/while/body/eval_jaxpr/ppermute | solution.py:16
  213.7 10.1 %convolution_convert_fusion = bf16[512,8192]{1,0:T(8,128)(2,1)} fusion(bf16[512,512]{0,1:T(8,128)(2,1)S(1)} %bitcast.161, bf16[512,8192]{1,0:T(8,128)(2,1)} %param.9), kind=kOutput, calls=%fused_computation.23 | convolution fusion | flops 4299161600 | bytes 17301504 | tf_op jit(solution)/shard_map/dot_general | solution.py:93
  223.9 118.3 %reduce-scatter.2.cloned.1.call-done = bf16[512,512]{1,0:T(8,128)(2,1)} async-done(((bf16[512,8192]{1,0:T(8,128)(2,1)}), bf16[512,512]{1,0:T(8,128)(2,1)}) %reduce-scatter.2.cloned.1.call-update) | async-done | bytes 524304 | tf_op jit(solution)/shard_map/reduce_scatter | solution.py:94
  (245 shorter events, 66.4 us)
Async XLA Ops:
  6.5 3.0 copy-start
  6.5 335.7 %reduce-scatter.2.cloned.1.call-start = ((), (), s32[]{:S(2)}) async-start(), calls=%async_computation.1 | async-start | bytes 8912896 | tf_op jit(solution)/shard_map/reduce_scatter | solution.py:94
  15.2 8.2 %collective-permute-start = (bf16[2,512,128]{2,1,0:T(8,128)(2,1)S(1)}, bf16[2,512,128]{2,1,0:T(8,128)(2,1)S(1)}, u32[]{:S(2)}, u32[]{:S(2)}) collective-permute-start(bf16[2,512,128]{2,1,0:T(8,128)(2,1)S(1)} %get-tuple-element.400), channel_id=1, source_target_pairs={{0,16},{16,32},{32,48},{48,64},{64,80},{80,96},{96,112},{112,128},... | collective-permute-start | bytes 786440 | tf_op jit(solution)/shard_map/while/body/eval_jaxpr/ppermute | solution.py:16
  23.4 2.0 copy-start.1
  28.3 8.2 %collective-permute-start = (bf16[2,512,128]{2,1,0:T(8,128)(2,1)S(1)}, bf16[2,512,128]{2,1,0:T(8,128)(2,1)S(1)}, u32[]{:S(2)}, u32[]{:S(2)}) collective-permute-start(bf16[2,512,128]{2,1,0:T(8,128)(2,1)S(1)} %get-tuple-element.400), channel_id=1, source_target_pairs={{0,16},{16,32},{32,48},{48,64},{64,80},{80,96},{96,112},{112,128},... | collective-permute-start | bytes 786440 | tf_op jit(solution)/shard_map/while/body/eval_jaxpr/ppermute | solution.py:16
  36.5 2.0 copy-start.1
  41.4 8.2 %collective-permute-start = (bf16[2,512,128]{2,1,0:T(8,128)(2,1)S(1)}, bf16[2,512,128]{2,1,0:T(8,128)(2,1)S(1)}, u32[]{:S(2)}, u32[]{:S(2)}) collective-permute-start(bf16[2,512,128]{2,1,0:T(8,128)(2,1)S(1)} %get-tuple-element.400), channel_id=1, source_target_pairs={{0,16},{16,32},{32,48},{48,64},{64,80},{80,96},{96,112},{112,128},... | collective-permute-start | bytes 786440 | tf_op jit(solution)/shard_map/while/body/eval_jaxpr/ppermute | solution.py:16
  49.6 2.0 copy-start.1
  54.6 8.2 %collective-permute-start = (bf16[2,512,128]{2,1,0:T(8,128)(2,1)S(1)}, bf16[2,512,128]{2,1,0:T(8,128)(2,1)S(1)}, u32[]{:S(2)}, u32[]{:S(2)}) collective-permute-start(bf16[2,512,128]{2,1,0:T(8,128)(2,1)S(1)} %get-tuple-element.400), channel_id=1, source_target_pairs={{0,16},{16,32},{32,48},{48,64},{64,80},{80,96},{96,112},{112,128},... | collective-permute-start | bytes 786440 | tf_op jit(solution)/shard_map/while/body/eval_jaxpr/ppermute | solution.py:16
  62.8 2.0 copy-start.1
  67.7 8.2 %collective-permute-start = (bf16[2,512,128]{2,1,0:T(8,128)(2,1)S(1)}, bf16[2,512,128]{2,1,0:T(8,128)(2,1)S(1)}, u32[]{:S(2)}, u32[]{:S(2)}) collective-permute-start(bf16[2,512,128]{2,1,0:T(8,128)(2,1)S(1)} %get-tuple-element.400), channel_id=1, source_target_pairs={{0,16},{16,32},{32,48},{48,64},{64,80},{80,96},{96,112},{112,128},... | collective-permute-start | bytes 786440 | tf_op jit(solution)/shard_map/while/body/eval_jaxpr/ppermute | solution.py:16
  75.9 2.0 copy-start.1
  80.8 8.2 %collective-permute-start = (bf16[2,512,128]{2,1,0:T(8,128)(2,1)S(1)}, bf16[2,512,128]{2,1,0:T(8,128)(2,1)S(1)}, u32[]{:S(2)}, u32[]{:S(2)}) collective-permute-start(bf16[2,512,128]{2,1,0:T(8,128)(2,1)S(1)} %get-tuple-element.400), channel_id=1, source_target_pairs={{0,16},{16,32},{32,48},{48,64},{64,80},{80,96},{96,112},{112,128},... | collective-permute-start | bytes 786440 | tf_op jit(solution)/shard_map/while/body/eval_jaxpr/ppermute | solution.py:16
  89.0 2.0 copy-start.1
  93.9 8.2 %collective-permute-start = (bf16[2,512,128]{2,1,0:T(8,128)(2,1)S(1)}, bf16[2,512,128]{2,1,0:T(8,128)(2,1)S(1)}, u32[]{:S(2)}, u32[]{:S(2)}) collective-permute-start(bf16[2,512,128]{2,1,0:T(8,128)(2,1)S(1)} %get-tuple-element.400), channel_id=1, source_target_pairs={{0,16},{16,32},{32,48},{48,64},{64,80},{80,96},{96,112},{112,128},... | collective-permute-start | bytes 786440 | tf_op jit(solution)/shard_map/while/body/eval_jaxpr/ppermute | solution.py:16
  102.1 2.0 copy-start.1
  107.0 8.2 %collective-permute-start = (bf16[2,512,128]{2,1,0:T(8,128)(2,1)S(1)}, bf16[2,512,128]{2,1,0:T(8,128)(2,1)S(1)}, u32[]{:S(2)}, u32[]{:S(2)}) collective-permute-start(bf16[2,512,128]{2,1,0:T(8,128)(2,1)S(1)} %get-tuple-element.400), channel_id=1, source_target_pairs={{0,16},{16,32},{32,48},{48,64},{64,80},{80,96},{96,112},{112,128},... | collective-permute-start | bytes 786440 | tf_op jit(solution)/shard_map/while/body/eval_jaxpr/ppermute | solution.py:16
  115.2 2.0 copy-start.1
  120.2 8.2 %collective-permute-start = (bf16[2,512,128]{2,1,0:T(8,128)(2,1)S(1)}, bf16[2,512,128]{2,1,0:T(8,128)(2,1)S(1)}, u32[]{:S(2)}, u32[]{:S(2)}) collective-permute-start(bf16[2,512,128]{2,1,0:T(8,128)(2,1)S(1)} %get-tuple-element.400), channel_id=1, source_target_pairs={{0,16},{16,32},{32,48},{48,64},{64,80},{80,96},{96,112},{112,128},... | collective-permute-start | bytes 786440 | tf_op jit(solution)/shard_map/while/body/eval_jaxpr/ppermute | solution.py:16
  128.4 2.0 copy-start.1
  133.3 8.2 %collective-permute-start = (bf16[2,512,128]{2,1,0:T(8,128)(2,1)S(1)}, bf16[2,512,128]{2,1,0:T(8,128)(2,1)S(1)}, u32[]{:S(2)}, u32[]{:S(2)}) collective-permute-start(bf16[2,512,128]{2,1,0:T(8,128)(2,1)S(1)} %get-tuple-element.400), channel_id=1, source_target_pairs={{0,16},{16,32},{32,48},{48,64},{64,80},{80,96},{96,112},{112,128},... | collective-permute-start | bytes 786440 | tf_op jit(solution)/shard_map/while/body/eval_jaxpr/ppermute | solution.py:16
  141.5 2.0 copy-start.1
  146.4 8.2 %collective-permute-start = (bf16[2,512,128]{2,1,0:T(8,128)(2,1)S(1)}, bf16[2,512,128]{2,1,0:T(8,128)(2,1)S(1)}, u32[]{:S(2)}, u32[]{:S(2)}) collective-permute-start(bf16[2,512,128]{2,1,0:T(8,128)(2,1)S(1)} %get-tuple-element.400), channel_id=1, source_target_pairs={{0,16},{16,32},{32,48},{48,64},{64,80},{80,96},{96,112},{112,128},... | collective-permute-start | bytes 786440 | tf_op jit(solution)/shard_map/while/body/eval_jaxpr/ppermute | solution.py:16
  154.6 2.0 copy-start.1
  159.5 8.2 %collective-permute-start = (bf16[2,512,128]{2,1,0:T(8,128)(2,1)S(1)}, bf16[2,512,128]{2,1,0:T(8,128)(2,1)S(1)}, u32[]{:S(2)}, u32[]{:S(2)}) collective-permute-start(bf16[2,512,128]{2,1,0:T(8,128)(2,1)S(1)} %get-tuple-element.400), channel_id=1, source_target_pairs={{0,16},{16,32},{32,48},{48,64},{64,80},{80,96},{96,112},{112,128},... | collective-permute-start | bytes 786440 | tf_op jit(solution)/shard_map/while/body/eval_jaxpr/ppermute | solution.py:16
  167.7 2.0 copy-start.1
  172.6 8.2 %collective-permute-start = (bf16[2,512,128]{2,1,0:T(8,128)(2,1)S(1)}, bf16[2,512,128]{2,1,0:T(8,128)(2,1)S(1)}, u32[]{:S(2)}, u32[]{:S(2)}) collective-permute-start(bf16[2,512,128]{2,1,0:T(8,128)(2,1)S(1)} %get-tuple-element.400), channel_id=1, source_target_pairs={{0,16},{16,32},{32,48},{48,64},{64,80},{80,96},{96,112},{112,128},... | collective-permute-start | bytes 786440 | tf_op jit(solution)/shard_map/while/body/eval_jaxpr/ppermute | solution.py:16
  180.8 2.0 copy-start.1
  185.8 8.2 %collective-permute-start = (bf16[2,512,128]{2,1,0:T(8,128)(2,1)S(1)}, bf16[2,512,128]{2,1,0:T(8,128)(2,1)S(1)}, u32[]{:S(2)}, u32[]{:S(2)}) collective-permute-start(bf16[2,512,128]{2,1,0:T(8,128)(2,1)S(1)} %get-tuple-element.400), channel_id=1, source_target_pairs={{0,16},{16,32},{32,48},{48,64},{64,80},{80,96},{96,112},{112,128},... | collective-permute-start | bytes 786440 | tf_op jit(solution)/shard_map/while/body/eval_jaxpr/ppermute | solution.py:16
  194.0 2.0 copy-start.1
  198.9 8.2 %collective-permute-start = (bf16[2,512,128]{2,1,0:T(8,128)(2,1)S(1)}, bf16[2,512,128]{2,1,0:T(8,128)(2,1)S(1)}, u32[]{:S(2)}, u32[]{:S(2)}) collective-permute-start(bf16[2,512,128]{2,1,0:T(8,128)(2,1)S(1)} %get-tuple-element.400), channel_id=1, source_target_pairs={{0,16},{16,32},{32,48},{48,64},{64,80},{80,96},{96,112},{112,128},... | collective-permute-start | bytes 786440 | tf_op jit(solution)/shard_map/while/body/eval_jaxpr/ppermute | solution.py:16
  207.1 2.0 copy-start.1
  (15 other events, 14.9 us)
Sparse Core Ops, SparseCore 0:
  224.0 118.1 reduce-scatter.1
where the time goes:
time: 350 us; the launch traced here: 349 us
  waiting for transfers between devices  231 us (66%)
  matrix products  56.3 us (16%)
  local copies, waits for them, and re-layouts  26.7 us (8%)
  other arithmetic  18.2 us (5%)
  between operations  13.5 us (4%)
    reduce_scatter x1, waiting for transfers between devices, shards(): lax.psum_scatter(partial_value.astype(jnp.bfloat16), 'tp', scatter_dimens...  118 us
    ppermute x15, waiting for transfers between devices, shifted(): lax.ppermute(array, axis, [(i, (i + by) % count) for i in range(count)])  112 us
    dot_general x16, matrix products, slice_update(): jnp.einsum('kgtu,ukd->kgtd', weights.astype(jnp.bfloat16), vals, preferre...  31.2 us
    while x105, local copies, waits for them, and re-layouts  17.1 us
    reduce_sum x16, other arithmetic, slice_update(): total = total * factor + jnp.sum(weights, axis=-1)  16.7 us
    dot_general x16, matrix products, slice_update(): jnp.einsum('tkgd,ukd->kgtu', q_heads, keys, preferred_element_type=jnp.fl...  15 us
    dot_general x1, matrix products, shards(): jnp.dot(attended, out_weight, preferred_element_type=jnp.float32)  10.1 us
  transfers between devices with their start and end apart: 16, of which 16 were waited for; matrix products, arithmetic and copies ran while one was open for 2% of the time, Pallas kernels for 0%

commit v1 on v0

v1 whole, which is shorter than its diff:
```python
import functools
import math

import jax
import jax.numpy as jnp
from jax import lax
from jax.experimental import pallas as pl
from jax.experimental.pallas import tpu as pltpu
from jax.sharding import PartitionSpec as P

HD = 128
BLOCK = 128
KMAX = 16
GROUP = 4
AXES = ("ctx", "tp")
NX, NYH, NC, NYL, NZ = 4, 2, 2, 2, 8
SLOTS = NX * NYH * NC
SCALE2 = HD ** (-0.5) * math.log2(math.e)
CHUNKS = 2
LOW = -1e30


def pairs(move):
    out = []
    for x in range(NX):
        for y in range(4):
            for c in range(NC):
                for z in range(NZ):
                    x2, y2, c2, z2 = move(x, y, c, z)
                    x2, y2, c2, z2 = x2 % NX, y2 % 4, c2 % NC, z2 % NZ

                    def index(x, y, c, z):
                        return (x * 4 + (y // 2) * 2 + c) * 16 + (y % 2) * 8 + z

                    out.append((index(x, y, c, z), index(x2, y2, c2, z2)))
    return out


MOVES = {
    "x+": pairs(lambda x, y, c, z: (x + 1, y, c, z)),
    "x-": pairs(lambda x, y, c, z: (x - 1, y, c, z)),
    "z+": pairs(lambda x, y, c, z: (x, y, c, z + 1)),
    "z-": pairs(lambda x, y, c, z: (x, y, c, z - 1)),
    "core": pairs(lambda x, y, c, z: (x, y, c + 1, z)),
    "y_near": pairs(lambda x, y, c, z: (x, y ^ 1, c, z)),
    "y_far": pairs(lambda x, y, c, z: (x, 3 - y, c, z)),
}


def send(array, move):
    return lax.ppermute(array, AXES, MOVES[move])


def attention_kernel(blocks_here, counts, listed, q_ref, *refs):
    pieces = refs[:SLOTS]
    out_ref, kv, scores, top, total, acc, sems = refs[SLOTS:]
    copies = []
    for slot in range(SLOTS):
        copy = pltpu.make_async_copy(
            pieces[slot], kv.at[:, pl.ds(slot * 512, 512), :], sems.at[slot]
        )
        copy.start()
        copies.append(copy)
    for copy in copies:
        copy.wait()

    def block_of(row, j, count):
        j = jnp.minimum(j, count - 1)
        return pl.multiple_of(listed[row * KMAX + j] * BLOCK, BLOCK)

    def both(which, row, pair, count):
        one = block_of(row, 2 * pair, count)
        two = block_of(row, 2 * pair + 1, count)
        return jnp.concatenate([kv[which, pl.ds(one, BLOCK), :], kv[which, pl.ds(two, BLOCK), :]], 0)

    def one_row(row, carry):
        count = counts[row]
        n_pairs = (count + 1) // 2
        here = pl.ds(pl.multiple_of(row * BLOCK, BLOCK), BLOCK)
        q = jnp.concatenate([q_ref[here, g * HD : (g + 1) * HD] for g in range(GROUP)], 0)
        top[...] = jnp.full(top.shape, LOW, jnp.float32)

        def first(pair, inner):
            keys = both(0, row, pair, count)
            s = lax.dot_general(
                q, keys, (((1,), (1,)), ((), ())), preferred_element_type=jnp.float32
            )
            left = s[:, :BLOCK]
            right = jnp.where(2 * pair + 1 < count, s[:, BLOCK:], LOW)
            scores[pair, :, :BLOCK] = left
            scores[pair, :, BLOCK:] = right
            top[...] = jnp.maximum(top[...], jnp.maximum(left, right))
            return inner

        lax.fori_loop(0, n_pairs, first, 0)
        row_top = jnp.max(top[...], axis=1, keepdims=True) * SCALE2
        top[...] = jnp.broadcast_to(row_top, top.shape)
        total[...] = jnp.zeros(total.shape, jnp.float32)
        acc[...] = jnp.zeros(acc.shape, jnp.float32)

        def second(pair, inner):
            vals = both(1, row, pair, count)
            high = top[...]
            left = jnp.exp2(scores[pair, :, :BLOCK] * SCALE2 - high)
            right = jnp.exp2(scores[pair, :, BLOCK:] * SCALE2 - high)
            total[...] += left + right
            weights = jnp.concatenate([left.astype(jnp.bfloat16), right.astype(jnp.bfloat16)], 1)
            acc[...] += jnp.dot(weights, vals, preferred_element_type=jnp.float32)
            return inner

        lax.fori_loop(0, n_pairs, second, 0)
        result = (acc[...] / jnp.sum(total[...], axis=1, keepdims=True)).astype(jnp.bfloat16)
        for g in range(GROUP):
            out_ref[here, g * HD : (g + 1) * HD] = result[g * BLOCK : (g + 1) * BLOCK, :]
        return carry

    lax.fori_loop(0, blocks_here, one_row, 0)


def attention(counts, listed, q, pieces):
    tok, width = q.shape
    rows = GROUP * BLOCK
    smem = pl.BlockSpec(memory_space=pltpu.SMEM)
    vmem = pl.BlockSpec(memory_space=pltpu.VMEM)
    return pl.pallas_call(
        functools.partial(attention_kernel, tok // BLOCK),
        out_shape=jax.ShapeDtypeStruct((tok, width), jnp.bfloat16),
        in_specs=[smem, smem, vmem] + [pl.BlockSpec(memory_space=pl.ANY)] * SLOTS,
        out_specs=vmem,
        scratch_shapes=[
            pltpu.VMEM((2, SLOTS * 512, HD), jnp.bfloat16),
            pltpu.VMEM((KMAX // 2, rows, 2 * BLOCK), jnp.float32),
            pltpu.VMEM((rows, HD), jnp.float32),
            pltpu.VMEM((rows, HD), jnp.float32),
            pltpu.VMEM((rows, HD), jnp.float32),
            pltpu.SemaphoreType.DMA((SLOTS,)),
        ],
        compiler_params=pltpu.CompilerParams(vmem_limit_bytes=20 * 2**20),
        cost_estimate=pl.CostEstimate(
            flops=tok * 2048 * GROUP * HD * 8, bytes_accessed=6 * 2**20, transcendentals=tok * 2048 * 4
        ),
        name="attention",
    )(counts, listed, q, *pieces)


def project_kernel(n_recv, where, own_ref, near_ref, w_ref, w0a, w0b, w1a, w1b, *refs):
    recvs, out_ref = refs[:n_recv], refs[n_recv]
    mine = where[2] == 1
    value = jnp.dot(own_ref[...], w_ref[...], preferred_element_type=jnp.float32)
    half = near_ref.shape[1] // 2
    value += jnp.dot(
        near_ref[:, :half],
        jnp.where(mine, w0a[...], w0b[...]),
        preferred_element_type=jnp.float32,
    )
    value += jnp.dot(
        near_ref[:, half:],
        jnp.where(mine, w1a[...], w1b[...]),
        preferred_element_type=jnp.float32,
    )
    for recv in recvs:
        value += recv[...].astype(jnp.float32)
    out_ref[...] = value.astype(jnp.bfloat16)


def project(where, own, near, weights, parts, recvs):
    rows, depth = own.shape
    tile = 256
    n = 512 // tile
    grid_spec = pltpu.PrefetchScalarGridSpec(
        num_scalar_prefetch=1,
        grid=(n,),
        in_specs=[
            pl.BlockSpec((rows, depth), lambda j, w: (0, 0)),
            pl.BlockSpec((rows, depth), lambda j, w: (0, 0)),
            pl.BlockSpec((depth, tile), lambda j, w: (0, w[0] * n + j)),
        ]
        + [pl.BlockSpec((depth // 2, tile), lambda j, w: (0, w[1] * n + j))] * 4
        + [pl.BlockSpec((rows, tile), lambda j, w: (0, j))] * len(recvs),
        out_specs=pl.BlockSpec((rows, tile), lambda j, w: (0, j)),
    )
    return pl.pallas_call(
        functools.partial(project_kernel, len(recvs)),
        out_shape=jax.ShapeDtypeStruct((rows, 512), jnp.bfloat16),
        grid_spec=grid_spec,
        compiler_params=pltpu.CompilerParams(vmem_limit_bytes=12 * 2**20),
        cost_estimate=pl.CostEstimate(
            flops=2 * rows * 2 * depth * 512, bytes_accessed=3 * 2**20, transcendentals=0
        ),
        name="project",
    )(where, own, near, weights, *parts, *recvs)


def shards(queries, keys_values, block_list, out_weight):
    ctx = lax.axis_index("ctx")
    tp = lax.axis_index("tp")
    x, yh, c = ctx // 4, (ctx // 2) % 2, ctx % 2
    yl, z = tp // NZ, tp % NZ
    tok = queries.shape[0]
    width = queries.shape[1]

    head = yl * 4 + z // 2
    far_head = (1 - yl) * 4 + z // 2
    own = lax.dynamic_slice_in_dim(keys_values, head * HD, HD, 2)
    for_far = lax.dynamic_slice_in_dim(keys_values, far_head * HD, HD, 2)
    far = send(for_far, "y_far")
    from_left = send(own, "x+")
    from_right = send(own, "x-")

    half = NZ * 512
    quarter = half // 2

    def for_neighbour(link):
        return lax.dynamic_slice(
            out_weight, (link * 256, (1 - yl) * half + c * quarter), (256, quarter)
        )

    near_part = send(for_neighbour(0), "y_near")

    far_left = send(far, "x+")
    far_right = send(far, "x-")
    far_weight, _ = lax.optimization_barrier((for_neighbour(1), far))
    far_part = send(far_weight, "y_far")
    two_own = send(from_left, "x+")
    two_far = send(far_right, "x-")
    here = [own, far, from_right, far_right, two_own, two_far, from_left, far_left]
    there = [send(piece, "core") for piece in here]
    pieces = []
    for at in range(len(here)):
        pieces += [here[at], there[at]]
    near_other = send(near_part, "core")
    far_other = send(far_part, "core")
    parts = [near_part, near_other, far_part, far_other]

    shard = block_list // 4
    sx, sy, sc = shard // 4, (shard // 2) % 2, shard % 2
    slot = ((sx - x) % NX) * 4 + ((sy - yh) % 2) * 2 + (sc - c) % 2
    placed = jnp.where(block_list >= 0, slot * 4 + block_list % 4, 0).astype(jnp.int32)
    counts = jnp.sum((block_list >= 0).astype(jnp.int32), axis=1)

    rows = tok // CHUNKS
    per = rows // BLOCK
    attended, near = [], []
    for k in range(CHUNKS):
        done = attention(
            counts[k * per : (k + 1) * per],
            placed[k * per : (k + 1) * per].reshape(-1),
            queries[k * rows : (k + 1) * rows],
            pieces,
        )
        attended.append(done)
        near.append(send(done, "y_near"))

    def where(target):
        target = target % NZ
        return jnp.stack(
            [yl * NZ + target, target % 4, (target // 4 == c).astype(jnp.int32)]
        ).astype(jnp.int32)

    def step(k, target, recvs):
        return project(where(target), attended[k], near[k], out_weight, parts, recvs)

    up = [[] for _ in range(CHUNKS)]
    down = [[] for _ in range(CHUNKS)]
    for distance in (4, 3, 2, 1):
        for k in range(CHUNKS):
            if distance < 4 or k % 2 == 0:
                up[k] = [send(step(k, z + distance, up[k]), "z+")]
            if distance < 4 or k % 2 == 1:
                down[k] = [send(step(k, z - distance, down[k]), "z-")]
    results = [step(k, z, up[k] + down[k]) for k in range(CHUNKS)]
    return jnp.concatenate(results, 0)


def solution(mesh):
    in_specs = (P("ctx", "tp"), P(None, "ctx", None), P("ctx", None), P("tp", None))
    return jax.shard_map(
        shards, mesh=mesh, in_specs=in_specs, out_specs=P("ctx", "tp"), check_vma=False
    )
```

time: 350 us -> 149 us (0.43)
  waiting for transfers between devices: 231 us -> 22.2 us
  matrix products: 56.3 us -> 0 us
  Pallas kernels: 0 us -> 56.3 us
  starting transfers between devices: 2.72 us -> 37.8 us
  other arithmetic: 18.2 us -> 2.34 us
  between operations: 13.5 us -> 0.33 us
    reduce_scatter x1 -> x0, waiting for transfers between devices: 118 us -> none  [shards(): lax.psum_scatter(partial_value.astype(jnp.bfloat16), 'tp', scatter_dimens...]
    ppermute x15 -> x35, waiting for transfers between devices: 112 us -> 22.2 us  [send(): return lax.ppermute(array, AXES, MOVES[move])]
    dot_general x33 -> x0, matrix products: 56.3 us -> none  [the longest x16 31.2 us: slice_update(): jnp.einsum('kgtu,ukd->kgtd', weights.astype(jnp.bfloat16), vals, preferre...]
    pallas_call x0 -> x18, Pallas kernels: none -> 56.3 us  [the longest x16 42.3 us: project(): pl.pallas_call(functools.partial(project_kernel, len(recvs)), out_shape=j...]
    ppermute x15 -> x35, starting transfers between devices: 2.72 us -> 37.8 us  [send(): return lax.ppermute(array, AXES, MOVES[move])]
    unnamed x4 -> x52, local copies, waits for them, and re-layouts: 1.39 us -> 22.2 us
    while x107 -> x0, local copies, waits for them, and re-layouts: 18.9 us -> none
    reduce_sum x16 -> x0, other arithmetic: 16.7 us -> none  [slice_update(): total = total * factor + jnp.sum(weights, axis=-1)]
  transfers between devices with their start and end apart: 16 -> 35, of which waited for: 16 -> 6; matrix products, arithmetic and copies ran while one was open for 2% -> 4% of each run, Pallas kernels for 0% -> 37%
where the time goes in v1:
time: 149 us; the launch traced here: 147 us
  Pallas kernels  56.3 us (38%)
  starting transfers between devices  37.8 us (25%)
  local copies, waits for them, and re-layouts  27.8 us (19%)
  waiting for transfers between devices  22.2 us (15%)
  other arithmetic  2.34 us (2%)
    pallas_call x16, Pallas kernels, project(): pl.pallas_call(functools.partial(project_kernel, len(recvs)), out_shape=j...  42.3 us
    ppermute x35, starting transfers between devices, send(): return lax.ppermute(array, AXES, MOVES[move])  37.8 us
    ppermute x35, waiting for transfers between devices, send(): return lax.ppermute(array, AXES, MOVES[move])  22.2 us
    unnamed x52, local copies, waits for them, and re-layouts  22.2 us
    pallas_call x2, Pallas kernels, attention(): pl.pallas_call(functools.partial(attention_kernel, tok // BLOCK), out_sha...  14 us
    dynamic_slice x1, local copies, waits for them, and re-layouts, for_neighbour(): lax.dynamic_slice(out_weight, (link * 256, (1 - yl) * half + c * quarter)...  3.14 us
  transfers between devices with their start and end apart: 35, of which 6 were waited for; matrix products, arithmetic and copies ran while one was open for 4% of the time, Pallas kernels for 37%

profile of v1, /device:TPU:6, one launch (start us, length us, event | category | flops | bytes accessed | tf_op | source)
XLA Modules:
  0.0 146.8 jit_solution(3999081541904172317)
XLA Ops:
  3.4 2.8 %collective-permute-start.1 = (bf16[2,512,128]{2,1,0:T(8,128)(2,1)S(1)}, bf16[2,512,128]{2,1,0:T(8,128)(2,1)S(1)}, u32[]{:S(2)}, u32[]{:S(2)}) collective-permute-start(bf16[2,512,128]{2,1,0:T(8,128)(2,1)S(1)} %get-tuple-element.9), channel_id=1, source_target_pairs={{0,40},{1,41},{2,42},{3,43},{4,44},{5,45},{6,46},{7,47},{16,56},{1... | collective-permute-start | bytes 786440 | tf_op jit(solution)/shard_map/ppermute | solution.py:51
  6.2 3.1 %constant_dynamic-slice_fusion.3 = (bf16[256,2048]{1,0:T(8,128)(2,1)}, bf16[256,2048]{1,0:T(8,128)(2,1)}) fusion(bf16[512,8192]{1,0:T(8,128)(2,1)} %w_ref.31, s32[]{:T(128)S(6)} %select_n.236), kind=kLoop, calls=%fused_computation.58 | loop fusion | bytes 4194308 | tf_op jit(solution)/shard_map/dynamic_slice | solution.py:214
  9.5 2.5 %collective-permute-done.1.refs_2_ = bf16[2,512,128]{2,1,0:T(8,128)(2,1)S(1)} collective-permute-done((bf16[2,512,128]{2,1,0:T(8,128)(2,1)S(1)}, bf16[2,512,128]{2,1,0:T(8,128)(2,1)S(1)}, u32[]{:S(2)}, u32[]{:S(2)}) %collective-permute-start.1) | collective-permute-done | bytes 262176 | tf_op jit(solution)/shard_map/ppermute | solution.py:51
  11.9 3.0 %collective-permute-start.18 = (bf16[256,2048]{1,0:T(8,128)(2,1)}, bf16[256,2048]{1,0:T(8,128)(2,1)S(1)}, u32[]{:S(2)}, u32[]{:S(2)}) collective-permute-start(bf16[256,2048]{1,0:T(8,128)(2,1)} %get-tuple-element.6), channel_id=1, source_target_pairs={{0,40},{1,41},{2,42},{3,43},{4,44},{5,45},{6,46},{7,47},{16,56},{1... | collective-permute-start | bytes 3145736 | tf_op jit(solution)/shard_map/ppermute | solution.py:51
  18.3 5.3 %collective-permute-done.13.refs_14_ = bf16[2,512,128]{2,1,0:T(8,128)(2,1)S(1)} collective-permute-done((bf16[2,512,128]{2,1,0:T(8,128)(2,1)S(1)}, bf16[2,512,128]{2,1,0:T(8,128)(2,1)S(1)}, u32[]{:S(2)}, u32[]{:S(2)}) %collective-permute-start.13) | collective-permute-done | bytes 262176 | tf_op jit(solution)/shard_map/ppermute | solution.py:51
  23.6 2.6 %collective-permute-done.5.refs_6_ = bf16[2,512,128]{2,1,0:T(8,128)(2,1)S(1)} collective-permute-done((bf16[2,512,128]{2,1,0:T(8,128)(2,1)S(1)}, bf16[2,512,128]{2,1,0:T(8,128)(2,1)S(1)}, u32[]{:S(2)}, u32[]{:S(2)}) %collective-permute-start.5) | collective-permute-done | bytes 262176 | tf_op jit(solution)/shard_map/ppermute | solution.py:51
  29.9 4.8 %collective-permute-done.8.refs_8_ = bf16[2,512,128]{2,1,0:T(8,128)(2,1)} collective-permute-done((bf16[2,512,128]{2,1,0:T(8,128)(2,1)S(1)}, bf16[2,512,128]{2,1,0:T(8,128)(2,1)}, u32[]{:S(2)}, u32[]{:S(2)}) %collective-permute-start.8) | collective-permute-done | bytes 262176 | tf_op jit(solution)/shard_map/ppermute | solution.py:51
  37.5 5.5 %collective-permute-done.10.refs_10_ = bf16[2,512,128]{2,1,0:T(8,128)(2,1)} collective-permute-done((bf16[2,512,128]{2,1,0:T(8,128)(2,1)}, bf16[2,512,128]{2,1,0:T(8,128)(2,1)}, u32[]{:S(2)}, u32[]{:S(2)}) %collective-permute-start.10) | collective-permute-done | bytes 262176 | tf_op jit(solution)/shard_map/ppermute | solution.py:51
  52.8 6.9 %attention.2.own_ref = bf16[256,512]{1,0:T(8,128)(2,1)} custom-call(s32[2]{0:T(128)S(1)} %get-tuple-element.17.counts, s32[32]{0:T(128)S(1)} %reshape.6.listed, bf16[256,512]{1,0:T(8,128)(2,1)S(1)} %get-tuple-element.11.q_ref, bf16[2,512,128]{2,1,0:T(8,128)(2,1)S(1)} %get-tuple-element.10.refs_0_, bf16[2,512,128]{2,1,0:T(8,128)(2,1)S(1)} %copy-done.14, ...), custom_call_target="tpu_custom_call" | custom-call | flops 2147483648 | bytes 6291456 | tf_op jit(solution)/shard_map/attention/pallas_call | solution.py:125
  62.7 7.1 %attention.3.own_ref = bf16[256,512]{1,0:T(8,128)(2,1)S(1)} custom-call(s32[2]{0:T(128)S(1)} %get-tuple-element.18.counts, s32[32]{0:T(128)S(1)} %reshape.7.listed, bf16[256,512]{1,0:T(8,128)(2,1)S(1)} %get-tuple-element.12.q_ref, bf16[2,512,128]{2,1,0:T(8,128)(2,1)S(1)} %copy-done.3, bf16[2,512,128]{2,1,0:T(8,128)(2,1)S(1)} %copy-done.15, ...), custom_call_target="tpu_custom_call" | custom-call | flops 2147483648 | bytes 6291456 | tf_op jit(solution)/shard_map/attention/pallas_call | solution.py:125
  72.1 3.4 %copy-done = bf16[512,8192]{1,0:T(8,128)(2,1)S(1)} copy-done((bf16[512,8192]{1,0:T(8,128)(2,1)S(1)}, bf16[512,8192]{1,0:T(8,128)(2,1)}, u32[]{:S(2)}) %copy-start) | copy-done | bytes 8388632
  75.5 2.5 %project.16 = bf16[256,512]{1,0:T(8,128)(2,1)S(1)} custom-call(s32[3]{0:T(128)S(1)} %pad_add_fusion.4.where, bf16[256,512]{1,0:T(8,128)(2,1)} %attention.2.own_ref, bf16[256,512]{1,0:T(8,128)(2,1)} %collective-permute-done.15.near_ref, bf16[512,8192]{1,0:T(8,128)(2,1)S(1)} %copy-done, bf16[256,2048]{1,0:T(8,128)(2,1)S(1)} %collective-permute-done.16.w0a, ...), custom_call_target="tpu_custom_call" | custom-call | flops 268435456 | bytes 3145728 | tf_op jit(solution)/shard_map/project/pallas_call | solution.py:182
  80.0 2.4 %project.27 = bf16[256,512]{1,0:T(8,128)(2,1)S(1)} custom-call(s32[3]{0:T(128)S(1)} %pad_add_fusion.8.where, bf16[256,512]{1,0:T(8,128)(2,1)S(1)} %attention.3.own_ref, bf16[256,512]{1,0:T(8,128)(2,1)} %collective-permute-done.27.near_ref, bf16[512,8192]{1,0:T(8,128)(2,1)S(1)} %copy-done, bf16[256,2048]{1,0:T(8,128)(2,1)S(1)} %collective-permute-done.16.w0a, ...), custom_call_target="tpu_custom_call" | custom-call | flops 268435456 | bytes 3145728 | tf_op jit(solution)/shard_map/project/pallas_call | solution.py:182
  82.4 4.1 %collective-permute-start.31 = (bf16[256,512]{1,0:T(8,128)(2,1)S(1)}, bf16[256,512]{1,0:T(8,128)(2,1)S(1)}, u32[]{:S(2)}, u32[]{:S(2)}) collective-permute-start(bf16[256,512]{1,0:T(8,128)(2,1)S(1)} %project.27), channel_id=1, source_target_pairs={{0,7},{1,0},{2,1},{3,2},{4,3},{5,4},{6,5},{7,6},{16,23},{17,16},{1... | collective-permute-start | bytes 786440 | tf_op jit(solution)/shard_map/ppermute | solution.py:51
  86.6 2.5 %project.20 = bf16[256,512]{1,0:T(8,128)(2,1)S(1)} custom-call(s32[3]{0:T(128)S(1)} %pad_add_fusion.7.where, bf16[256,512]{1,0:T(8,128)(2,1)} %attention.2.own_ref, bf16[256,512]{1,0:T(8,128)(2,1)} %collective-permute-done.15.near_ref, bf16[512,8192]{1,0:T(8,128)(2,1)S(1)} %copy-done, bf16[256,2048]{1,0:T(8,128)(2,1)S(1)} %collective-permute-done.16.w0a, ...), custom_call_target="tpu_custom_call" | custom-call | flops 268435456 | bytes 3145728 | tf_op jit(solution)/shard_map/project/pallas_call | solution.py:182
  91.2 2.4 %project.24 = bf16[256,512]{1,0:T(8,128)(2,1)S(1)} custom-call(s32[3]{0:T(128)S(1)} %pad_add_fusion.3.where, bf16[256,512]{1,0:T(8,128)(2,1)S(1)} %attention.3.own_ref, bf16[256,512]{1,0:T(8,128)(2,1)} %collective-permute-done.27.near_ref, bf16[512,8192]{1,0:T(8,128)(2,1)S(1)} %copy-done, bf16[256,2048]{1,0:T(8,128)(2,1)S(1)} %collective-permute-done.16.w0a, ...), custom_call_target="tpu_custom_call" | custom-call | flops 268435456 | bytes 3145728 | tf_op jit(solution)/shard_map/project/pallas_call | solution.py:182
  93.7 2.5 %project.17 = bf16[256,512]{1,0:T(8,128)(2,1)S(1)} custom-call(s32[3]{0:T(128)S(1)} %pad_add_fusion.3.where, bf16[256,512]{1,0:T(8,128)(2,1)} %attention.2.own_ref, bf16[256,512]{1,0:T(8,128)(2,1)} %collective-permute-done.15.near_ref, bf16[512,8192]{1,0:T(8,128)(2,1)S(1)} %copy-done, bf16[256,2048]{1,0:T(8,128)(2,1)S(1)} %collective-permute-done.16.w0a, ...), custom_call_target="tpu_custom_call" | custom-call | flops 268435456 | bytes 3145728 | tf_op jit(solution)/shard_map/project/pallas_call | solution.py:182
  96.4 2.4 %project.28 = bf16[256,512]{1,0:T(8,128)(2,1)S(1)} custom-call(s32[3]{0:T(128)S(1)} %pad_add_fusion.7.where, bf16[256,512]{1,0:T(8,128)(2,1)S(1)} %attention.3.own_ref, bf16[256,512]{1,0:T(8,128)(2,1)} %collective-permute-done.27.near_ref, bf16[512,8192]{1,0:T(8,128)(2,1)S(1)} %copy-done, bf16[256,2048]{1,0:T(8,128)(2,1)S(1)} %collective-permute-done.16.w0a, ...), custom_call_target="tpu_custom_call" | custom-call | flops 268435456 | bytes 3145728 | tf_op jit(solution)/shard_map/project/pallas_call | solution.py:182
  98.8 3.3 %collective-permute-start.32 = (bf16[256,512]{1,0:T(8,128)(2,1)S(1)}, bf16[256,512]{1,0:T(8,128)(2,1)S(1)}, u32[]{:S(2)}, u32[]{:S(2)}) collective-permute-start(bf16[256,512]{1,0:T(8,128)(2,1)S(1)} %project.28), channel_id=1, source_target_pairs={{0,7},{1,0},{2,1},{3,2},{4,3},{5,4},{6,5},{7,6},{16,23},{17,16},{1... | collective-permute-start | bytes 786440 | tf_op jit(solution)/shard_map/ppermute | solution.py:51
  102.2 2.5 %project.21 = bf16[256,512]{1,0:T(8,128)(2,1)S(1)} custom-call(s32[3]{0:T(128)S(1)} %pad_add_fusion.6.where, bf16[256,512]{1,0:T(8,128)(2,1)} %attention.2.own_ref, bf16[256,512]{1,0:T(8,128)(2,1)} %collective-permute-done.15.near_ref, bf16[512,8192]{1,0:T(8,128)(2,1)S(1)} %copy-done, bf16[256,2048]{1,0:T(8,128)(2,1)S(1)} %collective-permute-done.16.w0a, ...), custom_call_target="tpu_custom_call" | custom-call | flops 268435456 | bytes 3145728 | tf_op jit(solution)/shard_map/project/pallas_call | solution.py:182
  106.8 2.4 %project.25 = bf16[256,512]{1,0:T(8,128)(2,1)S(1)} custom-call(s32[3]{0:T(128)S(1)} %pad_add_fusion.2.where, bf16[256,512]{1,0:T(8,128)(2,1)S(1)} %attention.3.own_ref, bf16[256,512]{1,0:T(8,128)(2,1)} %collective-permute-done.27.near_ref, bf16[512,8192]{1,0:T(8,128)(2,1)S(1)} %copy-done, bf16[256,2048]{1,0:T(8,128)(2,1)S(1)} %collective-permute-done.16.w0a, ...), custom_call_target="tpu_custom_call" | custom-call | flops 268435456 | bytes 3145728 | tf_op jit(solution)/shard_map/project/pallas_call | solution.py:182
  109.6 2.5 %project.18 = bf16[256,512]{1,0:T(8,128)(2,1)S(1)} custom-call(s32[3]{0:T(128)S(1)} %pad_add_fusion.2.where, bf16[256,512]{1,0:T(8,128)(2,1)} %attention.2.own_ref, bf16[256,512]{1,0:T(8,128)(2,1)} %collective-permute-done.15.near_ref, bf16[512,8192]{1,0:T(8,128)(2,1)S(1)} %copy-done, bf16[256,2048]{1,0:T(8,128)(2,1)S(1)} %collective-permute-done.16.w0a, ...), custom_call_target="tpu_custom_call" | custom-call | flops 268435456 | bytes 3145728 | tf_op jit(solution)/shard_map/project/pallas_call | solution.py:182
  112.2 2.4 %project.29 = bf16[256,512]{1,0:T(8,128)(2,1)S(1)} custom-call(s32[3]{0:T(128)S(1)} %pad_add_fusion.6.where, bf16[256,512]{1,0:T(8,128)(2,1)S(1)} %attention.3.own_ref, bf16[256,512]{1,0:T(8,128)(2,1)} %collective-permute-done.27.near_ref, bf16[512,8192]{1,0:T(8,128)(2,1)S(1)} %copy-done, bf16[256,2048]{1,0:T(8,128)(2,1)S(1)} %collective-permute-done.16.w0a, ...), custom_call_target="tpu_custom_call" | custom-call | flops 268435456 | bytes 3145728 | tf_op jit(solution)/shard_map/project/pallas_call | solution.py:182
  114.7 3.3 %collective-permute-start.33 = (bf16[256,512]{1,0:T(8,128)(2,1)S(1)}, bf16[256,512]{1,0:T(8,128)(2,1)S(1)}, u32[]{:S(2)}, u32[]{:S(2)}) collective-permute-start(bf16[256,512]{1,0:T(8,128)(2,1)S(1)} %project.29), channel_id=1, source_target_pairs={{0,7},{1,0},{2,1},{3,2},{4,3},{5,4},{6,5},{7,6},{16,23},{17,16},{1... | collective-permute-start | bytes 786440 | tf_op jit(solution)/shard_map/ppermute | solution.py:51
  118.1 3.1 %project.22 = bf16[256,512]{1,0:T(8,128)(2,1)} custom-call(s32[3]{0:T(128)S(1)} %pad_add_fusion.5.where, bf16[256,512]{1,0:T(8,128)(2,1)} %attention.2.own_ref, bf16[256,512]{1,0:T(8,128)(2,1)} %collective-permute-done.15.near_ref, bf16[512,8192]{1,0:T(8,128)(2,1)S(1)} %copy-done, bf16[256,2048]{1,0:T(8,128)(2,1)S(1)} %collective-permute-done.16.w0a, ...), custom_call_target="tpu_custom_call" | custom-call | flops 268435456 | bytes 3145728 | tf_op jit(solution)/shard_map/project/pallas_call | solution.py:182
  123.2 3.0 %project.26 = bf16[256,512]{1,0:T(8,128)(2,1)} custom-call(s32[3]{0:T(128)S(1)} %pad_add_fusion.1.where, bf16[256,512]{1,0:T(8,128)(2,1)S(1)} %attention.3.own_ref, bf16[256,512]{1,0:T(8,128)(2,1)} %collective-permute-done.27.near_ref, bf16[512,8192]{1,0:T(8,128)(2,1)S(1)} %copy-done, bf16[256,2048]{1,0:T(8,128)(2,1)S(1)} %collective-permute-done.16.w0a, ...), custom_call_target="tpu_custom_call" | custom-call | flops 268435456 | bytes 3145728 | tf_op jit(solution)/shard_map/project/pallas_call | solution.py:182
  126.3 3.1 %project.19 = bf16[256,512]{1,0:T(8,128)(2,1)} custom-call(s32[3]{0:T(128)S(1)} %pad_add_fusion.1.where, bf16[256,512]{1,0:T(8,128)(2,1)} %attention.2.own_ref, bf16[256,512]{1,0:T(8,128)(2,1)} %collective-permute-done.15.near_ref, bf16[512,8192]{1,0:T(8,128)(2,1)S(1)} %copy-done, bf16[256,2048]{1,0:T(8,128)(2,1)S(1)} %collective-permute-done.16.w0a, ...), custom_call_target="tpu_custom_call" | custom-call | flops 268435456 | bytes 3145728 | tf_op jit(solution)/shard_map/project/pallas_call | solution.py:182
  129.5 3.0 %project.30 = bf16[256,512]{1,0:T(8,128)(2,1)} custom-call(s32[3]{0:T(128)S(1)} %pad_add_fusion.5.where, bf16[256,512]{1,0:T(8,128)(2,1)S(1)} %attention.3.own_ref, bf16[256,512]{1,0:T(8,128)(2,1)} %collective-permute-done.27.near_ref, bf16[512,8192]{1,0:T(8,128)(2,1)S(1)} %copy-done, bf16[256,2048]{1,0:T(8,128)(2,1)S(1)} %collective-permute-done.16.w0a, ...), custom_call_target="tpu_custom_call" | custom-call | flops 268435456 | bytes 3145728 | tf_op jit(solution)/shard_map/project/pallas_call | solution.py:182
  132.5 3.2 %collective-permute-start.34 = (bf16[256,512]{1,0:T(8,128)(2,1)}, bf16[256,512]{1,0:T(8,128)(2,1)}, u32[]{:S(2)}, u32[]{:S(2)}) collective-permute-start(bf16[256,512]{1,0:T(8,128)(2,1)} %project.30), channel_id=1, source_target_pairs={{0,7},{1,0},{2,1},{3,2},{4,3},{5,4},{6,5},{7,6},{16,23},{17,16},{1... | collective-permute-start | bytes 786440 | tf_op jit(solution)/shard_map/ppermute | solution.py:51
  137.4 3.4 %copy-done.1 = bf16[512,8192]{1,0:T(8,128)(2,1)S(1)} copy-done((bf16[512,8192]{1,0:T(8,128)(2,1)S(1)}, bf16[512,8192]{1,0:T(8,128)(2,1)}, u32[]{:S(2)}) %copy-start.1) | copy-done | bytes 8388632
  140.7 2.6 %project.23 = bf16[256,512]{1,0:T(8,128)(2,1)S(1)} custom-call(s32[3]{0:T(128)S(1)} %pad_add_fusion.where, bf16[256,512]{1,0:T(8,128)(2,1)} %attention.2.own_ref, bf16[256,512]{1,0:T(8,128)(2,1)} %collective-permute-done.15.near_ref, bf16[512,8192]{1,0:T(8,128)(2,1)S(1)} %copy-done.1, bf16[256,2048]{1,0:T(8,128)(2,1)S(1)} %collective-permute-done.16.w0a, ...), custom_call_target="tpu_custom_call" | custom-call | flops 268435456 | bytes 3145728 | tf_op jit(solution)/shard_map/project/pallas_call | solution.py:182
  143.4 2.6 %project.31 = bf16[256,512]{1,0:T(8,128)(2,1)S(1)} custom-call(s32[3]{0:T(128)S(1)} %pad_add_fusion.where, bf16[256,512]{1,0:T(8,128)(2,1)S(1)} %attention.3.own_ref, bf16[256,512]{1,0:T(8,128)(2,1)} %collective-permute-done.27.near_ref, bf16[512,8192]{1,0:T(8,128)(2,1)S(1)} %copy-done.1, bf16[256,2048]{1,0:T(8,128)(2,1)S(1)} %collective-permute-done.16.w0a, ...), custom_call_target="tpu_custom_call" | custom-call | flops 268435456 | bytes 3145728 | tf_op jit(solution)/shard_map/project/pallas_call | solution.py:182
  (126 shorter events, 40.1 us)
Async XLA Ops:
  1.1 13.8 %collective-permute-start.7 = (bf16[2,512,128]{2,1,0:T(8,128)(2,1)S(1)}, bf16[2,512,128]{2,1,0:T(8,128)(2,1)S(1)}, u32[]{:S(2)}, u32[]{:S(2)}) collective-permute-start(bf16[2,512,128]{2,1,0:T(8,128)(2,1)S(1)} %get-tuple-element.10.refs_0_), channel_id=1, source_target_pairs={{0,64},{1,65},{2,66},{3,67},{4,68},{5,69},{6,70},{7,71},{16,80},{1... | collective-permute-start | bytes 786440 | tf_op jit(solution)/shard_map/ppermute | solution.py:51
  3.4 13.2 %collective-permute-start.3 = (bf16[2,512,128]{2,1,0:T(8,128)(2,1)S(1)}, bf16[2,512,128]{2,1,0:T(8,128)(2,1)S(1)}, u32[]{:S(2)}, u32[]{:S(2)}) collective-permute-start(bf16[2,512,128]{2,1,0:T(8,128)(2,1)S(1)} %get-tuple-element.10.refs_0_), channel_id=1, source_target_pairs={{0,192},{1,193},{2,194},{3,195},{4,196},{5,197},{6,198},{7,199},{1... | collective-permute-start | bytes 786440 | tf_op jit(solution)/shard_map/ppermute | solution.py:51
  3.4 8.6 %collective-permute-start.1 = (bf16[2,512,128]{2,1,0:T(8,128)(2,1)S(1)}, bf16[2,512,128]{2,1,0:T(8,128)(2,1)S(1)}, u32[]{:S(2)}, u32[]{:S(2)}) collective-permute-start(bf16[2,512,128]{2,1,0:T(8,128)(2,1)S(1)} %get-tuple-element.9), channel_id=1, source_target_pairs={{0,40},{1,41},{2,42},{3,43},{4,44},{5,45},{6,46},{7,47},{16,56},{1... | collective-permute-start | bytes 786440 | tf_op jit(solution)/shard_map/ppermute | solution.py:51
  9.3 33.7 %collective-permute-start.16 = (bf16[256,2048]{1,0:T(8,128)(2,1)}, bf16[256,2048]{1,0:T(8,128)(2,1)S(1)}, u32[]{:S(2)}, u32[]{:S(2)}) collective-permute-start(bf16[256,2048]{1,0:T(8,128)(2,1)} %get-tuple-element.8), channel_id=1, source_target_pairs={{0,8},{1,9},{2,10},{3,11},{4,12},{5,13},{6,14},{7,15},{16,24},{17,... | collective-permute-start | bytes 3145736 | tf_op jit(solution)/shard_map/ppermute | solution.py:51
  11.9 31.6 %collective-permute-start.18 = (bf16[256,2048]{1,0:T(8,128)(2,1)}, bf16[256,2048]{1,0:T(8,128)(2,1)S(1)}, u32[]{:S(2)}, u32[]{:S(2)}) collective-permute-start(bf16[256,2048]{1,0:T(8,128)(2,1)} %get-tuple-element.6), channel_id=1, source_target_pairs={{0,40},{1,41},{2,42},{3,43},{4,44},{5,45},{6,46},{7,47},{16,56},{1... | collective-permute-start | bytes 3145736 | tf_op jit(solution)/shard_map/ppermute | solution.py:51
  14.9 8.7 %collective-permute-start.13 = (bf16[2,512,128]{2,1,0:T(8,128)(2,1)S(1)}, bf16[2,512,128]{2,1,0:T(8,128)(2,1)S(1)}, u32[]{:S(2)}, u32[]{:S(2)}) collective-permute-start(bf16[2,512,128]{2,1,0:T(8,128)(2,1)S(1)} %collective-permute-done.1.refs_2_), channel_id=1, source_target_pairs={{0,64},{1,65},{2,66},{3,67},{4,68},{5,69},{6,70},{7,71},{16,80},{1... | collective-permute-start | bytes 786440 | tf_op jit(solution)/shard_map/ppermute | solution.py:51
  16.6 9.6 %collective-permute-start.5 = (bf16[2,512,128]{2,1,0:T(8,128)(2,1)S(1)}, bf16[2,512,128]{2,1,0:T(8,128)(2,1)S(1)}, u32[]{:S(2)}, u32[]{:S(2)}) collective-permute-start(bf16[2,512,128]{2,1,0:T(8,128)(2,1)S(1)} %collective-permute-done.1.refs_2_), channel_id=1, source_target_pairs={{0,192},{1,193},{2,194},{3,195},{4,196},{5,197},{6,198},{7,199},{1... | collective-permute-start | bytes 786440 | tf_op jit(solution)/shard_map/ppermute | solution.py:51
  17.7 11.1 %collective-permute-start.2 = (bf16[2,512,128]{2,1,0:T(8,128)(2,1)S(1)}, bf16[2,512,128]{2,1,0:T(8,128)(2,1)}, u32[]{:S(2)}, u32[]{:S(2)}) collective-permute-start(bf16[2,512,128]{2,1,0:T(8,128)(2,1)S(1)} %collective-permute-done.1.refs_2_), channel_id=1, source_target_pairs={{0,16},{1,17},{2,18},{3,19},{4,20},{5,21},{6,22},{7,23},{16,0},{17... | collective-permute-start | bytes 786440 | tf_op jit(solution)/shard_map/ppermute | solution.py:51
  27.0 7.7 %collective-permute-start.8 = (bf16[2,512,128]{2,1,0:T(8,128)(2,1)S(1)}, bf16[2,512,128]{2,1,0:T(8,128)(2,1)}, u32[]{:S(2)}, u32[]{:S(2)}) collective-permute-start(bf16[2,512,128]{2,1,0:T(8,128)(2,1)S(1)} %collective-permute-done.7.refs_12_), channel_id=1, source_target_pairs={{0,64},{1,65},{2,66},{3,67},{4,68},{5,69},{6,70},{7,71},{16,80},{1... | collective-permute-start | bytes 786440 | tf_op jit(solution)/shard_map/ppermute | solution.py:51
  28.7 6.8 %collective-permute-start.4 = (bf16[2,512,128]{2,1,0:T(8,128)(2,1)S(1)}, bf16[2,512,128]{2,1,0:T(8,128)(2,1)S(1)}, u32[]{:S(2)}, u32[]{:S(2)}) collective-permute-start(bf16[2,512,128]{2,1,0:T(8,128)(2,1)S(1)} %collective-permute-done.3.refs_4_), channel_id=1, source_target_pairs={{0,16},{1,17},{2,18},{3,19},{4,20},{5,21},{6,22},{7,23},{16,0},{17... | collective-permute-start | bytes 786440 | tf_op jit(solution)/shard_map/ppermute | solution.py:51
  29.4 6.8 %collective-permute-start.14 = (bf16[2,512,128]{2,1,0:T(8,128)(2,1)}, bf16[2,512,128]{2,1,0:T(8,128)(2,1)S(1)}, u32[]{:S(2)}, u32[]{:S(2)}) collective-permute-start(bf16[2,512,128]{2,1,0:T(8,128)(2,1)} %copy-done.16), channel_id=1, source_target_pairs={{0,16},{1,17},{2,18},{3,19},{4,20},{5,21},{6,22},{7,23},{16,0},{17... | collective-permute-start | bytes 786440 | tf_op jit(solution)/shard_map/ppermute | solution.py:51
  34.7 8.3 %collective-permute-start.10 = (bf16[2,512,128]{2,1,0:T(8,128)(2,1)}, bf16[2,512,128]{2,1,0:T(8,128)(2,1)}, u32[]{:S(2)}, u32[]{:S(2)}) collective-permute-start(bf16[2,512,128]{2,1,0:T(8,128)(2,1)} %copy-done.18), channel_id=1, source_target_pairs={{0,192},{1,193},{2,194},{3,195},{4,196},{5,197},{6,198},{7,199},{1... | collective-permute-start | bytes 786440 | tf_op jit(solution)/shard_map/ppermute | solution.py:51
  36.3 8.9 %collective-permute-start.6 = (bf16[2,512,128]{2,1,0:T(8,128)(2,1)}, bf16[2,512,128]{2,1,0:T(8,128)(2,1)}, u32[]{:S(2)}, u32[]{:S(2)}) collective-permute-start(bf16[2,512,128]{2,1,0:T(8,128)(2,1)} %copy-done.18), channel_id=1, source_target_pairs={{0,16},{1,17},{2,18},{3,19},{4,20},{5,21},{6,22},{7,23},{16,0},{17... | collective-permute-start | bytes 786440 | tf_op jit(solution)/shard_map/ppermute | solution.py:51
  37.0 8.2 %collective-permute-start.9 = (bf16[2,512,128]{2,1,0:T(8,128)(2,1)}, bf16[2,512,128]{2,1,0:T(8,128)(2,1)}, u32[]{:S(2)}, u32[]{:S(2)}) collective-permute-start(bf16[2,512,128]{2,1,0:T(8,128)(2,1)} %collective-permute-done.8.refs_8_), channel_id=1, source_target_pairs={{0,16},{1,17},{2,18},{3,19},{4,20},{5,21},{6,22},{7,23},{16,0},{17... | collective-permute-start | bytes 786440 | tf_op jit(solution)/shard_map/ppermute | solution.py:51
  43.0 29.0 %collective-permute-start.17 = (bf16[256,2048]{1,0:T(8,128)(2,1)S(1)}, bf16[256,2048]{1,0:T(8,128)(2,1)S(1)}, u32[]{:S(2)}, u32[]{:S(2)}) collective-permute-start(bf16[256,2048]{1,0:T(8,128)(2,1)S(1)} %collective-permute-done.16.w0a), channel_id=1, source_target_pairs={{0,16},{1,17},{2,18},{3,19},{4,20},{5,21},{6,22},{7,23},{16,0},{17... | collective-permute-start | bytes 3145736 | tf_op jit(solution)/shard_map/ppermute | solution.py:51
  43.5 28.5 %collective-permute-start.19 = (bf16[256,2048]{1,0:T(8,128)(2,1)S(1)}, bf16[256,2048]{1,0:T(8,128)(2,1)}, u32[]{:S(2)}, u32[]{:S(2)}) collective-permute-start(bf16[256,2048]{1,0:T(8,128)(2,1)S(1)} %collective-permute-done.18.w1a), channel_id=1, source_target_pairs={{0,16},{1,17},{2,18},{3,19},{4,20},{5,21},{6,22},{7,23},{16,0},{17... | collective-permute-start | bytes 3145736 | tf_op jit(solution)/shard_map/ppermute | solution.py:51
  59.7 12.3 %collective-permute-start.15 = (bf16[256,512]{1,0:T(8,128)(2,1)}, bf16[256,512]{1,0:T(8,128)(2,1)}, u32[]{:S(2)}, u32[]{:S(2)}) collective-permute-start(bf16[256,512]{1,0:T(8,128)(2,1)} %attention.2.own_ref), channel_id=1, source_target_pairs={{0,8},{1,9},{2,10},{3,11},{4,12},{5,13},{6,14},{7,15},{16,24},{17,... | collective-permute-start | bytes 786440 | tf_op jit(solution)/shard_map/ppermute | solution.py:51
  69.9 10.1 %collective-permute-start.27 = (bf16[256,512]{1,0:T(8,128)(2,1)S(1)}, bf16[256,512]{1,0:T(8,128)(2,1)}, u32[]{:S(2)}, u32[]{:S(2)}) collective-permute-start(bf16[256,512]{1,0:T(8,128)(2,1)S(1)} %attention.3.own_ref), channel_id=1, source_target_pairs={{0,8},{1,9},{2,10},{3,11},{4,12},{5,13},{6,14},{7,15},{16,24},{17,... | collective-permute-start | bytes 786440 | tf_op jit(solution)/shard_map/ppermute | solution.py:51
  78.0 15.8 %collective-permute-start.20 = (bf16[256,512]{1,0:T(8,128)(2,1)S(1)}, bf16[256,512]{1,0:T(8,128)(2,1)S(1)}, u32[]{:S(2)}, u32[]{:S(2)}) collective-permute-start(bf16[256,512]{1,0:T(8,128)(2,1)S(1)} %project.16), channel_id=1, source_target_pairs={{0,1},{1,2},{2,3},{3,4},{4,5},{5,6},{6,7},{7,0},{16,17},{17,18},{1... | collective-permute-start | bytes 786440 | tf_op jit(solution)/shard_map/ppermute | solution.py:51
  82.4 14.0 %collective-permute-start.31 = (bf16[256,512]{1,0:T(8,128)(2,1)S(1)}, bf16[256,512]{1,0:T(8,128)(2,1)S(1)}, u32[]{:S(2)}, u32[]{:S(2)}) collective-permute-start(bf16[256,512]{1,0:T(8,128)(2,1)S(1)} %project.27), channel_id=1, source_target_pairs={{0,7},{1,0},{2,1},{3,2},{4,3},{5,4},{6,5},{7,6},{16,23},{17,16},{1... | collective-permute-start | bytes 786440 | tf_op jit(solution)/shard_map/ppermute | solution.py:51
  89.1 13.1 %collective-permute-start.24 = (bf16[256,512]{1,0:T(8,128)(2,1)S(1)}, bf16[256,512]{1,0:T(8,128)(2,1)S(1)}, u32[]{:S(2)}, u32[]{:S(2)}) collective-permute-start(bf16[256,512]{1,0:T(8,128)(2,1)S(1)} %project.20), channel_id=1, source_target_pairs={{0,7},{1,0},{2,1},{3,2},{4,3},{5,4},{6,5},{7,6},{16,23},{17,16},{1... | collective-permute-start | bytes 786440 | tf_op jit(solution)/shard_map/ppermute | solution.py:51
  93.6 13.2 %collective-permute-start.28 = (bf16[256,512]{1,0:T(8,128)(2,1)S(1)}, bf16[256,512]{1,0:T(8,128)(2,1)S(1)}, u32[]{:S(2)}, u32[]{:S(2)}) collective-permute-start(bf16[256,512]{1,0:T(8,128)(2,1)S(1)} %project.24), channel_id=1, source_target_pairs={{0,1},{1,2},{2,3},{3,4},{4,5},{5,6},{6,7},{7,0},{16,17},{17,18},{1... | collective-permute-start | bytes 786440 | tf_op jit(solution)/shard_map/ppermute | solution.py:51
  96.3 13.4 %collective-permute-start.21 = (bf16[256,512]{1,0:T(8,128)(2,1)S(1)}, bf16[256,512]{1,0:T(8,128)(2,1)S(1)}, u32[]{:S(2)}, u32[]{:S(2)}) collective-permute-start(bf16[256,512]{1,0:T(8,128)(2,1)S(1)} %project.17), channel_id=1, source_target_pairs={{0,1},{1,2},{2,3},{3,4},{4,5},{5,6},{6,7},{7,0},{16,17},{17,18},{1... | collective-permute-start | bytes 786440 | tf_op jit(solution)/shard_map/ppermute | solution.py:51
  98.8 13.4 %collective-permute-start.32 = (bf16[256,512]{1,0:T(8,128)(2,1)S(1)}, bf16[256,512]{1,0:T(8,128)(2,1)S(1)}, u32[]{:S(2)}, u32[]{:S(2)}) collective-permute-start(bf16[256,512]{1,0:T(8,128)(2,1)S(1)} %project.28), channel_id=1, source_target_pairs={{0,7},{1,0},{2,1},{3,2},{4,3},{5,4},{6,5},{7,6},{16,23},{17,16},{1... | collective-permute-start | bytes 786440 | tf_op jit(solution)/shard_map/ppermute | solution.py:51
  104.8 13.3 %collective-permute-start.25 = (bf16[256,512]{1,0:T(8,128)(2,1)S(1)}, bf16[256,512]{1,0:T(8,128)(2,1)S(1)}, u32[]{:S(2)}, u32[]{:S(2)}) collective-permute-start(bf16[256,512]{1,0:T(8,128)(2,1)S(1)} %project.21), channel_id=1, source_target_pairs={{0,7},{1,0},{2,1},{3,2},{4,3},{5,4},{6,5},{7,6},{16,23},{17,16},{1... | collective-permute-start | bytes 786440 | tf_op jit(solution)/shard_map/ppermute | solution.py:51
  109.3 14.0 %collective-permute-start.29 = (bf16[256,512]{1,0:T(8,128)(2,1)S(1)}, bf16[256,512]{1,0:T(8,128)(2,1)S(1)}, u32[]{:S(2)}, u32[]{:S(2)}) collective-permute-start(bf16[256,512]{1,0:T(8,128)(2,1)S(1)} %project.25), channel_id=1, source_target_pairs={{0,1},{1,2},{2,3},{3,4},{4,5},{5,6},{6,7},{7,0},{16,17},{17,18},{1... | collective-permute-start | bytes 786440 | tf_op jit(solution)/shard_map/ppermute | solution.py:51
  112.1 14.2 %collective-permute-start.22 = (bf16[256,512]{1,0:T(8,128)(2,1)S(1)}, bf16[256,512]{1,0:T(8,128)(2,1)S(1)}, u32[]{:S(2)}, u32[]{:S(2)}) collective-permute-start(bf16[256,512]{1,0:T(8,128)(2,1)S(1)} %project.18), channel_id=1, source_target_pairs={{0,1},{1,2},{2,3},{3,4},{4,5},{5,6},{6,7},{7,0},{16,17},{17,18},{1... | collective-permute-start | bytes 786440 | tf_op jit(solution)/shard_map/ppermute | solution.py:51
  114.7 14.8 %collective-permute-start.33 = (bf16[256,512]{1,0:T(8,128)(2,1)S(1)}, bf16[256,512]{1,0:T(8,128)(2,1)S(1)}, u32[]{:S(2)}, u32[]{:S(2)}) collective-permute-start(bf16[256,512]{1,0:T(8,128)(2,1)S(1)} %project.29), channel_id=1, source_target_pairs={{0,7},{1,0},{2,1},{3,2},{4,3},{5,4},{6,5},{7,6},{16,23},{17,16},{1... | collective-permute-start | bytes 786440 | tf_op jit(solution)/shard_map/ppermute | solution.py:51
  121.3 14.6 %collective-permute-start.26 = (bf16[256,512]{1,0:T(8,128)(2,1)}, bf16[256,512]{1,0:T(8,128)(2,1)}, u32[]{:S(2)}, u32[]{:S(2)}) collective-permute-start(bf16[256,512]{1,0:T(8,128)(2,1)} %project.22), channel_id=1, source_target_pairs={{0,7},{1,0},{2,1},{3,2},{4,3},{5,4},{6,5},{7,6},{16,23},{17,16},{1... | collective-permute-start | bytes 786440 | tf_op jit(solution)/shard_map/ppermute | solution.py:51
  126.3 17.1 %collective-permute-start.30 = (bf16[256,512]{1,0:T(8,128)(2,1)}, bf16[256,512]{1,0:T(8,128)(2,1)}, u32[]{:S(2)}, u32[]{:S(2)}) collective-permute-start(bf16[256,512]{1,0:T(8,128)(2,1)} %project.26), channel_id=1, source_target_pairs={{0,1},{1,2},{2,3},{3,4},{4,5},{5,6},{6,7},{7,0},{16,17},{17,18},{1... | collective-permute-start | bytes 786440 | tf_op jit(solution)/shard_map/ppermute | solution.py:51
  129.5 7.9 %collective-permute-start.23 = (bf16[256,512]{1,0:T(8,128)(2,1)}, bf16[256,512]{1,0:T(8,128)(2,1)}, u32[]{:S(2)}, u32[]{:S(2)}) collective-permute-start(bf16[256,512]{1,0:T(8,128)(2,1)} %project.19), channel_id=1, source_target_pairs={{0,1},{1,2},{2,3},{3,4},{4,5},{5,6},{6,7},{7,0},{16,17},{17,18},{1... | collective-permute-start | bytes 786440 | tf_op jit(solution)/shard_map/ppermute | solution.py:51
  132.5 10.9 %collective-permute-start.34 = (bf16[256,512]{1,0:T(8,128)(2,1)}, bf16[256,512]{1,0:T(8,128)(2,1)}, u32[]{:S(2)}, u32[]{:S(2)}) collective-permute-start(bf16[256,512]{1,0:T(8,128)(2,1)} %project.30), channel_id=1, source_target_pairs={{0,7},{1,0},{2,1},{3,2},{4,3},{5,4},{6,5},{7,6},{16,23},{17,16},{1... | collective-permute-start | bytes 786440 | tf_op jit(solution)/shard_map/ppermute | solution.py:51
  (29 other events, 156.9 us)

commit v2 on v1

v2 whole, which is shorter than its diff:
```python
import functools
import math

import jax
import jax.numpy as jnp
from jax import lax
from jax.experimental import pallas as pl
from jax.experimental.pallas import tpu as pltpu
from jax.sharding import PartitionSpec as P

HD = 128
BLOCK = 128
KMAX = 16
GROUP = 4
AXES = ("ctx", "tp")
NX, NYH, NC, NYL, NZ = 4, 2, 2, 2, 8
SLOTS = NX * NYH * NC
SCALE2 = HD ** (-0.5) * math.log2(math.e)
CHUNKS = 2
LOW = -1e30


def pairs(move):
    out = []
    for x in range(NX):
        for y in range(4):
            for c in range(NC):
                for z in range(NZ):
                    x2, y2, c2, z2 = move(x, y, c, z)
                    x2, y2, c2, z2 = x2 % NX, y2 % 4, c2 % NC, z2 % NZ

                    def index(x, y, c, z):
                        return (x * 4 + (y // 2) * 2 + c) * 16 + (y % 2) * 8 + z

                    out.append((index(x, y, c, z), index(x2, y2, c2, z2)))
    return out


MOVES = {
    "x+": pairs(lambda x, y, c, z: (x + 1, y, c, z)),
    "x-": pairs(lambda x, y, c, z: (x - 1, y, c, z)),
    "z+": pairs(lambda x, y, c, z: (x, y, c, z + 1)),
    "z-": pairs(lambda x, y, c, z: (x, y, c, z - 1)),
    "core": pairs(lambda x, y, c, z: (x, y, c + 1, z)),
    "y_near": pairs(lambda x, y, c, z: (x, y ^ 1, c, z)),
    "y_far": pairs(lambda x, y, c, z: (x, 3 - y, c, z)),
}


def send(array, move):
    return lax.ppermute(array, AXES, MOVES[move])


def attention_kernel(blocks_here, slots, counts, listed, q_ref, *refs):
    if slots:
        column, w_ref = refs[:2]
        pieces, refs = refs[2 : 2 + len(slots)], refs[2 + len(slots) :]
        out_ref, kv, wide_ref, scores, top, total, acc, sem = refs
        half = wide_ref.shape[1]
        start = pl.multiple_of(column[0] * half, half)
        fetch = pltpu.make_async_copy(w_ref.at[:, pl.ds(start, half)], wide_ref, sem)
        fetch.start()
        for piece, held in zip(pieces, slots):
            for at, slot in enumerate(held):
                value = piece[at] if len(held) > 1 else piece[...]
                kv[:, slot * 512 : (slot + 1) * 512, :] = value
    else:
        kv, out_ref, scores, top, total, acc = refs

    def block_of(row, j, count):
        j = jnp.minimum(j, count - 1)
        return pl.multiple_of(listed[row * KMAX + j] * BLOCK, BLOCK)

    def both(which, row, pair, count):
        one = block_of(row, 2 * pair, count)
        two = block_of(row, 2 * pair + 1, count)
        return jnp.concatenate([kv[which, pl.ds(one, BLOCK), :], kv[which, pl.ds(two, BLOCK), :]], 0)

    def one_row(row, carry):
        count = counts[row]
        n_pairs = (count + 1) // 2
        here = pl.ds(pl.multiple_of(row * BLOCK, BLOCK), BLOCK)
        q = jnp.concatenate([q_ref[here, g * HD : (g + 1) * HD] for g in range(GROUP)], 0)
        top[...] = jnp.full(top.shape, LOW, jnp.float32)

        def first(pair, inner):
            keys = both(0, row, pair, count)
            s = lax.dot_general(
                q, keys, (((1,), (1,)), ((), ())), preferred_element_type=jnp.float32
            )
            left = s[:, :BLOCK]
            right = jnp.where(2 * pair + 1 < count, s[:, BLOCK:], LOW)
            scores[pair, :, :BLOCK] = left
            scores[pair, :, BLOCK:] = right
            top[...] = jnp.maximum(top[...], jnp.maximum(left, right))
            return inner

        lax.fori_loop(0, n_pairs, first, 0)
        row_top = jnp.max(top[...], axis=1, keepdims=True) * SCALE2
        top[...] = jnp.broadcast_to(row_top, top.shape)
        total[...] = jnp.zeros(total.shape, jnp.float32)
        acc[...] = jnp.zeros(acc.shape, jnp.float32)

        def second(pair, inner):
            vals = both(1, row, pair, count)
            high = top[...]
            left = jnp.exp2(scores[pair, :, :BLOCK] * SCALE2 - high)
            right = jnp.exp2(scores[pair, :, BLOCK:] * SCALE2 - high)
            total[...] += left + right
            weights = jnp.concatenate([left.astype(jnp.bfloat16), right.astype(jnp.bfloat16)], 1)
            acc[...] += jnp.dot(weights, vals, preferred_element_type=jnp.float32)
            return inner

        lax.fori_loop(0, n_pairs, second, 0)
        result = (acc[...] / jnp.sum(total[...], axis=1, keepdims=True)).astype(jnp.bfloat16)
        for g in range(GROUP):
            out_ref[here, g * HD : (g + 1) * HD] = result[g * BLOCK : (g + 1) * BLOCK, :]
        return carry

    lax.fori_loop(0, blocks_here, one_row, 0)
    if slots:
        fetch.wait()


def attention(counts, listed, q, pieces, fetch=None):
    tok, width = q.shape
    rows = GROUP * BLOCK
    smem = pl.BlockSpec(memory_space=pltpu.SMEM)
    vmem = pl.BlockSpec(memory_space=pltpu.VMEM)
    out_shape = [jax.ShapeDtypeStruct((tok, width), jnp.bfloat16)]
    args, in_specs = [counts, listed, q], [smem, smem, vmem]
    scratch = [
        pltpu.VMEM((KMAX // 2, rows, 2 * BLOCK), jnp.float32),
        pltpu.VMEM((rows, HD), jnp.float32),
        pltpu.VMEM((rows, HD), jnp.float32),
        pltpu.VMEM((rows, HD), jnp.float32),
    ]
    slots = ()
    if fetch is not None:
        slots, column, weights = fetch
        args += [column, weights]
        in_specs += [smem, pl.BlockSpec(memory_space=pl.ANY)]
        depth, full = weights.shape
        out_shape.append(jax.ShapeDtypeStruct((2, SLOTS * 512, HD), jnp.bfloat16))
        out_shape.append(jax.ShapeDtypeStruct((depth, full // 2), jnp.bfloat16))
        scratch.append(pltpu.SemaphoreType.DMA)
    return pl.pallas_call(
        functools.partial(attention_kernel, tok // BLOCK, slots),
        out_shape=out_shape,
        in_specs=in_specs + [vmem] * len(pieces),
        out_specs=[vmem] * len(out_shape),
        scratch_shapes=scratch,
        compiler_params=pltpu.CompilerParams(vmem_limit_bytes=36 * 2**20),
        cost_estimate=pl.CostEstimate(
            flops=tok * 2048 * GROUP * HD * 8, bytes_accessed=6 * 2**20, transcendentals=tok * 2048 * 4
        ),
        name="attention",
    )(*args, *pieces)


def project_kernel(count, scalars, own_ref, near_ref, w_ref, w0a, w0b, w1a, w1b, *out_refs):
    core = scalars[0]
    half = near_ref.shape[1] // 2
    for i in range(count):
        target = scalars[1 + i]
        mine = target // 4 == core
        wide = pl.ds(pl.multiple_of(target * 512, 512), 512)
        part = pl.ds(pl.multiple_of((target % 4) * 512, 512), 512)
        value = jnp.dot(own_ref[...], w_ref[:, wide], preferred_element_type=jnp.float32)
        value += jnp.dot(
            near_ref[:, :half],
            jnp.where(mine, w0a[:, part], w0b[:, part]),
            preferred_element_type=jnp.float32,
        )
        value += jnp.dot(
            near_ref[:, half:],
            jnp.where(mine, w1a[:, part], w1b[:, part]),
            preferred_element_type=jnp.float32,
        )
        out_refs[i][...] = value.astype(jnp.bfloat16)


def project(core, targets, own, near, wide, parts):
    rows, depth = own.shape
    count = len(targets)
    smem = pl.BlockSpec(memory_space=pltpu.SMEM)
    vmem = pl.BlockSpec(memory_space=pltpu.VMEM)
    scalars = jnp.stack([core] + [t % NZ for t in targets]).astype(jnp.int32)
    return pl.pallas_call(
        functools.partial(project_kernel, count),
        out_shape=[jax.ShapeDtypeStruct((rows, 512), jnp.bfloat16)] * count,
        in_specs=[smem] + [vmem] * 7,
        out_specs=[vmem] * count,
        compiler_params=pltpu.CompilerParams(vmem_limit_bytes=36 * 2**20),
        cost_estimate=pl.CostEstimate(
            flops=2 * rows * 2 * depth * 512 * count, bytes_accessed=2**20 * count, transcendentals=0
        ),
        name="project",
    )(scalars, own, near, wide, *parts)


def shards(queries, keys_values, block_list, out_weight):
    ctx = lax.axis_index("ctx")
    tp = lax.axis_index("tp")
    x, yh, c = ctx // 4, (ctx // 2) % 2, ctx % 2
    yl, z = tp // NZ, tp % NZ
    tok = queries.shape[0]
    width = queries.shape[1]

    head = yl * 4 + z // 2
    far_head = (1 - yl) * 4 + z // 2
    own = lax.dynamic_slice_in_dim(keys_values, head * HD, HD, 2)
    for_far = lax.dynamic_slice_in_dim(keys_values, far_head * HD, HD, 2)
    far = send(for_far, "y_far")
    left = send(own, "x+")
    right = send(own, "x-")
    own_t = send(own, "core")

    half = NZ * 512
    quarter = half // 2

    def for_neighbour(weights, link):
        return lax.dynamic_slice(
            weights, (link * 256, (1 - yl) * half + c * quarter), (256, quarter)
        )

    weights_1, _ = lax.optimization_barrier((out_weight, own_t))
    near_part = send(for_neighbour(weights_1, 0), "y_near")

    far, left, right = lax.optimization_barrier((far, left, right))
    both = send(jnp.stack([far, left]), "x+")
    far_right = send(far, "x-")
    far_t, left_t, right_t = send(far, "core"), send(left, "core"), send(right, "core")
    weights_2, _ = lax.optimization_barrier((out_weight, far_t))
    far_part = send(for_neighbour(weights_2, 1), "y_far")
    two_far = send(far_right, "x-")
    far_right_t = send(far_right, "core")
    both_t = send(both, "core")
    two_far_t = send(two_far, "core")
    near_other = send(near_part, "core")
    far_other = send(far_part, "core")
    parts = [near_part, near_other, far_part, far_other]
    pieces = [own, own_t, far, far_t, right, right_t, far_right, far_right_t]
    pieces += [two_far, two_far_t, left, left_t, both, both_t]
    slots = ((0,), (1,), (2,), (3,), (4,), (5,), (6,), (7,))
    slots += ((10,), (11,), (12,), (13,), (14, 8), (15, 9))

    shard = block_list // 4
    sx, sy, sc = shard // 4, (shard // 2) % 2, shard % 2
    slot = ((sx - x) % NX) * 4 + ((sy - yh) % 2) * 2 + (sc - c) % 2
    placed = jnp.where(block_list >= 0, slot * 4 + block_list % 4, 0).astype(jnp.int32)
    counts = jnp.sum((block_list >= 0).astype(jnp.int32), axis=1)

    rows = tok // CHUNKS
    per = rows // BLOCK

    def attend(k, *rest):
        return attention(
            counts[k * per : (k + 1) * per],
            placed[k * per : (k + 1) * per].reshape(-1),
            queries[k * rows : (k + 1) * rows],
            *rest,
        )

    first, kv, wide = attend(0, pieces, (slots, yl.reshape(1), out_weight))
    attended = [first] + [attend(k, [kv])[0] for k in range(1, CHUNKS)]
    near = [send(done, "y_near") for done in attended]

    ways = []
    for k in range(CHUNKS):
        up, down = ((4, 3, 2, 1), (-3, -2, -1)) if k % 2 == 0 else ((3, 2, 1), (-4, -3, -2, -1))
        early = [up[0], down[0]]
        late = [*up[1:], *down[1:], 0]
        partial = {}
        for group in (early, late):
            done = project(c, [z + d for d in group], attended[k], near[k], wide, parts)
            partial.update(zip(group, done))
        ways.append((up, down, partial))

    def add(*terms):
        return sum(t.astype(jnp.float32) for t in terms).astype(jnp.bfloat16)

    moving = [[None, None] for _ in range(CHUNKS)]
    for step in range(4):
        for k in range(CHUNKS):
            up, down, partial = ways[k]
            for way, (order, move) in enumerate(((up, "z+"), (down, "z-"))):
                if step < len(order):
                    value = partial[order[step]]
                    if step:
                        value = add(moving[k][way], value)
                    moving[k][way] = send(value, move)
    results = [add(ways[k][2][0], *moving[k]) for k in range(CHUNKS)]
    return jnp.concatenate(results, 0)


def solution(mesh):
    in_specs = (P("ctx", "tp"), P(None, "ctx", None), P("ctx", None), P("tp", None))
    return jax.shard_map(
        shards, mesh=mesh, in_specs=in_specs, out_specs=P("ctx", "tp"), check_vma=False
    )
```

time: 149 us -> 140 us (0.940); the launches traced: 147 us -> 140 us
  Pallas kernels: 56.3 us -> 22.8 us
  waiting for transfers between devices: 22.2 us -> 54.8 us
  local copies, waits for them, and re-layouts: 27.8 us -> 23.5 us
  starting transfers between devices: 37.8 us -> 35.6 us
    pallas_call x18 -> x6, Pallas kernels: 56.3 us -> 22.8 us  [the longest x2 12.3 us: attention(): pl.pallas_call(functools.partial(attention_kernel, tok // BLOCK, slots),...]
    ppermute x35 -> x33, waiting for transfers between devices: 22.2 us -> 54.8 us  [send(): return lax.ppermute(array, AXES, MOVES[move])]
    unnamed x52 -> x44, local copies, waits for them, and re-layouts: 22.2 us -> 16.3 us
    ppermute x35 -> x33, starting transfers between devices: 37.8 us -> 35.6 us  [send(): return lax.ppermute(array, AXES, MOVES[move])]
    dynamic_slice x1 -> x2, local copies, waits for them, and re-layouts: 3.14 us -> 4.67 us  [for_neighbour(): lax.dynamic_slice(weights, (link * 256, (1 - yl) * half + c * quarter), (...]
  transfers between devices with their start and end apart: 35 -> 33, of which waited for: 6 -> 16; matrix products, arithmetic and copies ran while one was open for 4% -> 6% of each run, Pallas kernels for 37% -> 16%
where the time goes in v2:
time: 140 us
  waiting for transfers between devices  54.8 us (39%)
  starting transfers between devices  35.6 us (25%)
  local copies, waits for them, and re-layouts  23.5 us (17%)
  Pallas kernels  22.8 us (16%)
  other arithmetic  2.79 us (2%)
    ppermute x33, waiting for transfers between devices, send(): return lax.ppermute(array, AXES, MOVES[move])  54.8 us
    ppermute x33, starting transfers between devices, send(): return lax.ppermute(array, AXES, MOVES[move])  35.6 us
    unnamed x44, local copies, waits for them, and re-layouts  16.3 us
    pallas_call x2, Pallas kernels, attention(): pl.pallas_call(functools.partial(attention_kernel, tok // BLOCK, slots),...  12.3 us
    pallas_call x4, Pallas kernels, project(): pl.pallas_call(functools.partial(project_kernel, count), out_shape=[jax.S...  10.5 us
    dynamic_slice x2, local copies, waits for them, and re-layouts, for_neighbour(): lax.dynamic_slice(weights, (link * 256, (1 - yl) * half + c * quarter), (...  4.67 us
  transfers between devices with their start and end apart: 33, of which 16 were waited for; matrix products, arithmetic and copies ran while one was open for 6% of the time, Pallas kernels for 16%

profile of v2, /device:TPU:6, one launch (start us, length us, event | category | flops | bytes accessed | tf_op | source)
XLA Modules:
  0.0 139.9 jit_solution(17879650565699273689)
XLA Ops:
  1.1 3.1 %collective-permute-start.1 = (bf16[2,512,128]{2,1,0:T(8,128)(2,1)S(1)}, bf16[2,512,128]{2,1,0:T(8,128)(2,1)S(1)}, u32[]{:S(2)}, u32[]{:S(2)}) collective-permute-start(bf16[2,512,128]{2,1,0:T(8,128)(2,1)S(1)} %get-tuple-element.53), channel_id=1, source_target_pairs={{0,40},{1,41},{2,42},{3,43},{4,44},{5,45},{6,46},{7,47},{16,56},{1... | collective-permute-start | bytes 786440 | tf_op jit(solution)/shard_map/ppermute | solution.py:51
  4.7 1.5 %collective-permute-start.3 = (bf16[2,512,128]{2,1,0:T(8,128)(2,1)S(1)}, bf16[2,512,128]{2,1,0:T(8,128)(2,1)S(1)}, u32[]{:S(2)}, u32[]{:S(2)}) collective-permute-start(bf16[2,512,128]{2,1,0:T(8,128)(2,1)S(1)} %get-tuple-element.54.refs_2_), channel_id=1, source_target_pairs={{0,192},{1,193},{2,194},{3,195},{4,196},{5,197},{6,198},{7,199},{1... | collective-permute-start | bytes 786440 | tf_op jit(solution)/shard_map/ppermute | solution.py:51
  6.9 3.6 %collective-permute-done.1.refs_4_ = bf16[2,512,128]{2,1,0:T(8,128)(2,1)S(1)} collective-permute-done((bf16[2,512,128]{2,1,0:T(8,128)(2,1)S(1)}, bf16[2,512,128]{2,1,0:T(8,128)(2,1)S(1)}, u32[]{:S(2)}, u32[]{:S(2)}) %collective-permute-start.1) | collective-permute-done | bytes 262176 | tf_op jit(solution)/shard_map/ppermute | solution.py:51
  10.5 1.5 %collective-permute-done.2.refs_12_ = bf16[2,512,128]{2,1,0:T(8,128)(2,1)S(1)} collective-permute-done((bf16[2,512,128]{2,1,0:T(8,128)(2,1)S(1)}, bf16[2,512,128]{2,1,0:T(8,128)(2,1)S(1)}, u32[]{:S(2)}, u32[]{:S(2)}) %collective-permute-start.2) | collective-permute-done | bytes 262176 | tf_op jit(solution)/shard_map/ppermute | solution.py:51
  14.1 2.4 %constant_dynamic-slice_fusion = bf16[256,2048]{1,0:T(8,128)(2,1)} fusion(bf16[512,8192]{1,0:T(8,128)(2,1)} %refs_1_.1, s32[]{:T(128)S(6)} %select_n.155), kind=kLoop, calls=%fused_computation.59 | loop fusion | bytes 2097156 | tf_op jit(solution)/shard_map/dynamic_slice | solution.py:223
  17.3 2.3 %constant_dynamic-slice_fusion.3 = bf16[256,2048]{1,0:T(8,128)(2,1)} fusion(bf16[512,8192]{1,0:T(8,128)(2,1)} %refs_1_.1, s32[]{:T(128)S(6)} %select_n.155), kind=kLoop, calls=%fused_computation.64 | loop fusion | bytes 2097156 | tf_op jit(solution)/shard_map/dynamic_slice | solution.py:223
  22.0 1.5 %collective-permute-start.6 = (bf16[2,512,128]{2,1,0:T(8,128)(2,1)S(1)}, bf16[2,512,128]{2,1,0:T(8,128)(2,1)S(1)}, u32[]{:S(2)}, u32[]{:S(2)}) collective-permute-start(bf16[2,512,128]{2,1,0:T(8,128)(2,1)S(1)} %collective-permute-done.1.refs_4_), channel_id=1, source_target_pairs={{0,192},{1,193},{2,194},{3,195},{4,196},{5,197},{6,198},{7,199},{1... | collective-permute-start | bytes 786440 | tf_op jit(solution)/shard_map/ppermute | solution.py:51
  24.5 7.4 %collective-permute-done.6.refs_8_ = bf16[2,512,128]{2,1,0:T(8,128)(2,1)S(1)} collective-permute-done((bf16[2,512,128]{2,1,0:T(8,128)(2,1)S(1)}, bf16[2,512,128]{2,1,0:T(8,128)(2,1)S(1)}, u32[]{:S(2)}, u32[]{:S(2)}) %collective-permute-start.6) | collective-permute-done | bytes 262176 | tf_op jit(solution)/shard_map/ppermute | solution.py:51
  32.4 3.2 %collective-permute-done.11.refs_14_ = bf16[2,2,512,128]{3,2,1,0:T(8,128)(2,1)} collective-permute-done((bf16[2,2,512,128]{3,2,1,0:T(8,128)(2,1)}, bf16[2,2,512,128]{3,2,1,0:T(8,128)(2,1)}, u32[]{:S(2)}, u32[]{:S(2)}) %collective-permute-start.11) | collective-permute-done | bytes 524320 | tf_op jit(solution)/shard_map/ppermute | solution.py:51
  36.8 4.4 %collective-permute-done.8.refs_10_ = bf16[2,512,128]{2,1,0:T(8,128)(2,1)} collective-permute-done((bf16[2,512,128]{2,1,0:T(8,128)(2,1)S(1)}, bf16[2,512,128]{2,1,0:T(8,128)(2,1)}, u32[]{:S(2)}, u32[]{:S(2)}) %collective-permute-start.8) | collective-permute-done | bytes 262176 | tf_op jit(solution)/shard_map/ppermute | solution.py:51
  42.2 4.2 %collective-permute-done.16.w1a = bf16[256,2048]{1,0:T(8,128)(2,1)S(1)} collective-permute-done((bf16[256,2048]{1,0:T(8,128)(2,1)}, bf16[256,2048]{1,0:T(8,128)(2,1)S(1)}, u32[]{:S(2)}, u32[]{:S(2)}) %collective-permute-start.16) | collective-permute-done | bytes 1048608 | tf_op jit(solution)/shard_map/ppermute | solution.py:51
  56.3 8.1 %attention.2 = (bf16[256,512]{1,0:T(8,128)(2,1)S(1)}, bf16[2,8192,128]{2,1,0:T(8,128)(2,1)S(1)}, bf16[512,4096]{1,0:T(8,128)(2,1)S(1)}) custom-call(s32[2]{0:T(128)S(1)} %get-tuple-element.61.counts, s32[32]{0:T(128)S(1)} %reshape.9.listed, bf16[256,512]{1,0:T(8,128)(2,1)S(1)} %get-tuple-element.55.q_ref, s32[1]{0:T(128)} %bitcast.7.refs_0_, ...), custom_call_target="tpu_custom_call" | custom-call | flops 2147483648 | bytes 6291456 | tf_op jit(solution)/shard_map/attention/pallas_call | solution.py:147
  64.4 2.0 %copy-done = bf16[512,4096]{1,0:T(8,128)(2,1)} copy-done((bf16[512,4096]{1,0:T(8,128)(2,1)}, bf16[512,4096]{1,0:T(8,128)(2,1)S(1)}, u32[]{:S(2)}) %copy-start) | copy-done | bytes 4194328
  66.5 4.3 %attention.3.own_ref = bf16[256,512]{1,0:T(8,128)(2,1)} custom-call(s32[2]{0:T(128)S(1)} %get-tuple-element.62.counts, s32[32]{0:T(128)S(1)} %reshape.11.listed, bf16[256,512]{1,0:T(8,128)(2,1)S(1)} %get-tuple-element.56.q_ref, bf16[2,8192,128]{2,1,0:T(8,128)(2,1)S(1)} %get-tuple-element.44.refs_0_), custom_call_target="tpu_custom_call" | custom-call | flops 2147483648 | bytes 6291456 | tf_op jit(solution)/shard_map/attention/pallas_call | solution.py:147
  71.4 1.5 %collective-permute-start.13 = (bf16[256,512]{1,0:T(8,128)(2,1)S(1)}, bf16[256,512]{1,0:T(8,128)(2,1)S(1)}, u32[]{:S(2)}, u32[]{:S(2)}) collective-permute-start(bf16[256,512]{1,0:T(8,128)(2,1)S(1)} %get-tuple-element.32.own_ref), channel_id=1, source_target_pairs={{0,8},{1,9},{2,10},{3,11},{4,12},{5,13},{6,14},{7,15},{16,24},{17,... | collective-permute-start | bytes 786440 | tf_op jit(solution)/shard_map/ppermute | solution.py:51
  73.1 6.7 %collective-permute-done.25.near_ref = bf16[256,512]{1,0:T(8,128)(2,1)} collective-permute-done((bf16[256,512]{1,0:T(8,128)(2,1)}, bf16[256,512]{1,0:T(8,128)(2,1)}, u32[]{:S(2)}, u32[]{:S(2)}) %collective-permute-start.25) | collective-permute-done | bytes 262176 | tf_op jit(solution)/shard_map/ppermute | solution.py:51
  79.8 2.2 %copy-done.1 = bf16[512,4096]{1,0:T(8,128)(2,1)S(1)} copy-done((bf16[512,4096]{1,0:T(8,128)(2,1)S(1)}, bf16[512,4096]{1,0:T(8,128)(2,1)}, u32[]{:S(2)}) %copy-start.1) | copy-done | bytes 4194328
  82.0 2.3 %project.7 = (bf16[256,512]{1,0:T(8,128)(2,1)S(1)}, bf16[256,512]{1,0:T(8,128)(2,1)S(1)}) custom-call(s32[3]{0:T(128)S(1)} %pad_add_fusion.1.scalars, bf16[256,512]{1,0:T(8,128)(2,1)} %attention.3.own_ref, bf16[256,512]{1,0:T(8,128)(2,1)} %collective-permute-done.25.near_ref, bf16[512,4096]{1,0:T(8,128)(2,1)S(1)} %copy-done.1, ...), custom_call_target="tpu_custom_call" | custom-call | flops 536870912 | bytes 2097152 | tf_op jit(solution)/shard_map/project/pallas_call | solution.py:189
  84.3 6.0 %collective-permute-start.29 = (bf16[256,512]{1,0:T(8,128)(2,1)S(1)}, bf16[256,512]{1,0:T(8,128)(2,1)S(1)}, u32[]{:S(2)}, u32[]{:S(2)}) collective-permute-start(bf16[256,512]{1,0:T(8,128)(2,1)S(1)} %get-tuple-element.49), channel_id=1, source_target_pairs={{0,7},{1,0},{2,1},{3,2},{4,3},{5,4},{6,5},{7,6},{16,23},{17,16},{1... | collective-permute-start | bytes 786440 | tf_op jit(solution)/shard_map/ppermute | solution.py:51
  90.3 2.0 %project.5 = (bf16[256,512]{1,0:T(8,128)(2,1)S(1)}, bf16[256,512]{1,0:T(8,128)(2,1)S(1)}) custom-call(s32[3]{0:T(128)S(1)} %pad_add_fusion.scalars, bf16[256,512]{1,0:T(8,128)(2,1)S(1)} %get-tuple-element.32.own_ref, bf16[256,512]{1,0:T(8,128)(2,1)S(1)} %collective-permute-done.13.near_ref, bf16[512,4096]{1,0:T(8,128)(2,1)S(1)} %copy-done.2, ...), custom_call_target="tpu_custom_call" | custom-call | flops 536870912 | bytes 2097152 | tf_op jit(solution)/shard_map/project/pallas_call | solution.py:189
  92.2 3.3 %collective-permute-start.22 = (bf16[256,512]{1,0:T(8,128)(2,1)S(1)}, bf16[256,512]{1,0:T(8,128)(2,1)S(1)}, u32[]{:S(2)}, u32[]{:S(2)}) collective-permute-start(bf16[256,512]{1,0:T(8,128)(2,1)S(1)} %get-tuple-element.41), channel_id=1, source_target_pairs={{0,7},{1,0},{2,1},{3,2},{4,3},{5,4},{6,5},{7,6},{16,23},{17,16},{1... | collective-permute-start | bytes 786440 | tf_op jit(solution)/shard_map/ppermute | solution.py:51
  95.5 3.2 %project.6 = (bf16[256,512]{1,0:T(8,128)(2,1)S(1)}, bf16[256,512]{1,0:T(8,128)(2,1)S(1)}, bf16[256,512]{1,0:T(8,128)(2,1)S(1)}, bf16[256,512]{1,0:T(8,128)(2,1)S...) custom-call(s32[7]{0:T(128)S(1)} %stack.75.scalars, bf16[256,512]{1,0:T(8,128)(2,1)} %attention.3.own_ref, ...), custom_call_target="tpu_custom_call" | custom-call | flops 1610612736 | bytes 6291456 | tf_op jit(solution)/shard_map/project/pallas_call | solution.py:189
  98.7 3.0 %project.4 = (bf16[256,512]{1,0:T(8,128)(2,1)S(1)}, bf16[256,512]{1,0:T(8,128)(2,1)S(1)}, bf16[256,512]{1,0:T(8,128)(2,1)S(1)}, bf16[256,512]{1,0:T(8,128)(2,1)S...) custom-call(s32[7]{0:T(128)S(1)} %stack.68.scalars, bf16[256,512]{1,0:T(8,128)(2,1)S(1)} %get-tuple-element.32.own_ref, ...), custom_call_target="tpu_custom_call" | custom-call | flops 1610612736 | bytes 6291456 | tf_op jit(solution)/shard_map/project/pallas_call | solution.py:189
  101.9 3.3 %collective-permute-start.30 = (bf16[256,512]{1,0:T(8,128)(2,1)S(1)}, bf16[256,512]{1,0:T(8,128)(2,1)S(1)}, u32[]{:S(2)}, u32[]{:S(2)}) collective-permute-start(bf16[256,512]{1,0:T(8,128)(2,1)S(1)} %add_convert_fusion.3), channel_id=1, source_target_pairs={{0,7},{1,0},{2,1},{3,2},{4,3},{5,4},{6,5},{7,6},{16,23},{17,16},{1... | collective-permute-start | bytes 786440 | tf_op jit(solution)/shard_map/ppermute | solution.py:51
  105.4 3.3 %collective-permute-start.23 = (bf16[256,512]{1,0:T(8,128)(2,1)S(1)}, bf16[256,512]{1,0:T(8,128)(2,1)S(1)}, u32[]{:S(2)}, u32[]{:S(2)}) collective-permute-start(bf16[256,512]{1,0:T(8,128)(2,1)S(1)} %add_convert_fusion.8), channel_id=1, source_target_pairs={{0,7},{1,0},{2,1},{3,2},{4,3},{5,4},{6,5},{7,6},{16,23},{17,16},{1... | collective-permute-start | bytes 786440 | tf_op jit(solution)/shard_map/ppermute | solution.py:51
  109.1 2.8 %collective-permute-done.30 = bf16[256,512]{1,0:T(8,128)(2,1)S(1)} collective-permute-done((bf16[256,512]{1,0:T(8,128)(2,1)S(1)}, bf16[256,512]{1,0:T(8,128)(2,1)S(1)}, u32[]{:S(2)}, u32[]{:S(2)}) %collective-permute-start.30) | collective-permute-done | bytes 262176 | tf_op jit(solution)/shard_map/ppermute | solution.py:51
  112.0 3.8 %collective-permute-start.31 = (bf16[256,512]{1,0:T(8,128)(2,1)S(1)}, bf16[256,512]{1,0:T(8,128)(2,1)S(1)}, u32[]{:S(2)}, u32[]{:S(2)}) collective-permute-start(bf16[256,512]{1,0:T(8,128)(2,1)S(1)} %add_convert_fusion.2), channel_id=1, source_target_pairs={{0,7},{1,0},{2,1},{3,2},{4,3},{5,4},{6,5},{7,6},{16,23},{17,16},{1... | collective-permute-start | bytes 786440 | tf_op jit(solution)/shard_map/ppermute | solution.py:51
  115.9 5.5 %collective-permute-done.19 = bf16[256,512]{1,0:T(8,128)(2,1)S(1)} collective-permute-done((bf16[256,512]{1,0:T(8,128)(2,1)S(1)}, bf16[256,512]{1,0:T(8,128)(2,1)S(1)}, u32[]{:S(2)}, u32[]{:S(2)}) %collective-permute-start.19) | collective-permute-done | bytes 262176 | tf_op jit(solution)/shard_map/ppermute | solution.py:51
  121.9 3.8 %collective-permute-start.32 = (bf16[256,512]{1,0:T(8,128)(2,1)S(1)}, bf16[256,512]{1,0:T(8,128)(2,1)S(1)}, u32[]{:S(2)}, u32[]{:S(2)}) collective-permute-start(bf16[256,512]{1,0:T(8,128)(2,1)S(1)} %add_convert_fusion.1), channel_id=1, source_target_pairs={{0,7},{1,0},{2,1},{3,2},{4,3},{5,4},{6,5},{7,6},{16,23},{17,16},{1... | collective-permute-start | bytes 786440 | tf_op jit(solution)/shard_map/ppermute | solution.py:51
  125.8 5.2 %collective-permute-done.20 = bf16[256,512]{1,0:T(8,128)(2,1)S(1)} collective-permute-done((bf16[256,512]{1,0:T(8,128)(2,1)S(1)}, bf16[256,512]{1,0:T(8,128)(2,1)S(1)}, u32[]{:S(2)}, u32[]{:S(2)}) %collective-permute-start.20) | collective-permute-done | bytes 262176 | tf_op jit(solution)/shard_map/ppermute | solution.py:51
  132.5 3.2 %collective-permute-done.24 = bf16[256,512]{1,0:T(8,128)(2,1)S(1)} collective-permute-done((bf16[256,512]{1,0:T(8,128)(2,1)S(1)}, bf16[256,512]{1,0:T(8,128)(2,1)S(1)}, u32[]{:S(2)}, u32[]{:S(2)}) %collective-permute-start.24) | collective-permute-done | bytes 262176 | tf_op jit(solution)/shard_map/ppermute | solution.py:51
  135.7 3.3 %collective-permute-done.21 = bf16[256,512]{1,0:T(8,128)(2,1)S(1)} collective-permute-done((bf16[256,512]{1,0:T(8,128)(2,1)S(1)}, bf16[256,512]{1,0:T(8,128)(2,1)S(1)}, u32[]{:S(2)}, u32[]{:S(2)}) %collective-permute-start.21) | collective-permute-done | bytes 262176 | tf_op jit(solution)/shard_map/ppermute | solution.py:51
  (111 shorter events, 25.9 us)
Async XLA Ops:
  1.1 9.4 %collective-permute-start.1 = (bf16[2,512,128]{2,1,0:T(8,128)(2,1)S(1)}, bf16[2,512,128]{2,1,0:T(8,128)(2,1)S(1)}, u32[]{:S(2)}, u32[]{:S(2)}) collective-permute-start(bf16[2,512,128]{2,1,0:T(8,128)(2,1)S(1)} %get-tuple-element.53), channel_id=1, source_target_pairs={{0,40},{1,41},{2,42},{3,43},{4,44},{5,45},{6,46},{7,47},{16,56},{1... | collective-permute-start | bytes 786440 | tf_op jit(solution)/shard_map/ppermute | solution.py:51
  4.2 7.8 %collective-permute-start.2 = (bf16[2,512,128]{2,1,0:T(8,128)(2,1)S(1)}, bf16[2,512,128]{2,1,0:T(8,128)(2,1)S(1)}, u32[]{:S(2)}, u32[]{:S(2)}) collective-permute-start(bf16[2,512,128]{2,1,0:T(8,128)(2,1)S(1)} %get-tuple-element.54.refs_2_), channel_id=1, source_target_pairs={{0,64},{1,65},{2,66},{3,67},{4,68},{5,69},{6,70},{7,71},{16,80},{1... | collective-permute-start | bytes 786440 | tf_op jit(solution)/shard_map/ppermute | solution.py:51
  4.7 8.7 %collective-permute-start.3 = (bf16[2,512,128]{2,1,0:T(8,128)(2,1)S(1)}, bf16[2,512,128]{2,1,0:T(8,128)(2,1)S(1)}, u32[]{:S(2)}, u32[]{:S(2)}) collective-permute-start(bf16[2,512,128]{2,1,0:T(8,128)(2,1)S(1)} %get-tuple-element.54.refs_2_), channel_id=1, source_target_pairs={{0,192},{1,193},{2,194},{3,195},{4,196},{5,197},{6,198},{7,199},{1... | collective-permute-start | bytes 786440 | tf_op jit(solution)/shard_map/ppermute | solution.py:51
  6.2 7.2 %collective-permute-start = (bf16[2,512,128]{2,1,0:T(8,128)(2,1)S(1)}, bf16[2,512,128]{2,1,0:T(8,128)(2,1)S(1)}, u32[]{:S(2)}, u32[]{:S(2)}) collective-permute-start(bf16[2,512,128]{2,1,0:T(8,128)(2,1)S(1)} %get-tuple-element.54.refs_2_), channel_id=1, source_target_pairs={{0,16},{1,17},{2,18},{3,19},{4,20},{5,21},{6,22},{7,23},{16,0},{17... | collective-permute-start | bytes 786440 | tf_op jit(solution)/shard_map/ppermute | solution.py:51
  13.4 3.2 %collective-permute-start.4 = (bf16[2,512,128]{2,1,0:T(8,128)(2,1)S(1)}, bf16[2,512,128]{2,1,0:T(8,128)(2,1)S(1)}, u32[]{:S(2)}, u32[]{:S(2)}) collective-permute-start(bf16[2,512,128]{2,1,0:T(8,128)(2,1)S(1)} %collective-permute-done.1.refs_4_), channel_id=1, source_target_pairs={{0,16},{1,17},{2,18},{3,19},{4,20},{5,21},{6,22},{7,23},{16,0},{17... | collective-permute-start | bytes 786440 | tf_op jit(solution)/shard_map/ppermute | solution.py:51
  16.5 25.7 %collective-permute-start.14 = (bf16[256,2048]{1,0:T(8,128)(2,1)}, bf16[256,2048]{1,0:T(8,128)(2,1)S(1)}, u32[]{:S(2)}, u32[]{:S(2)}) collective-permute-start(bf16[256,2048]{1,0:T(8,128)(2,1)} %constant_dynamic-slice_fusion), channel_id=1, source_target_pairs={{0,8},{1,9},{2,10},{3,11},{4,12},{5,13},{6,14},{7,15},{16,24},{17,... | collective-permute-start | bytes 3145736 | tf_op jit(solution)/shard_map/ppermute | solution.py:51
  19.6 26.8 %collective-permute-start.16 = (bf16[256,2048]{1,0:T(8,128)(2,1)}, bf16[256,2048]{1,0:T(8,128)(2,1)S(1)}, u32[]{:S(2)}, u32[]{:S(2)}) collective-permute-start(bf16[256,2048]{1,0:T(8,128)(2,1)} %constant_dynamic-slice_fusion.3), channel_id=1, source_target_pairs={{0,40},{1,41},{2,42},{3,43},{4,44},{5,45},{6,46},{7,47},{16,56},{1... | collective-permute-start | bytes 3145736 | tf_op jit(solution)/shard_map/ppermute | solution.py:51
  21.5 14.1 %collective-permute-start.11 = (bf16[2,2,512,128]{3,2,1,0:T(8,128)(2,1)}, bf16[2,2,512,128]{3,2,1,0:T(8,128)(2,1)}, u32[]{:S(2)}, u32[]{:S(2)}) collective-permute-start(bf16[2,2,512,128]{3,2,1,0:T(8,128)(2,1)} %pad_maximum_fusion), channel_id=1, source_target_pairs={{0,64},{1,65},{2,66},{3,67},{4,68},{5,69},{6,70},{7,71},{16,80},{1... | collective-permute-start | bytes 1572872 | tf_op jit(solution)/shard_map/ppermute | solution.py:51
  22.0 9.9 %collective-permute-start.6 = (bf16[2,512,128]{2,1,0:T(8,128)(2,1)S(1)}, bf16[2,512,128]{2,1,0:T(8,128)(2,1)S(1)}, u32[]{:S(2)}, u32[]{:S(2)}) collective-permute-start(bf16[2,512,128]{2,1,0:T(8,128)(2,1)S(1)} %collective-permute-done.1.refs_4_), channel_id=1, source_target_pairs={{0,192},{1,193},{2,194},{3,195},{4,196},{5,197},{6,198},{7,199},{1... | collective-permute-start | bytes 786440 | tf_op jit(solution)/shard_map/ppermute | solution.py:51
  24.3 11.3 %collective-permute-start.10 = (bf16[2,512,128]{2,1,0:T(8,128)(2,1)S(1)}, bf16[2,512,128]{2,1,0:T(8,128)(2,1)S(1)}, u32[]{:S(2)}, u32[]{:S(2)}) collective-permute-start(bf16[2,512,128]{2,1,0:T(8,128)(2,1)S(1)} %collective-permute-done.2.refs_12_), channel_id=1, source_target_pairs={{0,16},{1,17},{2,18},{3,19},{4,20},{5,21},{6,22},{7,23},{16,0},{17... | collective-permute-start | bytes 786440 | tf_op jit(solution)/shard_map/ppermute | solution.py:51
  31.9 9.3 %collective-permute-start.8 = (bf16[2,512,128]{2,1,0:T(8,128)(2,1)S(1)}, bf16[2,512,128]{2,1,0:T(8,128)(2,1)}, u32[]{:S(2)}, u32[]{:S(2)}) collective-permute-start(bf16[2,512,128]{2,1,0:T(8,128)(2,1)S(1)} %collective-permute-done.6.refs_8_), channel_id=1, source_target_pairs={{0,192},{1,193},{2,194},{3,195},{4,196},{5,197},{6,198},{7,199},{1... | collective-permute-start | bytes 786440 | tf_op jit(solution)/shard_map/ppermute | solution.py:51
  35.6 12.2 %collective-permute-start.12 = (bf16[2,2,512,128]{3,2,1,0:T(8,128)(2,1)}, bf16[2,2,512,128]{3,2,1,0:T(8,128)(2,1)}, u32[]{:S(2)}, u32[]{:S(2)}) collective-permute-start(bf16[2,2,512,128]{3,2,1,0:T(8,128)(2,1)} %collective-permute-done.11.refs_14_), channel_id=1, source_target_pairs={{0,16},{1,17},{2,18},{3,19},{4,20},{5,21},{6,22},{7,23},{16,0},{17... | collective-permute-start | bytes 1572872 | tf_op jit(solution)/shard_map/ppermute | solution.py:51
  36.3 11.5 %collective-permute-start.7 = (bf16[2,512,128]{2,1,0:T(8,128)(2,1)S(1)}, bf16[2,512,128]{2,1,0:T(8,128)(2,1)}, u32[]{:S(2)}, u32[]{:S(2)}) collective-permute-start(bf16[2,512,128]{2,1,0:T(8,128)(2,1)S(1)} %collective-permute-done.6.refs_8_), channel_id=1, source_target_pairs={{0,16},{1,17},{2,18},{3,19},{4,20},{5,21},{6,22},{7,23},{16,0},{17... | collective-permute-start | bytes 786440 | tf_op jit(solution)/shard_map/ppermute | solution.py:51
  41.2 6.6 %collective-permute-start.9 = (bf16[2,512,128]{2,1,0:T(8,128)(2,1)}, bf16[2,512,128]{2,1,0:T(8,128)(2,1)}, u32[]{:S(2)}, u32[]{:S(2)}) collective-permute-start(bf16[2,512,128]{2,1,0:T(8,128)(2,1)} %collective-permute-done.8.refs_10_), channel_id=1, source_target_pairs={{0,16},{1,17},{2,18},{3,19},{4,20},{5,21},{6,22},{7,23},{16,0},{17... | collective-permute-start | bytes 786440 | tf_op jit(solution)/shard_map/ppermute | solution.py:51
  42.2 37.6 %collective-permute-start.15 = (bf16[256,2048]{1,0:T(8,128)(2,1)S(1)}, bf16[256,2048]{1,0:T(8,128)(2,1)S(1)}, u32[]{:S(2)}, u32[]{:S(2)}) collective-permute-start(bf16[256,2048]{1,0:T(8,128)(2,1)S(1)} %collective-permute-done.14.w0a), channel_id=1, source_target_pairs={{0,16},{1,17},{2,18},{3,19},{4,20},{5,21},{6,22},{7,23},{16,0},{17... | collective-permute-start | bytes 3145736 | tf_op jit(solution)/shard_map/ppermute | solution.py:51
  46.4 33.4 %collective-permute-start.17 = (bf16[256,2048]{1,0:T(8,128)(2,1)S(1)}, bf16[256,2048]{1,0:T(8,128)(2,1)}, u32[]{:S(2)}, u32[]{:S(2)}) collective-permute-start(bf16[256,2048]{1,0:T(8,128)(2,1)S(1)} %collective-permute-done.16.w1a), channel_id=1, source_target_pairs={{0,16},{1,17},{2,18},{3,19},{4,20},{5,21},{6,22},{7,23},{16,0},{17... | collective-permute-start | bytes 3145736 | tf_op jit(solution)/shard_map/ppermute | solution.py:51
  70.7 9.1 %collective-permute-start.25 = (bf16[256,512]{1,0:T(8,128)(2,1)}, bf16[256,512]{1,0:T(8,128)(2,1)}, u32[]{:S(2)}, u32[]{:S(2)}) collective-permute-start(bf16[256,512]{1,0:T(8,128)(2,1)} %attention.3.own_ref), channel_id=1, source_target_pairs={{0,8},{1,9},{2,10},{3,11},{4,12},{5,13},{6,14},{7,15},{16,24},{17,... | collective-permute-start | bytes 786440 | tf_op jit(solution)/shard_map/ppermute | solution.py:51
  71.4 18.8 %collective-permute-start.13 = (bf16[256,512]{1,0:T(8,128)(2,1)S(1)}, bf16[256,512]{1,0:T(8,128)(2,1)S(1)}, u32[]{:S(2)}, u32[]{:S(2)}) collective-permute-start(bf16[256,512]{1,0:T(8,128)(2,1)S(1)} %get-tuple-element.32.own_ref), channel_id=1, source_target_pairs={{0,8},{1,9},{2,10},{3,11},{4,12},{5,13},{6,14},{7,15},{16,24},{17,... | collective-permute-start | bytes 786440 | tf_op jit(solution)/shard_map/ppermute | solution.py:51
  84.3 17.5 %collective-permute-start.29 = (bf16[256,512]{1,0:T(8,128)(2,1)S(1)}, bf16[256,512]{1,0:T(8,128)(2,1)S(1)}, u32[]{:S(2)}, u32[]{:S(2)}) collective-permute-start(bf16[256,512]{1,0:T(8,128)(2,1)S(1)} %get-tuple-element.49), channel_id=1, source_target_pairs={{0,7},{1,0},{2,1},{3,2},{4,3},{5,4},{6,5},{7,6},{16,23},{17,16},{1... | collective-permute-start | bytes 786440 | tf_op jit(solution)/shard_map/ppermute | solution.py:51
  90.3 14.9 %collective-permute-start.26 = (bf16[256,512]{1,0:T(8,128)(2,1)S(1)}, bf16[256,512]{1,0:T(8,128)(2,1)S(1)}, u32[]{:S(2)}, u32[]{:S(2)}) collective-permute-start(bf16[256,512]{1,0:T(8,128)(2,1)S(1)} %get-tuple-element.46), channel_id=1, source_target_pairs={{0,1},{1,2},{2,3},{3,4},{4,5},{5,6},{6,7},{7,0},{16,17},{17,18},{1... | collective-permute-start | bytes 786440 | tf_op jit(solution)/shard_map/ppermute | solution.py:51
  92.2 13.1 %collective-permute-start.22 = (bf16[256,512]{1,0:T(8,128)(2,1)S(1)}, bf16[256,512]{1,0:T(8,128)(2,1)S(1)}, u32[]{:S(2)}, u32[]{:S(2)}) collective-permute-start(bf16[256,512]{1,0:T(8,128)(2,1)S(1)} %get-tuple-element.41), channel_id=1, source_target_pairs={{0,7},{1,0},{2,1},{3,2},{4,3},{5,4},{6,5},{7,6},{16,23},{17,16},{1... | collective-permute-start | bytes 786440 | tf_op jit(solution)/shard_map/ppermute | solution.py:51
  95.5 13.2 %collective-permute-start.18 = (bf16[256,512]{1,0:T(8,128)(2,1)S(1)}, bf16[256,512]{1,0:T(8,128)(2,1)S(1)}, u32[]{:S(2)}, u32[]{:S(2)}) collective-permute-start(bf16[256,512]{1,0:T(8,128)(2,1)S(1)} %get-tuple-element.37), channel_id=1, source_target_pairs={{0,1},{1,2},{2,3},{3,4},{4,5},{5,6},{6,7},{7,0},{16,17},{17,18},{1... | collective-permute-start | bytes 786440 | tf_op jit(solution)/shard_map/ppermute | solution.py:51
  101.9 10.1 %collective-permute-start.30 = (bf16[256,512]{1,0:T(8,128)(2,1)S(1)}, bf16[256,512]{1,0:T(8,128)(2,1)S(1)}, u32[]{:S(2)}, u32[]{:S(2)}) collective-permute-start(bf16[256,512]{1,0:T(8,128)(2,1)S(1)} %add_convert_fusion.3), channel_id=1, source_target_pairs={{0,7},{1,0},{2,1},{3,2},{4,3},{5,4},{6,5},{7,6},{16,23},{17,16},{1... | collective-permute-start | bytes 786440 | tf_op jit(solution)/shard_map/ppermute | solution.py:51
  105.3 10.5 %collective-permute-start.27 = (bf16[256,512]{1,0:T(8,128)(2,1)S(1)}, bf16[256,512]{1,0:T(8,128)(2,1)S(1)}, u32[]{:S(2)}, u32[]{:S(2)}) collective-permute-start(bf16[256,512]{1,0:T(8,128)(2,1)S(1)} %add_convert_fusion.5), channel_id=1, source_target_pairs={{0,1},{1,2},{2,3},{3,4},{4,5},{5,6},{6,7},{7,0},{16,17},{17,18},{1... | collective-permute-start | bytes 786440 | tf_op jit(solution)/shard_map/ppermute | solution.py:51
  105.4 20.2 %collective-permute-start.23 = (bf16[256,512]{1,0:T(8,128)(2,1)S(1)}, bf16[256,512]{1,0:T(8,128)(2,1)S(1)}, u32[]{:S(2)}, u32[]{:S(2)}) collective-permute-start(bf16[256,512]{1,0:T(8,128)(2,1)S(1)} %add_convert_fusion.8), channel_id=1, source_target_pairs={{0,7},{1,0},{2,1},{3,2},{4,3},{5,4},{6,5},{7,6},{16,23},{17,16},{1... | collective-permute-start | bytes 786440 | tf_op jit(solution)/shard_map/ppermute | solution.py:51
  108.8 12.6 %collective-permute-start.19 = (bf16[256,512]{1,0:T(8,128)(2,1)S(1)}, bf16[256,512]{1,0:T(8,128)(2,1)S(1)}, u32[]{:S(2)}, u32[]{:S(2)}) collective-permute-start(bf16[256,512]{1,0:T(8,128)(2,1)S(1)} %add_convert_fusion.11), channel_id=1, source_target_pairs={{0,1},{1,2},{2,3},{3,4},{4,5},{5,6},{6,7},{7,0},{16,17},{17,18},{1... | collective-permute-start | bytes 786440 | tf_op jit(solution)/shard_map/ppermute | solution.py:51
  112.0 9.8 %collective-permute-start.31 = (bf16[256,512]{1,0:T(8,128)(2,1)S(1)}, bf16[256,512]{1,0:T(8,128)(2,1)S(1)}, u32[]{:S(2)}, u32[]{:S(2)}) collective-permute-start(bf16[256,512]{1,0:T(8,128)(2,1)S(1)} %add_convert_fusion.2), channel_id=1, source_target_pairs={{0,7},{1,0},{2,1},{3,2},{4,3},{5,4},{6,5},{7,6},{16,23},{17,16},{1... | collective-permute-start | bytes 786440 | tf_op jit(solution)/shard_map/ppermute | solution.py:51
  115.9 15.3 %collective-permute-start.28 = (bf16[256,512]{1,0:T(8,128)(2,1)S(1)}, bf16[256,512]{1,0:T(8,128)(2,1)S(1)}, u32[]{:S(2)}, u32[]{:S(2)}) collective-permute-start(bf16[256,512]{1,0:T(8,128)(2,1)S(1)} %add_convert_fusion.4), channel_id=1, source_target_pairs={{0,1},{1,2},{2,3},{3,4},{4,5},{5,6},{6,7},{7,0},{16,17},{17,18},{1... | collective-permute-start | bytes 786440 | tf_op jit(solution)/shard_map/ppermute | solution.py:51
  121.5 9.5 %collective-permute-start.20 = (bf16[256,512]{1,0:T(8,128)(2,1)S(1)}, bf16[256,512]{1,0:T(8,128)(2,1)S(1)}, u32[]{:S(2)}, u32[]{:S(2)}) collective-permute-start(bf16[256,512]{1,0:T(8,128)(2,1)S(1)} %add_convert_fusion.10), channel_id=1, source_target_pairs={{0,1},{1,2},{2,3},{3,4},{4,5},{5,6},{6,7},{7,0},{16,17},{17,18},{1... | collective-permute-start | bytes 786440 | tf_op jit(solution)/shard_map/ppermute | solution.py:51
  121.9 10.5 %collective-permute-start.32 = (bf16[256,512]{1,0:T(8,128)(2,1)S(1)}, bf16[256,512]{1,0:T(8,128)(2,1)S(1)}, u32[]{:S(2)}, u32[]{:S(2)}) collective-permute-start(bf16[256,512]{1,0:T(8,128)(2,1)S(1)} %add_convert_fusion.1), channel_id=1, source_target_pairs={{0,7},{1,0},{2,1},{3,2},{4,3},{5,4},{6,5},{7,6},{16,23},{17,16},{1... | collective-permute-start | bytes 786440 | tf_op jit(solution)/shard_map/ppermute | solution.py:51
  125.7 10.0 %collective-permute-start.24 = (bf16[256,512]{1,0:T(8,128)(2,1)S(1)}, bf16[256,512]{1,0:T(8,128)(2,1)S(1)}, u32[]{:S(2)}, u32[]{:S(2)}) collective-permute-start(bf16[256,512]{1,0:T(8,128)(2,1)S(1)} %add_convert_fusion.7), channel_id=1, source_target_pairs={{0,7},{1,0},{2,1},{3,2},{4,3},{5,4},{6,5},{7,6},{16,23},{17,16},{1... | collective-permute-start | bytes 786440 | tf_op jit(solution)/shard_map/ppermute | solution.py:51
  131.0 7.9 %collective-permute-start.21 = (bf16[256,512]{1,0:T(8,128)(2,1)S(1)}, bf16[256,512]{1,0:T(8,128)(2,1)S(1)}, u32[]{:S(2)}, u32[]{:S(2)}) collective-permute-start(bf16[256,512]{1,0:T(8,128)(2,1)S(1)} %add_convert_fusion.9), channel_id=1, source_target_pairs={{0,1},{1,2},{2,3},{3,4},{4,5},{5,6},{6,7},{7,0},{16,17},{17,18},{1... | collective-permute-start | bytes 786440 | tf_op jit(solution)/shard_map/ppermute | solution.py:51
  (23 other events, 162.0 us)

commit v3 on v2

v3 whole, which is shorter than its diff:
```python
import functools
import math

import jax
import jax.numpy as jnp
from jax import lax
from jax.experimental import pallas as pl
from jax.experimental.pallas import tpu as pltpu
from jax.sharding import PartitionSpec as P

HD = 128
BLOCK = 128
KMAX = 16
GROUP = 4
AXES = ("ctx", "tp")
NX, NYH, NC, NYL, NZ = 4, 2, 2, 2, 8
SLOTS = NX * NYH * NC
SCALE2 = HD ** (-0.5) * math.log2(math.e)
CHUNKS = 2
LOW = -1e30
VMEM_LIMIT = 60 * 2**20
FREE = pl.CostEstimate(flops=0, bytes_accessed=0, transcendentals=0)


def pairs(move):
    out = []
    for x in range(NX):
        for y in range(4):
            for c in range(NC):
                for z in range(NZ):
                    x2, y2, c2, z2 = move(x, y, c, z)
                    x2, y2, c2, z2 = x2 % NX, y2 % 4, c2 % NC, z2 % NZ

                    def index(x, y, c, z):
                        return (x * 4 + (y // 2) * 2 + c) * 16 + (y % 2) * 8 + z

                    out.append((index(x, y, c, z), index(x2, y2, c2, z2)))
    return out


MOVES = {
    "x+": pairs(lambda x, y, c, z: (x + 1, y, c, z)),
    "x-": pairs(lambda x, y, c, z: (x - 1, y, c, z)),
    "z+": pairs(lambda x, y, c, z: (x, y, c, z + 1)),
    "z-": pairs(lambda x, y, c, z: (x, y, c, z - 1)),
    "core": pairs(lambda x, y, c, z: (x, y, c + 1, z)),
    "y_near": pairs(lambda x, y, c, z: (x, y ^ 1, c, z)),
    "y_far": pairs(lambda x, y, c, z: (x, 3 - y, c, z)),
}


def send(array, move):
    return lax.ppermute(array, AXES, MOVES[move])


SMEM = pl.BlockSpec(memory_space=pltpu.SMEM)
VMEM = pl.BlockSpec(memory_space=pltpu.VMEM)
HBM = pl.BlockSpec(memory_space=pltpu.HBM)


def pick_kernel(at, kv_ref, w_ref, own_ref, far_ref, near_w_ref, far_w_ref, sems):
    def lanes(i, n):
        return pl.ds(pl.multiple_of(at[i] * n, n), n)

    rows, columns = near_w_ref.shape
    copies = [
        pltpu.make_async_copy(kv_ref.at[:, :, lanes(0, HD)], own_ref, sems.at[0]),
        pltpu.make_async_copy(kv_ref.at[:, :, lanes(1, HD)], far_ref, sems.at[1]),
        pltpu.make_async_copy(w_ref.at[pl.ds(0, rows), lanes(2, columns)], near_w_ref, sems.at[2]),
        pltpu.make_async_copy(w_ref.at[pl.ds(rows, rows), lanes(2, columns)], far_w_ref, sems.at[3]),
    ]
    for copy in copies:
        copy.start()
    for copy in copies:
        copy.wait()


def pick(at, keys_values, weights):
    two, tok, _ = keys_values.shape
    depth, full = weights.shape
    piece = jax.ShapeDtypeStruct((two, tok, HD), jnp.bfloat16)
    part = jax.ShapeDtypeStruct((depth // 2, full // 4), jnp.bfloat16)
    return pl.pallas_call(
        pick_kernel,
        out_shape=[piece, piece, part, part],
        in_specs=[SMEM, HBM, HBM],
        out_specs=[HBM] * 4,
        scratch_shapes=[pltpu.SemaphoreType.DMA((4,))],
        compiler_params=pltpu.CompilerParams(vmem_limit_bytes=VMEM_LIMIT),
        cost_estimate=FREE,
        name="pick",
    )(at, keys_values, weights)


def attention_kernel(blocks_here, slots, counts, listed, q_ref, *refs):
    pieces, refs = refs[: len(slots)], refs[len(slots) :]
    out_ref, kv, scores, top, total, acc, sems = refs
    copies = []
    for piece, held in zip(pieces, slots):
        for at, slot in enumerate(held):
            source = piece.at[at] if len(held) > 1 else piece
            copies.append(
                pltpu.make_async_copy(source, kv.at[:, pl.ds(slot * 512, 512), :], sems.at[slot])
            )
    for copy in copies:
        copy.start()
    for copy in copies:
        copy.wait()

    def block_of(row, j, count):
        j = jnp.minimum(j, count - 1)
        return pl.multiple_of(listed[row * KMAX + j] * BLOCK, BLOCK)

    def both(which, row, pair, count):
        one = block_of(row, 2 * pair, count)
        two = block_of(row, 2 * pair + 1, count)
        return jnp.concatenate([kv[which, pl.ds(one, BLOCK), :], kv[which, pl.ds(two, BLOCK), :]], 0)

    def one_row(row, carry):
        count = counts[row]
        n_pairs = (count + 1) // 2
        here = pl.ds(pl.multiple_of(row * BLOCK, BLOCK), BLOCK)
        q = jnp.concatenate([q_ref[here, g * HD : (g + 1) * HD] for g in range(GROUP)], 0)
        top[...] = jnp.full(top.shape, LOW, jnp.float32)

        def first(pair, inner):
            keys = both(0, row, pair, count)
            s = lax.dot_general(
                q, keys, (((1,), (1,)), ((), ())), preferred_element_type=jnp.float32
            )
            left = s[:, :BLOCK]
            right = jnp.where(2 * pair + 1 < count, s[:, BLOCK:], LOW)
            scores[pair, :, :BLOCK] = left
            scores[pair, :, BLOCK:] = right
            top[...] = jnp.maximum(top[...], jnp.maximum(left, right))
            return inner

        lax.fori_loop(0, n_pairs, first, 0)
        row_top = jnp.max(top[...], axis=1, keepdims=True) * SCALE2
        top[...] = jnp.broadcast_to(row_top, top.shape)
        total[...] = jnp.zeros(total.shape, jnp.float32)
        acc[...] = jnp.zeros(acc.shape, jnp.float32)

        def second(pair, inner):
            vals = both(1, row, pair, count)
            high = top[...]
            left = jnp.exp2(scores[pair, :, :BLOCK] * SCALE2 - high)
            right = jnp.exp2(scores[pair, :, BLOCK:] * SCALE2 - high)
            total[...] += left + right
            weights = jnp.concatenate([left.astype(jnp.bfloat16), right.astype(jnp.bfloat16)], 1)
            acc[...] += jnp.dot(weights, vals, preferred_element_type=jnp.float32)
            return inner

        lax.fori_loop(0, n_pairs, second, 0)
        result = (acc[...] / jnp.sum(total[...], axis=1, keepdims=True)).astype(jnp.bfloat16)
        for g in range(GROUP):
            out_ref[here, g * HD : (g + 1) * HD] = result[g * BLOCK : (g + 1) * BLOCK, :]
        return carry

    lax.fori_loop(0, blocks_here, one_row, 0)


def attention(counts, listed, q, pieces, slots):
    tok, width = q.shape
    rows = GROUP * BLOCK
    return pl.pallas_call(
        functools.partial(attention_kernel, tok // BLOCK, slots),
        out_shape=jax.ShapeDtypeStruct((tok, width), jnp.bfloat16),
        in_specs=[SMEM, SMEM, VMEM] + [HBM] * len(pieces),
        out_specs=VMEM,
        scratch_shapes=[
            pltpu.VMEM((2, SLOTS * 512, HD), jnp.bfloat16),
            pltpu.VMEM((KMAX // 2, rows, 2 * BLOCK), jnp.float32),
            pltpu.VMEM((rows, HD), jnp.float32),
            pltpu.VMEM((rows, HD), jnp.float32),
            pltpu.VMEM((rows, HD), jnp.float32),
            pltpu.SemaphoreType.DMA((SLOTS,)),
        ],
        compiler_params=pltpu.CompilerParams(vmem_limit_bytes=VMEM_LIMIT),
        cost_estimate=FREE,
        name="attention",
    )(counts, listed, q, *pieces)


def project_kernel(count, scalars, own_ref, near_ref, w_ref, w0a, w0b, w1a, w1b, *refs):
    out_refs, (wide, sems, part_sems) = refs[:count], refs[count:]
    core, column = scalars[0], scalars[1]
    depth = own_ref.shape[1]
    half = depth // 2

    def lanes(block):
        return pl.ds(pl.multiple_of(block * 512, 512), 512)

    def own_copy(i, target):
        return pltpu.make_async_copy(
            w_ref.at[:, lanes(column * NZ + target)], wide.at[i, pl.ds(0, depth), :], sems.at[i]
        )

    def part_copy(i, target, which, source):
        return pltpu.make_async_copy(
            source.at[:, lanes(target % 4)],
            wide.at[i, pl.ds(depth + which * half, half), :],
            part_sems.at[i, which],
        )

    for i in range(count):
        target = scalars[2 + i]
        own_copy(i, target).start()

        @pl.when(target // 4 == core)
        def _():
            part_copy(i, target, 0, w0a).start()
            part_copy(i, target, 1, w1a).start()

        @pl.when(target // 4 != core)
        def _():
            part_copy(i, target, 0, w0b).start()
            part_copy(i, target, 1, w1b).start()

    for i in range(count):
        target = scalars[2 + i]
        own_copy(i, target).wait()
        part_copy(i, target, 0, w0a).wait()
        part_copy(i, target, 1, w1a).wait()
        value = jnp.dot(own_ref[...], wide[i, :depth, :], preferred_element_type=jnp.float32)
        value += jnp.dot(near_ref[...], wide[i, depth:, :], preferred_element_type=jnp.float32)
        out_refs[i][...] = value.astype(jnp.bfloat16)


def project(core, column, targets, own, near, weights, parts):
    rows, depth = own.shape
    count = len(targets)
    scalars = jnp.stack([core, column] + [t % NZ for t in targets]).astype(jnp.int32)
    return pl.pallas_call(
        functools.partial(project_kernel, count),
        out_shape=[jax.ShapeDtypeStruct((rows, 512), jnp.bfloat16)] * count,
        in_specs=[SMEM, VMEM, VMEM] + [HBM] * 5,
        out_specs=[VMEM] * count,
        scratch_shapes=[
            pltpu.VMEM((count, 2 * depth, 512), jnp.bfloat16),
            pltpu.SemaphoreType.DMA((count,)),
            pltpu.SemaphoreType.DMA((count, 2)),
        ],
        compiler_params=pltpu.CompilerParams(vmem_limit_bytes=VMEM_LIMIT),
        cost_estimate=FREE,
        name="project",
    )(scalars, own, near, weights, *parts)


def shards(queries, keys_values, block_list, out_weight):
    ctx = lax.axis_index("ctx")
    tp = lax.axis_index("tp")
    x, yh, c = ctx // 4, (ctx // 2) % 2, ctx % 2
    yl, z = tp // NZ, tp % NZ
    tok = queries.shape[0]
    width = queries.shape[1]

    head = yl * 4 + z // 2
    far_head = (1 - yl) * 4 + z // 2
    at = jnp.stack([head, far_head, (1 - yl) * 2 + c]).astype(jnp.int32)
    own, for_far, near_w, far_w = pick(at, keys_values, out_weight)
    far = send(for_far, "y_far")
    left = send(own, "x+")
    right = send(own, "x-")
    own_t = send(own, "core")
    near_part = send(near_w, "y_near")

    far, left, right, far_w = lax.optimization_barrier((far, left, right, far_w))
    first = jnp.stack([far, left])
    both = send(first, "x+")
    far_right = send(far, "x-")
    first_t = send(first, "core")
    right_t = send(right, "core")
    far_part = send(far_w, "y_far")
    two_far = send(far_right, "x-")
    far_right_t = send(far_right, "core")
    both_t = send(both, "core")
    two_far_t = send(two_far, "core")
    near_other = send(near_part, "core")
    far_other = send(far_part, "core")
    parts = [near_part, near_other, far_part, far_other]
    pieces = [own, own_t, first, first_t, right, right_t, far_right, far_right_t]
    pieces += [two_far, two_far_t, both, both_t]
    slots = ((0,), (1,), (2, 12), (3, 13), (4,), (5,), (6,), (7,))
    slots += ((10,), (11,), (14, 8), (15, 9))

    shard = block_list // 4
    sx, sy, sc = shard // 4, (shard // 2) % 2, shard % 2
    slot = ((sx - x) % NX) * 4 + ((sy - yh) % 2) * 2 + (sc - c) % 2
    placed = jnp.where(block_list >= 0, slot * 4 + block_list % 4, 0).astype(jnp.int32)
    counts = jnp.sum((block_list >= 0).astype(jnp.int32), axis=1)

    rows = tok // CHUNKS
    per = rows // BLOCK

    def attend(k):
        return attention(
            counts[k * per : (k + 1) * per],
            placed[k * per : (k + 1) * per].reshape(-1),
            queries[k * rows : (k + 1) * rows],
            pieces,
            slots,
        )

    attended = [attend(k) for k in range(CHUNKS)]
    near = [send(done, "y_near") for done in attended]

    ways = []
    for k in range(CHUNKS):
        up, down = ((4, 3, 2, 1), (-3, -2, -1)) if k % 2 == 0 else ((3, 2, 1), (-4, -3, -2, -1))
        early = [up[0], down[0]]
        late = [*up[1:], *down[1:], 0]
        partial = {}
        for group in (early, late):
            done = project(c, yl, [z + d for d in group], attended[k], near[k], out_weight, parts)
            partial.update(zip(group, done))
            if group is early and k + 1 < CHUNKS:
                near[k + 1], partial[up[0]], partial[down[0]] = lax.optimization_barrier(
                    (near[k + 1], partial[up[0]], partial[down[0]])
                )
        ways.append((up, down, partial))

    def add(*terms):
        return sum(t.astype(jnp.float32) for t in terms).astype(jnp.bfloat16)

    moving = [[None, None] for _ in range(CHUNKS)]
    for step in range(4):
        for k in range(CHUNKS):
            up, down, partial = ways[k]
            for way, (order, move) in enumerate(((up, "z+"), (down, "z-"))):
                if step < len(order):
                    value = partial[order[step]]
                    if step:
                        value = add(moving[k][way], value)
                    moving[k][way] = send(value, move)
    results = [add(ways[k][2][0], *moving[k]) for k in range(CHUNKS)]
    return jnp.concatenate(results, 0)


def solution(mesh):
    in_specs = (P("ctx", "tp"), P(None, "ctx", None), P("ctx", None), P("tp", None))
    return jax.shard_map(
        shards, mesh=mesh, in_specs=in_specs, out_specs=P("ctx", "tp"), check_vma=False
    )
```

time: 140 us -> 216 us (1.54)
  Pallas kernels: 22.8 us -> 114 us
  local copies, waits for them, and re-layouts: 23.5 us -> 6.3 us
  other arithmetic: 2.79 us -> 9.19 us
  waiting for transfers between devices: 54.8 us -> 49.1 us
    pallas_call x0 -> x1, Pallas kernels: none -> 81.2 us  [pick(): pl.pallas_call(pick_kernel, out_shape=[piece, piece, part, part], in_spec...]
    unnamed x44 -> x34, local copies, waits for them, and re-layouts: 16.3 us -> 1.1 us
    pallas_call x4, Pallas kernels: 10.5 us -> 19.5 us  [project(): pl.pallas_call(functools.partial(project_kernel, count), out_shape=[jax.S...]
    dynamic_slice x3 -> x0, local copies, waits for them, and re-layouts: 5.75 us -> none  [the longest x2 4.67 us: for_neighbour(): lax.dynamic_slice(weights, (link * 256, (1 - yl) * half + c * quarter), (...]
    ppermute x33 -> x32, waiting for transfers between devices: 54.8 us -> 49.1 us  [send(): return lax.ppermute(array, AXES, MOVES[move])]
    convert_element_type x12, other arithmetic: 0.86 us -> 5.62 us  [add(): return sum((t.astype(jnp.float32) for t in terms)).astype(jnp.bfloat16)]
    ppermute x33 -> x32, starting transfers between devices: 35.6 us -> 35.4 us  [send(): return lax.ppermute(array, AXES, MOVES[move])]
  transfers between devices with their start and end apart: 33 -> 32, of which waited for: 16 -> 14; matrix products, arithmetic and copies ran while one was open for 6% -> 6% of each run, Pallas kernels for 16% -> 14%
where the time goes in v3:
time: 216 us; the launch traced here: 215 us
  Pallas kernels  114 us (53%)
  waiting for transfers between devices  49.1 us (23%)
  starting transfers between devices  35.4 us (16%)
  other arithmetic  9.19 us (4%)
  local copies, waits for them, and re-layouts  6.3 us (3%)
    pallas_call x1, Pallas kernels, pick(): pl.pallas_call(pick_kernel, out_shape=[piece, piece, part, part], in_spec...  81.2 us
    ppermute x32, waiting for transfers between devices, send(): return lax.ppermute(array, AXES, MOVES[move])  49.1 us
    ppermute x32, starting transfers between devices, send(): return lax.ppermute(array, AXES, MOVES[move])  35.4 us
    pallas_call x4, Pallas kernels, project(): pl.pallas_call(functools.partial(project_kernel, count), out_shape=[jax.S...  19.5 us
    pallas_call x2, Pallas kernels, attention(): pl.pallas_call(functools.partial(attention_kernel, tok // BLOCK, slots),...  13.4 us
    convert_element_type x12, other arithmetic, add(): return sum((t.astype(jnp.float32) for t in terms)).astype(jnp.bfloat16)  5.62 us
  transfers between devices with their start and end apart: 32, of which 14 were waited for; matrix products, arithmetic and copies ran while one was open for 6% of the time, Pallas kernels for 14%

profile of v3, /device:TPU:6, one launch (start us, length us, event | category | flops | bytes accessed | tf_op | source)
XLA Modules:
  0.0 214.6 jit_solution(3961826907427224806)
XLA Ops:
  0.6 81.2 %pick.1 = (bf16[2,512,128]{2,1,0:T(8,128)(2,1)}, bf16[2,512,128]{2,1,0:T(8,128)(2,1)}, bf16[256,2048]{1,0:T(8,128)(2,1)}, bf16[256,2048]{1,0:T(8,128)(2,1)}) custom-call(s32[3]{0:T(128)} %pad_add_fusion.at, bf16[2,512,1024]{2,1,0:T(8,128)(2,1)} %kv_ref.1, bf16[512,8192]{1,0:T(8,128)(2,1)} %w_ref.9), custom_call_target="tpu_custom_call" | custom-call | tf_op jit(solution)/shard_map/pick/pallas_call | solution.py:83
  81.8 3.1 %collective-permute-start.1 = (bf16[2,512,128]{2,1,0:T(8,128)(2,1)}, bf16[2,512,128]{2,1,0:T(8,128)(2,1)S(1)}, u32[]{:S(2)}, u32[]{:S(2)}) collective-permute-start(bf16[2,512,128]{2,1,0:T(8,128)(2,1)} %get-tuple-element.33), channel_id=1, source_target_pairs={{0,40},{1,41},{2,42},{3,43},{4,44},{5,45},{6,46},{7,47},{16,56},{1... | collective-permute-start | bytes 786440 | tf_op jit(solution)/shard_map/ppermute | solution.py:53
  85.4 1.5 collective-permute-start.3
  87.0 4.3 %collective-permute-done.1 = bf16[2,512,128]{2,1,0:T(8,128)(2,1)S(1)} collective-permute-done((bf16[2,512,128]{2,1,0:T(8,128)(2,1)}, bf16[2,512,128]{2,1,0:T(8,128)(2,1)S(1)}, u32[]{:S(2)}, u32[]{:S(2)}) %collective-permute-start.1) | collective-permute-done | bytes 262176 | tf_op jit(solution)/shard_map/ppermute | solution.py:53
  91.4 1.5 collective-permute-done.2
  92.9 1.4 collective-permute-done.3.refs_4_
  97.2 1.3 collective-permute-start.6
  98.5 8.3 %collective-permute-done.6.refs_6_ = bf16[2,512,128]{2,1,0:T(8,128)(2,1)} collective-permute-done((bf16[2,512,128]{2,1,0:T(8,128)(2,1)S(1)}, bf16[2,512,128]{2,1,0:T(8,128)(2,1)}, u32[]{:S(2)}, u32[]{:S(2)}) %collective-permute-start.6) | collective-permute-done | bytes 262176 | tf_op jit(solution)/shard_map/ppermute | solution.py:53
  106.9 4.3 %collective-permute-done.13.w0a = bf16[256,2048]{1,0:T(8,128)(2,1)S(1)} collective-permute-done((bf16[256,2048]{1,0:T(8,128)(2,1)}, bf16[256,2048]{1,0:T(8,128)(2,1)S(1)}, u32[]{:S(2)}, u32[]{:S(2)}) %collective-permute-start.13) | collective-permute-done | bytes 1048608 | tf_op jit(solution)/shard_map/ppermute | solution.py:53
  111.2 7.9 %collective-permute-done.15.w1a = bf16[256,2048]{1,0:T(8,128)(2,1)S(1)} collective-permute-done((bf16[256,2048]{1,0:T(8,128)(2,1)}, bf16[256,2048]{1,0:T(8,128)(2,1)S(1)}, u32[]{:S(2)}, u32[]{:S(2)}) %collective-permute-start.15) | collective-permute-done | bytes 1048608 | tf_op jit(solution)/shard_map/ppermute | solution.py:53
  122.3 1.9 fusion.16
  124.2 7.4 %attention.2.own_ref = bf16[256,512]{1,0:T(8,128)(2,1)} custom-call(s32[2]{0:T(128)} %get-tuple-element.65.counts, s32[32]{0:T(128)} %reshape.6.listed, bf16[256,512]{1,0:T(8,128)(2,1)} %get-tuple-element.59.q_ref, bf16[2,512,128]{2,1,0:T(8,128)(2,1)} %get-tuple-element.32.refs_0_, bf16[2,512,128]{2,1,0:T(8,128)(2,1)} %copy-done.5, ...), custom_call_target="tpu_custom_call" | custom-call | tf_op jit(solution)/shard_map/attention/pallas_call | solution.py:166
  131.8 6.0 %attention.3.own_ref = bf16[256,512]{1,0:T(8,128)(2,1)} custom-call(s32[2]{0:T(128)} %get-tuple-element.66.counts, s32[32]{0:T(128)} %reshape.7.listed, bf16[256,512]{1,0:T(8,128)(2,1)} %get-tuple-element.60.q_ref, bf16[2,512,128]{2,1,0:T(8,128)(2,1)} %get-tuple-element.32.refs_0_, bf16[2,512,128]{2,1,0:T(8,128)(2,1)} %copy-done.5, ...), custom_call_target="tpu_custom_call" | custom-call | tf_op jit(solution)/shard_map/attention/pallas_call | solution.py:166
  137.7 2.3 %collective-permute-start.17 = (bf16[256,512]{1,0:T(8,128)(2,1)}, bf16[256,512]{1,0:T(8,128)(2,1)}, u32[]{:S(2)}, u32[]{:S(2)}) collective-permute-start(bf16[256,512]{1,0:T(8,128)(2,1)} %attention.3.own_ref), channel_id=1, source_target_pairs={{0,8},{1,9},{2,10},{3,11},{4,12},{5,13},{6,14},{7,15},{16,24},{17,... | collective-permute-start | bytes 786440 | tf_op jit(solution)/shard_map/ppermute | solution.py:53
  142.3 3.9 %project.5 = (bf16[256,512]{1,0:T(8,128)(2,1)}, bf16[256,512]{1,0:T(8,128)(2,1)}) custom-call(s32[4]{0:T(128)} %pad_add_fusion.1.scalars, bf16[256,512]{1,0:T(8,128)(2,1)} %attention.2.own_ref, bf16[256,512]{1,0:T(8,128)(2,1)} %copy-done.3, bf16[512,8192]{1,0:T(8,128)(2,1)} %w_ref.9, bf16[256,2048]{1,0:T(8,128)(2,1)} %copy-done, ...), custom_call_target="tpu_custom_call" | custom-call | tf_op jit(solution)/shard_map/project/pallas_call | solution.py:234
  146.3 3.9 %project.7 = (bf16[256,512]{1,0:T(8,128)(2,1)}, bf16[256,512]{1,0:T(8,128)(2,1)}) custom-call(s32[4]{0:T(128)} %pad_add_fusion.3.scalars, bf16[256,512]{1,0:T(8,128)(2,1)} %attention.3.own_ref, bf16[256,512]{1,0:T(8,128)(2,1)} %collective-permute-done.17.near_ref, bf16[512,8192]{1,0:T(8,128)(2,1)} %w_ref.9, bf16[256,2048]{1,0:T(8,128)(2,1)} %copy-done, ...), custom_call_target="tpu_custom_call" | custom-call | tf_op jit(solution)/shard_map/project/pallas_call | solution.py:234
  150.2 5.9 %collective-permute-start.28 = (bf16[256,512]{1,0:T(8,128)(2,1)}, bf16[256,512]{1,0:T(8,128)(2,1)S(1)}, u32[]{:S(2)}, u32[]{:S(2)}) collective-permute-start(bf16[256,512]{1,0:T(8,128)(2,1)} %get-tuple-element.55), channel_id=1, source_target_pairs={{0,7},{1,0},{2,1},{3,2},{4,3},{5,4},{6,5},{7,6},{16,23},{17,16},{1... | collective-permute-start | bytes 786440 | tf_op jit(solution)/shard_map/ppermute | solution.py:53
  157.5 3.2 %collective-permute-start.22 = (bf16[256,512]{1,0:T(8,128)(2,1)S(1)}, bf16[256,512]{1,0:T(8,128)(2,1)S(1)}, u32[]{:S(2)}, u32[]{:S(2)}) collective-permute-start(bf16[256,512]{1,0:T(8,128)(2,1)S(1)} %copy-done.16), channel_id=1, source_target_pairs={{0,7},{1,0},{2,1},{3,2},{4,3},{5,4},{6,5},{7,6},{16,23},{17,16},{1... | collective-permute-start | bytes 786440 | tf_op jit(solution)/shard_map/ppermute | solution.py:53
  160.7 5.8 %project.6 = (bf16[256,512]{1,0:T(8,128)(2,1)}, bf16[256,512]{1,0:T(8,128)(2,1)}, bf16[256,512]{1,0:T(8,128)(2,1)}, bf16[256,512]{1,0:T(8,128)(2,1)}, bf16[256,5...) custom-call(s32[8]{0:T(128)} %stack.98.scalars, bf16[256,512]{1,0:T(8,128)(2,1)} %attention.3.own_ref, ...), custom_call_target="tpu_custom_call" | custom-call | tf_op jit(solution)/shard_map/project/pallas_call | solution.py:234
  166.5 6.0 %project.4 = (bf16[256,512]{1,0:T(8,128)(2,1)}, bf16[256,512]{1,0:T(8,128)(2,1)}, bf16[256,512]{1,0:T(8,128)(2,1)}, bf16[256,512]{1,0:T(8,128)(2,1)}, bf16[256,5...) custom-call(s32[8]{0:T(128)} %stack.87.scalars, bf16[256,512]{1,0:T(8,128)(2,1)} %attention.2.own_ref, ...), custom_call_target="tpu_custom_call" | custom-call | tf_op jit(solution)/shard_map/project/pallas_call | solution.py:234
  172.6 3.3 %collective-permute-start.29 = (bf16[256,512]{1,0:T(8,128)(2,1)S(1)}, bf16[256,512]{1,0:T(8,128)(2,1)S(1)}, u32[]{:S(2)}, u32[]{:S(2)}) collective-permute-start(bf16[256,512]{1,0:T(8,128)(2,1)S(1)} %add_convert_fusion.3), channel_id=1, source_target_pairs={{0,7},{1,0},{2,1},{3,2},{4,3},{5,4},{6,5},{7,6},{16,23},{17,16},{1... | collective-permute-start | bytes 786440 | tf_op jit(solution)/shard_map/ppermute | solution.py:53
  176.1 1.0 add_convert_fusion.8
  177.1 3.3 %collective-permute-start.23 = (bf16[256,512]{1,0:T(8,128)(2,1)S(1)}, bf16[256,512]{1,0:T(8,128)(2,1)S(1)}, u32[]{:S(2)}, u32[]{:S(2)}) collective-permute-start(bf16[256,512]{1,0:T(8,128)(2,1)S(1)} %add_convert_fusion.8), channel_id=1, source_target_pairs={{0,7},{1,0},{2,1},{3,2},{4,3},{5,4},{6,5},{7,6},{16,23},{17,16},{1... | collective-permute-start | bytes 786440 | tf_op jit(solution)/shard_map/ppermute | solution.py:53
  180.4 1.0 add_convert_fusion.11
  182.4 3.8 %collective-permute-start.30 = (bf16[256,512]{1,0:T(8,128)(2,1)S(1)}, bf16[256,512]{1,0:T(8,128)(2,1)S(1)}, u32[]{:S(2)}, u32[]{:S(2)}) collective-permute-start(bf16[256,512]{1,0:T(8,128)(2,1)S(1)} %add_convert_fusion.2), channel_id=1, source_target_pairs={{0,7},{1,0},{2,1},{3,2},{4,3},{5,4},{6,5},{7,6},{16,23},{17,16},{1... | collective-permute-start | bytes 786440 | tf_op jit(solution)/shard_map/ppermute | solution.py:53
  186.8 5.2 %collective-permute-done.19 = bf16[256,512]{1,0:T(8,128)(2,1)S(1)} collective-permute-done((bf16[256,512]{1,0:T(8,128)(2,1)S(1)}, bf16[256,512]{1,0:T(8,128)(2,1)S(1)}, u32[]{:S(2)}, u32[]{:S(2)}) %collective-permute-start.19) | collective-permute-done | bytes 262176 | tf_op jit(solution)/shard_map/ppermute | solution.py:53
  192.0 1.0 add_convert_fusion.10
  193.6 3.8 %collective-permute-start.31 = (bf16[256,512]{1,0:T(8,128)(2,1)S(1)}, bf16[256,512]{1,0:T(8,128)(2,1)S(1)}, u32[]{:S(2)}, u32[]{:S(2)}) collective-permute-start(bf16[256,512]{1,0:T(8,128)(2,1)S(1)} %add_convert_fusion.1), channel_id=1, source_target_pairs={{0,7},{1,0},{2,1},{3,2},{4,3},{5,4},{6,5},{7,6},{16,23},{17,16},{1... | collective-permute-start | bytes 786440 | tf_op jit(solution)/shard_map/ppermute | solution.py:53
  198.5 4.8 %collective-permute-done.20 = bf16[256,512]{1,0:T(8,128)(2,1)S(1)} collective-permute-done((bf16[256,512]{1,0:T(8,128)(2,1)S(1)}, bf16[256,512]{1,0:T(8,128)(2,1)S(1)}, u32[]{:S(2)}, u32[]{:S(2)}) %collective-permute-start.20) | collective-permute-done | bytes 262176 | tf_op jit(solution)/shard_map/ppermute | solution.py:53
  203.3 1.0 add_convert_fusion.9
  204.6 4.3 %collective-permute-done.24 = bf16[256,512]{1,0:T(8,128)(2,1)S(1)} collective-permute-done((bf16[256,512]{1,0:T(8,128)(2,1)S(1)}, bf16[256,512]{1,0:T(8,128)(2,1)S(1)}, u32[]{:S(2)}, u32[]{:S(2)}) %collective-permute-start.24) | collective-permute-done | bytes 262176 | tf_op jit(solution)/shard_map/ppermute | solution.py:53
  208.8 4.8 %collective-permute-done.21 = bf16[256,512]{1,0:T(8,128)(2,1)S(1)} collective-permute-done((bf16[256,512]{1,0:T(8,128)(2,1)S(1)}, bf16[256,512]{1,0:T(8,128)(2,1)S(1)}, u32[]{:S(2)}, u32[]{:S(2)}) %collective-permute-start.21) | collective-permute-done | bytes 262176 | tf_op jit(solution)/shard_map/ppermute | solution.py:53
  (98 shorter events, 15.7 us)
Async XLA Ops:
  81.8 9.6 %collective-permute-start.1 = (bf16[2,512,128]{2,1,0:T(8,128)(2,1)}, bf16[2,512,128]{2,1,0:T(8,128)(2,1)S(1)}, u32[]{:S(2)}, u32[]{:S(2)}) collective-permute-start(bf16[2,512,128]{2,1,0:T(8,128)(2,1)} %get-tuple-element.33), channel_id=1, source_target_pairs={{0,40},{1,41},{2,42},{3,43},{4,44},{5,45},{6,46},{7,47},{16,56},{1... | collective-permute-start | bytes 786440 | tf_op jit(solution)/shard_map/ppermute | solution.py:53
  84.9 8.0 %collective-permute-start.2 = (bf16[2,512,128]{2,1,0:T(8,128)(2,1)}, bf16[2,512,128]{2,1,0:T(8,128)(2,1)S(1)}, u32[]{:S(2)}, u32[]{:S(2)}) collective-permute-start(bf16[2,512,128]{2,1,0:T(8,128)(2,1)} %get-tuple-element.32.refs_0_), channel_id=1, source_target_pairs={{0,64},{1,65},{2,66},{3,67},{4,68},{5,69},{6,70},{7,71},{16,80},{1... | collective-permute-start | bytes 786440 | tf_op jit(solution)/shard_map/ppermute | solution.py:53
  85.4 8.9 %collective-permute-start.3 = (bf16[2,512,128]{2,1,0:T(8,128)(2,1)}, bf16[2,512,128]{2,1,0:T(8,128)(2,1)S(1)}, u32[]{:S(2)}, u32[]{:S(2)}) collective-permute-start(bf16[2,512,128]{2,1,0:T(8,128)(2,1)} %get-tuple-element.32.refs_0_), channel_id=1, source_target_pairs={{0,192},{1,193},{2,194},{3,195},{4,196},{5,197},{6,198},{7,199},{1... | collective-permute-start | bytes 786440 | tf_op jit(solution)/shard_map/ppermute | solution.py:53
  86.9 24.3 %collective-permute-start.13 = (bf16[256,2048]{1,0:T(8,128)(2,1)}, bf16[256,2048]{1,0:T(8,128)(2,1)S(1)}, u32[]{:S(2)}, u32[]{:S(2)}) collective-permute-start(bf16[256,2048]{1,0:T(8,128)(2,1)} %get-tuple-element.38), channel_id=1, source_target_pairs={{0,8},{1,9},{2,10},{3,11},{4,12},{5,13},{6,14},{7,15},{16,24},{17,... | collective-permute-start | bytes 3145736 | tf_op jit(solution)/shard_map/ppermute | solution.py:53
  94.3 24.8 %collective-permute-start.15 = (bf16[256,2048]{1,0:T(8,128)(2,1)}, bf16[256,2048]{1,0:T(8,128)(2,1)S(1)}, u32[]{:S(2)}, u32[]{:S(2)}) collective-permute-start(bf16[256,2048]{1,0:T(8,128)(2,1)} %get-tuple-element.39), channel_id=1, source_target_pairs={{0,40},{1,41},{2,42},{3,43},{4,44},{5,45},{6,46},{7,47},{16,56},{1... | collective-permute-start | bytes 3145736 | tf_op jit(solution)/shard_map/ppermute | solution.py:53
  95.1 2.1 collective-permute-start
  95.1 3.4 %collective-permute-start.5 = (bf16[2,512,128]{2,1,0:T(8,128)(2,1)S(1)}, bf16[2,512,128]{2,1,0:T(8,128)(2,1)S(1)}, u32[]{:S(2)}, u32[]{:S(2)}) collective-permute-start(bf16[2,512,128]{2,1,0:T(8,128)(2,1)S(1)} %collective-permute-done.3.refs_4_), channel_id=1, source_target_pairs={{0,16},{1,17},{2,18},{3,19},{4,20},{5,21},{6,22},{7,23},{16,0},{17... | collective-permute-start | bytes 786440 | tf_op jit(solution)/shard_map/ppermute | solution.py:53
  96.5 22.8 %collective-permute-start.10 = (bf16[2,2,512,128]{3,2,1,0:T(8,128)(2,1)}, bf16[2,2,512,128]{3,2,1,0:T(8,128)(2,1)}, u32[]{:S(2)}, u32[]{:S(2)}) collective-permute-start(bf16[2,2,512,128]{3,2,1,0:T(8,128)(2,1)} %pad_maximum_fusion.refs_2_), channel_id=1, source_target_pairs={{0,64},{1,65},{2,66},{3,67},{4,68},{5,69},{6,70},{7,71},{16,80},{1... | collective-permute-start | bytes 1572872 | tf_op jit(solution)/shard_map/ppermute | solution.py:53
  97.2 9.7 %collective-permute-start.6 = (bf16[2,512,128]{2,1,0:T(8,128)(2,1)S(1)}, bf16[2,512,128]{2,1,0:T(8,128)(2,1)}, u32[]{:S(2)}, u32[]{:S(2)}) collective-permute-start(bf16[2,512,128]{2,1,0:T(8,128)(2,1)S(1)} %collective-permute-done.1), channel_id=1, source_target_pairs={{0,192},{1,193},{2,194},{3,195},{4,196},{5,197},{6,198},{7,199},{1... | collective-permute-start | bytes 786440 | tf_op jit(solution)/shard_map/ppermute | solution.py:53
  98.5 21.3 %collective-permute-start.4 = (bf16[2,2,512,128]{3,2,1,0:T(8,128)(2,1)}, bf16[2,2,512,128]{3,2,1,0:T(8,128)(2,1)}, u32[]{:S(2)}, u32[]{:S(2)}) collective-permute-start(bf16[2,2,512,128]{3,2,1,0:T(8,128)(2,1)} %pad_maximum_fusion.refs_2_), channel_id=1, source_target_pairs={{0,16},{1,17},{2,18},{3,19},{4,20},{5,21},{6,22},{7,23},{16,0},{17... | collective-permute-start | bytes 1572872 | tf_op jit(solution)/shard_map/ppermute | solution.py:53
  106.9 13.1 %collective-permute-start.8 = (bf16[2,512,128]{2,1,0:T(8,128)(2,1)}, bf16[2,512,128]{2,1,0:T(8,128)(2,1)}, u32[]{:S(2)}, u32[]{:S(2)}) collective-permute-start(bf16[2,512,128]{2,1,0:T(8,128)(2,1)} %collective-permute-done.6.refs_6_), channel_id=1, source_target_pairs={{0,192},{1,193},{2,194},{3,195},{4,196},{5,197},{6,198},{7,199},{1... | collective-permute-start | bytes 786440 | tf_op jit(solution)/shard_map/ppermute | solution.py:53
  111.2 30.1 %collective-permute-start.14 = (bf16[256,2048]{1,0:T(8,128)(2,1)S(1)}, bf16[256,2048]{1,0:T(8,128)(2,1)S(1)}, u32[]{:S(2)}, u32[]{:S(2)}) collective-permute-start(bf16[256,2048]{1,0:T(8,128)(2,1)S(1)} %collective-permute-done.13.w0a), channel_id=1, source_target_pairs={{0,16},{1,17},{2,18},{3,19},{4,20},{5,21},{6,22},{7,23},{16,0},{17... | collective-permute-start | bytes 3145736 | tf_op jit(solution)/shard_map/ppermute | solution.py:53
  119.1 22.2 %collective-permute-start.16 = (bf16[256,2048]{1,0:T(8,128)(2,1)S(1)}, bf16[256,2048]{1,0:T(8,128)(2,1)}, u32[]{:S(2)}, u32[]{:S(2)}) collective-permute-start(bf16[256,2048]{1,0:T(8,128)(2,1)S(1)} %collective-permute-done.15.w1a), channel_id=1, source_target_pairs={{0,16},{1,17},{2,18},{3,19},{4,20},{5,21},{6,22},{7,23},{16,0},{17... | collective-permute-start | bytes 3145736 | tf_op jit(solution)/shard_map/ppermute | solution.py:53
  119.2 5.0 %collective-permute-start.11 = (bf16[2,2,512,128]{3,2,1,0:T(8,128)(2,1)}, bf16[2,2,512,128]{3,2,1,0:T(8,128)(2,1)}, u32[]{:S(2)}, u32[]{:S(2)}) collective-permute-start(bf16[2,2,512,128]{3,2,1,0:T(8,128)(2,1)} %collective-permute-done.10.refs_10_), channel_id=1, source_target_pairs={{0,16},{1,17},{2,18},{3,19},{4,20},{5,21},{6,22},{7,23},{16,0},{17... | collective-permute-start | bytes 1572872 | tf_op jit(solution)/shard_map/ppermute | solution.py:53
  119.8 4.4 %collective-permute-start.7 = (bf16[2,512,128]{2,1,0:T(8,128)(2,1)}, bf16[2,512,128]{2,1,0:T(8,128)(2,1)}, u32[]{:S(2)}, u32[]{:S(2)}) collective-permute-start(bf16[2,512,128]{2,1,0:T(8,128)(2,1)} %collective-permute-done.6.refs_6_), channel_id=1, source_target_pairs={{0,16},{1,17},{2,18},{3,19},{4,20},{5,21},{6,22},{7,23},{16,0},{17... | collective-permute-start | bytes 786440 | tf_op jit(solution)/shard_map/ppermute | solution.py:53
  120.0 4.3 %collective-permute-start.9 = (bf16[2,512,128]{2,1,0:T(8,128)(2,1)}, bf16[2,512,128]{2,1,0:T(8,128)(2,1)}, u32[]{:S(2)}, u32[]{:S(2)}) collective-permute-start(bf16[2,512,128]{2,1,0:T(8,128)(2,1)} %collective-permute-done.8.refs_8_), channel_id=1, source_target_pairs={{0,16},{1,17},{2,18},{3,19},{4,20},{5,21},{6,22},{7,23},{16,0},{17... | collective-permute-start | bytes 786440 | tf_op jit(solution)/shard_map/ppermute | solution.py:53
  131.7 9.6 %collective-permute-start.12 = (bf16[256,512]{1,0:T(8,128)(2,1)}, bf16[256,512]{1,0:T(8,128)(2,1)S(1)}, u32[]{:S(2)}, u32[]{:S(2)}) collective-permute-start(bf16[256,512]{1,0:T(8,128)(2,1)} %attention.2.own_ref), channel_id=1, source_target_pairs={{0,8},{1,9},{2,10},{3,11},{4,12},{5,13},{6,14},{7,15},{16,24},{17,... | collective-permute-start | bytes 786440 | tf_op jit(solution)/shard_map/ppermute | solution.py:53
  137.7 8.5 %collective-permute-start.17 = (bf16[256,512]{1,0:T(8,128)(2,1)}, bf16[256,512]{1,0:T(8,128)(2,1)}, u32[]{:S(2)}, u32[]{:S(2)}) collective-permute-start(bf16[256,512]{1,0:T(8,128)(2,1)} %attention.3.own_ref), channel_id=1, source_target_pairs={{0,8},{1,9},{2,10},{3,11},{4,12},{5,13},{6,14},{7,15},{16,24},{17,... | collective-permute-start | bytes 786440 | tf_op jit(solution)/shard_map/ppermute | solution.py:53
  150.2 22.3 %collective-permute-start.28 = (bf16[256,512]{1,0:T(8,128)(2,1)}, bf16[256,512]{1,0:T(8,128)(2,1)S(1)}, u32[]{:S(2)}, u32[]{:S(2)}) collective-permute-start(bf16[256,512]{1,0:T(8,128)(2,1)} %get-tuple-element.55), channel_id=1, source_target_pairs={{0,7},{1,0},{2,1},{3,2},{4,3},{5,4},{6,5},{7,6},{16,23},{17,16},{1... | collective-permute-start | bytes 786440 | tf_op jit(solution)/shard_map/ppermute | solution.py:53
  156.1 19.8 %collective-permute-start.25 = (bf16[256,512]{1,0:T(8,128)(2,1)}, bf16[256,512]{1,0:T(8,128)(2,1)S(1)}, u32[]{:S(2)}, u32[]{:S(2)}) collective-permute-start(bf16[256,512]{1,0:T(8,128)(2,1)} %get-tuple-element.52), channel_id=1, source_target_pairs={{0,1},{1,2},{2,3},{3,4},{4,5},{5,6},{6,7},{7,0},{16,17},{17,18},{1... | collective-permute-start | bytes 786440 | tf_op jit(solution)/shard_map/ppermute | solution.py:53
  157.5 18.6 %collective-permute-start.22 = (bf16[256,512]{1,0:T(8,128)(2,1)S(1)}, bf16[256,512]{1,0:T(8,128)(2,1)S(1)}, u32[]{:S(2)}, u32[]{:S(2)}) collective-permute-start(bf16[256,512]{1,0:T(8,128)(2,1)S(1)} %copy-done.16), channel_id=1, source_target_pairs={{0,7},{1,0},{2,1},{3,2},{4,3},{5,4},{6,5},{7,6},{16,23},{17,16},{1... | collective-permute-start | bytes 786440 | tf_op jit(solution)/shard_map/ppermute | solution.py:53
  160.7 19.7 %collective-permute-start.18 = (bf16[256,512]{1,0:T(8,128)(2,1)S(1)}, bf16[256,512]{1,0:T(8,128)(2,1)S(1)}, u32[]{:S(2)}, u32[]{:S(2)}) collective-permute-start(bf16[256,512]{1,0:T(8,128)(2,1)S(1)} %copy-done.15), channel_id=1, source_target_pairs={{0,1},{1,2},{2,3},{3,4},{4,5},{5,6},{6,7},{7,0},{16,17},{17,18},{1... | collective-permute-start | bytes 786440 | tf_op jit(solution)/shard_map/ppermute | solution.py:53
  172.6 9.7 %collective-permute-start.29 = (bf16[256,512]{1,0:T(8,128)(2,1)S(1)}, bf16[256,512]{1,0:T(8,128)(2,1)S(1)}, u32[]{:S(2)}, u32[]{:S(2)}) collective-permute-start(bf16[256,512]{1,0:T(8,128)(2,1)S(1)} %add_convert_fusion.3), channel_id=1, source_target_pairs={{0,7},{1,0},{2,1},{3,2},{4,3},{5,4},{6,5},{7,6},{16,23},{17,16},{1... | collective-permute-start | bytes 786440 | tf_op jit(solution)/shard_map/ppermute | solution.py:53
  176.0 10.4 %collective-permute-start.26 = (bf16[256,512]{1,0:T(8,128)(2,1)S(1)}, bf16[256,512]{1,0:T(8,128)(2,1)S(1)}, u32[]{:S(2)}, u32[]{:S(2)}) collective-permute-start(bf16[256,512]{1,0:T(8,128)(2,1)S(1)} %add_convert_fusion.5), channel_id=1, source_target_pairs={{0,1},{1,2},{2,3},{3,4},{4,5},{5,6},{6,7},{7,0},{16,17},{17,18},{1... | collective-permute-start | bytes 786440 | tf_op jit(solution)/shard_map/ppermute | solution.py:53
  177.1 20.3 %collective-permute-start.23 = (bf16[256,512]{1,0:T(8,128)(2,1)S(1)}, bf16[256,512]{1,0:T(8,128)(2,1)S(1)}, u32[]{:S(2)}, u32[]{:S(2)}) collective-permute-start(bf16[256,512]{1,0:T(8,128)(2,1)S(1)} %add_convert_fusion.8), channel_id=1, source_target_pairs={{0,7},{1,0},{2,1},{3,2},{4,3},{5,4},{6,5},{7,6},{16,23},{17,16},{1... | collective-permute-start | bytes 786440 | tf_op jit(solution)/shard_map/ppermute | solution.py:53
  181.4 10.6 %collective-permute-start.19 = (bf16[256,512]{1,0:T(8,128)(2,1)S(1)}, bf16[256,512]{1,0:T(8,128)(2,1)S(1)}, u32[]{:S(2)}, u32[]{:S(2)}) collective-permute-start(bf16[256,512]{1,0:T(8,128)(2,1)S(1)} %add_convert_fusion.11), channel_id=1, source_target_pairs={{0,1},{1,2},{2,3},{3,4},{4,5},{5,6},{6,7},{7,0},{16,17},{17,18},{1... | collective-permute-start | bytes 786440 | tf_op jit(solution)/shard_map/ppermute | solution.py:53
  182.4 11.2 %collective-permute-start.30 = (bf16[256,512]{1,0:T(8,128)(2,1)S(1)}, bf16[256,512]{1,0:T(8,128)(2,1)S(1)}, u32[]{:S(2)}, u32[]{:S(2)}) collective-permute-start(bf16[256,512]{1,0:T(8,128)(2,1)S(1)} %add_convert_fusion.2), channel_id=1, source_target_pairs={{0,7},{1,0},{2,1},{3,2},{4,3},{5,4},{6,5},{7,6},{16,23},{17,16},{1... | collective-permute-start | bytes 786440 | tf_op jit(solution)/shard_map/ppermute | solution.py:53
  186.5 17.9 %collective-permute-start.27 = (bf16[256,512]{1,0:T(8,128)(2,1)S(1)}, bf16[256,512]{1,0:T(8,128)(2,1)S(1)}, u32[]{:S(2)}, u32[]{:S(2)}) collective-permute-start(bf16[256,512]{1,0:T(8,128)(2,1)S(1)} %add_convert_fusion.4), channel_id=1, source_target_pairs={{0,1},{1,2},{2,3},{3,4},{4,5},{5,6},{6,7},{7,0},{16,17},{17,18},{1... | collective-permute-start | bytes 786440 | tf_op jit(solution)/shard_map/ppermute | solution.py:53
  193.0 10.3 %collective-permute-start.20 = (bf16[256,512]{1,0:T(8,128)(2,1)S(1)}, bf16[256,512]{1,0:T(8,128)(2,1)S(1)}, u32[]{:S(2)}, u32[]{:S(2)}) collective-permute-start(bf16[256,512]{1,0:T(8,128)(2,1)S(1)} %add_convert_fusion.10), channel_id=1, source_target_pairs={{0,1},{1,2},{2,3},{3,4},{4,5},{5,6},{6,7},{7,0},{16,17},{17,18},{1... | collective-permute-start | bytes 786440 | tf_op jit(solution)/shard_map/ppermute | solution.py:53
  193.6 10.8 %collective-permute-start.31 = (bf16[256,512]{1,0:T(8,128)(2,1)S(1)}, bf16[256,512]{1,0:T(8,128)(2,1)S(1)}, u32[]{:S(2)}, u32[]{:S(2)}) collective-permute-start(bf16[256,512]{1,0:T(8,128)(2,1)S(1)} %add_convert_fusion.1), channel_id=1, source_target_pairs={{0,7},{1,0},{2,1},{3,2},{4,3},{5,4},{6,5},{7,6},{16,23},{17,16},{1... | collective-permute-start | bytes 786440 | tf_op jit(solution)/shard_map/ppermute | solution.py:53
  198.4 10.5 %collective-permute-start.24 = (bf16[256,512]{1,0:T(8,128)(2,1)S(1)}, bf16[256,512]{1,0:T(8,128)(2,1)S(1)}, u32[]{:S(2)}, u32[]{:S(2)}) collective-permute-start(bf16[256,512]{1,0:T(8,128)(2,1)S(1)} %add_convert_fusion.7), channel_id=1, source_target_pairs={{0,7},{1,0},{2,1},{3,2},{4,3},{5,4},{6,5},{7,6},{16,23},{17,16},{1... | collective-permute-start | bytes 786440 | tf_op jit(solution)/shard_map/ppermute | solution.py:53
  204.3 9.3 %collective-permute-start.21 = (bf16[256,512]{1,0:T(8,128)(2,1)S(1)}, bf16[256,512]{1,0:T(8,128)(2,1)S(1)}, u32[]{:S(2)}, u32[]{:S(2)}) collective-permute-start(bf16[256,512]{1,0:T(8,128)(2,1)S(1)} %add_convert_fusion.9), channel_id=1, source_target_pairs={{0,1},{1,2},{2,3},{3,4},{4,5},{5,6},{6,7},{7,0},{16,17},{17,18},{1... | collective-permute-start | bytes 786440 | tf_op jit(solution)/shard_map/ppermute | solution.py:53
  (17 other events, 404.2 us)

commit v4 on v0

v4 whole, which is shorter than its diff:
```python
import functools
import math

import jax
import jax.numpy as jnp
from jax import lax
from jax.experimental import pallas as pl
from jax.experimental.pallas import tpu as pltpu
from jax.sharding import PartitionSpec as P

HD = 128
BLOCK = 128
KMAX = 16
GROUP = 4
AXES = ("ctx", "tp")
NX, NYH, NC, NYL, NZ = 4, 2, 2, 2, 8
SLOTS = NX * NYH * NC
SCALE2 = HD ** (-0.5) * math.log2(math.e)
CHUNKS = 2
LOW = -1e30
NEAR_ROWS = 256
ATTENTION_VMEM = 14 * 2**20
PROJECT_VMEM = 8 * 2**20
WIDE = 4
ATT_FLOPS = 3_000_000_000
VMEM_LIMIT = 50 * 2**20
FREE = pl.CostEstimate(flops=0, bytes_accessed=0, transcendentals=0)


def pairs(move):
    out = []
    for x in range(NX):
        for y in range(4):
            for c in range(NC):
                for z in range(NZ):
                    x2, y2, c2, z2 = move(x, y, c, z)
                    x2, y2, c2, z2 = x2 % NX, y2 % 4, c2 % NC, z2 % NZ

                    def index(x, y, c, z):
                        return (x * 4 + (y // 2) * 2 + c) * 16 + (y % 2) * 8 + z

                    out.append((index(x, y, c, z), index(x2, y2, c2, z2)))
    return out


MOVES = {
    "x+": pairs(lambda x, y, c, z: (x + 1, y, c, z)),
    "x-": pairs(lambda x, y, c, z: (x - 1, y, c, z)),
    "z+": pairs(lambda x, y, c, z: (x, y, c, z + 1)),
    "z-": pairs(lambda x, y, c, z: (x, y, c, z - 1)),
    "core": pairs(lambda x, y, c, z: (x, y, c + 1, z)),
    "y_near": pairs(lambda x, y, c, z: (x, y ^ 1, c, z)),
    "y_far": pairs(lambda x, y, c, z: (x, 3 - y, c, z)),
}


def send(array, move):
    return lax.ppermute(array, AXES, MOVES[move])


SMEM = pl.BlockSpec(memory_space=pltpu.SMEM)
VMEM = pl.BlockSpec(memory_space=pltpu.VMEM)
HBM = pl.BlockSpec(memory_space=pltpu.HBM)


def pick_kernel(coords, w_ref, near_w_ref, far_w_ref, sems):
    c, yl = coords[2], coords[3]
    columns = near_w_ref.shape[1]
    near_rows, far_rows = near_w_ref.shape[0], far_w_ref.shape[0]
    there = pl.ds(pl.multiple_of(((1 - yl) * 2 + c) * columns, columns), columns)
    copies = [
        pltpu.make_async_copy(w_ref.at[pl.ds(0, near_rows), there], near_w_ref, sems.at[0]),
        pltpu.make_async_copy(w_ref.at[pl.ds(near_rows, far_rows), there], far_w_ref, sems.at[1]),
    ]
    for copy in copies:
        copy.start()
    for copy in copies:
        copy.wait()


def pick(coords, weights):
    depth, full = weights.shape
    parts = [jax.ShapeDtypeStruct((n, full // 4), jnp.bfloat16) for n in (NEAR_ROWS, depth - NEAR_ROWS)]
    return pl.pallas_call(
        pick_kernel,
        out_shape=parts,
        in_specs=[SMEM, HBM],
        out_specs=[VMEM] * 2,
        scratch_shapes=[pltpu.SemaphoreType.DMA((2,))],
        compiler_params=pltpu.CompilerParams(vmem_limit_bytes=VMEM_LIMIT),
        cost_estimate=FREE,
        name="pick",
    )(coords, weights)


def attention_kernel(first_row, n_rows, slots, coords, block_list, q_ref, *refs):
    pieces, refs = refs[: len(slots)], refs[len(slots) :]
    out_ref, kv, scores, top, total, acc, placed = refs
    x, yh, c = coords[0], coords[1], coords[2]

    for piece, held in zip(pieces, slots):
        for i, slot in enumerate(held):
            kv[:, slot * 512 : (slot + 1) * 512, :] = piece[i] if len(held) > 1 else piece[...]

    counts = []
    for row in range(n_rows):

        def place(j, count):
            block = block_list[first_row + row, j]
            shard = jnp.maximum(block, 0) // 4
            slot = ((shard // 4 - x) % NX) * 4 + (((shard // 2) % 2 - yh) % 2) * 2 + (shard - c) % 2
            placed[row, j] = (slot * 4 + block % 4) * BLOCK
            return count + (block >= 0).astype(jnp.int32)

        counts.append(lax.fori_loop(0, KMAX, place, 0))

    for row in range(n_rows):
        count = counts[row]
        groups = (count + WIDE - 1) // WIDE

        def gather(which, group):
            tiles = []
            for i in range(WIDE):
                j = jnp.minimum(group * WIDE + i, count - 1)
                tiles.append(kv[which, pl.ds(pl.multiple_of(placed[row, j], BLOCK), BLOCK), :])
            return jnp.concatenate(tiles, 0)

        here = slice(row * BLOCK, (row + 1) * BLOCK)
        rows = slice((first_row + row) * BLOCK, (first_row + row + 1) * BLOCK)
        q = jnp.concatenate([q_ref[rows, g * HD : (g + 1) * HD] for g in range(GROUP)], 0)
        top[...] = jnp.full(top.shape, LOW, jnp.float32)

        def first(group, carry):
            s = lax.dot_general(
                q, gather(0, group), (((1,), (1,)), ((), ())), preferred_element_type=jnp.float32
            )
            high = top[...]
            for i in range(WIDE):
                tile = s[:, i * BLOCK : (i + 1) * BLOCK]
                if i:
                    tile = jnp.where(group * WIDE + i < count, tile, LOW)
                scores[group, :, i * BLOCK : (i + 1) * BLOCK] = tile
                high = jnp.maximum(high, tile)
            top[...] = high
            return carry

        lax.fori_loop(0, groups, first, 0)
        top[...] = jnp.broadcast_to(jnp.max(top[...], axis=1, keepdims=True) * SCALE2, top.shape)
        total[...] = jnp.zeros(total.shape, jnp.float32)
        acc[...] = jnp.zeros(acc.shape, jnp.float32)

        def second(group, carry):
            high = top[...]
            added, weights = total[...], []
            for i in range(WIDE):
                tile = jnp.exp2(scores[group, :, i * BLOCK : (i + 1) * BLOCK] * SCALE2 - high)
                added += tile
                weights.append(tile.astype(jnp.bfloat16))
            total[...] = added
            acc[...] += jnp.dot(
                jnp.concatenate(weights, 1), gather(1, group), preferred_element_type=jnp.float32
            )
            return carry

        lax.fori_loop(0, groups, second, 0)
        result = (acc[...] / jnp.sum(total[...], axis=1, keepdims=True)).astype(jnp.bfloat16)
        for g in range(GROUP):
            out_ref[here, g * HD : (g + 1) * HD] = result[g * BLOCK : (g + 1) * BLOCK, :]


def attention(coords, block_list, q, first_row, n_rows, pieces, slots):
    rows = GROUP * BLOCK
    tok, width = n_rows * BLOCK, q.shape[1]
    return pl.pallas_call(
        functools.partial(attention_kernel, first_row, n_rows, slots),
        out_shape=jax.ShapeDtypeStruct((tok, width), jnp.bfloat16),
        in_specs=[SMEM, SMEM, VMEM] + [VMEM] * len(pieces),
        out_specs=VMEM,
        scratch_shapes=[
            pltpu.VMEM((2, SLOTS * 512, HD), jnp.bfloat16),
            pltpu.VMEM((KMAX // WIDE, rows, WIDE * BLOCK), jnp.float32),
            pltpu.VMEM((rows, HD), jnp.float32),
            pltpu.VMEM((rows, HD), jnp.float32),
            pltpu.VMEM((rows, HD), jnp.float32),
            pltpu.SMEM((n_rows, KMAX), jnp.int32),
        ],
        compiler_params=pltpu.CompilerParams(vmem_limit_bytes=ATTENTION_VMEM),
        cost_estimate=pl.CostEstimate(flops=ATT_FLOPS, bytes_accessed=0, transcendentals=0),
        name="attention",
    )(coords, block_list, q, *pieces)


def stack_kernel(groups, *refs):
    pieces, outs = refs[: -len(groups)], refs[-len(groups) :]
    for group, out in zip(groups, outs):
        for i, at in enumerate(group):
            out[i] = pieces[at][...]


def stack(pieces, groups):
    return pl.pallas_call(
        functools.partial(stack_kernel, groups),
        out_shape=[
            jax.ShapeDtypeStruct((len(group), *pieces[0].shape), pieces[0].dtype) for group in groups
        ],
        in_specs=[VMEM] * len(pieces),
        out_specs=[VMEM] * len(groups),
        compiler_params=pltpu.CompilerParams(vmem_limit_bytes=PROJECT_VMEM),
        cost_estimate=FREE,
        name="stack",
    )(*pieces)


def project_kernel(steps, coords, own_ref, near_ref, w_ref, w0a, w0b, w1a, w1b, *out_refs):
    core, yl, z = coords[2], coords[3], coords[4]

    def lanes(block):
        return pl.ds(pl.multiple_of(block * 512, 512), 512)

    for step, out_ref in zip(steps, out_refs):
        target = (z + step + NZ) % NZ
        mine = target // 4 == core
        part = lanes(target % 4)
        value = jnp.dot(
            own_ref[...], w_ref[:, lanes(yl * NZ + target)], preferred_element_type=jnp.float32
        )
        value += jnp.dot(
            near_ref[:, :NEAR_ROWS],
            jnp.where(mine, w0a[:, part], w0b[:, part]),
            preferred_element_type=jnp.float32,
        )
        value += jnp.dot(
            near_ref[:, NEAR_ROWS:],
            jnp.where(mine, w1a[:, part], w1b[:, part]),
            preferred_element_type=jnp.float32,
        )
        out_ref[...] = value.astype(jnp.bfloat16)


def project(coords, steps, own, near, weights, parts):
    rows = own.shape[0]
    count = len(steps)
    return pl.pallas_call(
        functools.partial(project_kernel, steps),
        out_shape=[jax.ShapeDtypeStruct((rows, 512), jnp.bfloat16)] * count,
        in_specs=[SMEM] + [VMEM] * 7,
        out_specs=[VMEM] * count,
        compiler_params=pltpu.CompilerParams(vmem_limit_bytes=PROJECT_VMEM),
        cost_estimate=FREE,
        name="project",
    )(coords, own, near, weights, *parts)


def shards(queries, keys_values, block_list, out_weight):
    ctx = lax.axis_index("ctx")
    tp = lax.axis_index("tp")
    coords = jnp.stack([ctx // 4, (ctx // 2) % 2, ctx % 2, tp // NZ, tp % NZ]).astype(jnp.int32)
    n_rows = queries.shape[0] // BLOCK // CHUNKS
    barrier = lax.optimization_barrier

    yl, z = tp // NZ, tp % NZ
    own = lax.dynamic_slice_in_dim(keys_values, (yl * 4 + z // 2) * HD, HD, 2)
    for_far = lax.dynamic_slice_in_dim(keys_values, ((1 - yl) * 4 + z // 2) * HD, HD, 2)
    far = send(for_far, "y_far")
    left = send(own, "x+")
    right = send(own, "x-")

    near_w, far_w = pick(coords, out_weight)
    far, left, right, near_w = barrier((far, left, right, near_w))
    near_part = send(near_w, "y_near")
    one, other = stack([own, far, left, right], ((1, 2), (0, 3)))
    both = send(one, "x+")
    far_right = send(far, "x-")
    one_t = send(one, "core")
    other_t = send(other, "core")
    far_w, _ = barrier((far_w, other_t))
    far_part = send(far_w, "y_far")
    two_far = send(far_right, "x-")
    late = [both, far_right, two_far]
    pieces = [one, other, one_t, other_t, *late, *(send(piece, "core") for piece in late)]
    slots = ((2, 12), (0, 4), (3, 13), (1, 5), (14, 8), (6,), (10,), (15, 9), (7,), (11,))

    attended = [
        attention(coords, block_list, queries, k * n_rows, n_rows, pieces, slots)
        for k in range(CHUNKS)
    ]
    near = [send(done, "y_near") for done in attended]
    near_part, far_part, _ = barrier((near_part, far_part, attended[0]))
    near_other = send(near_part, "core")
    far_part, near_other = barrier((far_part, near_other))
    parts = [near_part, near_other, far_part, send(far_part, "core")]

    def add(*terms):
        return sum(t.astype(jnp.float32) for t in terms).astype(jnp.bfloat16)

    moves = ("z+", "z-")
    ways, moving = [], []
    for k in range(CHUNKS):
        orders = ((4, 3, 2, 1), (-3, -2, -1)) if k % 2 == 0 else ((3, 2, 1), (-4, -3, -2, -1))
        if k:
            near[k], moving[k - 1][1] = barrier((near[k], moving[k - 1][1]))
        early = tuple(order[0] for order in orders)
        late = (*orders[0][1:], *orders[1][1:], 0)
        begun = project(coords, early, attended[k], near[k], out_weight, parts)
        moving.append([send(value, move) for value, move in zip(begun, moves)])
        partial = dict(zip(late, project(coords, late, attended[k], near[k], out_weight, parts)))
        ways.append((orders, partial))

    for step in range(1, 4):
        for k in range(CHUNKS):
            orders, partial = ways[k]
            for way, order in enumerate(orders):
                if step < len(order):
                    moving[k][way] = send(add(moving[k][way], partial[order[step]]), moves[way])
    results = [add(ways[k][1][0], *moving[k]) for k in range(CHUNKS)]
    return jnp.concatenate(results, 0)


def solution(mesh):
    in_specs = (P("ctx", "tp"), P(None, "ctx", None), P("ctx", None), P("tp", None))
    return jax.shard_map(
        shards, mesh=mesh, in_specs=in_specs, out_specs=P("ctx", "tp"), check_vma=False
    )
```

time: 350 us -> 110 us (0.31)
  waiting for transfers between devices: 231 us -> 48.9 us
  matrix products: 56.3 us -> 0 us
  starting transfers between devices: 2.72 us -> 37.7 us
  local copies, waits for them, and re-layouts: 26.7 us -> 1.18 us
  Pallas kernels: 0 us -> 19.8 us
  other arithmetic: 18.2 us -> 1.7 us
  between operations: 13.5 us -> 0.24 us
    reduce_scatter x1 -> x0, waiting for transfers between devices: 118 us -> none  [shards(): lax.psum_scatter(partial_value.astype(jnp.bfloat16), 'tp', scatter_dimens...]
    ppermute x15 -> x31, waiting for transfers between devices: 112 us -> 48.9 us  [send(): return lax.ppermute(array, AXES, MOVES[move])]
    dot_general x33 -> x0, matrix products: 56.3 us -> none  [the longest x16 31.2 us: slice_update(): jnp.einsum('kgtu,ukd->kgtd', weights.astype(jnp.bfloat16), vals, preferre...]
    ppermute x15 -> x31, starting transfers between devices: 2.72 us -> 37.7 us  [send(): return lax.ppermute(array, AXES, MOVES[move])]
    pallas_call x0 -> x8, Pallas kernels: none -> 19.8 us  [the longest x2 10.2 us: attention(): pl.pallas_call(functools.partial(attention_kernel, first_row, n_rows, slo...]
    while x107 -> x0, local copies, waits for them, and re-layouts: 18.9 us -> none
    reduce_sum x16 -> x0, other arithmetic: 16.7 us -> none  [slice_update(): total = total * factor + jnp.sum(weights, axis=-1)]
  transfers between devices with their start and end apart: 16 -> 31, of which waited for: 16 -> 18; matrix products, arithmetic and copies ran while one was open for 2% -> 1% of each run, Pallas kernels for 0% -> 18%
where the time goes in v4:
time: 110 us; the launch traced here: 109 us
  waiting for transfers between devices  48.9 us (44%)
  starting transfers between devices  37.7 us (34%)
  Pallas kernels  19.8 us (18%)
  other arithmetic  1.7 us (2%)
  local copies, waits for them, and re-layouts  1.18 us (1%)
    ppermute x31, waiting for transfers between devices, send(): return lax.ppermute(array, AXES, MOVES[move])  48.9 us
    ppermute x31, starting transfers between devices, send(): return lax.ppermute(array, AXES, MOVES[move])  37.7 us
    pallas_call x2, Pallas kernels, attention(): pl.pallas_call(functools.partial(attention_kernel, first_row, n_rows, slo...  10.2 us
    pallas_call x4, Pallas kernels, project(): pl.pallas_call(functools.partial(project_kernel, steps), out_shape=[jax.S...  7.46 us
  transfers between devices with their start and end apart: 31, of which 18 were waited for; matrix products, arithmetic and copies ran while one was open for 1% of the time, Pallas kernels for 18%

profile of v4, /device:TPU:6, one launch (start us, length us, event | category | flops | bytes accessed | tf_op | source)
XLA Modules:
  0.0 109.5 jit_solution(10951901506343710450)
XLA Ops:
  1.1 3.1 %collective-permute-start = (bf16[2,512,128]{2,1,0:T(8,128)(2,1)S(1)}, bf16[2,512,128]{2,1,0:T(8,128)(2,1)S(1)}, u32[]{:S(2)}, u32[]{:S(2)}) collective-permute-start(bf16[2,512,128]{2,1,0:T(8,128)(2,1)S(1)} %get-tuple-element.67), channel_id=1, source_target_pairs={{0,40},{1,41},{2,42},{3,43},{4,44},{5,45},{6,46},{7,47},{16,56},{1... | collective-permute-start | bytes 786440 | tf_op jit(solution)/shard_map/ppermute | solution.py:58
  4.7 1.5 %collective-permute-start.2 = (bf16[2,512,128]{2,1,0:T(8,128)(2,1)S(1)}, bf16[2,512,128]{2,1,0:T(8,128)(2,1)S(1)}, u32[]{:S(2)}, u32[]{:S(2)}) collective-permute-start(bf16[2,512,128]{2,1,0:T(8,128)(2,1)S(1)} %get-tuple-element.68.refs_0_), channel_id=1, source_target_pairs={{0,192},{1,193},{2,194},{3,195},{4,196},{5,197},{6,198},{7,199},{1... | collective-permute-start | bytes 786440 | tf_op jit(solution)/shard_map/ppermute | solution.py:58
  6.3 2.1 %pick.1 = (bf16[256,2048]{1,0:T(8,128)(2,1)S(1)}, bf16[256,2048]{1,0:T(8,128)(2,1)S(1)}) custom-call(s32[5]{0:T(128)S(1)} %stack.24.coords, bf16[512,8192]{1,0:T(8,128)(2,1)} %w_ref.9), custom_call_target="tpu_custom_call" | custom-call | tf_op jit(solution)/shard_map/pick/pallas_call | solution.py:84
  8.4 2.1 %collective-permute-done.refs_1_ = bf16[2,512,128]{2,1,0:T(8,128)(2,1)S(1)} collective-permute-done((bf16[2,512,128]{2,1,0:T(8,128)(2,1)S(1)}, bf16[2,512,128]{2,1,0:T(8,128)(2,1)S(1)}, u32[]{:S(2)}, u32[]{:S(2)}) %collective-permute-start) | collective-permute-done | bytes 262176 | tf_op jit(solution)/shard_map/ppermute | solution.py:58
  10.5 1.5 %collective-permute-done.1.refs_2_ = bf16[2,512,128]{2,1,0:T(8,128)(2,1)S(1)} collective-permute-done((bf16[2,512,128]{2,1,0:T(8,128)(2,1)S(1)}, bf16[2,512,128]{2,1,0:T(8,128)(2,1)S(1)}, u32[]{:S(2)}, u32[]{:S(2)}) %collective-permute-start.1) | collective-permute-done | bytes 262176 | tf_op jit(solution)/shard_map/ppermute | solution.py:58
  11.9 1.4 %collective-permute-done.2.refs_3_ = bf16[2,512,128]{2,1,0:T(8,128)(2,1)S(1)} collective-permute-done((bf16[2,512,128]{2,1,0:T(8,128)(2,1)S(1)}, bf16[2,512,128]{2,1,0:T(8,128)(2,1)S(1)}, u32[]{:S(2)}, u32[]{:S(2)}) %collective-permute-start.2) | collective-permute-done | bytes 262176 | tf_op jit(solution)/shard_map/ppermute | solution.py:58
  14.0 1.8 %collective-permute-start.6 = (bf16[2,512,128]{2,1,0:T(8,128)(2,1)S(1)}, bf16[2,512,128]{2,1,0:T(8,128)(2,1)S(1)}, u32[]{:S(2)}, u32[]{:S(2)}) collective-permute-start(bf16[2,512,128]{2,1,0:T(8,128)(2,1)S(1)} %collective-permute-done.refs_1_), channel_id=1, source_target_pairs={{0,192},{1,193},{2,194},{3,195},{4,196},{5,197},{6,198},{7,199},{1... | collective-permute-start | bytes 786440 | tf_op jit(solution)/shard_map/ppermute | solution.py:58
  17.0 6.8 %collective-permute-done.6.refs_5_ = bf16[2,512,128]{2,1,0:T(8,128)(2,1)S(1)} collective-permute-done((bf16[2,512,128]{2,1,0:T(8,128)(2,1)S(1)}, bf16[2,512,128]{2,1,0:T(8,128)(2,1)S(1)}, u32[]{:S(2)}, u32[]{:S(2)}) %collective-permute-start.6) | collective-permute-done | bytes 262176 | tf_op jit(solution)/shard_map/ppermute | solution.py:58
  24.4 3.5 %collective-permute-done.5.refs_4_ = bf16[2,2,512,128]{3,2,1,0:T(8,128)(2,1)S(1)} collective-permute-done((bf16[2,2,512,128]{3,2,1,0:T(8,128)(2,1)S(1)}, bf16[2,2,512,128]{3,2,1,0:T(8,128)(2,1)S(1)}, u32[]{:S(2)}, u32[]{:S(2)}) %collective-permute-start.5) | collective-permute-done | bytes 524320 | tf_op jit(solution)/shard_map/ppermute | solution.py:58
  28.4 4.4 %collective-permute-done.7.refs_6_ = bf16[2,512,128]{2,1,0:T(8,128)(2,1)S(1)} collective-permute-done((bf16[2,512,128]{2,1,0:T(8,128)(2,1)S(1)}, bf16[2,512,128]{2,1,0:T(8,128)(2,1)S(1)}, u32[]{:S(2)}, u32[]{:S(2)}) %collective-permute-start.7) | collective-permute-done | bytes 262176 | tf_op jit(solution)/shard_map/ppermute | solution.py:58
  32.8 1.5 %collective-permute-done.10.refs_9_ = bf16[2,512,128]{2,1,0:T(8,128)(2,1)S(1)} collective-permute-done((bf16[2,512,128]{2,1,0:T(8,128)(2,1)S(1)}, bf16[2,512,128]{2,1,0:T(8,128)(2,1)S(1)}, u32[]{:S(2)}, u32[]{:S(2)}) %collective-permute-start.10) | collective-permute-done | bytes 262176 | tf_op jit(solution)/shard_map/ppermute | solution.py:58
  34.3 5.1 %attention.2.own_ref = bf16[256,512]{1,0:T(8,128)(2,1)S(1)} custom-call(s32[5]{0:T(128)S(1)} %stack.24.coords, s32[4,16]{1,0:T(4,128)S(1)} %copy-done.1, bf16[512,512]{1,0:T(8,128)(2,1)S(1)} %copy-done, bf16[2,2,512,128]{3,2,1,0:T(8,128)(2,1)S(1)} %get-tuple-element.40.refs_0_, bf16[2,2,512,128]{3,2,1,0:T(8,128)(2,1)S(1)} %get-tuple-element.41.refs_1_, ...), custom_call_target="tpu_custom_call" | custom-call | flops 3000000000 | tf_op jit(solution)/shard_map/attention/pallas_call | solution.py:174
  39.5 1.5 %collective-permute-done.12.w0a = bf16[256,2048]{1,0:T(8,128)(2,1)S(1)} collective-permute-done((bf16[256,2048]{1,0:T(8,128)(2,1)S(1)}, bf16[256,2048]{1,0:T(8,128)(2,1)S(1)}, u32[]{:S(2)}, u32[]{:S(2)}) %collective-permute-start.12) | collective-permute-done | bytes 1048608 | tf_op jit(solution)/shard_map/ppermute | solution.py:58
  42.1 2.7 %collective-permute-done.14.w0b = bf16[256,2048]{1,0:T(8,128)(2,1)S(1)} collective-permute-done((bf16[256,2048]{1,0:T(8,128)(2,1)S(1)}, bf16[256,2048]{1,0:T(8,128)(2,1)S(1)}, u32[]{:S(2)}, u32[]{:S(2)}) %collective-permute-start.14) | collective-permute-done | bytes 1048608 | tf_op jit(solution)/shard_map/ppermute | solution.py:58
  45.5 5.1 %attention.3.own_ref = bf16[256,512]{1,0:T(8,128)(2,1)S(1)} custom-call(s32[5]{0:T(128)S(1)} %stack.24.coords, s32[4,16]{1,0:T(4,128)S(1)} %copy-done.1, bf16[512,512]{1,0:T(8,128)(2,1)S(1)} %copy-done, bf16[2,2,512,128]{3,2,1,0:T(8,128)(2,1)S(1)} %get-tuple-element.40.refs_0_, bf16[2,2,512,128]{3,2,1,0:T(8,128)(2,1)S(1)} %get-tuple-element.41.refs_1_, ...), custom_call_target="tpu_custom_call" | custom-call | flops 3000000000 | tf_op jit(solution)/shard_map/attention/pallas_call | solution.py:174
  50.6 1.6 %collective-permute-start.20 = (bf16[256,512]{1,0:T(8,128)(2,1)S(1)}, bf16[256,512]{1,0:T(8,128)(2,1)S(1)}, u32[]{:S(2)}, u32[]{:S(2)}) collective-permute-start(bf16[256,512]{1,0:T(8,128)(2,1)S(1)} %attention.3.own_ref), channel_id=1, source_target_pairs={{0,8},{1,9},{2,10},{3,11},{4,12},{5,13},{6,14},{7,15},{16,24},{17,... | collective-permute-start | bytes 786440 | tf_op jit(solution)/shard_map/ppermute | solution.py:58
  52.2 1.4 %collective-permute-done.11.near_ref = bf16[256,512]{1,0:T(8,128)(2,1)S(1)} collective-permute-done((bf16[256,512]{1,0:T(8,128)(2,1)S(1)}, bf16[256,512]{1,0:T(8,128)(2,1)S(1)}, u32[]{:S(2)}, u32[]{:S(2)}) %collective-permute-start.11) | collective-permute-done | bytes 262176 | tf_op jit(solution)/shard_map/ppermute | solution.py:58
  53.5 1.3 %project.5 = (bf16[256,512]{1,0:T(8,128)(2,1)S(1)}, bf16[256,512]{1,0:T(8,128)(2,1)S(1)}) custom-call(s32[5]{0:T(128)S(1)} %stack.24.coords, bf16[256,512]{1,0:T(8,128)(2,1)S(1)} %attention.2.own_ref, bf16[256,512]{1,0:T(8,128)(2,1)S(1)} %collective-permute-done.11.near_ref, bf16[512,8192]{1,0:T(8,128)(2,1)S(1)} %bitcast.6, ...), custom_call_target="tpu_custom_call" | custom-call | tf_op jit(solution)/shard_map/project/pallas_call | solution.py:243
  54.8 5.9 %collective-permute-start.21 = (bf16[256,512]{1,0:T(8,128)(2,1)S(1)}, bf16[256,512]{1,0:T(8,128)(2,1)S(1)}, u32[]{:S(2)}, u32[]{:S(2)}) collective-permute-start(bf16[256,512]{1,0:T(8,128)(2,1)S(1)} %get-tuple-element.54), channel_id=1, source_target_pairs={{0,7},{1,0},{2,1},{3,2},{4,3},{5,4},{6,5},{7,6},{16,23},{17,16},{1... | collective-permute-start | bytes 786440 | tf_op jit(solution)/shard_map/ppermute | solution.py:58
  60.8 2.4 %project.4 = (bf16[256,512]{1,0:T(8,128)(2,1)S(1)}, bf16[256,512]{1,0:T(8,128)(2,1)S(1)}, bf16[256,512]{1,0:T(8,128)(2,1)S(1)}, bf16[256,512]{1,0:T(8,128)(2,1)S...) custom-call(s32[5]{0:T(128)S(1)} %stack.24.coords, bf16[256,512]{1,0:T(8,128)(2,1)S(1)} %attention.2.own_ref, ...), custom_call_target="tpu_custom_call" | custom-call | tf_op jit(solution)/shard_map/project/pallas_call | solution.py:243
  63.2 2.8 %collective-permute-done.21 = bf16[256,512]{1,0:T(8,128)(2,1)S(1)} collective-permute-done((bf16[256,512]{1,0:T(8,128)(2,1)S(1)}, bf16[256,512]{1,0:T(8,128)(2,1)S(1)}, u32[]{:S(2)}, u32[]{:S(2)}) %collective-permute-start.21) | collective-permute-done | bytes 262176 | tf_op jit(solution)/shard_map/ppermute | solution.py:58
  67.4 3.8 %collective-permute-start.27 = (bf16[256,512]{1,0:T(8,128)(2,1)S(1)}, bf16[256,512]{1,0:T(8,128)(2,1)S(1)}, u32[]{:S(2)}, u32[]{:S(2)}) collective-permute-start(bf16[256,512]{1,0:T(8,128)(2,1)S(1)} %get-tuple-element.63), channel_id=1, source_target_pairs={{0,7},{1,0},{2,1},{3,2},{4,3},{5,4},{6,5},{7,6},{16,23},{17,16},{1... | collective-permute-start | bytes 786440 | tf_op jit(solution)/shard_map/ppermute | solution.py:58
  71.2 3.3 %collective-permute-start.22 = (bf16[256,512]{1,0:T(8,128)(2,1)S(1)}, bf16[256,512]{1,0:T(8,128)(2,1)S(1)}, u32[]{:S(2)}, u32[]{:S(2)}) collective-permute-start(bf16[256,512]{1,0:T(8,128)(2,1)S(1)} %add_convert_fusion.8), channel_id=1, source_target_pairs={{0,7},{1,0},{2,1},{3,2},{4,3},{5,4},{6,5},{7,6},{16,23},{17,16},{1... | collective-permute-start | bytes 786440 | tf_op jit(solution)/shard_map/ppermute | solution.py:58
  74.7 2.4 %project.6 = (bf16[256,512]{1,0:T(8,128)(2,1)S(1)}, bf16[256,512]{1,0:T(8,128)(2,1)S(1)}, bf16[256,512]{1,0:T(8,128)(2,1)S(1)}, bf16[256,512]{1,0:T(8,128)(2,1)S...) custom-call(s32[5]{0:T(128)S(1)} %stack.24.coords, bf16[256,512]{1,0:T(8,128)(2,1)S(1)} %attention.3.own_ref, ...), custom_call_target="tpu_custom_call" | custom-call | tf_op jit(solution)/shard_map/project/pallas_call | solution.py:243
  78.0 3.8 %collective-permute-start.28 = (bf16[256,512]{1,0:T(8,128)(2,1)S(1)}, bf16[256,512]{1,0:T(8,128)(2,1)S(1)}, u32[]{:S(2)}, u32[]{:S(2)}) collective-permute-start(bf16[256,512]{1,0:T(8,128)(2,1)S(1)} %add_convert_fusion.3), channel_id=1, source_target_pairs={{0,7},{1,0},{2,1},{3,2},{4,3},{5,4},{6,5},{7,6},{16,23},{17,16},{1... | collective-permute-start | bytes 786440 | tf_op jit(solution)/shard_map/ppermute | solution.py:58
  82.1 5.0 %collective-permute-done.17 = bf16[256,512]{1,0:T(8,128)(2,1)S(1)} collective-permute-done((bf16[256,512]{1,0:T(8,128)(2,1)S(1)}, bf16[256,512]{1,0:T(8,128)(2,1)S(1)}, u32[]{:S(2)}, u32[]{:S(2)}) %collective-permute-start.17) | collective-permute-done | bytes 262176 | tf_op jit(solution)/shard_map/ppermute | solution.py:58
  87.3 3.3 %collective-permute-start.23 = (bf16[256,512]{1,0:T(8,128)(2,1)S(1)}, bf16[256,512]{1,0:T(8,128)(2,1)S(1)}, u32[]{:S(2)}, u32[]{:S(2)}) collective-permute-start(bf16[256,512]{1,0:T(8,128)(2,1)S(1)} %add_convert_fusion.7), channel_id=1, source_target_pairs={{0,7},{1,0},{2,1},{3,2},{4,3},{5,4},{6,5},{7,6},{16,23},{17,16},{1... | collective-permute-start | bytes 786440 | tf_op jit(solution)/shard_map/ppermute | solution.py:58
  91.9 3.9 %collective-permute-done.18 = bf16[256,512]{1,0:T(8,128)(2,1)S(1)} collective-permute-done((bf16[256,512]{1,0:T(8,128)(2,1)S(1)}, bf16[256,512]{1,0:T(8,128)(2,1)S(1)}, u32[]{:S(2)}, u32[]{:S(2)}) %collective-permute-start.18) | collective-permute-done | bytes 262176 | tf_op jit(solution)/shard_map/ppermute | solution.py:58
  96.1 2.7 %collective-permute-done.29 = bf16[256,512]{1,0:T(8,128)(2,1)S(1)} collective-permute-done((bf16[256,512]{1,0:T(8,128)(2,1)S(1)}, bf16[256,512]{1,0:T(8,128)(2,1)S(1)}, u32[]{:S(2)}, u32[]{:S(2)}) %collective-permute-start.29) | collective-permute-done | bytes 262176 | tf_op jit(solution)/shard_map/ppermute | solution.py:58
  98.9 3.8 %collective-permute-start.30 = (bf16[256,512]{1,0:T(8,128)(2,1)S(1)}, bf16[256,512]{1,0:T(8,128)(2,1)S(1)}, u32[]{:S(2)}, u32[]{:S(2)}) collective-permute-start(bf16[256,512]{1,0:T(8,128)(2,1)S(1)} %add_convert_fusion.1), channel_id=1, source_target_pairs={{0,7},{1,0},{2,1},{3,2},{4,3},{5,4},{6,5},{7,6},{16,23},{17,16},{1... | collective-permute-start | bytes 786440 | tf_op jit(solution)/shard_map/ppermute | solution.py:58
  102.7 3.0 %collective-permute-done.19 = bf16[256,512]{1,0:T(8,128)(2,1)S(1)} collective-permute-done((bf16[256,512]{1,0:T(8,128)(2,1)S(1)}, bf16[256,512]{1,0:T(8,128)(2,1)S(1)}, u32[]{:S(2)}, u32[]{:S(2)}) %collective-permute-start.19) | collective-permute-done | bytes 262176 | tf_op jit(solution)/shard_map/ppermute | solution.py:58
  105.8 2.7 %collective-permute-done.26 = bf16[256,512]{1,0:T(8,128)(2,1)S(1)} collective-permute-done((bf16[256,512]{1,0:T(8,128)(2,1)S(1)}, bf16[256,512]{1,0:T(8,128)(2,1)S(1)}, u32[]{:S(2)}, u32[]{:S(2)}) %collective-permute-start.26) | collective-permute-done | bytes 262176 | tf_op jit(solution)/shard_map/ppermute | solution.py:58
  (62 shorter events, 12.1 us)
Async XLA Ops:
  1.1 9.4 %collective-permute-start = (bf16[2,512,128]{2,1,0:T(8,128)(2,1)S(1)}, bf16[2,512,128]{2,1,0:T(8,128)(2,1)S(1)}, u32[]{:S(2)}, u32[]{:S(2)}) collective-permute-start(bf16[2,512,128]{2,1,0:T(8,128)(2,1)S(1)} %get-tuple-element.67), channel_id=1, source_target_pairs={{0,40},{1,41},{2,42},{3,43},{4,44},{5,45},{6,46},{7,47},{16,56},{1... | collective-permute-start | bytes 786440 | tf_op jit(solution)/shard_map/ppermute | solution.py:58
  4.2 7.8 %collective-permute-start.1 = (bf16[2,512,128]{2,1,0:T(8,128)(2,1)S(1)}, bf16[2,512,128]{2,1,0:T(8,128)(2,1)S(1)}, u32[]{:S(2)}, u32[]{:S(2)}) collective-permute-start(bf16[2,512,128]{2,1,0:T(8,128)(2,1)S(1)} %get-tuple-element.68.refs_0_), channel_id=1, source_target_pairs={{0,64},{1,65},{2,66},{3,67},{4,68},{5,69},{6,70},{7,71},{16,80},{1... | collective-permute-start | bytes 786440 | tf_op jit(solution)/shard_map/ppermute | solution.py:58
  4.7 8.7 %collective-permute-start.2 = (bf16[2,512,128]{2,1,0:T(8,128)(2,1)S(1)}, bf16[2,512,128]{2,1,0:T(8,128)(2,1)S(1)}, u32[]{:S(2)}, u32[]{:S(2)}) collective-permute-start(bf16[2,512,128]{2,1,0:T(8,128)(2,1)S(1)} %get-tuple-element.68.refs_0_), channel_id=1, source_target_pairs={{0,192},{1,193},{2,194},{3,195},{4,196},{5,197},{6,198},{7,199},{1... | collective-permute-start | bytes 786440 | tf_op jit(solution)/shard_map/ppermute | solution.py:58
  6.3 28.0 %copy-start.1 = (s32[4,16]{1,0:T(4,128)S(1)}, s32[4,16]{1,0:T(4,128)}, u32[]{:S(2)}) copy-start(s32[4,16]{1,0:T(4,128)} %block_list.3) | copy-start | bytes 772
  13.4 2.5 %collective-permute-start.4 = (bf16[2,2,512,128]{3,2,1,0:T(8,128)(2,1)S(1)}, bf16[2,2,512,128]{3,2,1,0:T(8,128)(2,1)S(1)}, u32[]{:S(2)}, u32[]{:S(2)}) collective-permute-start(bf16[2,2,512,128]{3,2,1,0:T(8,128)(2,1)S(1)} %get-tuple-element.41.refs_1_), channel_id=1, source_target_pairs={{0,16},{1,17},{2,18},{3,19},{4,20},{5,21},{6,22},{7,23},{16,0},{17... | collective-permute-start | bytes 1572872 | tf_op jit(solution)/shard_map/ppermute | solution.py:58
  13.5 14.3 %collective-permute-start.5 = (bf16[2,2,512,128]{3,2,1,0:T(8,128)(2,1)S(1)}, bf16[2,2,512,128]{3,2,1,0:T(8,128)(2,1)S(1)}, u32[]{:S(2)}, u32[]{:S(2)}) collective-permute-start(bf16[2,2,512,128]{3,2,1,0:T(8,128)(2,1)S(1)} %get-tuple-element.40.refs_0_), channel_id=1, source_target_pairs={{0,64},{1,65},{2,66},{3,67},{4,68},{5,69},{6,70},{7,71},{16,80},{1... | collective-permute-start | bytes 1572872 | tf_op jit(solution)/shard_map/ppermute | solution.py:58
  13.9 14.0 %collective-permute-start.3 = (bf16[2,2,512,128]{3,2,1,0:T(8,128)(2,1)S(1)}, bf16[2,2,512,128]{3,2,1,0:T(8,128)(2,1)S(1)}, u32[]{:S(2)}, u32[]{:S(2)}) collective-permute-start(bf16[2,2,512,128]{3,2,1,0:T(8,128)(2,1)S(1)} %get-tuple-element.40.refs_0_), channel_id=1, source_target_pairs={{0,16},{1,17},{2,18},{3,19},{4,20},{5,21},{6,22},{7,23},{16,0},{17... | collective-permute-start | bytes 1572872 | tf_op jit(solution)/shard_map/ppermute | solution.py:58
  14.0 9.8 %collective-permute-start.6 = (bf16[2,512,128]{2,1,0:T(8,128)(2,1)S(1)}, bf16[2,512,128]{2,1,0:T(8,128)(2,1)S(1)}, u32[]{:S(2)}, u32[]{:S(2)}) collective-permute-start(bf16[2,512,128]{2,1,0:T(8,128)(2,1)S(1)} %collective-permute-done.refs_1_), channel_id=1, source_target_pairs={{0,192},{1,193},{2,194},{3,195},{4,196},{5,197},{6,198},{7,199},{1... | collective-permute-start | bytes 786440 | tf_op jit(solution)/shard_map/ppermute | solution.py:58
  15.8 25.1 %collective-permute-start.12 = (bf16[256,2048]{1,0:T(8,128)(2,1)S(1)}, bf16[256,2048]{1,0:T(8,128)(2,1)S(1)}, u32[]{:S(2)}, u32[]{:S(2)}) collective-permute-start(bf16[256,2048]{1,0:T(8,128)(2,1)S(1)} %get-tuple-element.42), channel_id=1, source_target_pairs={{0,8},{1,9},{2,10},{3,11},{4,12},{5,13},{6,14},{7,15},{16,24},{17,... | collective-permute-start | bytes 3145736 | tf_op jit(solution)/shard_map/ppermute | solution.py:58
  15.9 26.2 %collective-permute-start.13 = (bf16[256,2048]{1,0:T(8,128)(2,1)S(1)}, bf16[256,2048]{1,0:T(8,128)(2,1)S(1)}, u32[]{:S(2)}, u32[]{:S(2)}) collective-permute-start(bf16[256,2048]{1,0:T(8,128)(2,1)S(1)} %get-tuple-element.44), channel_id=1, source_target_pairs={{0,40},{1,41},{2,42},{3,43},{4,44},{5,45},{6,46},{7,47},{16,56},{1... | collective-permute-start | bytes 3145736 | tf_op jit(solution)/shard_map/ppermute | solution.py:58
  23.8 9.0 %collective-permute-start.7 = (bf16[2,512,128]{2,1,0:T(8,128)(2,1)S(1)}, bf16[2,512,128]{2,1,0:T(8,128)(2,1)S(1)}, u32[]{:S(2)}, u32[]{:S(2)}) collective-permute-start(bf16[2,512,128]{2,1,0:T(8,128)(2,1)S(1)} %collective-permute-done.6.refs_5_), channel_id=1, source_target_pairs={{0,192},{1,193},{2,194},{3,195},{4,196},{5,197},{6,198},{7,199},{1... | collective-permute-start | bytes 786440 | tf_op jit(solution)/shard_map/ppermute | solution.py:58
  27.9 6.5 %collective-permute-start.8 = (bf16[2,2,512,128]{3,2,1,0:T(8,128)(2,1)S(1)}, bf16[2,2,512,128]{3,2,1,0:T(8,128)(2,1)S(1)}, u32[]{:S(2)}, u32[]{:S(2)}) collective-permute-start(bf16[2,2,512,128]{3,2,1,0:T(8,128)(2,1)S(1)} %collective-permute-done.5.refs_4_), channel_id=1, source_target_pairs={{0,16},{1,17},{2,18},{3,19},{4,20},{5,21},{6,22},{7,23},{16,0},{17... | collective-permute-start | bytes 1572872 | tf_op jit(solution)/shard_map/ppermute | solution.py:58
  27.9 4.9 %collective-permute-start.9 = (bf16[2,512,128]{2,1,0:T(8,128)(2,1)S(1)}, bf16[2,512,128]{2,1,0:T(8,128)(2,1)S(1)}, u32[]{:S(2)}, u32[]{:S(2)}) collective-permute-start(bf16[2,512,128]{2,1,0:T(8,128)(2,1)S(1)} %collective-permute-done.6.refs_5_), channel_id=1, source_target_pairs={{0,16},{1,17},{2,18},{3,19},{4,20},{5,21},{6,22},{7,23},{16,0},{17... | collective-permute-start | bytes 786440 | tf_op jit(solution)/shard_map/ppermute | solution.py:58
  32.8 1.5 %collective-permute-start.10 = (bf16[2,512,128]{2,1,0:T(8,128)(2,1)S(1)}, bf16[2,512,128]{2,1,0:T(8,128)(2,1)S(1)}, u32[]{:S(2)}, u32[]{:S(2)}) collective-permute-start(bf16[2,512,128]{2,1,0:T(8,128)(2,1)S(1)} %collective-permute-done.7.refs_6_), channel_id=1, source_target_pairs={{0,16},{1,17},{2,18},{3,19},{4,20},{5,21},{6,22},{7,23},{16,0},{17... | collective-permute-start | bytes 786440 | tf_op jit(solution)/shard_map/ppermute | solution.py:58
  42.1 2.7 %collective-permute-start.14 = (bf16[256,2048]{1,0:T(8,128)(2,1)S(1)}, bf16[256,2048]{1,0:T(8,128)(2,1)S(1)}, u32[]{:S(2)}, u32[]{:S(2)}) collective-permute-start(bf16[256,2048]{1,0:T(8,128)(2,1)S(1)} %collective-permute-done.12.w0a), channel_id=1, source_target_pairs={{0,16},{1,17},{2,18},{3,19},{4,20},{5,21},{6,22},{7,23},{16,0},{17... | collective-permute-start | bytes 3145736 | tf_op jit(solution)/shard_map/ppermute | solution.py:58
  44.8 8.7 %collective-permute-start.15 = (bf16[256,2048]{1,0:T(8,128)(2,1)S(1)}, bf16[256,2048]{1,0:T(8,128)(2,1)S(1)}, u32[]{:S(2)}, u32[]{:S(2)}) collective-permute-start(bf16[256,2048]{1,0:T(8,128)(2,1)S(1)} %collective-permute-done.13.w1a), channel_id=1, source_target_pairs={{0,16},{1,17},{2,18},{3,19},{4,20},{5,21},{6,22},{7,23},{16,0},{17... | collective-permute-start | bytes 3145736 | tf_op jit(solution)/shard_map/ppermute | solution.py:58
  44.9 8.6 %collective-permute-start.11 = (bf16[256,512]{1,0:T(8,128)(2,1)S(1)}, bf16[256,512]{1,0:T(8,128)(2,1)S(1)}, u32[]{:S(2)}, u32[]{:S(2)}) collective-permute-start(bf16[256,512]{1,0:T(8,128)(2,1)S(1)} %attention.2.own_ref), channel_id=1, source_target_pairs={{0,8},{1,9},{2,10},{3,11},{4,12},{5,13},{6,14},{7,15},{16,24},{17,... | collective-permute-start | bytes 786440 | tf_op jit(solution)/shard_map/ppermute | solution.py:58
  50.6 12.6 %collective-permute-start.20 = (bf16[256,512]{1,0:T(8,128)(2,1)S(1)}, bf16[256,512]{1,0:T(8,128)(2,1)S(1)}, u32[]{:S(2)}, u32[]{:S(2)}) collective-permute-start(bf16[256,512]{1,0:T(8,128)(2,1)S(1)} %attention.3.own_ref), channel_id=1, source_target_pairs={{0,8},{1,9},{2,10},{3,11},{4,12},{5,13},{6,14},{7,15},{16,24},{17,... | collective-permute-start | bytes 786440 | tf_op jit(solution)/shard_map/ppermute | solution.py:58
  54.8 11.2 %collective-permute-start.21 = (bf16[256,512]{1,0:T(8,128)(2,1)S(1)}, bf16[256,512]{1,0:T(8,128)(2,1)S(1)}, u32[]{:S(2)}, u32[]{:S(2)}) collective-permute-start(bf16[256,512]{1,0:T(8,128)(2,1)S(1)} %get-tuple-element.54), channel_id=1, source_target_pairs={{0,7},{1,0},{2,1},{3,2},{4,3},{5,4},{6,5},{7,6},{16,23},{17,16},{1... | collective-permute-start | bytes 786440 | tf_op jit(solution)/shard_map/ppermute | solution.py:58
  60.8 13.7 %collective-permute-start.16 = (bf16[256,512]{1,0:T(8,128)(2,1)S(1)}, bf16[256,512]{1,0:T(8,128)(2,1)S(1)}, u32[]{:S(2)}, u32[]{:S(2)}) collective-permute-start(bf16[256,512]{1,0:T(8,128)(2,1)S(1)} %get-tuple-element.50), channel_id=1, source_target_pairs={{0,1},{1,2},{2,3},{3,4},{4,5},{5,6},{6,7},{7,0},{16,17},{17,18},{1... | collective-permute-start | bytes 786440 | tf_op jit(solution)/shard_map/ppermute | solution.py:58
  67.4 10.5 %collective-permute-start.27 = (bf16[256,512]{1,0:T(8,128)(2,1)S(1)}, bf16[256,512]{1,0:T(8,128)(2,1)S(1)}, u32[]{:S(2)}, u32[]{:S(2)}) collective-permute-start(bf16[256,512]{1,0:T(8,128)(2,1)S(1)} %get-tuple-element.63), channel_id=1, source_target_pairs={{0,7},{1,0},{2,1},{3,2},{4,3},{5,4},{6,5},{7,6},{16,23},{17,16},{1... | collective-permute-start | bytes 786440 | tf_op jit(solution)/shard_map/ppermute | solution.py:58
  71.1 10.6 %collective-permute-start.24 = (bf16[256,512]{1,0:T(8,128)(2,1)S(1)}, bf16[256,512]{1,0:T(8,128)(2,1)S(1)}, u32[]{:S(2)}, u32[]{:S(2)}) collective-permute-start(bf16[256,512]{1,0:T(8,128)(2,1)S(1)} %get-tuple-element.60), channel_id=1, source_target_pairs={{0,1},{1,2},{2,3},{3,4},{4,5},{5,6},{6,7},{7,0},{16,17},{17,18},{1... | collective-permute-start | bytes 786440 | tf_op jit(solution)/shard_map/ppermute | solution.py:58
  71.2 16.0 %collective-permute-start.22 = (bf16[256,512]{1,0:T(8,128)(2,1)S(1)}, bf16[256,512]{1,0:T(8,128)(2,1)S(1)}, u32[]{:S(2)}, u32[]{:S(2)}) collective-permute-start(bf16[256,512]{1,0:T(8,128)(2,1)S(1)} %add_convert_fusion.8), channel_id=1, source_target_pairs={{0,7},{1,0},{2,1},{3,2},{4,3},{5,4},{6,5},{7,6},{16,23},{17,16},{1... | collective-permute-start | bytes 786440 | tf_op jit(solution)/shard_map/ppermute | solution.py:58
  74.6 12.5 %collective-permute-start.17 = (bf16[256,512]{1,0:T(8,128)(2,1)S(1)}, bf16[256,512]{1,0:T(8,128)(2,1)S(1)}, u32[]{:S(2)}, u32[]{:S(2)}) collective-permute-start(bf16[256,512]{1,0:T(8,128)(2,1)S(1)} %add_convert_fusion.11), channel_id=1, source_target_pairs={{0,1},{1,2},{2,3},{3,4},{4,5},{5,6},{6,7},{7,0},{16,17},{17,18},{1... | collective-permute-start | bytes 786440 | tf_op jit(solution)/shard_map/ppermute | solution.py:58
  78.0 12.7 %collective-permute-start.28 = (bf16[256,512]{1,0:T(8,128)(2,1)S(1)}, bf16[256,512]{1,0:T(8,128)(2,1)S(1)}, u32[]{:S(2)}, u32[]{:S(2)}) collective-permute-start(bf16[256,512]{1,0:T(8,128)(2,1)S(1)} %add_convert_fusion.3), channel_id=1, source_target_pairs={{0,7},{1,0},{2,1},{3,2},{4,3},{5,4},{6,5},{7,6},{16,23},{17,16},{1... | collective-permute-start | bytes 786440 | tf_op jit(solution)/shard_map/ppermute | solution.py:58
  81.8 14.1 %collective-permute-start.25 = (bf16[256,512]{1,0:T(8,128)(2,1)S(1)}, bf16[256,512]{1,0:T(8,128)(2,1)S(1)}, u32[]{:S(2)}, u32[]{:S(2)}) collective-permute-start(bf16[256,512]{1,0:T(8,128)(2,1)S(1)} %add_convert_fusion.5), channel_id=1, source_target_pairs={{0,1},{1,2},{2,3},{3,4},{4,5},{5,6},{6,7},{7,0},{16,17},{17,18},{1... | collective-permute-start | bytes 786440 | tf_op jit(solution)/shard_map/ppermute | solution.py:58
  87.1 8.6 %collective-permute-start.18 = (bf16[256,512]{1,0:T(8,128)(2,1)S(1)}, bf16[256,512]{1,0:T(8,128)(2,1)S(1)}, u32[]{:S(2)}, u32[]{:S(2)}) collective-permute-start(bf16[256,512]{1,0:T(8,128)(2,1)S(1)} %add_convert_fusion.10), channel_id=1, source_target_pairs={{0,1},{1,2},{2,3},{3,4},{4,5},{5,6},{6,7},{7,0},{16,17},{17,18},{1... | collective-permute-start | bytes 786440 | tf_op jit(solution)/shard_map/ppermute | solution.py:58
  87.3 15.4 %collective-permute-start.23 = (bf16[256,512]{1,0:T(8,128)(2,1)S(1)}, bf16[256,512]{1,0:T(8,128)(2,1)S(1)}, u32[]{:S(2)}, u32[]{:S(2)}) collective-permute-start(bf16[256,512]{1,0:T(8,128)(2,1)S(1)} %add_convert_fusion.7), channel_id=1, source_target_pairs={{0,7},{1,0},{2,1},{3,2},{4,3},{5,4},{6,5},{7,6},{16,23},{17,16},{1... | collective-permute-start | bytes 786440 | tf_op jit(solution)/shard_map/ppermute | solution.py:58
  90.7 8.2 %collective-permute-start.29 = (bf16[256,512]{1,0:T(8,128)(2,1)S(1)}, bf16[256,512]{1,0:T(8,128)(2,1)S(1)}, u32[]{:S(2)}, u32[]{:S(2)}) collective-permute-start(bf16[256,512]{1,0:T(8,128)(2,1)S(1)} %add_convert_fusion.2), channel_id=1, source_target_pairs={{0,7},{1,0},{2,1},{3,2},{4,3},{5,4},{6,5},{7,6},{16,23},{17,16},{1... | collective-permute-start | bytes 786440 | tf_op jit(solution)/shard_map/ppermute | solution.py:58
  95.8 9.9 %collective-permute-start.19 = (bf16[256,512]{1,0:T(8,128)(2,1)S(1)}, bf16[256,512]{1,0:T(8,128)(2,1)S(1)}, u32[]{:S(2)}, u32[]{:S(2)}) collective-permute-start(bf16[256,512]{1,0:T(8,128)(2,1)S(1)} %add_convert_fusion.9), channel_id=1, source_target_pairs={{0,1},{1,2},{2,3},{3,4},{4,5},{5,6},{6,7},{7,0},{16,17},{17,18},{1... | collective-permute-start | bytes 786440 | tf_op jit(solution)/shard_map/ppermute | solution.py:58
  96.0 12.5 %collective-permute-start.26 = (bf16[256,512]{1,0:T(8,128)(2,1)S(1)}, bf16[256,512]{1,0:T(8,128)(2,1)S(1)}, u32[]{:S(2)}, u32[]{:S(2)}) collective-permute-start(bf16[256,512]{1,0:T(8,128)(2,1)S(1)} %add_convert_fusion.4), channel_id=1, source_target_pairs={{0,1},{1,2},{2,3},{3,4},{4,5},{5,6},{6,7},{7,0},{16,17},{17,18},{1... | collective-permute-start | bytes 786440 | tf_op jit(solution)/shard_map/ppermute | solution.py:58
  98.9 9.6 %collective-permute-start.30 = (bf16[256,512]{1,0:T(8,128)(2,1)S(1)}, bf16[256,512]{1,0:T(8,128)(2,1)S(1)}, u32[]{:S(2)}, u32[]{:S(2)}) collective-permute-start(bf16[256,512]{1,0:T(8,128)(2,1)S(1)} %add_convert_fusion.1), channel_id=1, source_target_pairs={{0,7},{1,0},{2,1},{3,2},{4,3},{5,4},{6,5},{7,6},{16,23},{17,16},{1... | collective-permute-start | bytes 786440 | tf_op jit(solution)/shard_map/ppermute | solution.py:58
  (3 other events, 61.3 us)

commit v5 on v4

--- a/solution.py
+++ b/solution.py
@@ -22,7 +22,8 @@
 ATTENTION_VMEM = 14 * 2**20
 PROJECT_VMEM = 8 * 2**20
 WIDE = 4
-ATT_FLOPS = 3_000_000_000
+MARK_FLOPS = 0
+ATT_FLOPS = 0
 VMEM_LIMIT = 50 * 2**20
 FREE = pl.CostEstimate(flops=0, bytes_accessed=0, transcendentals=0)
 
@@ -94,13 +95,22 @@
 
 
 def attention_kernel(first_row, n_rows, slots, coords, block_list, q_ref, *refs):
-    pieces, refs = refs[: len(slots)], refs[len(slots) :]
-    out_ref, kv, scores, top, total, acc, placed = refs
+    if slots:
+        pieces, refs = refs[: len(slots)], refs[len(slots) :]
+        out_ref, kv, scores, top, total, acc, placed = refs
+        for piece, held in zip(pieces, slots):
+            for i, slot in enumerate(held):
+                kv[:, slot * 512 : (slot + 1) * 512, :] = piece[i] if len(held) > 1 else piece[...]
+    else:
+        kv, refs = refs[0], refs[1:]
+        before, refs = refs[:-6], refs[-6:]
+        out_ref, scores, top, total, acc, placed = refs
+        done = 0
+        for ref in before:
+            out_ref[done : done + ref.shape[0], :] = ref[...]
+            done += ref.shape[0]
+    ahead = out_ref.shape[0] - n_rows * BLOCK
     x, yh, c = coords[0], coords[1], coords[2]
-
-    for piece, held in zip(pieces, slots):
-        for i, slot in enumerate(held):
-            kv[:, slot * 512 : (slot + 1) * 512, :] = piece[i] if len(held) > 1 else piece[...]
 
     counts = []
     for row in range(n_rows):
@@ -125,7 +135,6 @@
                 tiles.append(kv[which, pl.ds(pl.multiple_of(placed[row, j], BLOCK), BLOCK), :])
             return jnp.concatenate(tiles, 0)
 
-        here = slice(row * BLOCK, (row + 1) * BLOCK)
         rows = slice((first_row + row) * BLOCK, (first_row + row + 1) * BLOCK)
         q = jnp.concatenate([q_ref[rows, g * HD : (g + 1) * HD] for g in range(GROUP)], 0)
         top[...] = jnp.full(top.shape, LOW, jnp.float32)
@@ -164,20 +173,25 @@
 
         lax.fori_loop(0, groups, second, 0)
         result = (acc[...] / jnp.sum(total[...], axis=1, keepdims=True)).astype(jnp.bfloat16)
+        here = slice(ahead + row * BLOCK, ahead + (row + 1) * BLOCK)
         for g in range(GROUP):
             out_ref[here, g * HD : (g + 1) * HD] = result[g * BLOCK : (g + 1) * BLOCK, :]
 
 
-def attention(coords, block_list, q, first_row, n_rows, pieces, slots):
+def attention(coords, block_list, q, first_row, n_rows, pieces, slots=()):
     rows = GROUP * BLOCK
-    tok, width = n_rows * BLOCK, q.shape[1]
+    width = q.shape[1]
+    tok = n_rows * BLOCK + (0 if slots else sum(piece.shape[0] for piece in pieces[1:]))
+    kv_shape = (2, SLOTS * 512, HD)
+    out_shape = [jax.ShapeDtypeStruct((tok, width), jnp.bfloat16)]
+    if slots:
+        out_shape.append(jax.ShapeDtypeStruct(kv_shape, jnp.bfloat16))
     return pl.pallas_call(
         functools.partial(attention_kernel, first_row, n_rows, slots),
-        out_shape=jax.ShapeDtypeStruct((tok, width), jnp.bfloat16),
+        out_shape=out_shape,
         in_specs=[SMEM, SMEM, VMEM] + [VMEM] * len(pieces),
-        out_specs=VMEM,
+        out_specs=[VMEM] * len(out_shape),
         scratch_shapes=[
-            pltpu.VMEM((2, SLOTS * 512, HD), jnp.bfloat16),
             pltpu.VMEM((KMAX // WIDE, rows, WIDE * BLOCK), jnp.float32),
             pltpu.VMEM((rows, HD), jnp.float32),
             pltpu.VMEM((rows, HD), jnp.float32),
@@ -193,15 +207,20 @@
 def stack_kernel(groups, *refs):
     pieces, outs = refs[: -len(groups)], refs[-len(groups) :]
     for group, out in zip(groups, outs):
-        for i, at in enumerate(group):
-            out[i] = pieces[at][...]
+        at = 0
+        for piece in (pieces[i] for i in group):
+            n = piece.shape[0] if len(piece.shape) == 4 else 1
+            out[at : at + n] = piece[...].reshape(n, *out.shape[1:])
+            at += n
 
 
 def stack(pieces, groups):
+    sizes = [piece.shape[0] if piece.ndim == 4 else 1 for piece in pieces]
+    shape, dtype = pieces[0].shape[-3:], pieces[0].dtype
     return pl.pallas_call(
         functools.partial(stack_kernel, groups),
         out_shape=[
-            jax.ShapeDtypeStruct((len(group), *pieces[0].shape), pieces[0].dtype) for group in groups
+            jax.ShapeDtypeStruct((sum(sizes[i] for i in group), *shape), dtype) for group in groups
         ],
         in_specs=[VMEM] * len(pieces),
         out_specs=[VMEM] * len(groups),
@@ -209,6 +228,23 @@
         cost_estimate=FREE,
         name="stack",
     )(*pieces)
+
+
+def mark_kernel(coords, *refs):
+    for i in range(coords.shape[0]):
+        refs[-1][i] = coords[i]
+
+
+def mark(coords, *arrays):
+    return pl.pallas_call(
+        mark_kernel,
+        out_shape=jax.ShapeDtypeStruct(coords.shape, coords.dtype),
+        in_specs=[SMEM] + [VMEM] * len(arrays),
+        out_specs=SMEM,
+        compiler_params=pltpu.CompilerParams(vmem_limit_bytes=PROJECT_VMEM),
+        cost_estimate=pl.CostEstimate(flops=MARK_FLOPS, bytes_accessed=0, transcendentals=0),
+        name="mark",
+    )(coords, *arrays)
 
 
 def project_kernel(steps, coords, own_ref, near_ref, w_ref, w0a, w0b, w1a, w1b, *out_refs):
@@ -266,29 +302,27 @@
     right = send(own, "x-")
 
     near_w, far_w = pick(coords, out_weight)
-    far, left, right, near_w = barrier((far, left, right, near_w))
+    far, left, right, near_w, far_w = barrier((far, left, right, near_w, far_w))
     near_part = send(near_w, "y_near")
-    one, other = stack([own, far, left, right], ((1, 2), (0, 3)))
+    far_part = send(far_w, "y_far")
+    one, four = stack([own, far, left, right], ((1, 2), (0, 1, 2, 3)))
+    far_right = send(far, "x-")
     both = send(one, "x+")
-    far_right = send(far, "x-")
-    one_t = send(one, "core")
-    other_t = send(other, "core")
-    far_w, _ = barrier((far_w, other_t))
-    far_part = send(far_w, "y_far")
     two_far = send(far_right, "x-")
     late = [both, far_right, two_far]
-    pieces = [one, other, one_t, other_t, *late, *(send(piece, "core") for piece in late)]
-    slots = ((2, 12), (0, 4), (3, 13), (1, 5), (14, 8), (6,), (10,), (15, 9), (7,), (11,))
-
-    attended = [
-        attention(coords, block_list, queries, k * n_rows, n_rows, pieces, slots)
-        for k in range(CHUNKS)
+    pieces = [four, send(four, "core"), *late, *(send(piece, "core") for piece in late)]
+    slots = ((0, 2, 12, 4), (1, 3, 13, 5), (14, 8), (6,), (10,), (15, 9), (7,), (11,))
+
+    first, kv = attention(coords, block_list, queries, 0, n_rows, pieces, slots)
+    attended = [first] + [
+        attention(coords, block_list, queries, k * n_rows, n_rows, [kv])[0] for k in range(1, CHUNKS)
     ]
-    near = [send(done, "y_near") for done in attended]
-    near_part, far_part, _ = barrier((near_part, far_part, attended[0]))
-    near_other = send(near_part, "core")
-    far_part, near_other = barrier((far_part, near_other))
-    parts = [near_part, near_other, far_part, send(far_part, "core")]
+    near = [send(first, "y_near"), None]
+    near_part, far_part, near[0], near[1] = barrier((near_part, far_part, near[0], attended[1]))
+    near[1] = send(near[1], "y_near")
+    near_other, far_other = send(near_part, "core"), send(far_part, "core")
+    parts = [near_part, near_other, far_part, far_other]
+    coords = mark(coords, near_other, far_other)
 
     def add(*terms):
         return sum(t.astype(jnp.float32) for t in terms).astype(jnp.bfloat16)

time: 110 us -> 113 us (1.027)
  starting transfers between devices: 37.7 us -> 40.2 us
  Pallas kernels: 19.8 us -> 21.7 us
    ppermute x31 -> x30, starting transfers between devices: 37.7 us -> 40.2 us  [send(): return lax.ppermute(array, AXES, MOVES[move])]
    pallas_call x0 -> x1, Pallas kernels: none -> 1.14 us  [mark(): pl.pallas_call(mark_kernel, out_shape=jax.ShapeDtypeStruct(coords.shape,...]
    ppermute x31 -> x30, waiting for transfers between devices: 48.9 us -> 48.4 us  [send(): return lax.ppermute(array, AXES, MOVES[move])]
  transfers between devices with their start and end apart: 31 -> 30, of which waited for: 18 -> 20; matrix products, arithmetic and copies ran while one was open for 1% -> 1% of each run, Pallas kernels for 18% -> 19%
where the time goes in v5:
time: 113 us
  waiting for transfers between devices  48.4 us (43%)
  starting transfers between devices  40.2 us (36%)
  Pallas kernels  21.7 us (19%)
  other arithmetic  1.7 us (2%)
  local copies, waits for them, and re-layouts  1.17 us (1%)
    ppermute x30, waiting for transfers between devices, send(): return lax.ppermute(array, AXES, MOVES[move])  48.4 us
    ppermute x30, starting transfers between devices, send(): return lax.ppermute(array, AXES, MOVES[move])  40.2 us
    pallas_call x2, Pallas kernels, attention(): pl.pallas_call(functools.partial(attention_kernel, first_row, n_rows, slo...  10.6 us
    pallas_call x4, Pallas kernels, project(): pl.pallas_call(functools.partial(project_kernel, steps), out_shape=[jax.S...  7.45 us
    pallas_call x1, Pallas kernels, pick(): pl.pallas_call(pick_kernel, out_shape=parts, in_specs=[SMEM, HBM], out_sp...  2.4 us
  transfers between devices with their start and end apart: 30, of which 20 were waited for; matrix products, arithmetic and copies ran while one was open for 1% of the time, Pallas kernels for 19%

profile of v5, /device:TPU:6, one launch (start us, length us, event | category | flops | bytes accessed | tf_op | source)
XLA Modules:
  0.0 113.4 jit_solution(3061984961095124708)
XLA Ops:
  1.1 3.1 %collective-permute-start = (bf16[2,512,128]{2,1,0:T(8,128)(2,1)S(1)}, bf16[2,512,128]{2,1,0:T(8,128)(2,1)S(1)}, u32[]{:S(2)}, u32[]{:S(2)}) collective-permute-start(bf16[2,512,128]{2,1,0:T(8,128)(2,1)S(1)} %get-tuple-element.72), channel_id=1, source_target_pairs={{0,40},{1,41},{2,42},{3,43},{4,44},{5,45},{6,46},{7,47},{16,56},{1... | collective-permute-start | bytes 786440 | tf_op jit(solution)/shard_map/ppermute | solution.py:59
  5.0 2.4 %collective-permute-start.1 = (bf16[2,512,128]{2,1,0:T(8,128)(2,1)S(1)}, bf16[2,512,128]{2,1,0:T(8,128)(2,1)S(1)}, u32[]{:S(2)}, u32[]{:S(2)}) collective-permute-start(bf16[2,512,128]{2,1,0:T(8,128)(2,1)S(1)} %get-tuple-element.71.refs_0_), channel_id=1, source_target_pairs={{0,64},{1,65},{2,66},{3,67},{4,68},{5,69},{6,70},{7,71},{16,80},{1... | collective-permute-start | bytes 786440 | tf_op jit(solution)/shard_map/ppermute | solution.py:59
  7.5 2.4 %pick.1 = (bf16[256,2048]{1,0:T(8,128)(2,1)S(1)}, bf16[256,2048]{1,0:T(8,128)(2,1)S(1)}) custom-call(s32[5]{0:T(128)S(1)} %stack.24.coords, bf16[512,8192]{1,0:T(8,128)(2,1)} %w_ref.9), custom_call_target="tpu_custom_call" | custom-call | tf_op jit(solution)/shard_map/pick/pallas_call | solution.py:85
  10.5 2.7 %collective-permute-done.2.refs_3_ = bf16[2,512,128]{2,1,0:T(8,128)(2,1)S(1)} collective-permute-done((bf16[2,512,128]{2,1,0:T(8,128)(2,1)S(1)}, bf16[2,512,128]{2,1,0:T(8,128)(2,1)S(1)}, u32[]{:S(2)}, u32[]{:S(2)}) %collective-permute-start.2) | collective-permute-done | bytes 262176 | tf_op jit(solution)/shard_map/ppermute | solution.py:59
  13.3 3.3 %collective-permute-start.6 = (bf16[2,2,512,128]{3,2,1,0:T(8,128)(2,1)S(1)}, bf16[2,2,512,128]{3,2,1,0:T(8,128)(2,1)S(1)}, u32[]{:S(2)}, u32[]{:S(2)}) collective-permute-start(bf16[2,2,512,128]{3,2,1,0:T(8,128)(2,1)S(1)} %get-tuple-element.46), channel_id=1, source_target_pairs={{0,64},{1,65},{2,66},{3,67},{4,68},{5,69},{6,70},{7,71},{16,80},{1... | collective-permute-start | bytes 1572872 | tf_op jit(solution)/shard_map/ppermute | solution.py:59
  16.6 4.6 %collective-permute-done.7.refs_3_ = bf16[2,512,128]{2,1,0:T(8,128)(2,1)S(1)} collective-permute-done((bf16[2,512,128]{2,1,0:T(8,128)(2,1)S(1)}, bf16[2,512,128]{2,1,0:T(8,128)(2,1)S(1)}, u32[]{:S(2)}, u32[]{:S(2)}) %collective-permute-start.7) | collective-permute-done | bytes 262176 | tf_op jit(solution)/shard_map/ppermute | solution.py:59
  22.8 3.5 %collective-permute-done.6.refs_2_ = bf16[2,2,512,128]{3,2,1,0:T(8,128)(2,1)S(1)} collective-permute-done((bf16[2,2,512,128]{3,2,1,0:T(8,128)(2,1)S(1)}, bf16[2,2,512,128]{3,2,1,0:T(8,128)(2,1)S(1)}, u32[]{:S(2)}, u32[]{:S(2)}) %collective-permute-start.6) | collective-permute-done | bytes 524320 | tf_op jit(solution)/shard_map/ppermute | solution.py:59
  26.3 6.0 %collective-permute-done.8.refs_4_ = bf16[2,512,128]{2,1,0:T(8,128)(2,1)S(1)} collective-permute-done((bf16[2,512,128]{2,1,0:T(8,128)(2,1)S(1)}, bf16[2,512,128]{2,1,0:T(8,128)(2,1)S(1)}, u32[]{:S(2)}, u32[]{:S(2)}) %collective-permute-start.8) | collective-permute-done | bytes 262176 | tf_op jit(solution)/shard_map/ppermute | solution.py:59
  32.3 1.5 %collective-permute-done.11.refs_7_ = bf16[2,512,128]{2,1,0:T(8,128)(2,1)S(1)} collective-permute-done((bf16[2,512,128]{2,1,0:T(8,128)(2,1)S(1)}, bf16[2,512,128]{2,1,0:T(8,128)(2,1)S(1)}, u32[]{:S(2)}, u32[]{:S(2)}) %collective-permute-start.11) | collective-permute-done | bytes 262176 | tf_op jit(solution)/shard_map/ppermute | solution.py:59
  33.9 5.7 %attention.2 = (bf16[256,512]{1,0:T(8,128)(2,1)S(1)}, bf16[2,8192,128]{2,1,0:T(8,128)(2,1)S(1)}) custom-call(s32[5]{0:T(128)S(1)} %stack.24.coords, s32[4,16]{1,0:T(4,128)S(1)} %copy-done.1, bf16[512,512]{1,0:T(8,128)(2,1)S(1)} %copy-done, bf16[4,2,512,128]{3,2,1,0:T(8,128)(2,1)S(1)} %get-tuple-element.45.refs_0_, ...), custom_call_target="tpu_custom_call" | custom-call | tf_op jit(solution)/shard_map/attention/pallas_call | solution.py:189
  40.3 4.9 %attention.3.own_ref = bf16[256,512]{1,0:T(8,128)(2,1)S(1)} custom-call(s32[5]{0:T(128)S(1)} %stack.24.coords, s32[4,16]{1,0:T(4,128)S(1)} %copy-done.1, bf16[512,512]{1,0:T(8,128)(2,1)S(1)} %copy-done, bf16[2,8192,128]{2,1,0:T(8,128)(2,1)S(1)} %get-tuple-element.48.refs_0_), custom_call_target="tpu_custom_call" | custom-call | tf_op jit(solution)/shard_map/attention/pallas_call | solution.py:189
  45.2 2.0 %collective-permute-done.3.w0a = bf16[256,2048]{1,0:T(8,128)(2,1)S(1)} collective-permute-done((bf16[256,2048]{1,0:T(8,128)(2,1)S(1)}, bf16[256,2048]{1,0:T(8,128)(2,1)S(1)}, u32[]{:S(2)}, u32[]{:S(2)}) %collective-permute-start.3) | collective-permute-done | bytes 1048608 | tf_op jit(solution)/shard_map/ppermute | solution.py:59
  48.0 4.4 %collective-permute-done.12.near_ref = bf16[256,512]{1,0:T(8,128)(2,1)S(1)} collective-permute-done((bf16[256,512]{1,0:T(8,128)(2,1)S(1)}, bf16[256,512]{1,0:T(8,128)(2,1)S(1)}, u32[]{:S(2)}, u32[]{:S(2)}) %collective-permute-start.12) | collective-permute-done | bytes 262176 | tf_op jit(solution)/shard_map/ppermute | solution.py:59
  53.2 1.9 %collective-permute-done.13.refs_0_.w0b = bf16[256,2048]{1,0:T(8,128)(2,1)S(1)} collective-permute-done((bf16[256,2048]{1,0:T(8,128)(2,1)S(1)}, bf16[256,2048]{1,0:T(8,128)(2,1)S(1)}, u32[]{:S(2)}, u32[]{:S(2)}) %collective-permute-start.13) | collective-permute-done | bytes 1048608 | tf_op jit(solution)/shard_map/ppermute | solution.py:59
  55.1 1.5 %collective-permute-done.14.refs_1_.w1b = bf16[256,2048]{1,0:T(8,128)(2,1)S(1)} collective-permute-done((bf16[256,2048]{1,0:T(8,128)(2,1)S(1)}, bf16[256,2048]{1,0:T(8,128)(2,1)S(1)}, u32[]{:S(2)}, u32[]{:S(2)}) %collective-permute-start.14) | collective-permute-done | bytes 1048608 | tf_op jit(solution)/shard_map/ppermute | solution.py:59
  57.8 1.3 %project.5 = (bf16[256,512]{1,0:T(8,128)(2,1)S(1)}, bf16[256,512]{1,0:T(8,128)(2,1)S(1)}) custom-call(s32[5]{0:T(128)S(1)} %mark.1.coords, bf16[256,512]{1,0:T(8,128)(2,1)S(1)} %get-tuple-element.47.own_ref, bf16[256,512]{1,0:T(8,128)(2,1)S(1)} %collective-permute-done.12.near_ref, bf16[512,8192]{1,0:T(8,128)(2,1)S(1)} %bitcast.6, ...), custom_call_target="tpu_custom_call" | custom-call | tf_op jit(solution)/shard_map/project/pallas_call | solution.py:279
  59.1 5.9 %collective-permute-start.20 = (bf16[256,512]{1,0:T(8,128)(2,1)S(1)}, bf16[256,512]{1,0:T(8,128)(2,1)S(1)}, u32[]{:S(2)}, u32[]{:S(2)}) collective-permute-start(bf16[256,512]{1,0:T(8,128)(2,1)S(1)} %get-tuple-element.58), channel_id=1, source_target_pairs={{0,7},{1,0},{2,1},{3,2},{4,3},{5,4},{6,5},{7,6},{16,23},{17,16},{1... | collective-permute-start | bytes 786440 | tf_op jit(solution)/shard_map/ppermute | solution.py:59
  65.0 2.4 %project.4 = (bf16[256,512]{1,0:T(8,128)(2,1)S(1)}, bf16[256,512]{1,0:T(8,128)(2,1)S(1)}, bf16[256,512]{1,0:T(8,128)(2,1)S(1)}, bf16[256,512]{1,0:T(8,128)(2,1)S...) custom-call(s32[5]{0:T(128)S(1)} %mark.1.coords, bf16[256,512]{1,0:T(8,128)(2,1)S(1)} %get-tuple-element.47.own_ref, ...), custom_call_target="tpu_custom_call" | custom-call | tf_op jit(solution)/shard_map/project/pallas_call | solution.py:279
  67.4 3.4 %collective-permute-done.20 = bf16[256,512]{1,0:T(8,128)(2,1)S(1)} collective-permute-done((bf16[256,512]{1,0:T(8,128)(2,1)S(1)}, bf16[256,512]{1,0:T(8,128)(2,1)S(1)}, u32[]{:S(2)}, u32[]{:S(2)}) %collective-permute-start.20) | collective-permute-done | bytes 262176 | tf_op jit(solution)/shard_map/ppermute | solution.py:59
  70.9 1.3 %project.7 = (bf16[256,512]{1,0:T(8,128)(2,1)S(1)}, bf16[256,512]{1,0:T(8,128)(2,1)S(1)}) custom-call(s32[5]{0:T(128)S(1)} %mark.1.coords, bf16[256,512]{1,0:T(8,128)(2,1)S(1)} %attention.3.own_ref, bf16[256,512]{1,0:T(8,128)(2,1)S(1)} %collective-permute-done.19.near_ref, bf16[512,8192]{1,0:T(8,128)(2,1)S(1)} %bitcast.6, ...), custom_call_target="tpu_custom_call" | custom-call | tf_op jit(solution)/shard_map/project/pallas_call | solution.py:279
  72.2 3.8 %collective-permute-start.26 = (bf16[256,512]{1,0:T(8,128)(2,1)S(1)}, bf16[256,512]{1,0:T(8,128)(2,1)S(1)}, u32[]{:S(2)}, u32[]{:S(2)}) collective-permute-start(bf16[256,512]{1,0:T(8,128)(2,1)S(1)} %get-tuple-element.67), channel_id=1, source_target_pairs={{0,7},{1,0},{2,1},{3,2},{4,3},{5,4},{6,5},{7,6},{16,23},{17,16},{1... | collective-permute-start | bytes 786440 | tf_op jit(solution)/shard_map/ppermute | solution.py:59
  76.2 3.3 %collective-permute-start.21 = (bf16[256,512]{1,0:T(8,128)(2,1)S(1)}, bf16[256,512]{1,0:T(8,128)(2,1)S(1)}, u32[]{:S(2)}, u32[]{:S(2)}) collective-permute-start(bf16[256,512]{1,0:T(8,128)(2,1)S(1)} %add_convert_fusion.8), channel_id=1, source_target_pairs={{0,7},{1,0},{2,1},{3,2},{4,3},{5,4},{6,5},{7,6},{16,23},{17,16},{1... | collective-permute-start | bytes 786440 | tf_op jit(solution)/shard_map/ppermute | solution.py:59
  79.5 2.4 %project.6 = (bf16[256,512]{1,0:T(8,128)(2,1)S(1)}, bf16[256,512]{1,0:T(8,128)(2,1)S(1)}, bf16[256,512]{1,0:T(8,128)(2,1)S(1)}, bf16[256,512]{1,0:T(8,128)(2,1)S...) custom-call(s32[5]{0:T(128)S(1)} %mark.1.coords, bf16[256,512]{1,0:T(8,128)(2,1)S(1)} %attention.3.own_ref, ...), custom_call_target="tpu_custom_call" | custom-call | tf_op jit(solution)/shard_map/project/pallas_call | solution.py:279
  83.4 3.3 %collective-permute-start.27 = (bf16[256,512]{1,0:T(8,128)(2,1)S(1)}, bf16[256,512]{1,0:T(8,128)(2,1)S(1)}, u32[]{:S(2)}, u32[]{:S(2)}) collective-permute-start(bf16[256,512]{1,0:T(8,128)(2,1)S(1)} %add_convert_fusion.3), channel_id=1, source_target_pairs={{0,7},{1,0},{2,1},{3,2},{4,3},{5,4},{6,5},{7,6},{16,23},{17,16},{1... | collective-permute-start | bytes 786440 | tf_op jit(solution)/shard_map/ppermute | solution.py:59
  86.7 2.1 %collective-permute-done.16 = bf16[256,512]{1,0:T(8,128)(2,1)S(1)} collective-permute-done((bf16[256,512]{1,0:T(8,128)(2,1)S(1)}, bf16[256,512]{1,0:T(8,128)(2,1)S(1)}, u32[]{:S(2)}, u32[]{:S(2)}) %collective-permute-start.16) | collective-permute-done | bytes 262176 | tf_op jit(solution)/shard_map/ppermute | solution.py:59
  89.2 3.3 %collective-permute-start.22 = (bf16[256,512]{1,0:T(8,128)(2,1)S(1)}, bf16[256,512]{1,0:T(8,128)(2,1)S(1)}, u32[]{:S(2)}, u32[]{:S(2)}) collective-permute-start(bf16[256,512]{1,0:T(8,128)(2,1)S(1)} %add_convert_fusion.7), channel_id=1, source_target_pairs={{0,7},{1,0},{2,1},{3,2},{4,3},{5,4},{6,5},{7,6},{16,23},{17,16},{1... | collective-permute-start | bytes 786440 | tf_op jit(solution)/shard_map/ppermute | solution.py:59
  92.5 1.5 %collective-permute-done.27 = bf16[256,512]{1,0:T(8,128)(2,1)S(1)} collective-permute-done((bf16[256,512]{1,0:T(8,128)(2,1)S(1)}, bf16[256,512]{1,0:T(8,128)(2,1)S(1)}, u32[]{:S(2)}, u32[]{:S(2)}) %collective-permute-start.27) | collective-permute-done | bytes 262176 | tf_op jit(solution)/shard_map/ppermute | solution.py:59
  94.1 3.8 %collective-permute-start.28 = (bf16[256,512]{1,0:T(8,128)(2,1)S(1)}, bf16[256,512]{1,0:T(8,128)(2,1)S(1)}, u32[]{:S(2)}, u32[]{:S(2)}) collective-permute-start(bf16[256,512]{1,0:T(8,128)(2,1)S(1)} %add_convert_fusion.2), channel_id=1, source_target_pairs={{0,7},{1,0},{2,1},{3,2},{4,3},{5,4},{6,5},{7,6},{16,23},{17,16},{1... | collective-permute-start | bytes 786440 | tf_op jit(solution)/shard_map/ppermute | solution.py:59
  98.9 4.6 %collective-permute-done.28 = bf16[256,512]{1,0:T(8,128)(2,1)S(1)} collective-permute-done((bf16[256,512]{1,0:T(8,128)(2,1)S(1)}, bf16[256,512]{1,0:T(8,128)(2,1)S(1)}, u32[]{:S(2)}, u32[]{:S(2)}) %collective-permute-start.28) | collective-permute-done | bytes 262176 | tf_op jit(solution)/shard_map/ppermute | solution.py:59
  103.6 3.8 %collective-permute-start.29 = (bf16[256,512]{1,0:T(8,128)(2,1)S(1)}, bf16[256,512]{1,0:T(8,128)(2,1)S(1)}, u32[]{:S(2)}, u32[]{:S(2)}) collective-permute-start(bf16[256,512]{1,0:T(8,128)(2,1)S(1)} %add_convert_fusion.1), channel_id=1, source_target_pairs={{0,7},{1,0},{2,1},{3,2},{4,3},{5,4},{6,5},{7,6},{16,23},{17,16},{1... | collective-permute-start | bytes 786440 | tf_op jit(solution)/shard_map/ppermute | solution.py:59
  107.4 1.8 %collective-permute-done.18 = bf16[256,512]{1,0:T(8,128)(2,1)S(1)} collective-permute-done((bf16[256,512]{1,0:T(8,128)(2,1)S(1)}, bf16[256,512]{1,0:T(8,128)(2,1)S(1)}, u32[]{:S(2)}, u32[]{:S(2)}) %collective-permute-start.18) | collective-permute-done | bytes 262176 | tf_op jit(solution)/shard_map/ppermute | solution.py:59
  109.3 3.2 %collective-permute-done.25 = bf16[256,512]{1,0:T(8,128)(2,1)S(1)} collective-permute-done((bf16[256,512]{1,0:T(8,128)(2,1)S(1)}, bf16[256,512]{1,0:T(8,128)(2,1)S(1)}, u32[]{:S(2)}, u32[]{:S(2)}) %collective-permute-start.25) | collective-permute-done | bytes 262176 | tf_op jit(solution)/shard_map/ppermute | solution.py:59
  (61 shorter events, 11.9 us)
Async XLA Ops:
  1.1 9.4 %collective-permute-start = (bf16[2,512,128]{2,1,0:T(8,128)(2,1)S(1)}, bf16[2,512,128]{2,1,0:T(8,128)(2,1)S(1)}, u32[]{:S(2)}, u32[]{:S(2)}) collective-permute-start(bf16[2,512,128]{2,1,0:T(8,128)(2,1)S(1)} %get-tuple-element.72), channel_id=1, source_target_pairs={{0,40},{1,41},{2,42},{3,43},{4,44},{5,45},{6,46},{7,47},{16,56},{1... | collective-permute-start | bytes 786440 | tf_op jit(solution)/shard_map/ppermute | solution.py:59
  4.2 9.0 %collective-permute-start.2 = (bf16[2,512,128]{2,1,0:T(8,128)(2,1)S(1)}, bf16[2,512,128]{2,1,0:T(8,128)(2,1)S(1)}, u32[]{:S(2)}, u32[]{:S(2)}) collective-permute-start(bf16[2,512,128]{2,1,0:T(8,128)(2,1)S(1)} %get-tuple-element.71.refs_0_), channel_id=1, source_target_pairs={{0,192},{1,193},{2,194},{3,195},{4,196},{5,197},{6,198},{7,199},{1... | collective-permute-start | bytes 786440 | tf_op jit(solution)/shard_map/ppermute | solution.py:59
  5.0 8.2 %collective-permute-start.1 = (bf16[2,512,128]{2,1,0:T(8,128)(2,1)S(1)}, bf16[2,512,128]{2,1,0:T(8,128)(2,1)S(1)}, u32[]{:S(2)}, u32[]{:S(2)}) collective-permute-start(bf16[2,512,128]{2,1,0:T(8,128)(2,1)S(1)} %get-tuple-element.71.refs_0_), channel_id=1, source_target_pairs={{0,64},{1,65},{2,66},{3,67},{4,68},{5,69},{6,70},{7,71},{16,80},{1... | collective-permute-start | bytes 786440 | tf_op jit(solution)/shard_map/ppermute | solution.py:59
  7.5 50.2 %slice-start = ((s8[8388608]{0:T(1024)(128)(4,1)}), s8[4194304]{0:T(1024)(128)(4,1)S(1)}, s32[]{:S(2)}) async-start(s8[8388608]{0:T(1024)(128)(4,1)} %bitcast.5), calls=%async_computation | async-start | bytes 8388608
  13.2 8.1 %collective-permute-start.7 = (bf16[2,512,128]{2,1,0:T(8,128)(2,1)S(1)}, bf16[2,512,128]{2,1,0:T(8,128)(2,1)S(1)}, u32[]{:S(2)}, u32[]{:S(2)}) collective-permute-start(bf16[2,512,128]{2,1,0:T(8,128)(2,1)S(1)} %collective-permute-done.refs_1_), channel_id=1, source_target_pairs={{0,192},{1,193},{2,194},{3,195},{4,196},{5,197},{6,198},{7,199},{1... | collective-permute-start | bytes 786440 | tf_op jit(solution)/shard_map/ppermute | solution.py:59
  13.3 13.0 %collective-permute-start.6 = (bf16[2,2,512,128]{3,2,1,0:T(8,128)(2,1)S(1)}, bf16[2,2,512,128]{3,2,1,0:T(8,128)(2,1)S(1)}, u32[]{:S(2)}, u32[]{:S(2)}) collective-permute-start(bf16[2,2,512,128]{3,2,1,0:T(8,128)(2,1)S(1)} %get-tuple-element.46), channel_id=1, source_target_pairs={{0,64},{1,65},{2,66},{3,67},{4,68},{5,69},{6,70},{7,71},{16,80},{1... | collective-permute-start | bytes 1572872 | tf_op jit(solution)/shard_map/ppermute | solution.py:59
  16.6 41.2 %slice-start.1 = ((s8[8388608]{0:T(1024)(128)(4,1)}), s8[4194304]{0:T(1024)(128)(4,1)S(1)}, s32[]{:S(2)}) async-start(s8[8388608]{0:T(1024)(128)(4,1)} %bitcast.5), calls=%async_computation.1 | async-start | bytes 8388608
  16.6 17.3 %collective-permute-start.5 = (bf16[4,2,512,128]{3,2,1,0:T(8,128)(2,1)S(1)}, bf16[4,2,512,128]{3,2,1,0:T(8,128)(2,1)S(1)}, u32[]{:S(2)}, u32[]{:S(2)}) collective-permute-start(bf16[4,2,512,128]{3,2,1,0:T(8,128)(2,1)S(1)} %get-tuple-element.45.refs_0_), channel_id=1, source_target_pairs={{0,16},{1,17},{2,18},{3,19},{4,20},{5,21},{6,22},{7,23},{16,0},{17... | collective-permute-start | bytes 3145736 | tf_op jit(solution)/shard_map/ppermute | solution.py:59
  21.2 1.5 %collective-permute-start.10 = (bf16[2,512,128]{2,1,0:T(8,128)(2,1)S(1)}, bf16[2,512,128]{2,1,0:T(8,128)(2,1)S(1)}, u32[]{:S(2)}, u32[]{:S(2)}) collective-permute-start(bf16[2,512,128]{2,1,0:T(8,128)(2,1)S(1)} %collective-permute-done.7.refs_3_), channel_id=1, source_target_pairs={{0,16},{1,17},{2,18},{3,19},{4,20},{5,21},{6,22},{7,23},{16,0},{17... | collective-permute-start | bytes 786440 | tf_op jit(solution)/shard_map/ppermute | solution.py:59
  21.2 26.0 %collective-permute-start.3 = (bf16[256,2048]{1,0:T(8,128)(2,1)S(1)}, bf16[256,2048]{1,0:T(8,128)(2,1)S(1)}, u32[]{:S(2)}, u32[]{:S(2)}) collective-permute-start(bf16[256,2048]{1,0:T(8,128)(2,1)S(1)} %get-tuple-element.40), channel_id=1, source_target_pairs={{0,8},{1,9},{2,10},{3,11},{4,12},{5,13},{6,14},{7,15},{16,24},{17,... | collective-permute-start | bytes 3145736 | tf_op jit(solution)/shard_map/ppermute | solution.py:59
  21.4 26.6 %collective-permute-start.4 = (bf16[256,2048]{1,0:T(8,128)(2,1)S(1)}, bf16[256,2048]{1,0:T(8,128)(2,1)S(1)}, u32[]{:S(2)}, u32[]{:S(2)}) collective-permute-start(bf16[256,2048]{1,0:T(8,128)(2,1)S(1)} %get-tuple-element.41), channel_id=1, source_target_pairs={{0,40},{1,41},{2,42},{3,43},{4,44},{5,45},{6,46},{7,47},{16,56},{1... | collective-permute-start | bytes 3145736 | tf_op jit(solution)/shard_map/ppermute | solution.py:59
  22.8 9.6 %collective-permute-start.8 = (bf16[2,512,128]{2,1,0:T(8,128)(2,1)S(1)}, bf16[2,512,128]{2,1,0:T(8,128)(2,1)S(1)}, u32[]{:S(2)}, u32[]{:S(2)}) collective-permute-start(bf16[2,512,128]{2,1,0:T(8,128)(2,1)S(1)} %collective-permute-done.7.refs_3_), channel_id=1, source_target_pairs={{0,192},{1,193},{2,194},{3,195},{4,196},{5,197},{6,198},{7,199},{1... | collective-permute-start | bytes 786440 | tf_op jit(solution)/shard_map/ppermute | solution.py:59
  26.3 7.6 %collective-permute-start.9 = (bf16[2,2,512,128]{3,2,1,0:T(8,128)(2,1)S(1)}, bf16[2,2,512,128]{3,2,1,0:T(8,128)(2,1)S(1)}, u32[]{:S(2)}, u32[]{:S(2)}) collective-permute-start(bf16[2,2,512,128]{3,2,1,0:T(8,128)(2,1)S(1)} %collective-permute-done.6.refs_2_), channel_id=1, source_target_pairs={{0,16},{1,17},{2,18},{3,19},{4,20},{5,21},{6,22},{7,23},{16,0},{17... | collective-permute-start | bytes 1572872 | tf_op jit(solution)/shard_map/ppermute | solution.py:59
  32.3 1.5 %collective-permute-start.11 = (bf16[2,512,128]{2,1,0:T(8,128)(2,1)S(1)}, bf16[2,512,128]{2,1,0:T(8,128)(2,1)S(1)}, u32[]{:S(2)}, u32[]{:S(2)}) collective-permute-start(bf16[2,512,128]{2,1,0:T(8,128)(2,1)S(1)} %collective-permute-done.8.refs_4_), channel_id=1, source_target_pairs={{0,16},{1,17},{2,18},{3,19},{4,20},{5,21},{6,22},{7,23},{16,0},{17... | collective-permute-start | bytes 786440 | tf_op jit(solution)/shard_map/ppermute | solution.py:59
  39.6 12.8 %collective-permute-start.12 = (bf16[256,512]{1,0:T(8,128)(2,1)S(1)}, bf16[256,512]{1,0:T(8,128)(2,1)S(1)}, u32[]{:S(2)}, u32[]{:S(2)}) collective-permute-start(bf16[256,512]{1,0:T(8,128)(2,1)S(1)} %get-tuple-element.47.own_ref), channel_id=1, source_target_pairs={{0,8},{1,9},{2,10},{3,11},{4,12},{5,13},{6,14},{7,15},{16,24},{17,... | collective-permute-start | bytes 786440 | tf_op jit(solution)/shard_map/ppermute | solution.py:59
  52.4 2.7 %collective-permute-start.13 = (bf16[256,2048]{1,0:T(8,128)(2,1)S(1)}, bf16[256,2048]{1,0:T(8,128)(2,1)S(1)}, u32[]{:S(2)}, u32[]{:S(2)}) collective-permute-start(bf16[256,2048]{1,0:T(8,128)(2,1)S(1)} %collective-permute-done.3.w0a), channel_id=1, source_target_pairs={{0,16},{1,17},{2,18},{3,19},{4,20},{5,21},{6,22},{7,23},{16,0},{17... | collective-permute-start | bytes 3145736 | tf_op jit(solution)/shard_map/ppermute | solution.py:59
  52.4 4.2 %collective-permute-start.14 = (bf16[256,2048]{1,0:T(8,128)(2,1)S(1)}, bf16[256,2048]{1,0:T(8,128)(2,1)S(1)}, u32[]{:S(2)}, u32[]{:S(2)}) collective-permute-start(bf16[256,2048]{1,0:T(8,128)(2,1)S(1)} %collective-permute-done.4.w1a), channel_id=1, source_target_pairs={{0,16},{1,17},{2,18},{3,19},{4,20},{5,21},{6,22},{7,23},{16,0},{17... | collective-permute-start | bytes 3145736 | tf_op jit(solution)/shard_map/ppermute | solution.py:59
  52.9 14.5 %collective-permute-start.19 = (bf16[256,512]{1,0:T(8,128)(2,1)S(1)}, bf16[256,512]{1,0:T(8,128)(2,1)S(1)}, u32[]{:S(2)}, u32[]{:S(2)}) collective-permute-start(bf16[256,512]{1,0:T(8,128)(2,1)S(1)} %attention.3.own_ref), channel_id=1, source_target_pairs={{0,8},{1,9},{2,10},{3,11},{4,12},{5,13},{6,14},{7,15},{16,24},{17,... | collective-permute-start | bytes 786440 | tf_op jit(solution)/shard_map/ppermute | solution.py:59
  59.1 11.8 %collective-permute-start.20 = (bf16[256,512]{1,0:T(8,128)(2,1)S(1)}, bf16[256,512]{1,0:T(8,128)(2,1)S(1)}, u32[]{:S(2)}, u32[]{:S(2)}) collective-permute-start(bf16[256,512]{1,0:T(8,128)(2,1)S(1)} %get-tuple-element.58), channel_id=1, source_target_pairs={{0,7},{1,0},{2,1},{3,2},{4,3},{5,4},{6,5},{7,6},{16,23},{17,16},{1... | collective-permute-start | bytes 786440 | tf_op jit(solution)/shard_map/ppermute | solution.py:59
  65.0 11.0 %collective-permute-start.15 = (bf16[256,512]{1,0:T(8,128)(2,1)S(1)}, bf16[256,512]{1,0:T(8,128)(2,1)S(1)}, u32[]{:S(2)}, u32[]{:S(2)}) collective-permute-start(bf16[256,512]{1,0:T(8,128)(2,1)S(1)} %get-tuple-element.53), channel_id=1, source_target_pairs={{0,1},{1,2},{2,3},{3,4},{4,5},{5,6},{6,7},{7,0},{16,17},{17,18},{1... | collective-permute-start | bytes 786440 | tf_op jit(solution)/shard_map/ppermute | solution.py:59
  72.1 11.0 %collective-permute-start.23 = (bf16[256,512]{1,0:T(8,128)(2,1)S(1)}, bf16[256,512]{1,0:T(8,128)(2,1)S(1)}, u32[]{:S(2)}, u32[]{:S(2)}) collective-permute-start(bf16[256,512]{1,0:T(8,128)(2,1)S(1)} %get-tuple-element.64), channel_id=1, source_target_pairs={{0,1},{1,2},{2,3},{3,4},{4,5},{5,6},{6,7},{7,0},{16,17},{17,18},{1... | collective-permute-start | bytes 786440 | tf_op jit(solution)/shard_map/ppermute | solution.py:59
  72.2 11.0 %collective-permute-start.26 = (bf16[256,512]{1,0:T(8,128)(2,1)S(1)}, bf16[256,512]{1,0:T(8,128)(2,1)S(1)}, u32[]{:S(2)}, u32[]{:S(2)}) collective-permute-start(bf16[256,512]{1,0:T(8,128)(2,1)S(1)} %get-tuple-element.67), channel_id=1, source_target_pairs={{0,7},{1,0},{2,1},{3,2},{4,3},{5,4},{6,5},{7,6},{16,23},{17,16},{1... | collective-permute-start | bytes 786440 | tf_op jit(solution)/shard_map/ppermute | solution.py:59
  76.1 12.7 %collective-permute-start.16 = (bf16[256,512]{1,0:T(8,128)(2,1)S(1)}, bf16[256,512]{1,0:T(8,128)(2,1)S(1)}, u32[]{:S(2)}, u32[]{:S(2)}) collective-permute-start(bf16[256,512]{1,0:T(8,128)(2,1)S(1)} %add_convert_fusion.11), channel_id=1, source_target_pairs={{0,1},{1,2},{2,3},{3,4},{4,5},{5,6},{6,7},{7,0},{16,17},{17,18},{1... | collective-permute-start | bytes 786440 | tf_op jit(solution)/shard_map/ppermute | solution.py:59
  76.2 12.9 %collective-permute-start.21 = (bf16[256,512]{1,0:T(8,128)(2,1)S(1)}, bf16[256,512]{1,0:T(8,128)(2,1)S(1)}, u32[]{:S(2)}, u32[]{:S(2)}) collective-permute-start(bf16[256,512]{1,0:T(8,128)(2,1)S(1)} %add_convert_fusion.8), channel_id=1, source_target_pairs={{0,7},{1,0},{2,1},{3,2},{4,3},{5,4},{6,5},{7,6},{16,23},{17,16},{1... | collective-permute-start | bytes 786440 | tf_op jit(solution)/shard_map/ppermute | solution.py:59
  83.2 15.5 %collective-permute-start.24 = (bf16[256,512]{1,0:T(8,128)(2,1)S(1)}, bf16[256,512]{1,0:T(8,128)(2,1)S(1)}, u32[]{:S(2)}, u32[]{:S(2)}) collective-permute-start(bf16[256,512]{1,0:T(8,128)(2,1)S(1)} %add_convert_fusion.5), channel_id=1, source_target_pairs={{0,1},{1,2},{2,3},{3,4},{4,5},{5,6},{6,7},{7,0},{16,17},{17,18},{1... | collective-permute-start | bytes 786440 | tf_op jit(solution)/shard_map/ppermute | solution.py:59
  83.4 10.6 %collective-permute-start.27 = (bf16[256,512]{1,0:T(8,128)(2,1)S(1)}, bf16[256,512]{1,0:T(8,128)(2,1)S(1)}, u32[]{:S(2)}, u32[]{:S(2)}) collective-permute-start(bf16[256,512]{1,0:T(8,128)(2,1)S(1)} %add_convert_fusion.3), channel_id=1, source_target_pairs={{0,7},{1,0},{2,1},{3,2},{4,3},{5,4},{6,5},{7,6},{16,23},{17,16},{1... | collective-permute-start | bytes 786440 | tf_op jit(solution)/shard_map/ppermute | solution.py:59
  88.8 9.7 %collective-permute-start.17 = (bf16[256,512]{1,0:T(8,128)(2,1)S(1)}, bf16[256,512]{1,0:T(8,128)(2,1)S(1)}, u32[]{:S(2)}, u32[]{:S(2)}) collective-permute-start(bf16[256,512]{1,0:T(8,128)(2,1)S(1)} %add_convert_fusion.10), channel_id=1, source_target_pairs={{0,1},{1,2},{2,3},{3,4},{4,5},{5,6},{6,7},{7,0},{16,17},{17,18},{1... | collective-permute-start | bytes 786440 | tf_op jit(solution)/shard_map/ppermute | solution.py:59
  89.2 18.2 %collective-permute-start.22 = (bf16[256,512]{1,0:T(8,128)(2,1)S(1)}, bf16[256,512]{1,0:T(8,128)(2,1)S(1)}, u32[]{:S(2)}, u32[]{:S(2)}) collective-permute-start(bf16[256,512]{1,0:T(8,128)(2,1)S(1)} %add_convert_fusion.7), channel_id=1, source_target_pairs={{0,7},{1,0},{2,1},{3,2},{4,3},{5,4},{6,5},{7,6},{16,23},{17,16},{1... | collective-permute-start | bytes 786440 | tf_op jit(solution)/shard_map/ppermute | solution.py:59
  94.1 9.4 %collective-permute-start.28 = (bf16[256,512]{1,0:T(8,128)(2,1)S(1)}, bf16[256,512]{1,0:T(8,128)(2,1)S(1)}, u32[]{:S(2)}, u32[]{:S(2)}) collective-permute-start(bf16[256,512]{1,0:T(8,128)(2,1)S(1)} %add_convert_fusion.2), channel_id=1, source_target_pairs={{0,7},{1,0},{2,1},{3,2},{4,3},{5,4},{6,5},{7,6},{16,23},{17,16},{1... | collective-permute-start | bytes 786440 | tf_op jit(solution)/shard_map/ppermute | solution.py:59
  98.6 10.5 %collective-permute-start.18 = (bf16[256,512]{1,0:T(8,128)(2,1)S(1)}, bf16[256,512]{1,0:T(8,128)(2,1)S(1)}, u32[]{:S(2)}, u32[]{:S(2)}) collective-permute-start(bf16[256,512]{1,0:T(8,128)(2,1)S(1)} %add_convert_fusion.9), channel_id=1, source_target_pairs={{0,1},{1,2},{2,3},{3,4},{4,5},{5,6},{6,7},{7,0},{16,17},{17,18},{1... | collective-permute-start | bytes 786440 | tf_op jit(solution)/shard_map/ppermute | solution.py:59
  98.8 13.6 %collective-permute-start.25 = (bf16[256,512]{1,0:T(8,128)(2,1)S(1)}, bf16[256,512]{1,0:T(8,128)(2,1)S(1)}, u32[]{:S(2)}, u32[]{:S(2)}) collective-permute-start(bf16[256,512]{1,0:T(8,128)(2,1)S(1)} %add_convert_fusion.4), channel_id=1, source_target_pairs={{0,1},{1,2},{2,3},{3,4},{4,5},{5,6},{6,7},{7,0},{16,17},{17,18},{1... | collective-permute-start | bytes 786440 | tf_op jit(solution)/shard_map/ppermute | solution.py:59
  103.6 8.8 %collective-permute-start.29 = (bf16[256,512]{1,0:T(8,128)(2,1)S(1)}, bf16[256,512]{1,0:T(8,128)(2,1)S(1)}, u32[]{:S(2)}, u32[]{:S(2)}) collective-permute-start(bf16[256,512]{1,0:T(8,128)(2,1)S(1)} %add_convert_fusion.1), channel_id=1, source_target_pairs={{0,7},{1,0},{2,1},{3,2},{4,3},{5,4},{6,5},{7,6},{16,23},{17,16},{1... | collective-permute-start | bytes 786440 | tf_op jit(solution)/shard_map/ppermute | solution.py:59
  (2 other events, 52.7 us)

commit v6 on v5

--- a/solution.py
+++ b/solution.py
@@ -22,13 +22,12 @@
 ATTENTION_VMEM = 14 * 2**20
 PROJECT_VMEM = 8 * 2**20
 WIDE = 4
-MARK_FLOPS = 0
 ATT_FLOPS = 0
 VMEM_LIMIT = 50 * 2**20
 FREE = pl.CostEstimate(flops=0, bytes_accessed=0, transcendentals=0)
 
 
-def pairs(move):
+def pairs(move, sends=lambda x, y, c, z: True):
     out = []
     for x in range(NX):
         for y in range(4):
@@ -40,7 +39,8 @@
                     def index(x, y, c, z):
                         return (x * 4 + (y // 2) * 2 + c) * 16 + (y % 2) * 8 + z
 
-                    out.append((index(x, y, c, z), index(x2, y2, c2, z2)))
+                    if sends(x, y, c, z):
+                        out.append((index(x, y, c, z), index(x2, y2, c2, z2)))
     return out
 
 
@@ -49,6 +49,19 @@
     "x-": pairs(lambda x, y, c, z: (x - 1, y, c, z)),
     "z+": pairs(lambda x, y, c, z: (x, y, c, z + 1)),
     "z-": pairs(lambda x, y, c, z: (x, y, c, z - 1)),
+    **{
+        f"swing{sign}{parity}": pairs(
+            lambda x, y, c, z: (x, y, c, z + (sign if (z + c) % 2 == parity else -sign))
+        )
+        for sign in (1, -1)
+        for parity in (0, 1)
+    },
+    **{
+        f"last{sign}": pairs(
+            lambda x, y, c, z: (x, y, c, z + sign), lambda x, y, c, z: (z + c) % 2 == 1
+        )
+        for sign in (1, -1)
+    },
     "core": pairs(lambda x, y, c, z: (x, y, c + 1, z)),
     "y_near": pairs(lambda x, y, c, z: (x, y ^ 1, c, z)),
     "y_far": pairs(lambda x, y, c, z: (x, 3 - y, c, z)),
@@ -64,15 +77,22 @@
 HBM = pl.BlockSpec(memory_space=pltpu.HBM)
 
 
+REACH = ((4, -2, 2, 0), (-3, 3, -1, 1))
+
+
 def pick_kernel(coords, w_ref, near_w_ref, far_w_ref, sems):
     c, yl = coords[2], coords[3]
-    columns = near_w_ref.shape[1]
-    near_rows, far_rows = near_w_ref.shape[0], far_w_ref.shape[0]
-    there = pl.ds(pl.multiple_of(((1 - yl) * 2 + c) * columns, columns), columns)
-    copies = [
-        pltpu.make_async_copy(w_ref.at[pl.ds(0, near_rows), there], near_w_ref, sems.at[0]),
-        pltpu.make_async_copy(w_ref.at[pl.ds(near_rows, far_rows), there], far_w_ref, sems.at[1]),
-    ]
+    copies = []
+    for j in range(NZ // 2):
+        there = pl.ds(pl.multiple_of(((1 - yl) * NZ + 2 * j + c) * 512, 512), 512)
+        here = pl.ds(j * 512, 512)
+        row = 0
+        for i, out in enumerate((near_w_ref, far_w_ref)):
+            rows = pl.ds(row, out.shape[0])
+            copies.append(
+                pltpu.make_async_copy(w_ref.at[rows, there], out.at[:, here], sems.at[2 * j + i])
+            )
+            row += out.shape[0]
     for copy in copies:
         copy.start()
     for copy in copies:
@@ -87,7 +107,7 @@
         out_shape=parts,
         in_specs=[SMEM, HBM],
         out_specs=[VMEM] * 2,
-        scratch_shapes=[pltpu.SemaphoreType.DMA((2,))],
+        scratch_shapes=[pltpu.SemaphoreType.DMA((NZ,))],
         compiler_params=pltpu.CompilerParams(vmem_limit_bytes=VMEM_LIMIT),
         cost_estimate=FREE,
         name="pick",
@@ -230,61 +250,40 @@
     )(*pieces)
 
 
-def mark_kernel(coords, *refs):
-    for i in range(coords.shape[0]):
-        refs[-1][i] = coords[i]
-
-
-def mark(coords, *arrays):
-    return pl.pallas_call(
-        mark_kernel,
-        out_shape=jax.ShapeDtypeStruct(coords.shape, coords.dtype),
-        in_specs=[SMEM] + [VMEM] * len(arrays),
-        out_specs=SMEM,
-        compiler_params=pltpu.CompilerParams(vmem_limit_bytes=PROJECT_VMEM),
-        cost_estimate=pl.CostEstimate(flops=MARK_FLOPS, bytes_accessed=0, transcendentals=0),
-        name="mark",
-    )(coords, *arrays)
-
-
-def project_kernel(steps, coords, own_ref, near_ref, w_ref, w0a, w0b, w1a, w1b, *out_refs):
-    core, yl, z = coords[2], coords[3], coords[4]
+def project_kernel(
+    steps, sign, coords, own_ref, other_ref, near_ref, other_near_ref, w_ref, w0_ref, w1_ref, *out_refs
+):
+    c, yl, z = coords[2], coords[3], coords[4]
+    odd = (z + c) % 2
+    own = jnp.concatenate([own_ref[...], other_ref[...]], 0)
+    near = jnp.concatenate([near_ref[...], other_near_ref[...]], 0)
 
     def lanes(block):
         return pl.ds(pl.multiple_of(block * 512, 512), 512)
 
     for step, out_ref in zip(steps, out_refs):
-        target = (z + step + NZ) % NZ
-        mine = target // 4 == core
-        part = lanes(target % 4)
+        target = (z + sign * jnp.where(odd == 0, REACH[0][step], REACH[1][step]) + NZ) % NZ
+        part = lanes(target // 2)
         value = jnp.dot(
-            own_ref[...], w_ref[:, lanes(yl * NZ + target)], preferred_element_type=jnp.float32
+            own, w_ref[:, lanes(yl * NZ + target)], preferred_element_type=jnp.float32
         )
-        value += jnp.dot(
-            near_ref[:, :NEAR_ROWS],
-            jnp.where(mine, w0a[:, part], w0b[:, part]),
-            preferred_element_type=jnp.float32,
-        )
-        value += jnp.dot(
-            near_ref[:, NEAR_ROWS:],
-            jnp.where(mine, w1a[:, part], w1b[:, part]),
-            preferred_element_type=jnp.float32,
-        )
+        value += jnp.dot(near[:, :NEAR_ROWS], w0_ref[:, part], preferred_element_type=jnp.float32)
+        value += jnp.dot(near[:, NEAR_ROWS:], w1_ref[:, part], preferred_element_type=jnp.float32)
         out_ref[...] = value.astype(jnp.bfloat16)
 
 
-def project(coords, steps, own, near, weights, parts):
-    rows = own.shape[0]
+def project(coords, steps, sign, rows, weights, parts):
     count = len(steps)
+    shape = (2 * rows[0].shape[0], 512)
     return pl.pallas_call(
-        functools.partial(project_kernel, steps),
-        out_shape=[jax.ShapeDtypeStruct((rows, 512), jnp.bfloat16)] * count,
+        functools.partial(project_kernel, steps, sign),
+        out_shape=[jax.ShapeDtypeStruct(shape, jnp.bfloat16)] * count,
         in_specs=[SMEM] + [VMEM] * 7,
         out_specs=[VMEM] * count,
         compiler_params=pltpu.CompilerParams(vmem_limit_bytes=PROJECT_VMEM),
         cost_estimate=FREE,
         name="project",
-    )(coords, own, near, weights, *parts)
+    )(coords, *rows, weights, *parts)
 
 
 def shards(queries, keys_values, block_list, out_weight):
@@ -302,51 +301,57 @@
     right = send(own, "x-")
 
     near_w, far_w = pick(coords, out_weight)
-    far, left, right, near_w, far_w = barrier((far, left, right, near_w, far_w))
     near_part = send(near_w, "y_near")
     far_part = send(far_w, "y_far")
+
     one, four = stack([own, far, left, right], ((1, 2), (0, 1, 2, 3)))
-    far_right = send(far, "x-")
-    both = send(one, "x+")
-    two_far = send(far_right, "x-")
+
+    def spread(_, held):
+        far, one, four, _ = held
+        far_right = send(far, "x-")
+        both = send(one, "x+")
+        return (far_right, both, send(four, "core"), send(far_right, "x-"))
+
+    once = (ctx >= 0).astype(jnp.int32)
+    far_right, both, four_t, two_far = lax.fori_loop(0, once, spread, (far, one, four, right))
     late = [both, far_right, two_far]
-    pieces = [four, send(four, "core"), *late, *(send(piece, "core") for piece in late)]
+    pieces = [four, four_t, *late, *(send(piece, "core") for piece in late)]
     slots = ((0, 2, 12, 4), (1, 3, 13, 5), (14, 8), (6,), (10,), (15, 9), (7,), (11,))
 
     first, kv = attention(coords, block_list, queries, 0, n_rows, pieces, slots)
-    attended = [first] + [
-        attention(coords, block_list, queries, k * n_rows, n_rows, [kv])[0] for k in range(1, CHUNKS)
+    kv, near_part, far_part = barrier((kv, near_part, far_part))
+    parts = [near_part, far_part]
+    second = attention(coords, block_list, queries, n_rows, n_rows, [kv])[0]
+    near = send(first, "y_near")
+    near, second = barrier((near, second))
+    rows = [
+        (a, send(a, "core"), n, send(n, "core"))
+        for a, n in ((first, near), (second, send(second, "y_near")))
     ]
-    near = [send(first, "y_near"), None]
-    near_part, far_part, near[0], near[1] = barrier((near_part, far_part, near[0], attended[1]))
-    near[1] = send(near[1], "y_near")
-    near_other, far_other = send(near_part, "core"), send(far_part, "core")
-    parts = [near_part, near_other, far_part, far_other]
-    coords = mark(coords, near_other, far_other)
-
-    def add(*terms):
-        return sum(t.astype(jnp.float32) for t in terms).astype(jnp.bfloat16)
-
-    moves = ("z+", "z-")
-    ways, moving = [], []
+
+    def add(a, b):
+        return (a.astype(jnp.float32) + b.astype(jnp.float32)).astype(jnp.bfloat16)
+
+    signs = (1, -1)
+    moving, partial = [], []
     for k in range(CHUNKS):
-        orders = ((4, 3, 2, 1), (-3, -2, -1)) if k % 2 == 0 else ((3, 2, 1), (-4, -3, -2, -1))
         if k:
-            near[k], moving[k - 1][1] = barrier((near[k], moving[k - 1][1]))
-        early = tuple(order[0] for order in orders)
-        late = (*orders[0][1:], *orders[1][1:], 0)
-        begun = project(coords, early, attended[k], near[k], out_weight, parts)
-        moving.append([send(value, move) for value, move in zip(begun, moves)])
-        partial = dict(zip(late, project(coords, late, attended[k], near[k], out_weight, parts)))
-        ways.append((orders, partial))
-
+            tied = barrier((*rows[k], moving[k - 1]))
+            rows[k], moving[k - 1] = tied[:-1], tied[-1]
+        (begun,) = project(coords, (0,), signs[k], rows[k], out_weight, parts)
+        moving.append(send(begun, f"swing{signs[k]}0"))
+        partial.append(list(project(coords, (1, 2, 3), signs[k], rows[k], out_weight, parts)))
     for step in range(1, 4):
         for k in range(CHUNKS):
-            orders, partial = ways[k]
-            for way, order in enumerate(orders):
-                if step < len(order):
-                    moving[k][way] = send(add(moving[k][way], partial[order[step]]), moves[way])
-    results = [add(ways[k][1][0], *moving[k]) for k in range(CHUNKS)]
+            partial[k][step - 1] = add(moving[k], partial[k][step - 1])
+            move = f"swing{signs[k]}{step % 2}" if step < 3 else f"last{signs[k]}"
+            moving[k] = send(partial[k][step - 1], move)
+    results = []
+    for k in range(CHUNKS):
+        whole = add(partial[k][2], moving[k])
+        half = whole.shape[0] // 2
+        other = send(whole[half:], "core")
+        results.append(jnp.where((ctx + z) % 2 == 0, whole[:half], other))
     return jnp.concatenate(results, 0)
 
 

time: 113 us -> 132 us (1.17); the launches traced: 113 us -> 130 us
  local copies, waits for them, and re-layouts: 1.17 us -> 14.2 us
  waiting for transfers between devices: 48.4 us -> 60.4 us
  starting transfers between devices: 40.2 us -> 29.4 us
  Pallas kernels: 21.7 us -> 24.3 us
    ppermute x30 -> x28, waiting for transfers between devices: 48.4 us -> 60.4 us  [send(): return lax.ppermute(array, AXES, MOVES[move])]
    ppermute x30 -> x28, starting transfers between devices: 40.2 us -> 29.4 us  [send(): return lax.ppermute(array, AXES, MOVES[move])]
    unnamed x8 -> x13, local copies, waits for them, and re-layouts: 0.01 us -> 7.09 us
    while x0 -> x3, local copies, waits for them, and re-layouts: none -> 5.87 us
    pallas_call x1, Pallas kernels: 0.1 us -> 1.87 us  [stack(): pl.pallas_call(functools.partial(stack_kernel, groups), out_shape=[jax.Sh...]
    pallas_call x5 -> x4, Pallas kernels: 8.58 us -> 7.27 us  [project(): pl.pallas_call(functools.partial(project_kernel, steps, sign), out_shape=...]
  transfers between devices with their start and end apart: 30 -> 28, of which waited for: 20 -> 17; matrix products, arithmetic and copies ran while one was open for 1% -> 6% of each run, Pallas kernels for 19% -> 18%
where the time goes in v6:
time: 132 us; the launch traced here: 130 us
  waiting for transfers between devices  60.4 us (46%)
  starting transfers between devices  29.4 us (22%)
  Pallas kernels  24.3 us (18%)
  local copies, waits for them, and re-layouts  14.2 us (11%)
  other arithmetic  1.96 us (1%)
    ppermute x28, waiting for transfers between devices, send(): return lax.ppermute(array, AXES, MOVES[move])  60.4 us
    ppermute x28, starting transfers between devices, send(): return lax.ppermute(array, AXES, MOVES[move])  29.4 us
    pallas_call x2, Pallas kernels, attention(): pl.pallas_call(functools.partial(attention_kernel, first_row, n_rows, slo...  11.6 us
    pallas_call x4, Pallas kernels, project(): pl.pallas_call(functools.partial(project_kernel, steps, sign), out_shape=...  7.27 us
    unnamed x13, local copies, waits for them, and re-layouts  7.09 us
    while x3, local copies, waits for them, and re-layouts  5.87 us
    pallas_call x1, Pallas kernels, pick(): pl.pallas_call(pick_kernel, out_shape=parts, in_specs=[SMEM, HBM], out_sp...  3.49 us
  transfers between devices with their start and end apart: 28, of which 17 were waited for; matrix products, arithmetic and copies ran while one was open for 6% of the time, Pallas kernels for 18%

profile of v6, /device:TPU:6, one launch (start us, length us, event | category | flops | bytes accessed | tf_op | source)
XLA Modules:
  0.0 130.4 jit_solution(10690400852820172301)
XLA Ops:
  1.1 3.1 %collective-permute-start.4 = (bf16[2,512,128]{2,1,0:T(8,128)(2,1)S(1)}, bf16[2,512,128]{2,1,0:T(8,128)(2,1)S(1)}, u32[]{:S(2)}, u32[]{:S(2)}) collective-permute-start(bf16[2,512,128]{2,1,0:T(8,128)(2,1)S(1)} %get-tuple-element.100), channel_id=1, source_target_pairs={{0,40},{1,41},{2,42},{3,43},{4,44},{5,45},{6,46},{7,47},{16,56},{1... | collective-permute-start | bytes 786440 | tf_op jit(solution)/shard_map/ppermute | solution.py:72
  5.0 2.4 %collective-permute-start.5 = (bf16[2,512,128]{2,1,0:T(8,128)(2,1)S(1)}, bf16[2,512,128]{2,1,0:T(8,128)(2,1)S(1)}, u32[]{:S(2)}, u32[]{:S(2)}) collective-permute-start(bf16[2,512,128]{2,1,0:T(8,128)(2,1)S(1)} %get-tuple-element.101.refs_0_), channel_id=1, source_target_pairs={{0,64},{1,65},{2,66},{3,67},{4,68},{5,69},{6,70},{7,71},{16,80},{1... | collective-permute-start | bytes 786440 | tf_op jit(solution)/shard_map/ppermute | solution.py:72
  7.5 3.5 %pick.1 = (bf16[256,2048]{1,0:T(8,128)(2,1)}, bf16[256,2048]{1,0:T(8,128)(2,1)}) custom-call(s32[5]{0:T(128)S(1)} %stack.24.coords, bf16[512,8192]{1,0:T(8,128)(2,1)} %w_ref.9), custom_call_target="tpu_custom_call" | custom-call | tf_op jit(solution)/shard_map/pick/pallas_call | solution.py:105
  14.9 1.9 %stack.25 = (bf16[2,2,512,128]{3,2,1,0:T(8,128)(2,1)}, bf16[4,2,512,128]{3,2,1,0:T(8,128)(2,1)S(1)}) custom-call(bf16[2,512,128]{2,1,0:T(8,128)(2,1)S(1)} %get-tuple-element.101.refs_0_, bf16[2,512,128]{2,1,0:T(8,128)(2,1)} %copy-done.5, bf16[2,512,128]{2,1,0:T(8,128)(2,1)S(1)} %copy-done.3, bf16[2,512,128]{2,1,0:T(8,128)(2,1)} %collective-permute-done.6.refs_3_), custom_call_target="tpu_custom_call" | custom-call | tf_op jit(solution)/shard_map/stack/pallas_call | solution.py:240
  17.8 22.0 %while.16 = (s32[]{:T(128)}, bf16[2,512,128]{2,1,0:T(8,128)(2,1)}, bf16[2,2,512,128]{3,2,1,0:T(8,128)(2,1)}, bf16[4,2,512,128]{3,2,1,0:T(8,128)(2,1)}, bf16[2,512,128]{2,1,0:T(8,128)(2,1)}, /*index=5*/s32[]{:T(128)}, s32[]{:T(128)}) while((s32[]{:T(128)}, bf16[2,512,128]{2,1,0:T(8,128)(2,1)}, bf16[2,2,512,128]{3,2,1,0:T(8,128)(2,1)}, ...), condition=%wide.region_1.2_spmd, body=%wide.region_0.1_spmd.sunk | while | flops 2 | bytes 12058861 | solution.py:316
  17.8 2.8 %collective-permute-start.1 = (bf16[2,2,512,128]{3,2,1,0:T(8,128)(2,1)}, bf16[2,2,512,128]{3,2,1,0:T(8,128)(2,1)}, u32[]{:S(2)}, u32[]{:S(2)}) collective-permute-start(bf16[2,2,512,128]{3,2,1,0:T(8,128)(2,1)} %get-tuple-element.147), channel_id=1, source_target_pairs={{0,64},{1,65},{2,66},{3,67},{4,68},{5,69},{6,70},{7,71},{16,80},{1... | collective-permute-start | bytes 1572872 | tf_op jit(solution)/shard_map/while/body/ppermute | solution.py:72
  20.7 10.0 %collective-permute-done = bf16[2,512,128]{2,1,0:T(8,128)(2,1)} collective-permute-done((bf16[2,512,128]{2,1,0:T(8,128)(2,1)}, bf16[2,512,128]{2,1,0:T(8,128)(2,1)}, u32[]{:S(2)}, u32[]{:S(2)}) %collective-permute-start) | collective-permute-done | bytes 262176 | tf_op jit(solution)/shard_map/while/body/ppermute | solution.py:72
  30.6 1.7 %copy.16 = bf16[2,512,128]{2,1,0:T(8,128)(2,1)} copy(bf16[2,512,128]{2,1,0:T(8,128)(2,1)} %collective-permute-done) | data formatting | bytes 524288 | tf_op jit(solution)/shard_map/while
  32.8 1.9 %copy.17 = bf16[2,2,512,128]{3,2,1,0:T(8,128)(2,1)} copy(bf16[2,2,512,128]{3,2,1,0:T(8,128)(2,1)} %collective-permute-done.1) | data formatting | bytes 1048576 | tf_op jit(solution)/shard_map/while
  34.7 2.3 %copy.18 = bf16[4,2,512,128]{3,2,1,0:T(8,128)(2,1)} copy(bf16[4,2,512,128]{3,2,1,0:T(8,128)(2,1)} %collective-permute-done.2) | data formatting | bytes 2097152 | tf_op jit(solution)/shard_map/while
  37.0 2.8 %collective-permute-done.3 = bf16[2,512,128]{2,1,0:T(8,128)(2,1)} collective-permute-done((bf16[2,512,128]{2,1,0:T(8,128)(2,1)}, bf16[2,512,128]{2,1,0:T(8,128)(2,1)}, u32[]{:S(2)}, u32[]{:S(2)}) %collective-permute-start.3) | collective-permute-done | bytes 262176 | tf_op jit(solution)/shard_map/while/body/ppermute | solution.py:72
  40.3 2.0 %collective-permute-done.9.refs_7_ = bf16[2,512,128]{2,1,0:T(8,128)(2,1)S(1)} collective-permute-done((bf16[2,512,128]{2,1,0:T(8,128)(2,1)}, bf16[2,512,128]{2,1,0:T(8,128)(2,1)S(1)}, u32[]{:S(2)}, u32[]{:S(2)}) %collective-permute-start.9) | collective-permute-done | bytes 262176 | tf_op jit(solution)/shard_map/ppermute | solution.py:72
  43.7 4.8 %attention.2 = (bf16[256,512]{1,0:T(8,128)(2,1)S(1)}, bf16[2,8192,128]{2,1,0:T(8,128)(2,1)S(1)}) custom-call(s32[5]{0:T(128)S(1)} %stack.24.coords, s32[4,16]{1,0:T(4,128)S(1)} %copy-done.4, bf16[512,512]{1,0:T(8,128)(2,1)S(1)} %copy-done.1, bf16[4,2,512,128]{3,2,1,0:T(8,128)(2,1)S(1)} %get-tuple-element.141.refs_0_, ...), custom_call_target="tpu_custom_call" | custom-call | tf_op jit(solution)/shard_map/attention/pallas_call | solution.py:209
  48.7 1.4 %collective-permute-start.16 = (bf16[256,512]{1,0:T(8,128)(2,1)S(1)}, bf16[256,512]{1,0:T(8,128)(2,1)S(1)}, u32[]{:S(2)}, u32[]{:S(2)}) collective-permute-start(bf16[256,512]{1,0:T(8,128)(2,1)S(1)} %get-tuple-element.68.own_ref), channel_id=1, source_target_pairs={{0,16},{1,17},{2,18},{3,19},{4,20},{5,21},{6,22},{7,23},{16,0},{17... | collective-permute-start | bytes 786440 | tf_op jit(solution)/shard_map/ppermute | solution.py:72
  50.1 6.9 %attention.3.own_ref = bf16[256,512]{1,0:T(8,128)(2,1)S(1)} custom-call(s32[5]{0:T(128)S(1)} %stack.24.coords, s32[4,16]{1,0:T(4,128)S(1)} %copy-done.4, bf16[512,512]{1,0:T(8,128)(2,1)S(1)} %copy-done.1, bf16[2,8192,128]{2,1,0:T(8,128)(2,1)S(1)} %get-tuple-element.72.refs_0_), custom_call_target="tpu_custom_call" | custom-call | tf_op jit(solution)/shard_map/attention/pallas_call | solution.py:209
  57.5 1.3 collective-permute-start.14
  58.9 3.4 %copy-done = bf16[512,8192]{1,0:T(8,128)(2,1)S(1)} copy-done((bf16[512,8192]{1,0:T(8,128)(2,1)S(1)}, bf16[512,8192]{1,0:T(8,128)(2,1)}, u32[]{:S(2)}) %copy-start) | copy-done | bytes 8388632
  62.3 1.3 project.4
  63.6 2.0 %collective-permute-start.18 = (bf16[512,512]{1,0:T(8,128)(2,1)S(1)}, bf16[512,512]{1,0:T(8,128)(2,1)S(1)}, u32[]{:S(2)}, u32[]{:S(2)}) collective-permute-start(bf16[512,512]{1,0:T(8,128)(2,1)S(1)} %project.4), channel_id=1, source_target_pairs={{0,1},{1,0},{2,3},{3,2},{4,5},{5,4},{6,7},{7,6},{16,23},{17,18},{1... | collective-permute-start | bytes 1572872 | tf_op jit(solution)/shard_map/ppermute | solution.py:72
  65.6 3.8 %collective-permute-start.13 = (bf16[256,512]{1,0:T(8,128)(2,1)S(1)}, bf16[256,512]{1,0:T(8,128)(2,1)S(1)}, u32[]{:S(2)}, u32[]{:S(2)}) collective-permute-start(bf16[256,512]{1,0:T(8,128)(2,1)S(1)} %attention.3.own_ref), channel_id=1, source_target_pairs={{0,16},{1,17},{2,18},{3,19},{4,20},{5,21},{6,22},{7,23},{16,0},{17... | collective-permute-start | bytes 786440 | tf_op jit(solution)/shard_map/ppermute | solution.py:72
  69.4 1.2 collective-permute-done.13.other_ref
  70.9 1.9 %collective-permute-done.18 = bf16[512,512]{1,0:T(8,128)(2,1)S(1)} collective-permute-done((bf16[512,512]{1,0:T(8,128)(2,1)S(1)}, bf16[512,512]{1,0:T(8,128)(2,1)S(1)}, u32[]{:S(2)}, u32[]{:S(2)}) %collective-permute-start.18) | collective-permute-done | bytes 524320 | tf_op jit(solution)/shard_map/ppermute | solution.py:72
  72.8 1.3 project.6
  74.1 5.9 %collective-permute-start.23 = (bf16[512,512]{1,0:T(8,128)(2,1)S(1)}, bf16[512,512]{1,0:T(8,128)(2,1)S(1)}, u32[]{:S(2)}, u32[]{:S(2)}) collective-permute-start(bf16[512,512]{1,0:T(8,128)(2,1)S(1)} %project.6), channel_id=1, source_target_pairs={{0,7},{1,2},{2,1},{3,4},{4,3},{5,6},{6,5},{7,0},{16,17},{17,16},{1... | collective-permute-start | bytes 1572872 | tf_op jit(solution)/shard_map/ppermute | solution.py:72
  80.0 2.4 %project.5 = (bf16[512,512]{1,0:T(8,128)(2,1)S(1)}, bf16[512,512]{1,0:T(8,128)(2,1)S(1)}, bf16[512,512]{1,0:T(8,128)(2,1)S(1)}) custom-call(s32[5]{0:T(128)S(1)} %stack.24.coords, bf16[256,512]{1,0:T(8,128)(2,1)S(1)} %get-tuple-element.68.own_ref, bf16[256,512]{1,0:T(8,128)(2,1)S(1)} %collective-permute-done.16.other_ref, ...), custom_call_target="tpu_custom_call" | custom-call | tf_op jit(solution)/shard_map/project/pallas_call | solution.py:278
  82.4 2.4 %project.7 = (bf16[512,512]{1,0:T(8,128)(2,1)S(1)}, bf16[512,512]{1,0:T(8,128)(2,1)S(1)}, bf16[512,512]{1,0:T(8,128)(2,1)S(1)}) custom-call(s32[5]{0:T(128)S(1)} %stack.24.coords, bf16[256,512]{1,0:T(8,128)(2,1)S(1)} %attention.3.own_ref, bf16[256,512]{1,0:T(8,128)(2,1)S(1)} %collective-permute-done.13.other_ref, ...), custom_call_target="tpu_custom_call" | custom-call | tf_op jit(solution)/shard_map/project/pallas_call | solution.py:278
  85.0 2.2 %collective-permute-done.23 = bf16[512,512]{1,0:T(8,128)(2,1)S(1)} collective-permute-done((bf16[512,512]{1,0:T(8,128)(2,1)S(1)}, bf16[512,512]{1,0:T(8,128)(2,1)S(1)}, u32[]{:S(2)}, u32[]{:S(2)}) %collective-permute-start.23) | collective-permute-done | bytes 524320 | tf_op jit(solution)/shard_map/ppermute | solution.py:72
  87.4 13.6 %collective-permute-done.19 = bf16[512,512]{1,0:T(8,128)(2,1)S(1)} collective-permute-done((bf16[512,512]{1,0:T(8,128)(2,1)S(1)}, bf16[512,512]{1,0:T(8,128)(2,1)S(1)}, u32[]{:S(2)}, u32[]{:S(2)}) %collective-permute-start.19) | collective-permute-done | bytes 524320 | tf_op jit(solution)/shard_map/ppermute | solution.py:72
  101.5 13.5 %collective-permute-done.20 = bf16[512,512]{1,0:T(8,128)(2,1)S(1)} collective-permute-done((bf16[512,512]{1,0:T(8,128)(2,1)S(1)}, bf16[512,512]{1,0:T(8,128)(2,1)S(1)}, u32[]{:S(2)}, u32[]{:S(2)}) %collective-permute-start.20) | collective-permute-done | bytes 524320 | tf_op jit(solution)/shard_map/ppermute | solution.py:72
  115.1 1.3 collective-permute-start.21
  116.6 1.3 collective-permute-start.26
  117.9 9.5 %collective-permute-done.21 = bf16[512,512]{1,0:T(8,128)(2,1)S(1)} collective-permute-done((bf16[512,512]{1,0:T(8,128)(2,1)S(1)}, bf16[512,512]{1,0:T(8,128)(2,1)S(1)}, u32[]{:S(2)}, u32[]{:S(2)}) %collective-permute-start.21) | collective-permute-done | bytes 524320 | tf_op jit(solution)/shard_map/ppermute | solution.py:72
  (64 shorter events, 14.8 us)
Async XLA Ops:
  1.1 11.2 %collective-permute-start.4 = (bf16[2,512,128]{2,1,0:T(8,128)(2,1)S(1)}, bf16[2,512,128]{2,1,0:T(8,128)(2,1)S(1)}, u32[]{:S(2)}, u32[]{:S(2)}) collective-permute-start(bf16[2,512,128]{2,1,0:T(8,128)(2,1)S(1)} %get-tuple-element.100), channel_id=1, source_target_pairs={{0,40},{1,41},{2,42},{3,43},{4,44},{5,45},{6,46},{7,47},{16,56},{1... | collective-permute-start | bytes 786440 | tf_op jit(solution)/shard_map/ppermute | solution.py:72
  4.2 9.1 %collective-permute-start.6 = (bf16[2,512,128]{2,1,0:T(8,128)(2,1)S(1)}, bf16[2,512,128]{2,1,0:T(8,128)(2,1)}, u32[]{:S(2)}, u32[]{:S(2)}) collective-permute-start(bf16[2,512,128]{2,1,0:T(8,128)(2,1)S(1)} %get-tuple-element.101.refs_0_), channel_id=1, source_target_pairs={{0,192},{1,193},{2,194},{3,195},{4,196},{5,197},{6,198},{7,199},{1... | collective-permute-start | bytes 786440 | tf_op jit(solution)/shard_map/ppermute | solution.py:72
  5.0 8.3 %collective-permute-start.5 = (bf16[2,512,128]{2,1,0:T(8,128)(2,1)S(1)}, bf16[2,512,128]{2,1,0:T(8,128)(2,1)S(1)}, u32[]{:S(2)}, u32[]{:S(2)}) collective-permute-start(bf16[2,512,128]{2,1,0:T(8,128)(2,1)S(1)} %get-tuple-element.101.refs_0_), channel_id=1, source_target_pairs={{0,64},{1,65},{2,66},{3,67},{4,68},{5,69},{6,70},{7,71},{16,80},{1... | collective-permute-start | bytes 786440 | tf_op jit(solution)/shard_map/ppermute | solution.py:72
  11.0 39.0 %collective-permute-start.11 = (bf16[256,2048]{1,0:T(8,128)(2,1)}, bf16[256,2048]{1,0:T(8,128)(2,1)S(1)}, u32[]{:S(2)}, u32[]{:S(2)}) collective-permute-start(bf16[256,2048]{1,0:T(8,128)(2,1)} %get-tuple-element.70), channel_id=1, source_target_pairs={{0,8},{1,9},{2,10},{3,11},{4,12},{5,13},{6,14},{7,15},{16,24},{17,... | collective-permute-start | bytes 3145736 | tf_op jit(solution)/shard_map/ppermute | solution.py:72
  11.2 38.8 %collective-permute-start.12 = (bf16[256,2048]{1,0:T(8,128)(2,1)}, bf16[256,2048]{1,0:T(8,128)(2,1)S(1)}, u32[]{:S(2)}, u32[]{:S(2)}) collective-permute-start(bf16[256,2048]{1,0:T(8,128)(2,1)} %get-tuple-element.71), channel_id=1, source_target_pairs={{0,40},{1,41},{2,42},{3,43},{4,44},{5,45},{6,46},{7,47},{16,56},{1... | collective-permute-start | bytes 3145736 | tf_op jit(solution)/shard_map/ppermute | solution.py:72
  12.3 1.0 copy-start.5
  17.8 24.8 %copy-start.4 = (s32[4,16]{1,0:T(4,128)S(1)}, s32[4,16]{1,0:T(4,128)}, u32[]{:S(2)}) copy-start(s32[4,16]{1,0:T(4,128)} %block_list.3) | copy-start | bytes 772
  17.8 16.9 %collective-permute-start.2 = (bf16[4,2,512,128]{3,2,1,0:T(8,128)(2,1)}, bf16[4,2,512,128]{3,2,1,0:T(8,128)(2,1)}, u32[]{:S(2)}, u32[]{:S(2)}) collective-permute-start(bf16[4,2,512,128]{3,2,1,0:T(8,128)(2,1)} %get-tuple-element.148), channel_id=1, source_target_pairs={{0,16},{1,17},{2,18},{3,19},{4,20},{5,21},{6,22},{7,23},{16,0},{17... | collective-permute-start | bytes 3145736 | tf_op jit(solution)/shard_map/while/body/ppermute | solution.py:72
  17.8 15.0 %collective-permute-start.1 = (bf16[2,2,512,128]{3,2,1,0:T(8,128)(2,1)}, bf16[2,2,512,128]{3,2,1,0:T(8,128)(2,1)}, u32[]{:S(2)}, u32[]{:S(2)}) collective-permute-start(bf16[2,2,512,128]{3,2,1,0:T(8,128)(2,1)} %get-tuple-element.147), channel_id=1, source_target_pairs={{0,64},{1,65},{2,66},{3,67},{4,68},{5,69},{6,70},{7,71},{16,80},{1... | collective-permute-start | bytes 1572872 | tf_op jit(solution)/shard_map/while/body/ppermute | solution.py:72
  20.7 10.0 %collective-permute-start = (bf16[2,512,128]{2,1,0:T(8,128)(2,1)}, bf16[2,512,128]{2,1,0:T(8,128)(2,1)}, u32[]{:S(2)}, u32[]{:S(2)}) collective-permute-start(bf16[2,512,128]{2,1,0:T(8,128)(2,1)} %get-tuple-element.146), channel_id=1, source_target_pairs={{0,192},{1,193},{2,194},{3,195},{4,196},{5,197},{6,198},{7,199},{1... | collective-permute-start | bytes 786440 | tf_op jit(solution)/shard_map/while/body/ppermute | solution.py:72
  30.6 9.1 %collective-permute-start.3 = (bf16[2,512,128]{2,1,0:T(8,128)(2,1)}, bf16[2,512,128]{2,1,0:T(8,128)(2,1)}, u32[]{:S(2)}, u32[]{:S(2)}) collective-permute-start(bf16[2,512,128]{2,1,0:T(8,128)(2,1)} %collective-permute-done), channel_id=1, source_target_pairs={{0,192},{1,193},{2,194},{3,195},{4,196},{5,197},{6,198},{7,199},{1... | collective-permute-start | bytes 786440 | tf_op jit(solution)/shard_map/while/body/ppermute | solution.py:72
  39.8 2.9 %collective-permute-start.7 = (bf16[2,2,512,128]{3,2,1,0:T(8,128)(2,1)}, bf16[2,2,512,128]{3,2,1,0:T(8,128)(2,1)S(1)}, u32[]{:S(2)}, u32[]{:S(2)}) collective-permute-start(bf16[2,2,512,128]{3,2,1,0:T(8,128)(2,1)} %get-tuple-element.65.refs_2_), channel_id=1, source_target_pairs={{0,16},{1,17},{2,18},{3,19},{4,20},{5,21},{6,22},{7,23},{16,0},{17... | collective-permute-start | bytes 1572872 | tf_op jit(solution)/shard_map/ppermute | solution.py:72
  39.8 2.5 %collective-permute-start.9 = (bf16[2,512,128]{2,1,0:T(8,128)(2,1)}, bf16[2,512,128]{2,1,0:T(8,128)(2,1)S(1)}, u32[]{:S(2)}, u32[]{:S(2)}) collective-permute-start(bf16[2,512,128]{2,1,0:T(8,128)(2,1)} %get-tuple-element.67.refs_4_), channel_id=1, source_target_pairs={{0,16},{1,17},{2,18},{3,19},{4,20},{5,21},{6,22},{7,23},{16,0},{17... | collective-permute-start | bytes 786440 | tf_op jit(solution)/shard_map/ppermute | solution.py:72
  40.3 2.4 %collective-permute-start.8 = (bf16[2,512,128]{2,1,0:T(8,128)(2,1)}, bf16[2,512,128]{2,1,0:T(8,128)(2,1)S(1)}, u32[]{:S(2)}, u32[]{:S(2)}) collective-permute-start(bf16[2,512,128]{2,1,0:T(8,128)(2,1)} %get-tuple-element.66.refs_3_), channel_id=1, source_target_pairs={{0,16},{1,17},{2,18},{3,19},{4,20},{5,21},{6,22},{7,23},{16,0},{17... | collective-permute-start | bytes 786440 | tf_op jit(solution)/shard_map/ppermute | solution.py:72
  42.6 1.0 copy-start.1
  48.4 8.9 %collective-permute-start.10 = (bf16[256,512]{1,0:T(8,128)(2,1)S(1)}, bf16[256,512]{1,0:T(8,128)(2,1)S(1)}, u32[]{:S(2)}, u32[]{:S(2)}) collective-permute-start(bf16[256,512]{1,0:T(8,128)(2,1)S(1)} %get-tuple-element.68.own_ref), channel_id=1, source_target_pairs={{0,8},{1,9},{2,10},{3,11},{4,12},{5,13},{6,14},{7,15},{16,24},{17,... | collective-permute-start | bytes 786440 | tf_op jit(solution)/shard_map/ppermute | solution.py:72
  48.7 10.1 %collective-permute-start.16 = (bf16[256,512]{1,0:T(8,128)(2,1)S(1)}, bf16[256,512]{1,0:T(8,128)(2,1)S(1)}, u32[]{:S(2)}, u32[]{:S(2)}) collective-permute-start(bf16[256,512]{1,0:T(8,128)(2,1)S(1)} %get-tuple-element.68.own_ref), channel_id=1, source_target_pairs={{0,16},{1,17},{2,18},{3,19},{4,20},{5,21},{6,22},{7,23},{16,0},{17... | collective-permute-start | bytes 786440 | tf_op jit(solution)/shard_map/ppermute | solution.py:72
  57.4 1.5 %collective-permute-start.17 = (bf16[256,512]{1,0:T(8,128)(2,1)S(1)}, bf16[256,512]{1,0:T(8,128)(2,1)S(1)}, u32[]{:S(2)}, u32[]{:S(2)}) collective-permute-start(bf16[256,512]{1,0:T(8,128)(2,1)S(1)} %collective-permute-done.10.near_ref), channel_id=1, source_target_pairs={{0,16},{1,17},{2,18},{3,19},{4,20},{5,21},{6,22},{7,23},{16,0},{17... | collective-permute-start | bytes 786440 | tf_op jit(solution)/shard_map/ppermute | solution.py:72
  57.5 11.9 %collective-permute-start.14 = (bf16[256,512]{1,0:T(8,128)(2,1)S(1)}, bf16[256,512]{1,0:T(8,128)(2,1)S(1)}, u32[]{:S(2)}, u32[]{:S(2)}) collective-permute-start(bf16[256,512]{1,0:T(8,128)(2,1)S(1)} %attention.3.own_ref), channel_id=1, source_target_pairs={{0,8},{1,9},{2,10},{3,11},{4,12},{5,13},{6,14},{7,15},{16,24},{17,... | collective-permute-start | bytes 786440 | tf_op jit(solution)/shard_map/ppermute | solution.py:72
  58.9 3.4 %copy-start = (bf16[512,8192]{1,0:T(8,128)(2,1)S(1)}, bf16[512,8192]{1,0:T(8,128)(2,1)}, u32[]{:S(2)}) copy-start(bf16[512,8192]{1,0:T(8,128)(2,1)} %w_ref.9) | copy-start | bytes 25165828
  63.6 9.3 %collective-permute-start.18 = (bf16[512,512]{1,0:T(8,128)(2,1)S(1)}, bf16[512,512]{1,0:T(8,128)(2,1)S(1)}, u32[]{:S(2)}, u32[]{:S(2)}) collective-permute-start(bf16[512,512]{1,0:T(8,128)(2,1)S(1)} %project.4), channel_id=1, source_target_pairs={{0,1},{1,0},{2,3},{3,2},{4,5},{5,4},{6,7},{7,6},{16,23},{17,18},{1... | collective-permute-start | bytes 1572872 | tf_op jit(solution)/shard_map/ppermute | solution.py:72
  65.6 5.0 %collective-permute-start.13 = (bf16[256,512]{1,0:T(8,128)(2,1)S(1)}, bf16[256,512]{1,0:T(8,128)(2,1)S(1)}, u32[]{:S(2)}, u32[]{:S(2)}) collective-permute-start(bf16[256,512]{1,0:T(8,128)(2,1)S(1)} %attention.3.own_ref), channel_id=1, source_target_pairs={{0,16},{1,17},{2,18},{3,19},{4,20},{5,21},{6,22},{7,23},{16,0},{17... | collective-permute-start | bytes 786440 | tf_op jit(solution)/shard_map/ppermute | solution.py:72
  69.4 1.5 %collective-permute-start.15 = (bf16[256,512]{1,0:T(8,128)(2,1)S(1)}, bf16[256,512]{1,0:T(8,128)(2,1)S(1)}, u32[]{:S(2)}, u32[]{:S(2)}) collective-permute-start(bf16[256,512]{1,0:T(8,128)(2,1)S(1)} %collective-permute-done.14.near_ref), channel_id=1, source_target_pairs={{0,16},{1,17},{2,18},{3,19},{4,20},{5,21},{6,22},{7,23},{16,0},{17... | collective-permute-start | bytes 786440 | tf_op jit(solution)/shard_map/ppermute | solution.py:72
  74.1 13.1 %collective-permute-start.23 = (bf16[512,512]{1,0:T(8,128)(2,1)S(1)}, bf16[512,512]{1,0:T(8,128)(2,1)S(1)}, u32[]{:S(2)}, u32[]{:S(2)}) collective-permute-start(bf16[512,512]{1,0:T(8,128)(2,1)S(1)} %project.6), channel_id=1, source_target_pairs={{0,7},{1,2},{2,1},{3,4},{4,3},{5,6},{6,5},{7,0},{16,17},{17,16},{1... | collective-permute-start | bytes 1572872 | tf_op jit(solution)/shard_map/ppermute | solution.py:72
  84.9 16.1 %collective-permute-start.19 = (bf16[512,512]{1,0:T(8,128)(2,1)S(1)}, bf16[512,512]{1,0:T(8,128)(2,1)S(1)}, u32[]{:S(2)}, u32[]{:S(2)}) collective-permute-start(bf16[512,512]{1,0:T(8,128)(2,1)S(1)} %add_convert_fusion.7), channel_id=1, source_target_pairs={{0,7},{1,2},{2,1},{3,4},{4,3},{5,6},{6,5},{7,0},{16,17},{17,16},{1... | collective-permute-start | bytes 1572872 | tf_op jit(solution)/shard_map/ppermute | solution.py:72
  87.3 13.9 %collective-permute-start.24 = (bf16[512,512]{1,0:T(8,128)(2,1)S(1)}, bf16[512,512]{1,0:T(8,128)(2,1)S(1)}, u32[]{:S(2)}, u32[]{:S(2)}) collective-permute-start(bf16[512,512]{1,0:T(8,128)(2,1)S(1)} %add_convert_fusion.3), channel_id=1, source_target_pairs={{0,1},{1,0},{2,3},{3,2},{4,5},{5,4},{6,7},{7,6},{16,23},{17,18},{1... | collective-permute-start | bytes 1572872 | tf_op jit(solution)/shard_map/ppermute | solution.py:72
  101.2 13.8 %collective-permute-start.20 = (bf16[512,512]{1,0:T(8,128)(2,1)S(1)}, bf16[512,512]{1,0:T(8,128)(2,1)S(1)}, u32[]{:S(2)}, u32[]{:S(2)}) collective-permute-start(bf16[512,512]{1,0:T(8,128)(2,1)S(1)} %add_convert_fusion.6), channel_id=1, source_target_pairs={{0,1},{1,0},{2,3},{3,2},{4,5},{5,4},{6,7},{7,6},{16,23},{17,18},{1... | collective-permute-start | bytes 1572872 | tf_op jit(solution)/shard_map/ppermute | solution.py:72
  101.4 15.0 %collective-permute-start.25 = (bf16[512,512]{1,0:T(8,128)(2,1)S(1)}, bf16[512,512]{1,0:T(8,128)(2,1)S(1)}, u32[]{:S(2)}, u32[]{:S(2)}) collective-permute-start(bf16[512,512]{1,0:T(8,128)(2,1)S(1)} %add_convert_fusion.2), channel_id=1, source_target_pairs={{0,7},{1,2},{2,1},{3,4},{4,3},{5,6},{6,5},{7,0},{16,17},{17,16},{1... | collective-permute-start | bytes 1572872 | tf_op jit(solution)/shard_map/ppermute | solution.py:72
  115.1 12.3 %collective-permute-start.21 = (bf16[512,512]{1,0:T(8,128)(2,1)S(1)}, bf16[512,512]{1,0:T(8,128)(2,1)S(1)}, u32[]{:S(2)}, u32[]{:S(2)}) collective-permute-start(bf16[512,512]{1,0:T(8,128)(2,1)S(1)} %add_convert_fusion.5), channel_id=1, source_target_pairs={{1,2},{3,4},{5,6},{7,0},{16,17},{18,19},{20,21},{22,23},{9,10},{11... | collective-permute-start | bytes 1572872 | tf_op jit(solution)/shard_map/ppermute | solution.py:72
  116.6 11.1 %collective-permute-start.26 = (bf16[512,512]{1,0:T(8,128)(2,1)S(1)}, bf16[512,512]{1,0:T(8,128)(2,1)S(1)}, u32[]{:S(2)}, u32[]{:S(2)}) collective-permute-start(bf16[512,512]{1,0:T(8,128)(2,1)S(1)} %add_convert_fusion.1), channel_id=1, source_target_pairs={{1,0},{3,2},{5,4},{7,6},{16,23},{18,17},{20,19},{22,21},{9,8},{11,... | collective-permute-start | bytes 1572872 | tf_op jit(solution)/shard_map/ppermute | solution.py:72
  127.6 1.6 %collective-permute-start.22 = (bf16[256,512]{1,0:T(8,128)(2,1)S(1)}, bf16[256,512]{1,0:T(8,128)(2,1)S(1)}, u32[]{:S(2)}, u32[]{:S(2)}) collective-permute-start(bf16[256,512]{1,0:T(8,128)(2,1)S(1)} %slice.17), channel_id=1, source_target_pairs={{0,16},{1,17},{2,18},{3,19},{4,20},{5,21},{6,22},{7,23},{16,0},{17... | collective-permute-start | bytes 786440 | tf_op jit(solution)/shard_map/ppermute | solution.py:72
  127.9 1.7 %collective-permute-start.27 = (bf16[256,512]{1,0:T(8,128)(2,1)S(1)}, bf16[256,512]{1,0:T(8,128)(2,1)S(1)}, u32[]{:S(2)}, u32[]{:S(2)}) collective-permute-start(bf16[256,512]{1,0:T(8,128)(2,1)S(1)} %slice.19), channel_id=1, source_target_pairs={{0,16},{1,17},{2,18},{3,19},{4,20},{5,21},{6,22},{7,23},{16,0},{17... | collective-permute-start | bytes 786440 | tf_op jit(solution)/shard_map/ppermute | solution.py:72
  (2 other events, 1.7 us)

commit v7 on v5

--- a/solution.py
+++ b/solution.py
@@ -18,11 +18,10 @@
 SCALE2 = HD ** (-0.5) * math.log2(math.e)
 CHUNKS = 2
 LOW = -1e30
-NEAR_ROWS = 256
+NEAR_ROWS = 224
 ATTENTION_VMEM = 14 * 2**20
 PROJECT_VMEM = 8 * 2**20
 WIDE = 4
-MARK_FLOPS = 0
 ATT_FLOPS = 0
 VMEM_LIMIT = 50 * 2**20
 FREE = pl.CostEstimate(flops=0, bytes_accessed=0, transcendentals=0)
@@ -230,23 +229,6 @@
     )(*pieces)
 
 
-def mark_kernel(coords, *refs):
-    for i in range(coords.shape[0]):
-        refs[-1][i] = coords[i]
-
-
-def mark(coords, *arrays):
-    return pl.pallas_call(
-        mark_kernel,
-        out_shape=jax.ShapeDtypeStruct(coords.shape, coords.dtype),
-        in_specs=[SMEM] + [VMEM] * len(arrays),
-        out_specs=SMEM,
-        compiler_params=pltpu.CompilerParams(vmem_limit_bytes=PROJECT_VMEM),
-        cost_estimate=pl.CostEstimate(flops=MARK_FLOPS, bytes_accessed=0, transcendentals=0),
-        name="mark",
-    )(coords, *arrays)
-
-
 def project_kernel(steps, coords, own_ref, near_ref, w_ref, w0a, w0b, w1a, w1b, *out_refs):
     core, yl, z = coords[2], coords[3], coords[4]
 
@@ -309,8 +291,10 @@
     far_right = send(far, "x-")
     both = send(one, "x+")
     two_far = send(far_right, "x-")
+    far_right_there, both = barrier((far_right, both))
     late = [both, far_right, two_far]
-    pieces = [four, send(four, "core"), *late, *(send(piece, "core") for piece in late)]
+    pieces = [four, send(four, "core"), *late]
+    pieces += [send(piece, "core") for piece in (both, far_right_there, two_far)]
     slots = ((0, 2, 12, 4), (1, 3, 13, 5), (14, 8), (6,), (10,), (15, 9), (7,), (11,))
 
     first, kv = attention(coords, block_list, queries, 0, n_rows, pieces, slots)
@@ -322,7 +306,6 @@
     near[1] = send(near[1], "y_near")
     near_other, far_other = send(near_part, "core"), send(far_part, "core")
     parts = [near_part, near_other, far_part, far_other]
-    coords = mark(coords, near_other, far_other)
 
     def add(*terms):
         return sum(t.astype(jnp.float32) for t in terms).astype(jnp.bfloat16)
@@ -331,8 +314,6 @@
     ways, moving = [], []
     for k in range(CHUNKS):
         orders = ((4, 3, 2, 1), (-3, -2, -1)) if k % 2 == 0 else ((3, 2, 1), (-4, -3, -2, -1))
-        if k:
-            near[k], moving[k - 1][1] = barrier((near[k], moving[k - 1][1]))
         early = tuple(order[0] for order in orders)
         late = (*orders[0][1:], *orders[1][1:], 0)
         begun = project(coords, early, attended[k], near[k], out_weight, parts)

time: 113 us -> 106 us (0.938)
  the two profiles are of different devices: /device:TPU:6 before, /device:TPU:96 now
where the time goes in v7:
time: 106 us
  waiting for transfers between devices  51.9 us (49%)
  starting transfers between devices  32.4 us (31%)
  Pallas kernels  18.5 us (17%)
  other arithmetic  1.7 us (2%)
  local copies, waits for them, and re-layouts  1.17 us (1%)
    ppermute x30, waiting for transfers between devices, send(): return lax.ppermute(array, AXES, MOVES[move])  51.9 us
    ppermute x30, starting transfers between devices, send(): return lax.ppermute(array, AXES, MOVES[move])  32.4 us
    pallas_call x4, Pallas kernels, project(): pl.pallas_call(functools.partial(project_kernel, steps), out_shape=[jax.S...  8.6 us
    pallas_call x2, Pallas kernels, attention(): pl.pallas_call(functools.partial(attention_kernel, first_row, n_rows, slo...  7.39 us
    pallas_call x1, Pallas kernels, pick(): pl.pallas_call(pick_kernel, out_shape=parts, in_specs=[SMEM, HBM], out_sp...  2.4 us
  transfers between devices with their start and end apart: 30, of which 18 were waited for; matrix products, arithmetic and copies ran while one was open for 1% of the time, Pallas kernels for 17%

profile of v7, /device:TPU:96, one launch (start us, length us, event | category | flops | bytes accessed | tf_op | source)
XLA Modules:
  0.0 105.8 jit_solution(2437763143370132530)
XLA Ops:
  0.0 1.1 %constant_dynamic-slice_fusion = (bf16[2,512,128]{2,1,0:T(8,128)(2,1)S(1)}, bf16[2,512,128]{2,1,0:T(8,128)(2,1)S(1)}) fusion(bf16[2,512,1024]{2,1,0:T(8,128)(2,1)} %param.5, s32[]{:T(128)S(6)} %select_n.46, s32[]{:T(128)S(6)} %select_n.45), kind=kLoop, calls=%fused_computation.13 | loop fusion | bytes 1048584 | tf_op jit(solution)/shard_map/dynamic_slice | solution.py:281
  1.1 3.1 %collective-permute-start = (bf16[2,512,128]{2,1,0:T(8,128)(2,1)S(1)}, bf16[2,512,128]{2,1,0:T(8,128)(2,1)S(1)}, u32[]{:S(2)}, u32[]{:S(2)}) collective-permute-start(bf16[2,512,128]{2,1,0:T(8,128)(2,1)S(1)} %get-tuple-element.71), channel_id=1, source_target_pairs={{0,40},{1,41},{2,42},{3,43},{4,44},{5,45},{6,46},{7,47},{16,56},{1... | collective-permute-start | bytes 786440 | tf_op jit(solution)/shard_map/ppermute | solution.py:58
  4.2 2.8 %collective-permute-start.2 = (bf16[2,512,128]{2,1,0:T(8,128)(2,1)S(1)}, bf16[2,512,128]{2,1,0:T(8,128)(2,1)S(1)}, u32[]{:S(2)}, u32[]{:S(2)}) collective-permute-start(bf16[2,512,128]{2,1,0:T(8,128)(2,1)S(1)} %get-tuple-element.72.refs_0_), channel_id=1, source_target_pairs={{0,192},{1,193},{2,194},{3,195},{4,196},{5,197},{6,198},{7,199},{1... | collective-permute-start | bytes 786440 | tf_op jit(solution)/shard_map/ppermute | solution.py:58
  7.0 2.4 %pick.1 = (bf16[224,2048]{1,0:T(8,128)(2,1)S(1)}, bf16[288,2048]{1,0:T(8,128)(2,1)S(1)}) custom-call(s32[5]{0:T(128)S(1)} %stack.24.coords, bf16[512,8192]{1,0:T(8,128)(2,1)} %w_ref.9), custom_call_target="tpu_custom_call" | custom-call | tf_op jit(solution)/shard_map/pick/pallas_call | solution.py:84
  10.5 1.7 %collective-permute-done.2.refs_3_ = bf16[2,512,128]{2,1,0:T(8,128)(2,1)S(1)} collective-permute-done((bf16[2,512,128]{2,1,0:T(8,128)(2,1)S(1)}, bf16[2,512,128]{2,1,0:T(8,128)(2,1)S(1)}, u32[]{:S(2)}, u32[]{:S(2)}) %collective-permute-start.2) | collective-permute-done | bytes 262176 | tf_op jit(solution)/shard_map/ppermute | solution.py:58
  12.2 3.4 %collective-permute-done.1.refs_2_ = bf16[2,512,128]{2,1,0:T(8,128)(2,1)S(1)} collective-permute-done((bf16[2,512,128]{2,1,0:T(8,128)(2,1)S(1)}, bf16[2,512,128]{2,1,0:T(8,128)(2,1)S(1)}, u32[]{:S(2)}, u32[]{:S(2)}) %collective-permute-start.1) | collective-permute-done | bytes 262176 | tf_op jit(solution)/shard_map/ppermute | solution.py:58
  16.0 1.8 %collective-permute-start.5 = (bf16[2,2,512,128]{3,2,1,0:T(8,128)(2,1)S(1)}, bf16[2,2,512,128]{3,2,1,0:T(8,128)(2,1)S(1)}, u32[]{:S(2)}, u32[]{:S(2)}) collective-permute-start(bf16[2,2,512,128]{3,2,1,0:T(8,128)(2,1)S(1)} %get-tuple-element.44), channel_id=1, source_target_pairs={{0,64},{1,65},{2,66},{3,67},{4,68},{5,69},{6,70},{7,71},{16,80},{1... | collective-permute-start | bytes 1572872 | tf_op jit(solution)/shard_map/ppermute | solution.py:58
  18.2 4.0 %collective-permute-done.4.refs_3_ = bf16[2,512,128]{2,1,0:T(8,128)(2,1)S(1)} collective-permute-done((bf16[2,512,128]{2,1,0:T(8,128)(2,1)S(1)}, bf16[2,512,128]{2,1,0:T(8,128)(2,1)S(1)}, u32[]{:S(2)}, u32[]{:S(2)}) %collective-permute-start.4) | collective-permute-done | bytes 262176 | tf_op jit(solution)/shard_map/ppermute | solution.py:58
  22.2 1.8 %collective-permute-start.6 = (bf16[2,512,128]{2,1,0:T(8,128)(2,1)S(1)}, bf16[2,512,128]{2,1,0:T(8,128)(2,1)S(1)}, u32[]{:S(2)}, u32[]{:S(2)}) collective-permute-start(bf16[2,512,128]{2,1,0:T(8,128)(2,1)S(1)} %collective-permute-done.4.refs_3_), channel_id=1, source_target_pairs={{0,192},{1,193},{2,194},{3,195},{4,196},{5,197},{6,198},{7,199},{1... | collective-permute-start | bytes 786440 | tf_op jit(solution)/shard_map/ppermute | solution.py:58
  24.1 4.4 %collective-permute-done.6.refs_4_ = bf16[2,512,128]{2,1,0:T(8,128)(2,1)S(1)} collective-permute-done((bf16[2,512,128]{2,1,0:T(8,128)(2,1)S(1)}, bf16[2,512,128]{2,1,0:T(8,128)(2,1)S(1)}, u32[]{:S(2)}, u32[]{:S(2)}) %collective-permute-start.6) | collective-permute-done | bytes 262176 | tf_op jit(solution)/shard_map/ppermute | solution.py:58
  30.2 1.6 %collective-permute-done.8.refs_6_ = bf16[2,512,128]{2,1,0:T(8,128)(2,1)S(1)} collective-permute-done((bf16[2,512,128]{2,1,0:T(8,128)(2,1)S(1)}, bf16[2,512,128]{2,1,0:T(8,128)(2,1)S(1)}, u32[]{:S(2)}, u32[]{:S(2)}) %collective-permute-start.8) | collective-permute-done | bytes 262176 | tf_op jit(solution)/shard_map/ppermute | solution.py:58
  31.8 3.8 %attention.2 = (bf16[256,512]{1,0:T(8,128)(2,1)S(1)}, bf16[2,8192,128]{2,1,0:T(8,128)(2,1)S(1)}) custom-call(s32[5]{0:T(128)S(1)} %stack.24.coords, s32[4,16]{1,0:T(4,128)S(1)} %copy-done.1, bf16[512,512]{1,0:T(8,128)(2,1)S(1)} %copy-done, bf16[4,2,512,128]{3,2,1,0:T(8,128)(2,1)S(1)} %get-tuple-element.43.refs_0_, ...), custom_call_target="tpu_custom_call" | custom-call | tf_op jit(solution)/shard_map/attention/pallas_call | solution.py:188
  35.9 3.6 %attention.3.own_ref = bf16[256,512]{1,0:T(8,128)(2,1)S(1)} custom-call(s32[5]{0:T(128)S(1)} %stack.24.coords, s32[4,16]{1,0:T(4,128)S(1)} %copy-done.1, bf16[512,512]{1,0:T(8,128)(2,1)S(1)} %copy-done, bf16[2,8192,128]{2,1,0:T(8,128)(2,1)S(1)} %get-tuple-element.50.refs_0_), custom_call_target="tpu_custom_call" | custom-call | tf_op jit(solution)/shard_map/attention/pallas_call | solution.py:188
  39.4 7.0 %collective-permute-done.10.w0a = bf16[224,2048]{1,0:T(8,128)(2,1)S(1)} collective-permute-done((bf16[224,2048]{1,0:T(8,128)(2,1)S(1)}, bf16[224,2048]{1,0:T(8,128)(2,1)S(1)}, u32[]{:S(2)}, u32[]{:S(2)}) %collective-permute-start.10) | collective-permute-done | bytes 917536 | tf_op jit(solution)/shard_map/ppermute | solution.py:58
  47.4 1.9 %collective-permute-done.12.near_ref = bf16[256,512]{1,0:T(8,128)(2,1)S(1)} collective-permute-done((bf16[256,512]{1,0:T(8,128)(2,1)S(1)}, bf16[256,512]{1,0:T(8,128)(2,1)S(1)}, u32[]{:S(2)}, u32[]{:S(2)}) %collective-permute-start.12) | collective-permute-done | bytes 262176 | tf_op jit(solution)/shard_map/ppermute | solution.py:58
  50.1 3.4 %collective-permute-done.13.w0b = bf16[224,2048]{1,0:T(8,128)(2,1)S(1)} collective-permute-done((bf16[224,2048]{1,0:T(8,128)(2,1)S(1)}, bf16[224,2048]{1,0:T(8,128)(2,1)S(1)}, u32[]{:S(2)}, u32[]{:S(2)}) %collective-permute-start.13) | collective-permute-done | bytes 917536 | tf_op jit(solution)/shard_map/ppermute | solution.py:58
  53.5 1.4 %project.5 = (bf16[256,512]{1,0:T(8,128)(2,1)S(1)}, bf16[256,512]{1,0:T(8,128)(2,1)S(1)}) custom-call(s32[5]{0:T(128)S(1)} %stack.24.coords, bf16[256,512]{1,0:T(8,128)(2,1)S(1)} %get-tuple-element.47.own_ref, bf16[256,512]{1,0:T(8,128)(2,1)S(1)} %collective-permute-done.12.near_ref, bf16[512,8192]{1,0:T(8,128)(2,1)S(1)} %bitcast.6, ...), custom_call_target="tpu_custom_call" | custom-call | tf_op jit(solution)/shard_map/project/pallas_call | solution.py:261
  54.9 3.2 %collective-permute-start.15 = (bf16[256,512]{1,0:T(8,128)(2,1)S(1)}, bf16[256,512]{1,0:T(8,128)(2,1)S(1)}, u32[]{:S(2)}, u32[]{:S(2)}) collective-permute-start(bf16[256,512]{1,0:T(8,128)(2,1)S(1)} %get-tuple-element.55), channel_id=1, source_target_pairs={{0,1},{1,2},{2,3},{3,4},{4,5},{5,6},{6,7},{7,0},{16,17},{17,18},{1... | collective-permute-start | bytes 786440 | tf_op jit(solution)/shard_map/ppermute | solution.py:58
  58.1 1.4 %project.7 = (bf16[256,512]{1,0:T(8,128)(2,1)S(1)}, bf16[256,512]{1,0:T(8,128)(2,1)S(1)}) custom-call(s32[5]{0:T(128)S(1)} %stack.24.coords, bf16[256,512]{1,0:T(8,128)(2,1)S(1)} %attention.3.own_ref, bf16[256,512]{1,0:T(8,128)(2,1)S(1)} %collective-permute-done.22.near_ref, bf16[512,8192]{1,0:T(8,128)(2,1)S(1)} %bitcast.6, ...), custom_call_target="tpu_custom_call" | custom-call | tf_op jit(solution)/shard_map/project/pallas_call | solution.py:261
  59.6 3.3 %collective-permute-start.23 = (bf16[256,512]{1,0:T(8,128)(2,1)S(1)}, bf16[256,512]{1,0:T(8,128)(2,1)S(1)}, u32[]{:S(2)}, u32[]{:S(2)}) collective-permute-start(bf16[256,512]{1,0:T(8,128)(2,1)S(1)} %get-tuple-element.64), channel_id=1, source_target_pairs={{0,1},{1,2},{2,3},{3,4},{4,5},{5,6},{6,7},{7,0},{16,17},{17,18},{1... | collective-permute-start | bytes 786440 | tf_op jit(solution)/shard_map/ppermute | solution.py:58
  62.9 2.9 %project.4 = (bf16[256,512]{1,0:T(8,128)(2,1)S(1)}, bf16[256,512]{1,0:T(8,128)(2,1)S(1)}, bf16[256,512]{1,0:T(8,128)(2,1)S(1)}, bf16[256,512]{1,0:T(8,128)(2,1)S...) custom-call(s32[5]{0:T(128)S(1)} %stack.24.coords, bf16[256,512]{1,0:T(8,128)(2,1)S(1)} %get-tuple-element.47.own_ref, ...), custom_call_target="tpu_custom_call" | custom-call | tf_op jit(solution)/shard_map/project/pallas_call | solution.py:261
  65.8 2.9 %project.6 = (bf16[256,512]{1,0:T(8,128)(2,1)S(1)}, bf16[256,512]{1,0:T(8,128)(2,1)S(1)}, bf16[256,512]{1,0:T(8,128)(2,1)S(1)}, bf16[256,512]{1,0:T(8,128)(2,1)S...) custom-call(s32[5]{0:T(128)S(1)} %stack.24.coords, bf16[256,512]{1,0:T(8,128)(2,1)S(1)} %attention.3.own_ref, ...), custom_call_target="tpu_custom_call" | custom-call | tf_op jit(solution)/shard_map/project/pallas_call | solution.py:261
  68.7 3.3 %collective-permute-start.16 = (bf16[256,512]{1,0:T(8,128)(2,1)S(1)}, bf16[256,512]{1,0:T(8,128)(2,1)S(1)}, u32[]{:S(2)}, u32[]{:S(2)}) collective-permute-start(bf16[256,512]{1,0:T(8,128)(2,1)S(1)} %add_convert_fusion.11), channel_id=1, source_target_pairs={{0,1},{1,2},{2,3},{3,4},{4,5},{5,6},{6,7},{7,0},{16,17},{17,18},{1... | collective-permute-start | bytes 786440 | tf_op jit(solution)/shard_map/ppermute | solution.py:58
  72.3 3.3 %collective-permute-start.24 = (bf16[256,512]{1,0:T(8,128)(2,1)S(1)}, bf16[256,512]{1,0:T(8,128)(2,1)S(1)}, u32[]{:S(2)}, u32[]{:S(2)}) collective-permute-start(bf16[256,512]{1,0:T(8,128)(2,1)S(1)} %add_convert_fusion.5), channel_id=1, source_target_pairs={{0,1},{1,2},{2,3},{3,4},{4,5},{5,6},{6,7},{7,0},{16,17},{17,18},{1... | collective-permute-start | bytes 786440 | tf_op jit(solution)/shard_map/ppermute | solution.py:58
  75.8 3.1 %collective-permute-done.16 = bf16[256,512]{1,0:T(8,128)(2,1)S(1)} collective-permute-done((bf16[256,512]{1,0:T(8,128)(2,1)S(1)}, bf16[256,512]{1,0:T(8,128)(2,1)S(1)}, u32[]{:S(2)}, u32[]{:S(2)}) %collective-permute-start.16) | collective-permute-done | bytes 262176 | tf_op jit(solution)/shard_map/ppermute | solution.py:58
  78.9 4.0 %collective-permute-start.17 = (bf16[256,512]{1,0:T(8,128)(2,1)S(1)}, bf16[256,512]{1,0:T(8,128)(2,1)S(1)}, u32[]{:S(2)}, u32[]{:S(2)}) collective-permute-start(bf16[256,512]{1,0:T(8,128)(2,1)S(1)} %add_convert_fusion.10), channel_id=1, source_target_pairs={{0,1},{1,2},{2,3},{3,4},{4,5},{5,6},{6,7},{7,0},{16,17},{17,18},{1... | collective-permute-start | bytes 786440 | tf_op jit(solution)/shard_map/ppermute | solution.py:58
  83.0 5.2 %collective-permute-done.27 = bf16[256,512]{1,0:T(8,128)(2,1)S(1)} collective-permute-done((bf16[256,512]{1,0:T(8,128)(2,1)S(1)}, bf16[256,512]{1,0:T(8,128)(2,1)S(1)}, u32[]{:S(2)}, u32[]{:S(2)}) %collective-permute-start.27) | collective-permute-done | bytes 262176 | tf_op jit(solution)/shard_map/ppermute | solution.py:58
  88.5 3.3 %collective-permute-start.18 = (bf16[256,512]{1,0:T(8,128)(2,1)S(1)}, bf16[256,512]{1,0:T(8,128)(2,1)S(1)}, u32[]{:S(2)}, u32[]{:S(2)}) collective-permute-start(bf16[256,512]{1,0:T(8,128)(2,1)S(1)} %add_convert_fusion.9), channel_id=1, source_target_pairs={{0,1},{1,2},{2,3},{3,4},{4,5},{5,6},{6,7},{7,0},{16,17},{17,18},{1... | collective-permute-start | bytes 786440 | tf_op jit(solution)/shard_map/ppermute | solution.py:58
  92.0 5.2 %collective-permute-done.28 = bf16[256,512]{1,0:T(8,128)(2,1)S(1)} collective-permute-done((bf16[256,512]{1,0:T(8,128)(2,1)S(1)}, bf16[256,512]{1,0:T(8,128)(2,1)S(1)}, u32[]{:S(2)}, u32[]{:S(2)}) %collective-permute-start.28) | collective-permute-done | bytes 262176 | tf_op jit(solution)/shard_map/ppermute | solution.py:58
  97.4 1.1 %collective-permute-done.18 = bf16[256,512]{1,0:T(8,128)(2,1)S(1)} collective-permute-done((bf16[256,512]{1,0:T(8,128)(2,1)S(1)}, bf16[256,512]{1,0:T(8,128)(2,1)S(1)}, u32[]{:S(2)}, u32[]{:S(2)}) %collective-permute-start.18) | collective-permute-done | bytes 262176 | tf_op jit(solution)/shard_map/ppermute | solution.py:58
  98.5 2.7 %collective-permute-done.25 = bf16[256,512]{1,0:T(8,128)(2,1)S(1)} collective-permute-done((bf16[256,512]{1,0:T(8,128)(2,1)S(1)}, bf16[256,512]{1,0:T(8,128)(2,1)S(1)}, u32[]{:S(2)}, u32[]{:S(2)}) %collective-permute-start.25) | collective-permute-done | bytes 262176 | tf_op jit(solution)/shard_map/ppermute | solution.py:58
  101.2 3.7 %collective-permute-done.29 = bf16[256,512]{1,0:T(8,128)(2,1)S(1)} collective-permute-done((bf16[256,512]{1,0:T(8,128)(2,1)S(1)}, bf16[256,512]{1,0:T(8,128)(2,1)S(1)}, u32[]{:S(2)}, u32[]{:S(2)}) %collective-permute-start.29) | collective-permute-done | bytes 262176 | tf_op jit(solution)/shard_map/ppermute | solution.py:58
  (60 shorter events, 7.9 us)
Async XLA Ops:
  1.1 9.4 %collective-permute-start = (bf16[2,512,128]{2,1,0:T(8,128)(2,1)S(1)}, bf16[2,512,128]{2,1,0:T(8,128)(2,1)S(1)}, u32[]{:S(2)}, u32[]{:S(2)}) collective-permute-start(bf16[2,512,128]{2,1,0:T(8,128)(2,1)S(1)} %get-tuple-element.71), channel_id=1, source_target_pairs={{0,40},{1,41},{2,42},{3,43},{4,44},{5,45},{6,46},{7,47},{16,56},{1... | collective-permute-start | bytes 786440 | tf_op jit(solution)/shard_map/ppermute | solution.py:58
  4.2 8.0 %collective-permute-start.2 = (bf16[2,512,128]{2,1,0:T(8,128)(2,1)S(1)}, bf16[2,512,128]{2,1,0:T(8,128)(2,1)S(1)}, u32[]{:S(2)}, u32[]{:S(2)}) collective-permute-start(bf16[2,512,128]{2,1,0:T(8,128)(2,1)S(1)} %get-tuple-element.72.refs_0_), channel_id=1, source_target_pairs={{0,192},{1,193},{2,194},{3,195},{4,196},{5,197},{6,198},{7,199},{1... | collective-permute-start | bytes 786440 | tf_op jit(solution)/shard_map/ppermute | solution.py:58
  6.9 8.7 %collective-permute-start.1 = (bf16[2,512,128]{2,1,0:T(8,128)(2,1)S(1)}, bf16[2,512,128]{2,1,0:T(8,128)(2,1)S(1)}, u32[]{:S(2)}, u32[]{:S(2)}) collective-permute-start(bf16[2,512,128]{2,1,0:T(8,128)(2,1)S(1)} %get-tuple-element.72.refs_0_), channel_id=1, source_target_pairs={{0,64},{1,65},{2,66},{3,67},{4,68},{5,69},{6,70},{7,71},{16,80},{1... | collective-permute-start | bytes 786440 | tf_op jit(solution)/shard_map/ppermute | solution.py:58
  7.0 46.4 %slice-start = ((s8[8388608]{0:T(1024)(128)(4,1)}), s8[4194304]{0:T(1024)(128)(4,1)S(1)}, s32[]{:S(2)}) async-start(s8[8388608]{0:T(1024)(128)(4,1)} %bitcast.5), calls=%async_computation | async-start | bytes 8388608
  15.6 6.6 %collective-permute-start.4 = (bf16[2,512,128]{2,1,0:T(8,128)(2,1)S(1)}, bf16[2,512,128]{2,1,0:T(8,128)(2,1)S(1)}, u32[]{:S(2)}, u32[]{:S(2)}) collective-permute-start(bf16[2,512,128]{2,1,0:T(8,128)(2,1)S(1)} %collective-permute-done.refs_1_), channel_id=1, source_target_pairs={{0,192},{1,193},{2,194},{3,195},{4,196},{5,197},{6,198},{7,199},{1... | collective-permute-start | bytes 786440 | tf_op jit(solution)/shard_map/ppermute | solution.py:58
  16.0 13.5 %collective-permute-start.5 = (bf16[2,2,512,128]{3,2,1,0:T(8,128)(2,1)S(1)}, bf16[2,2,512,128]{3,2,1,0:T(8,128)(2,1)S(1)}, u32[]{:S(2)}, u32[]{:S(2)}) collective-permute-start(bf16[2,2,512,128]{3,2,1,0:T(8,128)(2,1)S(1)} %get-tuple-element.44), channel_id=1, source_target_pairs={{0,64},{1,65},{2,66},{3,67},{4,68},{5,69},{6,70},{7,71},{16,80},{1... | collective-permute-start | bytes 1572872 | tf_op jit(solution)/shard_map/ppermute | solution.py:58
  17.8 35.6 %slice-start.1 = ((s8[8388608]{0:T(1024)(128)(4,1)}), s8[4194304]{0:T(1024)(128)(4,1)S(1)}, s32[]{:S(2)}) async-start(s8[8388608]{0:T(1024)(128)(4,1)} %bitcast.5), calls=%async_computation.1 | async-start | bytes 8388608
  17.8 14.0 %collective-permute-start.3 = (bf16[4,2,512,128]{3,2,1,0:T(8,128)(2,1)S(1)}, bf16[4,2,512,128]{3,2,1,0:T(8,128)(2,1)S(1)}, u32[]{:S(2)}, u32[]{:S(2)}) collective-permute-start(bf16[4,2,512,128]{3,2,1,0:T(8,128)(2,1)S(1)} %get-tuple-element.43.refs_0_), channel_id=1, source_target_pairs={{0,16},{1,17},{2,18},{3,19},{4,20},{5,21},{6,22},{7,23},{16,0},{17... | collective-permute-start | bytes 3145736 | tf_op jit(solution)/shard_map/ppermute | solution.py:58
  17.8 29.6 %collective-permute-start.11 = (bf16[288,2048]{1,0:T(8,128)(2,1)S(1)}, bf16[288,2048]{1,0:T(8,128)(2,1)S(1)}, u32[]{:S(2)}, u32[]{:S(2)}) collective-permute-start(bf16[288,2048]{1,0:T(8,128)(2,1)S(1)} %get-tuple-element.49), channel_id=1, source_target_pairs={{0,40},{1,41},{2,42},{3,43},{4,44},{5,45},{6,46},{7,47},{16,56},{1... | collective-permute-start | bytes 3538952 | tf_op jit(solution)/shard_map/ppermute | solution.py:58
  22.2 6.4 %collective-permute-start.6 = (bf16[2,512,128]{2,1,0:T(8,128)(2,1)S(1)}, bf16[2,512,128]{2,1,0:T(8,128)(2,1)S(1)}, u32[]{:S(2)}, u32[]{:S(2)}) collective-permute-start(bf16[2,512,128]{2,1,0:T(8,128)(2,1)S(1)} %collective-permute-done.4.refs_3_), channel_id=1, source_target_pairs={{0,192},{1,193},{2,194},{3,195},{4,196},{5,197},{6,198},{7,199},{1... | collective-permute-start | bytes 786440 | tf_op jit(solution)/shard_map/ppermute | solution.py:58
  24.0 22.5 %collective-permute-start.10 = (bf16[224,2048]{1,0:T(8,128)(2,1)S(1)}, bf16[224,2048]{1,0:T(8,128)(2,1)S(1)}, u32[]{:S(2)}, u32[]{:S(2)}) collective-permute-start(bf16[224,2048]{1,0:T(8,128)(2,1)S(1)} %get-tuple-element.48), channel_id=1, source_target_pairs={{0,8},{1,9},{2,10},{3,11},{4,12},{5,13},{6,14},{7,15},{16,24},{17,... | collective-permute-start | bytes 2752520 | tf_op jit(solution)/shard_map/ppermute | solution.py:58
  28.6 1.5 %collective-permute-start.9 = (bf16[2,512,128]{2,1,0:T(8,128)(2,1)S(1)}, bf16[2,512,128]{2,1,0:T(8,128)(2,1)S(1)}, u32[]{:S(2)}, u32[]{:S(2)}) collective-permute-start(bf16[2,512,128]{2,1,0:T(8,128)(2,1)S(1)} %collective-permute-done.6.refs_4_), channel_id=1, source_target_pairs={{0,16},{1,17},{2,18},{3,19},{4,20},{5,21},{6,22},{7,23},{16,0},{17... | collective-permute-start | bytes 786440 | tf_op jit(solution)/shard_map/ppermute | solution.py:58
  29.5 2.3 %collective-permute-start.7 = (bf16[2,2,512,128]{3,2,1,0:T(8,128)(2,1)S(1)}, bf16[2,2,512,128]{3,2,1,0:T(8,128)(2,1)S(1)}, u32[]{:S(2)}, u32[]{:S(2)}) collective-permute-start(bf16[2,2,512,128]{3,2,1,0:T(8,128)(2,1)S(1)} %collective-permute-done.5.refs_2_), channel_id=1, source_target_pairs={{0,16},{1,17},{2,18},{3,19},{4,20},{5,21},{6,22},{7,23},{16,0},{17... | collective-permute-start | bytes 1572872 | tf_op jit(solution)/shard_map/ppermute | solution.py:58
  30.1 1.7 %collective-permute-start.8 = (bf16[2,512,128]{2,1,0:T(8,128)(2,1)S(1)}, bf16[2,512,128]{2,1,0:T(8,128)(2,1)S(1)}, u32[]{:S(2)}, u32[]{:S(2)}) collective-permute-start(bf16[2,512,128]{2,1,0:T(8,128)(2,1)S(1)} %collective-permute-done.4.refs_3_), channel_id=1, source_target_pairs={{0,16},{1,17},{2,18},{3,19},{4,20},{5,21},{6,22},{7,23},{16,0},{17... | collective-permute-start | bytes 786440 | tf_op jit(solution)/shard_map/ppermute | solution.py:58
  35.6 13.7 %collective-permute-start.12 = (bf16[256,512]{1,0:T(8,128)(2,1)S(1)}, bf16[256,512]{1,0:T(8,128)(2,1)S(1)}, u32[]{:S(2)}, u32[]{:S(2)}) collective-permute-start(bf16[256,512]{1,0:T(8,128)(2,1)S(1)} %get-tuple-element.47.own_ref), channel_id=1, source_target_pairs={{0,8},{1,9},{2,10},{3,11},{4,12},{5,13},{6,14},{7,15},{16,24},{17,... | collective-permute-start | bytes 786440 | tf_op jit(solution)/shard_map/ppermute | solution.py:58
  49.3 4.2 %collective-permute-start.14 = (bf16[288,2048]{1,0:T(8,128)(2,1)S(1)}, bf16[288,2048]{1,0:T(8,128)(2,1)S(1)}, u32[]{:S(2)}, u32[]{:S(2)}) collective-permute-start(bf16[288,2048]{1,0:T(8,128)(2,1)S(1)} %collective-permute-done.11.w1a), channel_id=1, source_target_pairs={{0,16},{1,17},{2,18},{3,19},{4,20},{5,21},{6,22},{7,23},{16,0},{17... | collective-permute-start | bytes 3538952 | tf_op jit(solution)/shard_map/ppermute | solution.py:58
  49.3 4.2 %collective-permute-start.13 = (bf16[224,2048]{1,0:T(8,128)(2,1)S(1)}, bf16[224,2048]{1,0:T(8,128)(2,1)S(1)}, u32[]{:S(2)}, u32[]{:S(2)}) collective-permute-start(bf16[224,2048]{1,0:T(8,128)(2,1)S(1)} %collective-permute-done.10.w0a), channel_id=1, source_target_pairs={{0,16},{1,17},{2,18},{3,19},{4,20},{5,21},{6,22},{7,23},{16,0},{17... | collective-permute-start | bytes 2752520 | tf_op jit(solution)/shard_map/ppermute | solution.py:58
  49.8 8.3 %collective-permute-start.22 = (bf16[256,512]{1,0:T(8,128)(2,1)S(1)}, bf16[256,512]{1,0:T(8,128)(2,1)S(1)}, u32[]{:S(2)}, u32[]{:S(2)}) collective-permute-start(bf16[256,512]{1,0:T(8,128)(2,1)S(1)} %attention.3.own_ref), channel_id=1, source_target_pairs={{0,8},{1,9},{2,10},{3,11},{4,12},{5,13},{6,14},{7,15},{16,24},{17,... | collective-permute-start | bytes 786440 | tf_op jit(solution)/shard_map/ppermute | solution.py:58
  54.9 13.7 %collective-permute-start.15 = (bf16[256,512]{1,0:T(8,128)(2,1)S(1)}, bf16[256,512]{1,0:T(8,128)(2,1)S(1)}, u32[]{:S(2)}, u32[]{:S(2)}) collective-permute-start(bf16[256,512]{1,0:T(8,128)(2,1)S(1)} %get-tuple-element.55), channel_id=1, source_target_pairs={{0,1},{1,2},{2,3},{3,4},{4,5},{5,6},{6,7},{7,0},{16,17},{17,18},{1... | collective-permute-start | bytes 786440 | tf_op jit(solution)/shard_map/ppermute | solution.py:58
  58.1 13.9 %collective-permute-start.19 = (bf16[256,512]{1,0:T(8,128)(2,1)S(1)}, bf16[256,512]{1,0:T(8,128)(2,1)S(1)}, u32[]{:S(2)}, u32[]{:S(2)}) collective-permute-start(bf16[256,512]{1,0:T(8,128)(2,1)S(1)} %get-tuple-element.59), channel_id=1, source_target_pairs={{0,7},{1,0},{2,1},{3,2},{4,3},{5,4},{6,5},{7,6},{16,23},{17,16},{1... | collective-permute-start | bytes 786440 | tf_op jit(solution)/shard_map/ppermute | solution.py:58
  59.6 12.6 %collective-permute-start.23 = (bf16[256,512]{1,0:T(8,128)(2,1)S(1)}, bf16[256,512]{1,0:T(8,128)(2,1)S(1)}, u32[]{:S(2)}, u32[]{:S(2)}) collective-permute-start(bf16[256,512]{1,0:T(8,128)(2,1)S(1)} %get-tuple-element.64), channel_id=1, source_target_pairs={{0,1},{1,2},{2,3},{3,4},{4,5},{5,6},{6,7},{7,0},{16,17},{17,18},{1... | collective-permute-start | bytes 786440 | tf_op jit(solution)/shard_map/ppermute | solution.py:58
  62.9 12.7 %collective-permute-start.26 = (bf16[256,512]{1,0:T(8,128)(2,1)S(1)}, bf16[256,512]{1,0:T(8,128)(2,1)S(1)}, u32[]{:S(2)}, u32[]{:S(2)}) collective-permute-start(bf16[256,512]{1,0:T(8,128)(2,1)S(1)} %get-tuple-element.67), channel_id=1, source_target_pairs={{0,7},{1,0},{2,1},{3,2},{4,3},{5,4},{6,5},{7,6},{16,23},{17,16},{1... | collective-permute-start | bytes 786440 | tf_op jit(solution)/shard_map/ppermute | solution.py:58
  68.7 10.1 %collective-permute-start.16 = (bf16[256,512]{1,0:T(8,128)(2,1)S(1)}, bf16[256,512]{1,0:T(8,128)(2,1)S(1)}, u32[]{:S(2)}, u32[]{:S(2)}) collective-permute-start(bf16[256,512]{1,0:T(8,128)(2,1)S(1)} %add_convert_fusion.11), channel_id=1, source_target_pairs={{0,1},{1,2},{2,3},{3,4},{4,5},{5,6},{6,7},{7,0},{16,17},{17,18},{1... | collective-permute-start | bytes 786440 | tf_op jit(solution)/shard_map/ppermute | solution.py:58
  72.1 10.8 %collective-permute-start.20 = (bf16[256,512]{1,0:T(8,128)(2,1)S(1)}, bf16[256,512]{1,0:T(8,128)(2,1)S(1)}, u32[]{:S(2)}, u32[]{:S(2)}) collective-permute-start(bf16[256,512]{1,0:T(8,128)(2,1)S(1)} %add_convert_fusion.8), channel_id=1, source_target_pairs={{0,7},{1,0},{2,1},{3,2},{4,3},{5,4},{6,5},{7,6},{16,23},{17,16},{1... | collective-permute-start | bytes 786440 | tf_op jit(solution)/shard_map/ppermute | solution.py:58
  72.3 19.5 %collective-permute-start.24 = (bf16[256,512]{1,0:T(8,128)(2,1)S(1)}, bf16[256,512]{1,0:T(8,128)(2,1)S(1)}, u32[]{:S(2)}, u32[]{:S(2)}) collective-permute-start(bf16[256,512]{1,0:T(8,128)(2,1)S(1)} %add_convert_fusion.5), channel_id=1, source_target_pairs={{0,1},{1,2},{2,3},{3,4},{4,5},{5,6},{6,7},{7,0},{16,17},{17,18},{1... | collective-permute-start | bytes 786440 | tf_op jit(solution)/shard_map/ppermute | solution.py:58
  75.7 12.6 %collective-permute-start.27 = (bf16[256,512]{1,0:T(8,128)(2,1)S(1)}, bf16[256,512]{1,0:T(8,128)(2,1)S(1)}, u32[]{:S(2)}, u32[]{:S(2)}) collective-permute-start(bf16[256,512]{1,0:T(8,128)(2,1)S(1)} %add_convert_fusion.3), channel_id=1, source_target_pairs={{0,7},{1,0},{2,1},{3,2},{4,3},{5,4},{6,5},{7,6},{16,23},{17,16},{1... | collective-permute-start | bytes 786440 | tf_op jit(solution)/shard_map/ppermute | solution.py:58
  78.9 9.6 %collective-permute-start.17 = (bf16[256,512]{1,0:T(8,128)(2,1)S(1)}, bf16[256,512]{1,0:T(8,128)(2,1)S(1)}, u32[]{:S(2)}, u32[]{:S(2)}) collective-permute-start(bf16[256,512]{1,0:T(8,128)(2,1)S(1)} %add_convert_fusion.10), channel_id=1, source_target_pairs={{0,1},{1,2},{2,3},{3,4},{4,5},{5,6},{6,7},{7,0},{16,17},{17,18},{1... | collective-permute-start | bytes 786440 | tf_op jit(solution)/shard_map/ppermute | solution.py:58
  83.0 14.4 %collective-permute-start.21 = (bf16[256,512]{1,0:T(8,128)(2,1)S(1)}, bf16[256,512]{1,0:T(8,128)(2,1)S(1)}, u32[]{:S(2)}, u32[]{:S(2)}) collective-permute-start(bf16[256,512]{1,0:T(8,128)(2,1)S(1)} %add_convert_fusion.7), channel_id=1, source_target_pairs={{0,7},{1,0},{2,1},{3,2},{4,3},{5,4},{6,5},{7,6},{16,23},{17,16},{1... | collective-permute-start | bytes 786440 | tf_op jit(solution)/shard_map/ppermute | solution.py:58
  88.3 8.8 %collective-permute-start.28 = (bf16[256,512]{1,0:T(8,128)(2,1)S(1)}, bf16[256,512]{1,0:T(8,128)(2,1)S(1)}, u32[]{:S(2)}, u32[]{:S(2)}) collective-permute-start(bf16[256,512]{1,0:T(8,128)(2,1)S(1)} %add_convert_fusion.2), channel_id=1, source_target_pairs={{0,7},{1,0},{2,1},{3,2},{4,3},{5,4},{6,5},{7,6},{16,23},{17,16},{1... | collective-permute-start | bytes 786440 | tf_op jit(solution)/shard_map/ppermute | solution.py:58
  88.5 9.9 %collective-permute-start.18 = (bf16[256,512]{1,0:T(8,128)(2,1)S(1)}, bf16[256,512]{1,0:T(8,128)(2,1)S(1)}, u32[]{:S(2)}, u32[]{:S(2)}) collective-permute-start(bf16[256,512]{1,0:T(8,128)(2,1)S(1)} %add_convert_fusion.9), channel_id=1, source_target_pairs={{0,1},{1,2},{2,3},{3,4},{4,5},{5,6},{6,7},{7,0},{16,17},{17,18},{1... | collective-permute-start | bytes 786440 | tf_op jit(solution)/shard_map/ppermute | solution.py:58
  91.9 9.3 %collective-permute-start.25 = (bf16[256,512]{1,0:T(8,128)(2,1)S(1)}, bf16[256,512]{1,0:T(8,128)(2,1)S(1)}, u32[]{:S(2)}, u32[]{:S(2)}) collective-permute-start(bf16[256,512]{1,0:T(8,128)(2,1)S(1)} %add_convert_fusion.4), channel_id=1, source_target_pairs={{0,1},{1,2},{2,3},{3,4},{4,5},{5,6},{6,7},{7,0},{16,17},{17,18},{1... | collective-permute-start | bytes 786440 | tf_op jit(solution)/shard_map/ppermute | solution.py:58
  97.3 7.7 %collective-permute-start.29 = (bf16[256,512]{1,0:T(8,128)(2,1)S(1)}, bf16[256,512]{1,0:T(8,128)(2,1)S(1)}, u32[]{:S(2)}, u32[]{:S(2)}) collective-permute-start(bf16[256,512]{1,0:T(8,128)(2,1)S(1)} %add_convert_fusion.1), channel_id=1, source_target_pairs={{0,7},{1,0},{2,1},{3,2},{4,3},{5,4},{6,5},{7,6},{16,23},{17,16},{1... | collective-permute-start | bytes 786440 | tf_op jit(solution)/shard_map/ppermute | solution.py:58
  (2 other events, 49.6 us)

commit v8 on v7

--- a/solution.py
+++ b/solution.py
@@ -48,6 +48,13 @@
     "x-": pairs(lambda x, y, c, z: (x - 1, y, c, z)),
     "z+": pairs(lambda x, y, c, z: (x, y, c, z + 1)),
     "z-": pairs(lambda x, y, c, z: (x, y, c, z - 1)),
+    **{
+        f"swing{sign}{parity}": pairs(
+            lambda x, y, c, z: (x, y, c, z + (sign if (z + c) % 2 == parity else -sign))
+        )
+        for sign in (1, -1)
+        for parity in (0, 1)
+    },
     "core": pairs(lambda x, y, c, z: (x, y, c + 1, z)),
     "y_near": pairs(lambda x, y, c, z: (x, y ^ 1, c, z)),
     "y_far": pairs(lambda x, y, c, z: (x, 3 - y, c, z)),
@@ -63,15 +70,22 @@
 HBM = pl.BlockSpec(memory_space=pltpu.HBM)
 
 
+REACH = ((4, -2, 2, 0), (-3, 3, -1, 1))
+
+
 def pick_kernel(coords, w_ref, near_w_ref, far_w_ref, sems):
     c, yl = coords[2], coords[3]
-    columns = near_w_ref.shape[1]
-    near_rows, far_rows = near_w_ref.shape[0], far_w_ref.shape[0]
-    there = pl.ds(pl.multiple_of(((1 - yl) * 2 + c) * columns, columns), columns)
-    copies = [
-        pltpu.make_async_copy(w_ref.at[pl.ds(0, near_rows), there], near_w_ref, sems.at[0]),
-        pltpu.make_async_copy(w_ref.at[pl.ds(near_rows, far_rows), there], far_w_ref, sems.at[1]),
-    ]
+    copies = []
+    for j in range(NZ // 2):
+        there = pl.ds(pl.multiple_of(((1 - yl) * NZ + 2 * j + c) * 512, 512), 512)
+        here = pl.ds(j * 512, 512)
+        row = 0
+        for i, out in enumerate((near_w_ref, far_w_ref)):
+            rows = pl.ds(row, out.shape[0])
+            copies.append(
+                pltpu.make_async_copy(w_ref.at[rows, there], out.at[:, here], sems.at[2 * j + i])
+            )
+            row += out.shape[0]
     for copy in copies:
         copy.start()
     for copy in copies:
@@ -86,7 +100,7 @@
         out_shape=parts,
         in_specs=[SMEM, HBM],
         out_specs=[VMEM] * 2,
-        scratch_shapes=[pltpu.SemaphoreType.DMA((2,))],
+        scratch_shapes=[pltpu.SemaphoreType.DMA((NZ,))],
         compiler_params=pltpu.CompilerParams(vmem_limit_bytes=VMEM_LIMIT),
         cost_estimate=FREE,
         name="pick",
@@ -229,39 +243,38 @@
     )(*pieces)
 
 
-def project_kernel(steps, coords, own_ref, near_ref, w_ref, w0a, w0b, w1a, w1b, *out_refs):
-    core, yl, z = coords[2], coords[3], coords[4]
+def project_kernel(steps, sign, coords, own_ref, near_ref, w_ref, *refs):
+    out_refs = refs[-len(steps) :]
+    parts = refs[: -len(steps)]
+    c, yl, z = coords[2], coords[3], coords[4]
+    odd = (z + c) % 2
 
     def lanes(block):
         return pl.ds(pl.multiple_of(block * 512, 512), 512)
 
-    for step, out_ref in zip(steps, out_refs):
-        target = (z + step + NZ) % NZ
-        mine = target // 4 == core
-        part = lanes(target % 4)
+    for (other, step), out_ref in zip(steps, out_refs):
+        w0_ref, w1_ref = parts[2 * other : 2 * other + 2] if len(parts) > 2 else parts
+        reach = jnp.where(odd == other, REACH[0][step], REACH[1][step])
+        target = (z + sign * reach + NZ) % NZ
+        part = lanes(target // 2)
         value = jnp.dot(
             own_ref[...], w_ref[:, lanes(yl * NZ + target)], preferred_element_type=jnp.float32
         )
         value += jnp.dot(
-            near_ref[:, :NEAR_ROWS],
-            jnp.where(mine, w0a[:, part], w0b[:, part]),
-            preferred_element_type=jnp.float32,
+            near_ref[:, :NEAR_ROWS], w0_ref[:, part], preferred_element_type=jnp.float32
         )
         value += jnp.dot(
-            near_ref[:, NEAR_ROWS:],
-            jnp.where(mine, w1a[:, part], w1b[:, part]),
-            preferred_element_type=jnp.float32,
+            near_ref[:, NEAR_ROWS:], w1_ref[:, part], preferred_element_type=jnp.float32
         )
         out_ref[...] = value.astype(jnp.bfloat16)
 
 
-def project(coords, steps, own, near, weights, parts):
-    rows = own.shape[0]
+def project(coords, steps, sign, own, near, weights, parts):
     count = len(steps)
     return pl.pallas_call(
-        functools.partial(project_kernel, steps),
-        out_shape=[jax.ShapeDtypeStruct((rows, 512), jnp.bfloat16)] * count,
-        in_specs=[SMEM] + [VMEM] * 7,
+        functools.partial(project_kernel, steps, sign),
+        out_shape=[jax.ShapeDtypeStruct((own.shape[0], 512), jnp.bfloat16)] * count,
+        in_specs=[SMEM] + [VMEM] * (3 + len(parts)),
         out_specs=[VMEM] * count,
         compiler_params=pltpu.CompilerParams(vmem_limit_bytes=PROJECT_VMEM),
         cost_estimate=FREE,
@@ -305,29 +318,35 @@
     near_part, far_part, near[0], near[1] = barrier((near_part, far_part, near[0], attended[1]))
     near[1] = send(near[1], "y_near")
     near_other, far_other = send(near_part, "core"), send(far_part, "core")
-    parts = [near_part, near_other, far_part, far_other]
+    same, others = (near_part, far_part), (near_other, far_other)
 
     def add(*terms):
         return sum(t.astype(jnp.float32) for t in terms).astype(jnp.bfloat16)
 
-    moves = ("z+", "z-")
-    ways, moving = [], []
+    signs = (1, -1)
+    even = (ctx + z) % 2 == 0
+    partial, moving = [], []
     for k in range(CHUNKS):
-        orders = ((4, 3, 2, 1), (-3, -2, -1)) if k % 2 == 0 else ((3, 2, 1), (-4, -3, -2, -1))
-        early = tuple(order[0] for order in orders)
-        late = (*orders[0][1:], *orders[1][1:], 0)
-        begun = project(coords, early, attended[k], near[k], out_weight, parts)
-        moving.append([send(value, move) for value, move in zip(begun, moves)])
-        partial = dict(zip(late, project(coords, late, attended[k], near[k], out_weight, parts)))
-        ways.append((orders, partial))
-
-    for step in range(1, 4):
+        of_chunk = (signs[k], attended[k], near[k], out_weight)
+        if k:
+            begun = project(coords, ((0, 0), (1, 0)), *of_chunk, (*same, *others))
+        else:
+            begun = list(project(coords, ((0, 0),), *of_chunk, same))
+            begun += project(coords, ((1, 0),), *of_chunk, others)
+            near[1], begun[1] = barrier((near[1], begun[1]))
+        moving.append([send(begun[i], f"swing{signs[k]}{i}") for i in range(2)])
+        steps = tuple((i, step) for step in (1, 2, 3) for i in range(2))
+        partial.append(dict(zip(steps, project(coords, steps, *of_chunk, (*same, *others)))))
+    for step in (1, 2):
         for k in range(CHUNKS):
-            orders, partial = ways[k]
-            for way, order in enumerate(orders):
-                if step < len(order):
-                    moving[k][way] = send(add(moving[k][way], partial[order[step]]), moves[way])
-    results = [add(ways[k][1][0], *moving[k]) for k in range(CHUNKS)]
+            for i in range(2):
+                value = add(moving[k][i], partial[k][i, step])
+                moving[k][i] = send(value, f"swing{signs[k]}{(step + i) % 2}")
+    results = []
+    for k in range(CHUNKS):
+        last = [add(moving[k][i], partial[k][i, 3]) for i in range(2)]
+        held, going = jnp.where(even, last[0], last[1]), jnp.where(even, last[1], last[0])
+        results.append(add(held, send(going, "z+" if signs[k] > 0 else "z-")))
     return jnp.concatenate(results, 0)
 
 

time: 106 us -> 119 us (1.12)
  the two profiles are of different devices: /device:TPU:96 before, /device:TPU:6 now
where the time goes in v8:
time: 119 us; the launch traced here: 118 us
  waiting for transfers between devices  44.3 us (37%)
  starting transfers between devices  32.1 us (27%)
  Pallas kernels  24.6 us (21%)
  local copies, waits for them, and re-layouts  12.5 us (11%)
  other arithmetic  3.87 us (3%)
    ppermute x30, waiting for transfers between devices, send(): return lax.ppermute(array, AXES, MOVES[move])  44.3 us
    ppermute x30, starting transfers between devices, send(): return lax.ppermute(array, AXES, MOVES[move])  32.1 us
    pallas_call x2, Pallas kernels, attention(): pl.pallas_call(functools.partial(attention_kernel, first_row, n_rows, slo...  11.8 us
    unnamed x34, local copies, waits for them, and re-layouts  11.3 us
    pallas_call x5, Pallas kernels, project(): pl.pallas_call(functools.partial(project_kernel, steps, sign), out_shape=...  10.2 us
    convert_element_type x10, other arithmetic, add(): return sum((t.astype(jnp.float32) for t in terms)).astype(jnp.bfloat16)  2.77 us
    pallas_call x1, Pallas kernels, pick(): pl.pallas_call(pick_kernel, out_shape=parts, in_specs=[SMEM, HBM], out_sp...  2.47 us
  transfers between devices with their start and end apart: 30, of which 17 were waited for; matrix products, arithmetic and copies ran while one was open for 3% of the time, Pallas kernels for 21%

profile of v8, /device:TPU:6, one launch (start us, length us, event | category | flops | bytes accessed | tf_op | source)
XLA Modules:
  0.0 117.6 jit_solution(14977403473281116790)
XLA Ops:
  1.1 3.1 %collective-permute-start = (bf16[2,512,128]{2,1,0:T(8,128)(2,1)S(1)}, bf16[2,512,128]{2,1,0:T(8,128)(2,1)S(1)}, u32[]{:S(2)}, u32[]{:S(2)}) collective-permute-start(bf16[2,512,128]{2,1,0:T(8,128)(2,1)S(1)} %get-tuple-element.71), channel_id=1, source_target_pairs={{0,40},{1,41},{2,42},{3,43},{4,44},{5,45},{6,46},{7,47},{16,56},{1... | collective-permute-start | bytes 786440 | tf_op jit(solution)/shard_map/ppermute | solution.py:65
  5.0 2.4 %collective-permute-start.1 = (bf16[2,512,128]{2,1,0:T(8,128)(2,1)S(1)}, bf16[2,512,128]{2,1,0:T(8,128)(2,1)S(1)}, u32[]{:S(2)}, u32[]{:S(2)}) collective-permute-start(bf16[2,512,128]{2,1,0:T(8,128)(2,1)S(1)} %get-tuple-element.72.refs_0_), channel_id=1, source_target_pairs={{0,64},{1,65},{2,66},{3,67},{4,68},{5,69},{6,70},{7,71},{16,80},{1... | collective-permute-start | bytes 786440 | tf_op jit(solution)/shard_map/ppermute | solution.py:65
  7.5 2.5 %pick.1 = (bf16[224,2048]{1,0:T(8,128)(2,1)S(1)}, bf16[288,2048]{1,0:T(8,128)(2,1)S(1)}) custom-call(s32[5]{0:T(128)S(1)} %stack.24.coords, bf16[512,8192]{1,0:T(8,128)(2,1)} %w_ref.11), custom_call_target="tpu_custom_call" | custom-call | tf_op jit(solution)/shard_map/pick/pallas_call | solution.py:98
  10.5 2.7 %collective-permute-done.2.refs_3_ = bf16[2,512,128]{2,1,0:T(8,128)(2,1)S(1)} collective-permute-done((bf16[2,512,128]{2,1,0:T(8,128)(2,1)S(1)}, bf16[2,512,128]{2,1,0:T(8,128)(2,1)S(1)}, u32[]{:S(2)}, u32[]{:S(2)}) %collective-permute-start.2) | collective-permute-done | bytes 262176 | tf_op jit(solution)/shard_map/ppermute | solution.py:65
  13.3 3.3 %collective-permute-start.5 = (bf16[2,2,512,128]{3,2,1,0:T(8,128)(2,1)S(1)}, bf16[2,2,512,128]{3,2,1,0:T(8,128)(2,1)S(1)}, u32[]{:S(2)}, u32[]{:S(2)}) collective-permute-start(bf16[2,2,512,128]{3,2,1,0:T(8,128)(2,1)S(1)} %get-tuple-element.44), channel_id=1, source_target_pairs={{0,64},{1,65},{2,66},{3,67},{4,68},{5,69},{6,70},{7,71},{16,80},{1... | collective-permute-start | bytes 1572872 | tf_op jit(solution)/shard_map/ppermute | solution.py:65
  17.0 4.3 %collective-permute-done.4.refs_3_ = bf16[2,512,128]{2,1,0:T(8,128)(2,1)S(1)} collective-permute-done((bf16[2,512,128]{2,1,0:T(8,128)(2,1)S(1)}, bf16[2,512,128]{2,1,0:T(8,128)(2,1)S(1)}, u32[]{:S(2)}, u32[]{:S(2)}) %collective-permute-start.4) | collective-permute-done | bytes 262176 | tf_op jit(solution)/shard_map/ppermute | solution.py:65
  21.4 7.4 %collective-permute-done.6.refs_4_ = bf16[2,512,128]{2,1,0:T(8,128)(2,1)S(1)} collective-permute-done((bf16[2,512,128]{2,1,0:T(8,128)(2,1)S(1)}, bf16[2,512,128]{2,1,0:T(8,128)(2,1)S(1)}, u32[]{:S(2)}, u32[]{:S(2)}) %collective-permute-start.6) | collective-permute-done | bytes 262176 | tf_op jit(solution)/shard_map/ppermute | solution.py:65
  30.5 1.4 %collective-permute-done.8.refs_6_ = bf16[2,512,128]{2,1,0:T(8,128)(2,1)S(1)} collective-permute-done((bf16[2,512,128]{2,1,0:T(8,128)(2,1)S(1)}, bf16[2,512,128]{2,1,0:T(8,128)(2,1)S(1)}, u32[]{:S(2)}, u32[]{:S(2)}) %collective-permute-start.8) | collective-permute-done | bytes 262176 | tf_op jit(solution)/shard_map/ppermute | solution.py:65
  31.9 4.4 %attention.2 = (bf16[256,512]{1,0:T(8,128)(2,1)S(1)}, bf16[2,8192,128]{2,1,0:T(8,128)(2,1)S(1)}) custom-call(s32[5]{0:T(128)S(1)} %stack.24.coords, s32[4,16]{1,0:T(4,128)S(1)} %copy-done.13, bf16[512,512]{1,0:T(8,128)(2,1)S(1)} %copy-done.9, bf16[4,2,512,128]{3,2,1,0:T(8,128)(2,1)S(1)} %get-tuple-element.43.refs_0_, ...), custom_call_target="tpu_custom_call" | custom-call | tf_op jit(solution)/shard_map/attention/pallas_call | solution.py:202
  36.6 7.4 %attention.3.own_ref = bf16[256,512]{1,0:T(8,128)(2,1)S(1)} custom-call(s32[5]{0:T(128)S(1)} %stack.24.coords, s32[4,16]{1,0:T(4,128)S(1)} %copy-done.13, bf16[512,512]{1,0:T(8,128)(2,1)S(1)} %copy-done.9, bf16[2,8192,128]{2,1,0:T(8,128)(2,1)S(1)} %get-tuple-element.50.refs_0_), custom_call_target="tpu_custom_call" | custom-call | tf_op jit(solution)/shard_map/attention/pallas_call | solution.py:202
  44.0 2.2 %collective-permute-done.11.refs_1_ = bf16[288,2048]{1,0:T(8,128)(2,1)S(1)} collective-permute-done((bf16[288,2048]{1,0:T(8,128)(2,1)S(1)}, bf16[288,2048]{1,0:T(8,128)(2,1)S(1)}, u32[]{:S(2)}, u32[]{:S(2)}) %collective-permute-start.11) | collective-permute-done | bytes 1179680 | tf_op jit(solution)/shard_map/ppermute | solution.py:65
  47.6 1.8 %project.5 = bf16[256,512]{1,0:T(8,128)(2,1)} custom-call(s32[5]{0:T(128)S(1)} %stack.24.coords, bf16[256,512]{1,0:T(8,128)(2,1)S(1)} %get-tuple-element.47.own_ref, bf16[256,512]{1,0:T(8,128)(2,1)S(1)} %collective-permute-done.12.near_ref, bf16[512,8192]{1,0:T(8,128)(2,1)S(1)} %bitcast.6, bf16[224,2048]{1,0:T(8,128)(2,1)S(1)} %collective-permute-done.10.refs_0_, ...), custom_call_target="tpu_custom_call" | custom-call | tf_op jit(solution)/shard_map/project/pallas_call | solution.py:274
  49.4 1.9 %collective-permute-start.13 = (bf16[256,512]{1,0:T(8,128)(2,1)}, bf16[256,512]{1,0:T(8,128)(2,1)}, u32[]{:S(2)}, u32[]{:S(2)}) collective-permute-start(bf16[256,512]{1,0:T(8,128)(2,1)} %project.5), channel_id=1, source_target_pairs={{0,1},{1,0},{2,3},{3,2},{4,5},{5,4},{6,7},{7,6},{16,23},{17,18},{1... | collective-permute-start | bytes 786440 | tf_op jit(solution)/shard_map/ppermute | solution.py:65
  53.1 2.4 %collective-permute-done.18.near_ref = bf16[256,512]{1,0:T(8,128)(2,1)S(1)} collective-permute-done((bf16[256,512]{1,0:T(8,128)(2,1)S(1)}, bf16[256,512]{1,0:T(8,128)(2,1)S(1)}, u32[]{:S(2)}, u32[]{:S(2)}) %collective-permute-start.18) | collective-permute-done | bytes 262176 | tf_op jit(solution)/shard_map/ppermute | solution.py:65
  55.6 1.8 %project.8 = (bf16[256,512]{1,0:T(8,128)(2,1)}, bf16[256,512]{1,0:T(8,128)(2,1)S(1)}) custom-call(s32[5]{0:T(128)S(1)} %stack.24.coords, bf16[256,512]{1,0:T(8,128)(2,1)S(1)} %attention.3.own_ref, bf16[256,512]{1,0:T(8,128)(2,1)S(1)} %collective-permute-done.18.near_ref, bf16[512,8192]{1,0:T(8,128)(2,1)S(1)} %bitcast.6, ...), custom_call_target="tpu_custom_call" | custom-call | tf_op jit(solution)/shard_map/project/pallas_call | solution.py:274
  58.1 5.9 %collective-permute-start.23 = (bf16[256,512]{1,0:T(8,128)(2,1)}, bf16[256,512]{1,0:T(8,128)(2,1)}, u32[]{:S(2)}, u32[]{:S(2)}) collective-permute-start(bf16[256,512]{1,0:T(8,128)(2,1)} %get-tuple-element.63), channel_id=1, source_target_pairs={{0,7},{1,2},{2,1},{3,4},{4,3},{5,6},{6,5},{7,0},{16,17},{17,16},{1... | collective-permute-start | bytes 786440 | tf_op jit(solution)/shard_map/ppermute | solution.py:65
  64.0 3.4 %copy-done = bf16[512,8192]{1,0:T(8,128)(2,1)S(1)} copy-done((bf16[512,8192]{1,0:T(8,128)(2,1)S(1)}, bf16[512,8192]{1,0:T(8,128)(2,1)}, u32[]{:S(2)}) %copy-start) | copy-done | bytes 8388632
  67.4 1.2 %copy-done.3 = bf16[224,2048]{1,0:T(8,128)(2,1)S(1)} copy-done((bf16[224,2048]{1,0:T(8,128)(2,1)S(1)}, bf16[224,2048]{1,0:T(8,128)(2,1)}, u32[]{:S(2)}) %copy-start.3) | copy-done | bytes 917528
  70.5 2.8 %project.6 = (bf16[256,512]{1,0:T(8,128)(2,1)S(1)}, bf16[256,512]{1,0:T(8,128)(2,1)S(1)}, bf16[256,512]{1,0:T(8,128)(2,1)S(1)}, bf16[256,512]{1,0:T(8,128)(2,1)S...) custom-call(s32[5]{0:T(128)S(1)} %stack.24.coords, bf16[256,512]{1,0:T(8,128)(2,1)S(1)} %copy-done.6, ...), custom_call_target="tpu_custom_call" | custom-call | tf_op jit(solution)/shard_map/project/pallas_call | solution.py:274
  74.3 3.3 %collective-permute-start.16 = (bf16[256,512]{1,0:T(8,128)(2,1)S(1)}, bf16[256,512]{1,0:T(8,128)(2,1)S(1)}, u32[]{:S(2)}, u32[]{:S(2)}) collective-permute-start(bf16[256,512]{1,0:T(8,128)(2,1)S(1)} %add_convert_fusion.13), channel_id=1, source_target_pairs={{0,7},{1,2},{2,1},{3,4},{4,3},{5,6},{6,5},{7,0},{16,17},{17,16},{1... | collective-permute-start | bytes 786440 | tf_op jit(solution)/shard_map/ppermute | solution.py:65
  77.6 3.4 %copy-done.1 = bf16[512,8192]{1,0:T(8,128)(2,1)S(1)} copy-done((bf16[512,8192]{1,0:T(8,128)(2,1)S(1)}, bf16[512,8192]{1,0:T(8,128)(2,1)}, u32[]{:S(2)}) %copy-start.1) | copy-done | bytes 8388632
  80.9 2.8 %project.9 = (bf16[256,512]{1,0:T(8,128)(2,1)S(1)}, bf16[256,512]{1,0:T(8,128)(2,1)S(1)}, bf16[256,512]{1,0:T(8,128)(2,1)S(1)}, bf16[256,512]{1,0:T(8,128)(2,1)S...) custom-call(s32[5]{0:T(128)S(1)} %stack.24.coords, bf16[256,512]{1,0:T(8,128)(2,1)S(1)} %attention.3.own_ref, ...), custom_call_target="tpu_custom_call" | custom-call | tf_op jit(solution)/shard_map/project/pallas_call | solution.py:274
  85.0 3.1 %collective-permute-start.27 = (bf16[256,512]{1,0:T(8,128)(2,1)S(1)}, bf16[256,512]{1,0:T(8,128)(2,1)S(1)}, u32[]{:S(2)}, u32[]{:S(2)}) collective-permute-start(bf16[256,512]{1,0:T(8,128)(2,1)S(1)} %add_convert_fusion.3), channel_id=1, source_target_pairs={{0,7},{1,2},{2,1},{3,4},{4,3},{5,6},{6,5},{7,0},{16,17},{17,16},{1... | collective-permute-start | bytes 786440 | tf_op jit(solution)/shard_map/ppermute | solution.py:65
  88.3 4.2 %collective-permute-done.24 = bf16[256,512]{1,0:T(8,128)(2,1)S(1)} collective-permute-done((bf16[256,512]{1,0:T(8,128)(2,1)S(1)}, bf16[256,512]{1,0:T(8,128)(2,1)S(1)}, u32[]{:S(2)}, u32[]{:S(2)}) %collective-permute-start.24) | collective-permute-done | bytes 262176 | tf_op jit(solution)/shard_map/ppermute | solution.py:65
  92.5 1.5 %collective-permute-start.25 = (bf16[256,512]{1,0:T(8,128)(2,1)S(1)}, bf16[256,512]{1,0:T(8,128)(2,1)S(1)}, u32[]{:S(2)}, u32[]{:S(2)}) collective-permute-start(bf16[256,512]{1,0:T(8,128)(2,1)S(1)} %add_convert_fusion.5), channel_id=1, source_target_pairs={{0,7},{1,2},{2,1},{3,4},{4,3},{5,6},{6,5},{7,0},{16,17},{17,16},{1... | collective-permute-start | bytes 786440 | tf_op jit(solution)/shard_map/ppermute | solution.py:65
  95.4 1.9 %collective-permute-start.17 = (bf16[256,512]{1,0:T(8,128)(2,1)S(1)}, bf16[256,512]{1,0:T(8,128)(2,1)S(1)}, u32[]{:S(2)}, u32[]{:S(2)}) collective-permute-start(bf16[256,512]{1,0:T(8,128)(2,1)S(1)} %add_convert_fusion.12), channel_id=1, source_target_pairs={{0,1},{1,0},{2,3},{3,2},{4,5},{5,4},{6,7},{7,6},{16,23},{17,18},{1... | collective-permute-start | bytes 786440 | tf_op jit(solution)/shard_map/ppermute | solution.py:65
  98.2 1.5 %collective-permute-start.21 = (bf16[256,512]{1,0:T(8,128)(2,1)S(1)}, bf16[256,512]{1,0:T(8,128)(2,1)S(1)}, u32[]{:S(2)}, u32[]{:S(2)}) collective-permute-start(bf16[256,512]{1,0:T(8,128)(2,1)S(1)} %add_convert_fusion.9), channel_id=1, source_target_pairs={{0,7},{1,2},{2,1},{3,4},{4,3},{5,6},{6,5},{7,0},{16,17},{17,16},{1... | collective-permute-start | bytes 786440 | tf_op jit(solution)/shard_map/ppermute | solution.py:65
  99.6 3.2 %collective-permute-done.25 = bf16[256,512]{1,0:T(8,128)(2,1)S(1)} collective-permute-done((bf16[256,512]{1,0:T(8,128)(2,1)S(1)}, bf16[256,512]{1,0:T(8,128)(2,1)S(1)}, u32[]{:S(2)}, u32[]{:S(2)}) %collective-permute-start.25) | collective-permute-done | bytes 262176 | tf_op jit(solution)/shard_map/ppermute | solution.py:65
  102.8 1.5 %collective-permute-done.28 = bf16[256,512]{1,0:T(8,128)(2,1)S(1)} collective-permute-done((bf16[256,512]{1,0:T(8,128)(2,1)S(1)}, bf16[256,512]{1,0:T(8,128)(2,1)S(1)}, u32[]{:S(2)}, u32[]{:S(2)}) %collective-permute-start.28) | collective-permute-done | bytes 262176 | tf_op jit(solution)/shard_map/ppermute | solution.py:65
  104.9 3.9 %collective-permute-done.17 = bf16[256,512]{1,0:T(8,128)(2,1)S(1)} collective-permute-done((bf16[256,512]{1,0:T(8,128)(2,1)S(1)}, bf16[256,512]{1,0:T(8,128)(2,1)S(1)}, u32[]{:S(2)}, u32[]{:S(2)}) %collective-permute-start.17) | collective-permute-done | bytes 262176 | tf_op jit(solution)/shard_map/ppermute | solution.py:65
  109.0 2.6 %collective-permute-done.29 = bf16[256,512]{1,0:T(8,128)(2,1)S(1)} collective-permute-done((bf16[256,512]{1,0:T(8,128)(2,1)S(1)}, bf16[256,512]{1,0:T(8,128)(2,1)S(1)}, u32[]{:S(2)}, u32[]{:S(2)}) %collective-permute-start.29) | collective-permute-done | bytes 262176 | tf_op jit(solution)/shard_map/ppermute | solution.py:65
  111.8 4.8 %collective-permute-done.22 = bf16[256,512]{1,0:T(8,128)(2,1)S(1)} collective-permute-done((bf16[256,512]{1,0:T(8,128)(2,1)S(1)}, bf16[256,512]{1,0:T(8,128)(2,1)S(1)}, u32[]{:S(2)}, u32[]{:S(2)}) %collective-permute-start.22) | collective-permute-done | bytes 262176 | tf_op jit(solution)/shard_map/ppermute | solution.py:65
  (87 shorter events, 17.6 us)
Async XLA Ops:
  1.1 9.4 %collective-permute-start = (bf16[2,512,128]{2,1,0:T(8,128)(2,1)S(1)}, bf16[2,512,128]{2,1,0:T(8,128)(2,1)S(1)}, u32[]{:S(2)}, u32[]{:S(2)}) collective-permute-start(bf16[2,512,128]{2,1,0:T(8,128)(2,1)S(1)} %get-tuple-element.71), channel_id=1, source_target_pairs={{0,40},{1,41},{2,42},{3,43},{4,44},{5,45},{6,46},{7,47},{16,56},{1... | collective-permute-start | bytes 786440 | tf_op jit(solution)/shard_map/ppermute | solution.py:65
  4.2 9.0 %collective-permute-start.2 = (bf16[2,512,128]{2,1,0:T(8,128)(2,1)S(1)}, bf16[2,512,128]{2,1,0:T(8,128)(2,1)S(1)}, u32[]{:S(2)}, u32[]{:S(2)}) collective-permute-start(bf16[2,512,128]{2,1,0:T(8,128)(2,1)S(1)} %get-tuple-element.72.refs_0_), channel_id=1, source_target_pairs={{0,192},{1,193},{2,194},{3,195},{4,196},{5,197},{6,198},{7,199},{1... | collective-permute-start | bytes 786440 | tf_op jit(solution)/shard_map/ppermute | solution.py:65
  5.0 8.2 %collective-permute-start.1 = (bf16[2,512,128]{2,1,0:T(8,128)(2,1)S(1)}, bf16[2,512,128]{2,1,0:T(8,128)(2,1)S(1)}, u32[]{:S(2)}, u32[]{:S(2)}) collective-permute-start(bf16[2,512,128]{2,1,0:T(8,128)(2,1)S(1)} %get-tuple-element.72.refs_0_), channel_id=1, source_target_pairs={{0,64},{1,65},{2,66},{3,67},{4,68},{5,69},{6,70},{7,71},{16,80},{1... | collective-permute-start | bytes 786440 | tf_op jit(solution)/shard_map/ppermute | solution.py:65
  7.5 40.1 %slice-start = ((s8[8388608]{0:T(1024)(128)(4,1)}), s8[4194304]{0:T(1024)(128)(4,1)S(1)}, s32[]{:S(2)}) async-start(s8[8388608]{0:T(1024)(128)(4,1)} %bitcast.5), calls=%async_computation | async-start | bytes 8388608
  13.2 8.1 %collective-permute-start.4 = (bf16[2,512,128]{2,1,0:T(8,128)(2,1)S(1)}, bf16[2,512,128]{2,1,0:T(8,128)(2,1)S(1)}, u32[]{:S(2)}, u32[]{:S(2)}) collective-permute-start(bf16[2,512,128]{2,1,0:T(8,128)(2,1)S(1)} %collective-permute-done.refs_1_), channel_id=1, source_target_pairs={{0,192},{1,193},{2,194},{3,195},{4,196},{5,197},{6,198},{7,199},{1... | collective-permute-start | bytes 786440 | tf_op jit(solution)/shard_map/ppermute | solution.py:65
  13.3 15.5 %collective-permute-start.5 = (bf16[2,2,512,128]{3,2,1,0:T(8,128)(2,1)S(1)}, bf16[2,2,512,128]{3,2,1,0:T(8,128)(2,1)S(1)}, u32[]{:S(2)}, u32[]{:S(2)}) collective-permute-start(bf16[2,2,512,128]{3,2,1,0:T(8,128)(2,1)S(1)} %get-tuple-element.44), channel_id=1, source_target_pairs={{0,64},{1,65},{2,66},{3,67},{4,68},{5,69},{6,70},{7,71},{16,80},{1... | collective-permute-start | bytes 1572872 | tf_op jit(solution)/shard_map/ppermute | solution.py:65
  16.6 31.1 %slice-start.1 = ((s8[8388608]{0:T(1024)(128)(4,1)}), s8[4194304]{0:T(1024)(128)(4,1)S(1)}, s32[]{:S(2)}) async-start(s8[8388608]{0:T(1024)(128)(4,1)} %bitcast.5), calls=%async_computation.1 | async-start | bytes 8388608
  16.6 15.3 %collective-permute-start.3 = (bf16[4,2,512,128]{3,2,1,0:T(8,128)(2,1)S(1)}, bf16[4,2,512,128]{3,2,1,0:T(8,128)(2,1)S(1)}, u32[]{:S(2)}, u32[]{:S(2)}) collective-permute-start(bf16[4,2,512,128]{3,2,1,0:T(8,128)(2,1)S(1)} %get-tuple-element.43.refs_0_), channel_id=1, source_target_pairs={{0,16},{1,17},{2,18},{3,19},{4,20},{5,21},{6,22},{7,23},{16,0},{17... | collective-permute-start | bytes 3145736 | tf_op jit(solution)/shard_map/ppermute | solution.py:65
  16.6 29.6 %collective-permute-start.11 = (bf16[288,2048]{1,0:T(8,128)(2,1)S(1)}, bf16[288,2048]{1,0:T(8,128)(2,1)S(1)}, u32[]{:S(2)}, u32[]{:S(2)}) collective-permute-start(bf16[288,2048]{1,0:T(8,128)(2,1)S(1)} %get-tuple-element.49), channel_id=1, source_target_pairs={{0,40},{1,41},{2,42},{3,43},{4,44},{5,45},{6,46},{7,47},{16,56},{1... | collective-permute-start | bytes 3538952 | tf_op jit(solution)/shard_map/ppermute | solution.py:65
  21.2 7.6 %collective-permute-start.6 = (bf16[2,512,128]{2,1,0:T(8,128)(2,1)S(1)}, bf16[2,512,128]{2,1,0:T(8,128)(2,1)S(1)}, u32[]{:S(2)}, u32[]{:S(2)}) collective-permute-start(bf16[2,512,128]{2,1,0:T(8,128)(2,1)S(1)} %collective-permute-done.4.refs_3_), channel_id=1, source_target_pairs={{0,192},{1,193},{2,194},{3,195},{4,196},{5,197},{6,198},{7,199},{1... | collective-permute-start | bytes 786440 | tf_op jit(solution)/shard_map/ppermute | solution.py:65
  21.2 22.7 %collective-permute-start.10 = (bf16[224,2048]{1,0:T(8,128)(2,1)S(1)}, bf16[224,2048]{1,0:T(8,128)(2,1)S(1)}, u32[]{:S(2)}, u32[]{:S(2)}) collective-permute-start(bf16[224,2048]{1,0:T(8,128)(2,1)S(1)} %get-tuple-element.48), channel_id=1, source_target_pairs={{0,8},{1,9},{2,10},{3,11},{4,12},{5,13},{6,14},{7,15},{16,24},{17,... | collective-permute-start | bytes 2752520 | tf_op jit(solution)/shard_map/ppermute | solution.py:65
  28.8 1.5 %collective-permute-start.9 = (bf16[2,512,128]{2,1,0:T(8,128)(2,1)S(1)}, bf16[2,512,128]{2,1,0:T(8,128)(2,1)S(1)}, u32[]{:S(2)}, u32[]{:S(2)}) collective-permute-start(bf16[2,512,128]{2,1,0:T(8,128)(2,1)S(1)} %collective-permute-done.6.refs_4_), channel_id=1, source_target_pairs={{0,16},{1,17},{2,18},{3,19},{4,20},{5,21},{6,22},{7,23},{16,0},{17... | collective-permute-start | bytes 786440 | tf_op jit(solution)/shard_map/ppermute | solution.py:65
  28.8 3.1 %collective-permute-start.7 = (bf16[2,2,512,128]{3,2,1,0:T(8,128)(2,1)S(1)}, bf16[2,2,512,128]{3,2,1,0:T(8,128)(2,1)S(1)}, u32[]{:S(2)}, u32[]{:S(2)}) collective-permute-start(bf16[2,2,512,128]{3,2,1,0:T(8,128)(2,1)S(1)} %collective-permute-done.5.refs_2_), channel_id=1, source_target_pairs={{0,16},{1,17},{2,18},{3,19},{4,20},{5,21},{6,22},{7,23},{16,0},{17... | collective-permute-start | bytes 1572872 | tf_op jit(solution)/shard_map/ppermute | solution.py:65
  30.3 1.5 %collective-permute-start.8 = (bf16[2,512,128]{2,1,0:T(8,128)(2,1)S(1)}, bf16[2,512,128]{2,1,0:T(8,128)(2,1)S(1)}, u32[]{:S(2)}, u32[]{:S(2)}) collective-permute-start(bf16[2,512,128]{2,1,0:T(8,128)(2,1)S(1)} %collective-permute-done.4.refs_3_), channel_id=1, source_target_pairs={{0,16},{1,17},{2,18},{3,19},{4,20},{5,21},{6,22},{7,23},{16,0},{17... | collective-permute-start | bytes 786440 | tf_op jit(solution)/shard_map/ppermute | solution.py:65
  36.4 10.5 %collective-permute-start.12 = (bf16[256,512]{1,0:T(8,128)(2,1)S(1)}, bf16[256,512]{1,0:T(8,128)(2,1)S(1)}, u32[]{:S(2)}, u32[]{:S(2)}) collective-permute-start(bf16[256,512]{1,0:T(8,128)(2,1)S(1)} %get-tuple-element.47.own_ref), channel_id=1, source_target_pairs={{0,8},{1,9},{2,10},{3,11},{4,12},{5,13},{6,14},{7,15},{16,24},{17,... | collective-permute-start | bytes 786440 | tf_op jit(solution)/shard_map/ppermute | solution.py:65
  46.8 4.5 %collective-permute-start.15 = (bf16[288,2048]{1,0:T(8,128)(2,1)S(1)}, bf16[288,2048]{1,0:T(8,128)(2,1)S(1)}, u32[]{:S(2)}, u32[]{:S(2)}) collective-permute-start(bf16[288,2048]{1,0:T(8,128)(2,1)S(1)} %collective-permute-done.11.refs_1_), channel_id=1, source_target_pairs={{0,16},{1,17},{2,18},{3,19},{4,20},{5,21},{6,22},{7,23},{16,0},{17... | collective-permute-start | bytes 3538952 | tf_op jit(solution)/shard_map/ppermute | solution.py:65
  46.8 4.5 %collective-permute-start.14 = (bf16[224,2048]{1,0:T(8,128)(2,1)S(1)}, bf16[224,2048]{1,0:T(8,128)(2,1)S(1)}, u32[]{:S(2)}, u32[]{:S(2)}) collective-permute-start(bf16[224,2048]{1,0:T(8,128)(2,1)S(1)} %collective-permute-done.10.refs_0_), channel_id=1, source_target_pairs={{0,16},{1,17},{2,18},{3,19},{4,20},{5,21},{6,22},{7,23},{16,0},{17... | collective-permute-start | bytes 2752520 | tf_op jit(solution)/shard_map/ppermute | solution.py:65
  47.3 8.2 %collective-permute-start.18 = (bf16[256,512]{1,0:T(8,128)(2,1)S(1)}, bf16[256,512]{1,0:T(8,128)(2,1)S(1)}, u32[]{:S(2)}, u32[]{:S(2)}) collective-permute-start(bf16[256,512]{1,0:T(8,128)(2,1)S(1)} %attention.3.own_ref), channel_id=1, source_target_pairs={{0,8},{1,9},{2,10},{3,11},{4,12},{5,13},{6,14},{7,15},{16,24},{17,... | collective-permute-start | bytes 786440 | tf_op jit(solution)/shard_map/ppermute | solution.py:65
  49.4 23.8 %collective-permute-start.13 = (bf16[256,512]{1,0:T(8,128)(2,1)}, bf16[256,512]{1,0:T(8,128)(2,1)}, u32[]{:S(2)}, u32[]{:S(2)}) collective-permute-start(bf16[256,512]{1,0:T(8,128)(2,1)} %project.5), channel_id=1, source_target_pairs={{0,1},{1,0},{2,3},{3,2},{4,5},{5,4},{6,7},{7,6},{16,23},{17,18},{1... | collective-permute-start | bytes 786440 | tf_op jit(solution)/shard_map/ppermute | solution.py:65
  58.1 25.7 %collective-permute-start.23 = (bf16[256,512]{1,0:T(8,128)(2,1)}, bf16[256,512]{1,0:T(8,128)(2,1)}, u32[]{:S(2)}, u32[]{:S(2)}) collective-permute-start(bf16[256,512]{1,0:T(8,128)(2,1)} %get-tuple-element.63), channel_id=1, source_target_pairs={{0,7},{1,2},{2,1},{3,4},{4,3},{5,6},{6,5},{7,0},{16,17},{17,16},{1... | collective-permute-start | bytes 786440 | tf_op jit(solution)/shard_map/ppermute | solution.py:65
  64.0 24.1 %collective-permute-start.19 = (bf16[256,512]{1,0:T(8,128)(2,1)}, bf16[256,512]{1,0:T(8,128)(2,1)S(1)}, u32[]{:S(2)}, u32[]{:S(2)}) collective-permute-start(bf16[256,512]{1,0:T(8,128)(2,1)} %copy-done.12), channel_id=1, source_target_pairs={{0,7},{1,2},{2,1},{3,4},{4,3},{5,6},{6,5},{7,0},{16,17},{17,16},{1... | collective-permute-start | bytes 786440 | tf_op jit(solution)/shard_map/ppermute | solution.py:65
  64.0 20.9 %collective-permute-start.26 = (bf16[256,512]{1,0:T(8,128)(2,1)}, bf16[256,512]{1,0:T(8,128)(2,1)S(1)}, u32[]{:S(2)}, u32[]{:S(2)}) collective-permute-start(bf16[256,512]{1,0:T(8,128)(2,1)} %copy-done.14), channel_id=1, source_target_pairs={{0,1},{1,0},{2,3},{3,2},{4,5},{5,4},{6,7},{7,6},{16,23},{17,18},{1... | collective-permute-start | bytes 786440 | tf_op jit(solution)/shard_map/ppermute | solution.py:65
  74.3 21.0 %collective-permute-start.16 = (bf16[256,512]{1,0:T(8,128)(2,1)S(1)}, bf16[256,512]{1,0:T(8,128)(2,1)S(1)}, u32[]{:S(2)}, u32[]{:S(2)}) collective-permute-start(bf16[256,512]{1,0:T(8,128)(2,1)S(1)} %add_convert_fusion.13), channel_id=1, source_target_pairs={{0,7},{1,2},{2,1},{3,4},{4,3},{5,6},{6,5},{7,0},{16,17},{17,16},{1... | collective-permute-start | bytes 786440 | tf_op jit(solution)/shard_map/ppermute | solution.py:65
  84.8 7.7 %collective-permute-start.24 = (bf16[256,512]{1,0:T(8,128)(2,1)S(1)}, bf16[256,512]{1,0:T(8,128)(2,1)S(1)}, u32[]{:S(2)}, u32[]{:S(2)}) collective-permute-start(bf16[256,512]{1,0:T(8,128)(2,1)S(1)} %add_convert_fusion.6), channel_id=1, source_target_pairs={{0,1},{1,0},{2,3},{3,2},{4,5},{5,4},{6,7},{7,6},{16,23},{17,18},{1... | collective-permute-start | bytes 786440 | tf_op jit(solution)/shard_map/ppermute | solution.py:65
  85.0 9.7 %collective-permute-start.27 = (bf16[256,512]{1,0:T(8,128)(2,1)S(1)}, bf16[256,512]{1,0:T(8,128)(2,1)S(1)}, u32[]{:S(2)}, u32[]{:S(2)}) collective-permute-start(bf16[256,512]{1,0:T(8,128)(2,1)S(1)} %add_convert_fusion.3), channel_id=1, source_target_pairs={{0,7},{1,2},{2,1},{3,4},{4,3},{5,6},{6,5},{7,0},{16,17},{17,16},{1... | collective-permute-start | bytes 786440 | tf_op jit(solution)/shard_map/ppermute | solution.py:65
  88.2 9.9 %collective-permute-start.20 = (bf16[256,512]{1,0:T(8,128)(2,1)S(1)}, bf16[256,512]{1,0:T(8,128)(2,1)S(1)}, u32[]{:S(2)}, u32[]{:S(2)}) collective-permute-start(bf16[256,512]{1,0:T(8,128)(2,1)S(1)} %add_convert_fusion.10), channel_id=1, source_target_pairs={{0,1},{1,0},{2,3},{3,2},{4,5},{5,4},{6,7},{7,6},{16,23},{17,18},{1... | collective-permute-start | bytes 786440 | tf_op jit(solution)/shard_map/ppermute | solution.py:65
  92.5 10.3 %collective-permute-start.25 = (bf16[256,512]{1,0:T(8,128)(2,1)S(1)}, bf16[256,512]{1,0:T(8,128)(2,1)S(1)}, u32[]{:S(2)}, u32[]{:S(2)}) collective-permute-start(bf16[256,512]{1,0:T(8,128)(2,1)S(1)} %add_convert_fusion.5), channel_id=1, source_target_pairs={{0,7},{1,2},{2,1},{3,4},{4,3},{5,6},{6,5},{7,0},{16,17},{17,16},{1... | collective-permute-start | bytes 786440 | tf_op jit(solution)/shard_map/ppermute | solution.py:65
  94.7 9.6 %collective-permute-start.28 = (bf16[256,512]{1,0:T(8,128)(2,1)S(1)}, bf16[256,512]{1,0:T(8,128)(2,1)S(1)}, u32[]{:S(2)}, u32[]{:S(2)}) collective-permute-start(bf16[256,512]{1,0:T(8,128)(2,1)S(1)} %add_convert_fusion.2), channel_id=1, source_target_pairs={{0,1},{1,0},{2,3},{3,2},{4,5},{5,4},{6,7},{7,6},{16,23},{17,18},{1... | collective-permute-start | bytes 786440 | tf_op jit(solution)/shard_map/ppermute | solution.py:65
  95.4 13.4 %collective-permute-start.17 = (bf16[256,512]{1,0:T(8,128)(2,1)S(1)}, bf16[256,512]{1,0:T(8,128)(2,1)S(1)}, u32[]{:S(2)}, u32[]{:S(2)}) collective-permute-start(bf16[256,512]{1,0:T(8,128)(2,1)S(1)} %add_convert_fusion.12), channel_id=1, source_target_pairs={{0,1},{1,0},{2,3},{3,2},{4,5},{5,4},{6,7},{7,6},{16,23},{17,18},{1... | collective-permute-start | bytes 786440 | tf_op jit(solution)/shard_map/ppermute | solution.py:65
  98.2 10.6 %collective-permute-start.21 = (bf16[256,512]{1,0:T(8,128)(2,1)S(1)}, bf16[256,512]{1,0:T(8,128)(2,1)S(1)}, u32[]{:S(2)}, u32[]{:S(2)}) collective-permute-start(bf16[256,512]{1,0:T(8,128)(2,1)S(1)} %add_convert_fusion.9), channel_id=1, source_target_pairs={{0,7},{1,2},{2,1},{3,4},{4,3},{5,6},{6,5},{7,0},{16,17},{17,16},{1... | collective-permute-start | bytes 786440 | tf_op jit(solution)/shard_map/ppermute | solution.py:65
  104.4 7.2 %collective-permute-start.29 = (bf16[256,512]{1,0:T(8,128)(2,1)S(1)}, bf16[256,512]{1,0:T(8,128)(2,1)S(1)}, u32[]{:S(2)}, u32[]{:S(2)}) collective-permute-start(bf16[256,512]{1,0:T(8,128)(2,1)S(1)} %broadcast_select_fusion), channel_id=1, source_target_pairs={{0,7},{1,0},{2,1},{3,2},{4,3},{5,4},{6,5},{7,6},{16,23},{17,16},{1... | collective-permute-start | bytes 786440 | tf_op jit(solution)/shard_map/ppermute | solution.py:65
  108.9 7.7 %collective-permute-start.22 = (bf16[256,512]{1,0:T(8,128)(2,1)S(1)}, bf16[256,512]{1,0:T(8,128)(2,1)S(1)}, u32[]{:S(2)}, u32[]{:S(2)}) collective-permute-start(bf16[256,512]{1,0:T(8,128)(2,1)S(1)} %broadcast_select_fusion.1), channel_id=1, source_target_pairs={{0,1},{1,2},{2,3},{3,4},{4,5},{5,6},{6,7},{7,0},{16,17},{17,18},{1... | collective-permute-start | bytes 786440 | tf_op jit(solution)/shard_map/ppermute | solution.py:65
  (15 other events, 99.8 us)

commit v9 on v7

--- a/solution.py
+++ b/solution.py
@@ -18,7 +18,7 @@
 SCALE2 = HD ** (-0.5) * math.log2(math.e)
 CHUNKS = 2
 LOW = -1e30
-NEAR_ROWS = 224
+NEAR_ROWS = 208
 ATTENTION_VMEM = 14 * 2**20
 PROJECT_VMEM = 8 * 2**20
 WIDE = 4
@@ -291,11 +291,9 @@
     far_right = send(far, "x-")
     both = send(one, "x+")
     two_far = send(far_right, "x-")
-    far_right_there, both = barrier((far_right, both))
-    late = [both, far_right, two_far]
-    pieces = [four, send(four, "core"), *late]
-    pieces += [send(piece, "core") for piece in (both, far_right_there, two_far)]
-    slots = ((0, 2, 12, 4), (1, 3, 13, 5), (14, 8), (6,), (10,), (15, 9), (7,), (11,))
+    (pair,) = stack([far_right, two_far], ((0, 1),))
+    pieces = [four, send(four, "core"), both, send(both, "core"), pair, send(pair, "core")]
+    slots = ((0, 2, 12, 4), (1, 3, 13, 5), (14, 8), (15, 9), (6, 10), (7, 11))
 
     first, kv = attention(coords, block_list, queries, 0, n_rows, pieces, slots)
     attended = [first] + [

time: 106 us -> 105 us (level)
  the two profiles are of different devices: /device:TPU:96 before, /device:TPU:6 now
where the time goes in v9:
time: 105 us; the launch traced here: 104 us
  waiting for transfers between devices  41.3 us (39%)
  starting transfers between devices  38.9 us (37%)
  Pallas kernels  21 us (20%)
  other arithmetic  1.7 us (2%)
  local copies, waits for them, and re-layouts  1.18 us (1%)
    ppermute x29, waiting for transfers between devices, send(): return lax.ppermute(array, AXES, MOVES[move])  41.3 us
    ppermute x29, starting transfers between devices, send(): return lax.ppermute(array, AXES, MOVES[move])  38.9 us
    pallas_call x2, Pallas kernels, attention(): pl.pallas_call(functools.partial(attention_kernel, first_row, n_rows, slo...  9.92 us
    pallas_call x4, Pallas kernels, project(): pl.pallas_call(functools.partial(project_kernel, steps), out_shape=[jax.S...  8.58 us
    pallas_call x1, Pallas kernels, pick(): pl.pallas_call(pick_kernel, out_shape=parts, in_specs=[SMEM, HBM], out_sp...  2.38 us
  transfers between devices with their start and end apart: 29, of which 14 were waited for; matrix products, arithmetic and copies ran while one was open for 1% of the time, Pallas kernels for 20%

profile of v9, /device:TPU:6, one launch (start us, length us, event | category | flops | bytes accessed | tf_op | source)
XLA Modules:
  0.0 104.3 jit_solution(8555994934181842249)
XLA Ops:
  0.0 1.1 %constant_dynamic-slice_fusion = (bf16[2,512,128]{2,1,0:T(8,128)(2,1)S(1)}, bf16[2,512,128]{2,1,0:T(8,128)(2,1)S(1)}) fusion(bf16[2,512,1024]{2,1,0:T(8,128)(2,1)} %param.5, s32[]{:T(128)S(6)} %select_n.46, s32[]{:T(128)S(6)} %select_n.45), kind=kLoop, calls=%fused_computation.13 | loop fusion | bytes 1048584 | tf_op jit(solution)/shard_map/dynamic_slice | solution.py:281
  1.1 3.1 %collective-permute-start = (bf16[2,512,128]{2,1,0:T(8,128)(2,1)S(1)}, bf16[2,512,128]{2,1,0:T(8,128)(2,1)S(1)}, u32[]{:S(2)}, u32[]{:S(2)}) collective-permute-start(bf16[2,512,128]{2,1,0:T(8,128)(2,1)S(1)} %get-tuple-element.67), channel_id=1, source_target_pairs={{0,40},{1,41},{2,42},{3,43},{4,44},{5,45},{6,46},{7,47},{16,56},{1... | collective-permute-start | bytes 786440 | tf_op jit(solution)/shard_map/ppermute | solution.py:58
  4.2 0.8 collective-permute-start.2
  5.0 2.4 %collective-permute-start.1 = (bf16[2,512,128]{2,1,0:T(8,128)(2,1)S(1)}, bf16[2,512,128]{2,1,0:T(8,128)(2,1)S(1)}, u32[]{:S(2)}, u32[]{:S(2)}) collective-permute-start(bf16[2,512,128]{2,1,0:T(8,128)(2,1)S(1)} %get-tuple-element.68.refs_0_), channel_id=1, source_target_pairs={{0,64},{1,65},{2,66},{3,67},{4,68},{5,69},{6,70},{7,71},{16,80},{1... | collective-permute-start | bytes 786440 | tf_op jit(solution)/shard_map/ppermute | solution.py:58
  7.5 2.4 %pick.1 = (bf16[208,2048]{1,0:T(8,128)(2,1)S(1)}, bf16[304,2048]{1,0:T(8,128)(2,1)S(1)}) custom-call(s32[5]{0:T(128)S(1)} %stack.25.coords, bf16[512,8192]{1,0:T(8,128)(2,1)} %w_ref.9), custom_call_target="tpu_custom_call" | custom-call | tf_op jit(solution)/shard_map/pick/pallas_call | solution.py:84
  10.5 2.7 %collective-permute-done.2.refs_3_ = bf16[2,512,128]{2,1,0:T(8,128)(2,1)S(1)} collective-permute-done((bf16[2,512,128]{2,1,0:T(8,128)(2,1)S(1)}, bf16[2,512,128]{2,1,0:T(8,128)(2,1)S(1)}, u32[]{:S(2)}, u32[]{:S(2)}) %collective-permute-start.2) | collective-permute-done | bytes 262176 | tf_op jit(solution)/shard_map/ppermute | solution.py:58
  13.3 3.3 %collective-permute-start.4 = (bf16[2,2,512,128]{3,2,1,0:T(8,128)(2,1)S(1)}, bf16[2,2,512,128]{3,2,1,0:T(8,128)(2,1)S(1)}, u32[]{:S(2)}, u32[]{:S(2)}) collective-permute-start(bf16[2,2,512,128]{3,2,1,0:T(8,128)(2,1)S(1)} %get-tuple-element.42), channel_id=1, source_target_pairs={{0,64},{1,65},{2,66},{3,67},{4,68},{5,69},{6,70},{7,71},{16,80},{1... | collective-permute-start | bytes 1572872 | tf_op jit(solution)/shard_map/ppermute | solution.py:58
  17.0 4.3 %collective-permute-done.6.refs_0_ = bf16[2,512,128]{2,1,0:T(8,128)(2,1)S(1)} collective-permute-done((bf16[2,512,128]{2,1,0:T(8,128)(2,1)S(1)}, bf16[2,512,128]{2,1,0:T(8,128)(2,1)S(1)}, u32[]{:S(2)}, u32[]{:S(2)}) %collective-permute-start.6) | collective-permute-done | bytes 262176 | tf_op jit(solution)/shard_map/ppermute | solution.py:58
  21.4 7.4 %collective-permute-done.7.refs_1_ = bf16[2,512,128]{2,1,0:T(8,128)(2,1)S(1)} collective-permute-done((bf16[2,512,128]{2,1,0:T(8,128)(2,1)S(1)}, bf16[2,512,128]{2,1,0:T(8,128)(2,1)S(1)}, u32[]{:S(2)}, u32[]{:S(2)}) %collective-permute-start.7) | collective-permute-done | bytes 262176 | tf_op jit(solution)/shard_map/ppermute | solution.py:58
  29.4 1.4 %collective-permute-done.8.refs_5_ = bf16[2,2,512,128]{3,2,1,0:T(8,128)(2,1)S(1)} collective-permute-done((bf16[2,2,512,128]{3,2,1,0:T(8,128)(2,1)S(1)}, bf16[2,2,512,128]{3,2,1,0:T(8,128)(2,1)S(1)}, u32[]{:S(2)}, u32[]{:S(2)}) %collective-permute-start.8) | collective-permute-done | bytes 524320 | tf_op jit(solution)/shard_map/ppermute | solution.py:58
  31.6 4.5 %attention.2 = (bf16[256,512]{1,0:T(8,128)(2,1)S(1)}, bf16[2,8192,128]{2,1,0:T(8,128)(2,1)S(1)}) custom-call(s32[5]{0:T(128)S(1)} %stack.25.coords, s32[4,16]{1,0:T(4,128)S(1)} %copy-done.1, bf16[512,512]{1,0:T(8,128)(2,1)S(1)} %copy-done, bf16[4,2,512,128]{3,2,1,0:T(8,128)(2,1)S(1)} %get-tuple-element.41.refs_0_, ...), custom_call_target="tpu_custom_call" | custom-call | tf_op jit(solution)/shard_map/attention/pallas_call | solution.py:188
  36.3 5.5 %attention.3.own_ref = bf16[256,512]{1,0:T(8,128)(2,1)S(1)} custom-call(s32[5]{0:T(128)S(1)} %stack.25.coords, s32[4,16]{1,0:T(4,128)S(1)} %copy-done.1, bf16[512,512]{1,0:T(8,128)(2,1)S(1)} %copy-done, bf16[2,8192,128]{2,1,0:T(8,128)(2,1)S(1)} %get-tuple-element.46.refs_0_), custom_call_target="tpu_custom_call" | custom-call | tf_op jit(solution)/shard_map/attention/pallas_call | solution.py:188
  41.8 5.8 %collective-permute-done.10.w1a = bf16[304,2048]{1,0:T(8,128)(2,1)S(1)} collective-permute-done((bf16[304,2048]{1,0:T(8,128)(2,1)S(1)}, bf16[304,2048]{1,0:T(8,128)(2,1)S(1)}, u32[]{:S(2)}, u32[]{:S(2)}) %collective-permute-start.10) | collective-permute-done | bytes 1245216 | tf_op jit(solution)/shard_map/ppermute | solution.py:58
  48.1 3.6 %collective-permute-done.12.w0b = bf16[208,2048]{1,0:T(8,128)(2,1)S(1)} collective-permute-done((bf16[208,2048]{1,0:T(8,128)(2,1)S(1)}, bf16[208,2048]{1,0:T(8,128)(2,1)S(1)}, u32[]{:S(2)}, u32[]{:S(2)}) %collective-permute-start.12) | collective-permute-done | bytes 852000 | tf_op jit(solution)/shard_map/ppermute | solution.py:58
  51.8 1.4 %project.5 = (bf16[256,512]{1,0:T(8,128)(2,1)S(1)}, bf16[256,512]{1,0:T(8,128)(2,1)S(1)}) custom-call(s32[5]{0:T(128)S(1)} %stack.25.coords, bf16[256,512]{1,0:T(8,128)(2,1)S(1)} %get-tuple-element.43.own_ref, bf16[256,512]{1,0:T(8,128)(2,1)S(1)} %collective-permute-done.11.near_ref, bf16[512,8192]{1,0:T(8,128)(2,1)S(1)} %bitcast.6, ...), custom_call_target="tpu_custom_call" | custom-call | tf_op jit(solution)/shard_map/project/pallas_call | solution.py:261
  53.2 2.0 %collective-permute-start.14 = (bf16[256,512]{1,0:T(8,128)(2,1)S(1)}, bf16[256,512]{1,0:T(8,128)(2,1)S(1)}, u32[]{:S(2)}, u32[]{:S(2)}) collective-permute-start(bf16[256,512]{1,0:T(8,128)(2,1)S(1)} %get-tuple-element.51), channel_id=1, source_target_pairs={{0,1},{1,2},{2,3},{3,4},{4,5},{5,6},{6,7},{7,0},{16,17},{17,18},{1... | collective-permute-start | bytes 786440 | tf_op jit(solution)/shard_map/ppermute | solution.py:58
  55.2 4.0 %collective-permute-start.18 = (bf16[256,512]{1,0:T(8,128)(2,1)S(1)}, bf16[256,512]{1,0:T(8,128)(2,1)S(1)}, u32[]{:S(2)}, u32[]{:S(2)}) collective-permute-start(bf16[256,512]{1,0:T(8,128)(2,1)S(1)} %get-tuple-element.55), channel_id=1, source_target_pairs={{0,7},{1,0},{2,1},{3,2},{4,3},{5,4},{6,5},{7,6},{16,23},{17,16},{1... | collective-permute-start | bytes 786440 | tf_op jit(solution)/shard_map/ppermute | solution.py:58
  59.2 1.4 %project.7 = (bf16[256,512]{1,0:T(8,128)(2,1)S(1)}, bf16[256,512]{1,0:T(8,128)(2,1)S(1)}) custom-call(s32[5]{0:T(128)S(1)} %stack.25.coords, bf16[256,512]{1,0:T(8,128)(2,1)S(1)} %attention.3.own_ref, bf16[256,512]{1,0:T(8,128)(2,1)S(1)} %collective-permute-done.21.near_ref, bf16[512,8192]{1,0:T(8,128)(2,1)S(1)} %bitcast.6, ...), custom_call_target="tpu_custom_call" | custom-call | tf_op jit(solution)/shard_map/project/pallas_call | solution.py:261
  60.8 3.2 %collective-permute-start.25 = (bf16[256,512]{1,0:T(8,128)(2,1)S(1)}, bf16[256,512]{1,0:T(8,128)(2,1)S(1)}, u32[]{:S(2)}, u32[]{:S(2)}) collective-permute-start(bf16[256,512]{1,0:T(8,128)(2,1)S(1)} %get-tuple-element.63), channel_id=1, source_target_pairs={{0,7},{1,0},{2,1},{3,2},{4,3},{5,4},{6,5},{7,6},{16,23},{17,16},{1... | collective-permute-start | bytes 786440 | tf_op jit(solution)/shard_map/ppermute | solution.py:58
  64.0 2.9 %project.4 = (bf16[256,512]{1,0:T(8,128)(2,1)S(1)}, bf16[256,512]{1,0:T(8,128)(2,1)S(1)}, bf16[256,512]{1,0:T(8,128)(2,1)S(1)}, bf16[256,512]{1,0:T(8,128)(2,1)S...) custom-call(s32[5]{0:T(128)S(1)} %stack.25.coords, bf16[256,512]{1,0:T(8,128)(2,1)S(1)} %get-tuple-element.43.own_ref, ...), custom_call_target="tpu_custom_call" | custom-call | tf_op jit(solution)/shard_map/project/pallas_call | solution.py:261
  66.9 2.8 %project.6 = (bf16[256,512]{1,0:T(8,128)(2,1)S(1)}, bf16[256,512]{1,0:T(8,128)(2,1)S(1)}, bf16[256,512]{1,0:T(8,128)(2,1)S(1)}, bf16[256,512]{1,0:T(8,128)(2,1)S...) custom-call(s32[5]{0:T(128)S(1)} %stack.25.coords, bf16[256,512]{1,0:T(8,128)(2,1)S(1)} %attention.3.own_ref, ...), custom_call_target="tpu_custom_call" | custom-call | tf_op jit(solution)/shard_map/project/pallas_call | solution.py:261
  70.0 3.3 %collective-permute-start.19 = (bf16[256,512]{1,0:T(8,128)(2,1)S(1)}, bf16[256,512]{1,0:T(8,128)(2,1)S(1)}, u32[]{:S(2)}, u32[]{:S(2)}) collective-permute-start(bf16[256,512]{1,0:T(8,128)(2,1)S(1)} %add_convert_fusion.8), channel_id=1, source_target_pairs={{0,7},{1,0},{2,1},{3,2},{4,3},{5,4},{6,5},{7,6},{16,23},{17,16},{1... | collective-permute-start | bytes 786440 | tf_op jit(solution)/shard_map/ppermute | solution.py:58
  73.5 3.3 %collective-permute-start.26 = (bf16[256,512]{1,0:T(8,128)(2,1)S(1)}, bf16[256,512]{1,0:T(8,128)(2,1)S(1)}, u32[]{:S(2)}, u32[]{:S(2)}) collective-permute-start(bf16[256,512]{1,0:T(8,128)(2,1)S(1)} %add_convert_fusion.3), channel_id=1, source_target_pairs={{0,7},{1,0},{2,1},{3,2},{4,3},{5,4},{6,5},{7,6},{16,23},{17,16},{1... | collective-permute-start | bytes 786440 | tf_op jit(solution)/shard_map/ppermute | solution.py:58
  76.8 3.5 %collective-permute-done.15 = bf16[256,512]{1,0:T(8,128)(2,1)S(1)} collective-permute-done((bf16[256,512]{1,0:T(8,128)(2,1)S(1)}, bf16[256,512]{1,0:T(8,128)(2,1)S(1)}, u32[]{:S(2)}, u32[]{:S(2)}) %collective-permute-start.15) | collective-permute-done | bytes 262176 | tf_op jit(solution)/shard_map/ppermute | solution.py:58
  80.8 3.3 %collective-permute-start.20 = (bf16[256,512]{1,0:T(8,128)(2,1)S(1)}, bf16[256,512]{1,0:T(8,128)(2,1)S(1)}, u32[]{:S(2)}, u32[]{:S(2)}) collective-permute-start(bf16[256,512]{1,0:T(8,128)(2,1)S(1)} %add_convert_fusion.7), channel_id=1, source_target_pairs={{0,7},{1,0},{2,1},{3,2},{4,3},{5,4},{6,5},{7,6},{16,23},{17,16},{1... | collective-permute-start | bytes 786440 | tf_op jit(solution)/shard_map/ppermute | solution.py:58
  84.1 1.6 %collective-permute-done.26 = bf16[256,512]{1,0:T(8,128)(2,1)S(1)} collective-permute-done((bf16[256,512]{1,0:T(8,128)(2,1)S(1)}, bf16[256,512]{1,0:T(8,128)(2,1)S(1)}, u32[]{:S(2)}, u32[]{:S(2)}) %collective-permute-start.26) | collective-permute-done | bytes 262176 | tf_op jit(solution)/shard_map/ppermute | solution.py:58
  85.7 3.8 %collective-permute-start.27 = (bf16[256,512]{1,0:T(8,128)(2,1)S(1)}, bf16[256,512]{1,0:T(8,128)(2,1)S(1)}, u32[]{:S(2)}, u32[]{:S(2)}) collective-permute-start(bf16[256,512]{1,0:T(8,128)(2,1)S(1)} %add_convert_fusion.2), channel_id=1, source_target_pairs={{0,7},{1,0},{2,1},{3,2},{4,3},{5,4},{6,5},{7,6},{16,23},{17,16},{1... | collective-permute-start | bytes 786440 | tf_op jit(solution)/shard_map/ppermute | solution.py:58
  90.2 4.7 %collective-permute-done.27 = bf16[256,512]{1,0:T(8,128)(2,1)S(1)} collective-permute-done((bf16[256,512]{1,0:T(8,128)(2,1)S(1)}, bf16[256,512]{1,0:T(8,128)(2,1)S(1)}, u32[]{:S(2)}, u32[]{:S(2)}) %collective-permute-start.27) | collective-permute-done | bytes 262176 | tf_op jit(solution)/shard_map/ppermute | solution.py:58
  94.9 3.8 %collective-permute-start.28 = (bf16[256,512]{1,0:T(8,128)(2,1)S(1)}, bf16[256,512]{1,0:T(8,128)(2,1)S(1)}, u32[]{:S(2)}, u32[]{:S(2)}) collective-permute-start(bf16[256,512]{1,0:T(8,128)(2,1)S(1)} %add_convert_fusion.1), channel_id=1, source_target_pairs={{0,7},{1,0},{2,1},{3,2},{4,3},{5,4},{6,5},{7,6},{16,23},{17,16},{1... | collective-permute-start | bytes 786440 | tf_op jit(solution)/shard_map/ppermute | solution.py:58
  98.7 1.7 %collective-permute-done.17 = bf16[256,512]{1,0:T(8,128)(2,1)S(1)} collective-permute-done((bf16[256,512]{1,0:T(8,128)(2,1)S(1)}, bf16[256,512]{1,0:T(8,128)(2,1)S(1)}, u32[]{:S(2)}, u32[]{:S(2)}) %collective-permute-start.17) | collective-permute-done | bytes 262176 | tf_op jit(solution)/shard_map/ppermute | solution.py:58
  100.5 2.8 %collective-permute-done.24 = bf16[256,512]{1,0:T(8,128)(2,1)S(1)} collective-permute-done((bf16[256,512]{1,0:T(8,128)(2,1)S(1)}, bf16[256,512]{1,0:T(8,128)(2,1)S(1)}, u32[]{:S(2)}, u32[]{:S(2)}) %collective-permute-start.24) | collective-permute-done | bytes 262176 | tf_op jit(solution)/shard_map/ppermute | solution.py:58
  103.5 0.8 pad_maximum_fusion
  (59 shorter events, 5.4 us)
Async XLA Ops:
  1.1 9.4 %collective-permute-start = (bf16[2,512,128]{2,1,0:T(8,128)(2,1)S(1)}, bf16[2,512,128]{2,1,0:T(8,128)(2,1)S(1)}, u32[]{:S(2)}, u32[]{:S(2)}) collective-permute-start(bf16[2,512,128]{2,1,0:T(8,128)(2,1)S(1)} %get-tuple-element.67), channel_id=1, source_target_pairs={{0,40},{1,41},{2,42},{3,43},{4,44},{5,45},{6,46},{7,47},{16,56},{1... | collective-permute-start | bytes 786440 | tf_op jit(solution)/shard_map/ppermute | solution.py:58
  4.2 9.0 %collective-permute-start.2 = (bf16[2,512,128]{2,1,0:T(8,128)(2,1)S(1)}, bf16[2,512,128]{2,1,0:T(8,128)(2,1)S(1)}, u32[]{:S(2)}, u32[]{:S(2)}) collective-permute-start(bf16[2,512,128]{2,1,0:T(8,128)(2,1)S(1)} %get-tuple-element.68.refs_0_), channel_id=1, source_target_pairs={{0,192},{1,193},{2,194},{3,195},{4,196},{5,197},{6,198},{7,199},{1... | collective-permute-start | bytes 786440 | tf_op jit(solution)/shard_map/ppermute | solution.py:58
  5.0 8.2 %collective-permute-start.1 = (bf16[2,512,128]{2,1,0:T(8,128)(2,1)S(1)}, bf16[2,512,128]{2,1,0:T(8,128)(2,1)S(1)}, u32[]{:S(2)}, u32[]{:S(2)}) collective-permute-start(bf16[2,512,128]{2,1,0:T(8,128)(2,1)S(1)} %get-tuple-element.68.refs_0_), channel_id=1, source_target_pairs={{0,64},{1,65},{2,66},{3,67},{4,68},{5,69},{6,70},{7,71},{16,80},{1... | collective-permute-start | bytes 786440 | tf_op jit(solution)/shard_map/ppermute | solution.py:58
  7.5 44.3 %slice-start = ((s8[8388608]{0:T(1024)(128)(4,1)}), s8[4194304]{0:T(1024)(128)(4,1)S(1)}, s32[]{:S(2)}) async-start(s8[8388608]{0:T(1024)(128)(4,1)} %bitcast.5), calls=%async_computation | async-start | bytes 8388608
  9.9 21.7 %copy-start = (bf16[512,512]{1,0:T(8,128)(2,1)S(1)}, bf16[512,512]{1,0:T(8,128)(2,1)}, u32[]{:S(2)}) copy-start(bf16[512,512]{1,0:T(8,128)(2,1)} %q_ref.3) | copy-start | bytes 1572868
  13.2 8.1 %collective-permute-start.6 = (bf16[2,512,128]{2,1,0:T(8,128)(2,1)S(1)}, bf16[2,512,128]{2,1,0:T(8,128)(2,1)S(1)}, u32[]{:S(2)}, u32[]{:S(2)}) collective-permute-start(bf16[2,512,128]{2,1,0:T(8,128)(2,1)S(1)} %collective-permute-done.refs_1_), channel_id=1, source_target_pairs={{0,192},{1,193},{2,194},{3,195},{4,196},{5,197},{6,198},{7,199},{1... | collective-permute-start | bytes 786440 | tf_op jit(solution)/shard_map/ppermute | solution.py:58
  13.3 15.7 %collective-permute-start.4 = (bf16[2,2,512,128]{3,2,1,0:T(8,128)(2,1)S(1)}, bf16[2,2,512,128]{3,2,1,0:T(8,128)(2,1)S(1)}, u32[]{:S(2)}, u32[]{:S(2)}) collective-permute-start(bf16[2,2,512,128]{3,2,1,0:T(8,128)(2,1)S(1)} %get-tuple-element.42), channel_id=1, source_target_pairs={{0,64},{1,65},{2,66},{3,67},{4,68},{5,69},{6,70},{7,71},{16,80},{1... | collective-permute-start | bytes 1572872 | tf_op jit(solution)/shard_map/ppermute | solution.py:58
  16.6 35.2 %slice-start.1 = ((s8[8388608]{0:T(1024)(128)(4,1)}), s8[4194304]{0:T(1024)(128)(4,1)S(1)}, s32[]{:S(2)}) async-start(s8[8388608]{0:T(1024)(128)(4,1)} %bitcast.5), calls=%async_computation.1 | async-start | bytes 8388608
  16.6 15.0 %collective-permute-start.3 = (bf16[4,2,512,128]{3,2,1,0:T(8,128)(2,1)S(1)}, bf16[4,2,512,128]{3,2,1,0:T(8,128)(2,1)S(1)}, u32[]{:S(2)}, u32[]{:S(2)}) collective-permute-start(bf16[4,2,512,128]{3,2,1,0:T(8,128)(2,1)S(1)} %get-tuple-element.41.refs_0_), channel_id=1, source_target_pairs={{0,16},{1,17},{2,18},{3,19},{4,20},{5,21},{6,22},{7,23},{16,0},{17... | collective-permute-start | bytes 3145736 | tf_op jit(solution)/shard_map/ppermute | solution.py:58
  16.6 31.0 %collective-permute-start.10 = (bf16[304,2048]{1,0:T(8,128)(2,1)S(1)}, bf16[304,2048]{1,0:T(8,128)(2,1)S(1)}, u32[]{:S(2)}, u32[]{:S(2)}) collective-permute-start(bf16[304,2048]{1,0:T(8,128)(2,1)S(1)} %get-tuple-element.45), channel_id=1, source_target_pairs={{0,40},{1,41},{2,42},{3,43},{4,44},{5,45},{6,46},{7,47},{16,56},{1... | collective-permute-start | bytes 3735560 | tf_op jit(solution)/shard_map/ppermute | solution.py:58
  21.2 7.6 %collective-permute-start.7 = (bf16[2,512,128]{2,1,0:T(8,128)(2,1)S(1)}, bf16[2,512,128]{2,1,0:T(8,128)(2,1)S(1)}, u32[]{:S(2)}, u32[]{:S(2)}) collective-permute-start(bf16[2,512,128]{2,1,0:T(8,128)(2,1)S(1)} %collective-permute-done.6.refs_0_), channel_id=1, source_target_pairs={{0,192},{1,193},{2,194},{3,195},{4,196},{5,197},{6,198},{7,199},{1... | collective-permute-start | bytes 786440 | tf_op jit(solution)/shard_map/ppermute | solution.py:58
  21.2 20.5 %collective-permute-start.9 = (bf16[208,2048]{1,0:T(8,128)(2,1)S(1)}, bf16[208,2048]{1,0:T(8,128)(2,1)S(1)}, u32[]{:S(2)}, u32[]{:S(2)}) collective-permute-start(bf16[208,2048]{1,0:T(8,128)(2,1)S(1)} %get-tuple-element.44), channel_id=1, source_target_pairs={{0,8},{1,9},{2,10},{3,11},{4,12},{5,13},{6,14},{7,15},{16,24},{17,... | collective-permute-start | bytes 2555912 | tf_op jit(solution)/shard_map/ppermute | solution.py:58
  28.8 2.0 %collective-permute-start.8 = (bf16[2,2,512,128]{3,2,1,0:T(8,128)(2,1)S(1)}, bf16[2,2,512,128]{3,2,1,0:T(8,128)(2,1)S(1)}, u32[]{:S(2)}, u32[]{:S(2)}) collective-permute-start(bf16[2,2,512,128]{3,2,1,0:T(8,128)(2,1)S(1)} %stack.27.refs_4_), channel_id=1, source_target_pairs={{0,16},{1,17},{2,18},{3,19},{4,20},{5,21},{6,22},{7,23},{16,0},{17... | collective-permute-start | bytes 1572872 | tf_op jit(solution)/shard_map/ppermute | solution.py:58
  29.0 2.6 %collective-permute-start.5 = (bf16[2,2,512,128]{3,2,1,0:T(8,128)(2,1)S(1)}, bf16[2,2,512,128]{3,2,1,0:T(8,128)(2,1)S(1)}, u32[]{:S(2)}, u32[]{:S(2)}) collective-permute-start(bf16[2,2,512,128]{3,2,1,0:T(8,128)(2,1)S(1)} %collective-permute-done.4.refs_2_), channel_id=1, source_target_pairs={{0,16},{1,17},{2,18},{3,19},{4,20},{5,21},{6,22},{7,23},{16,0},{17... | collective-permute-start | bytes 1572872 | tf_op jit(solution)/shard_map/ppermute | solution.py:58
  36.1 11.5 %collective-permute-start.11 = (bf16[256,512]{1,0:T(8,128)(2,1)S(1)}, bf16[256,512]{1,0:T(8,128)(2,1)S(1)}, u32[]{:S(2)}, u32[]{:S(2)}) collective-permute-start(bf16[256,512]{1,0:T(8,128)(2,1)S(1)} %get-tuple-element.43.own_ref), channel_id=1, source_target_pairs={{0,8},{1,9},{2,10},{3,11},{4,12},{5,13},{6,14},{7,15},{16,24},{17,... | collective-permute-start | bytes 786440 | tf_op jit(solution)/shard_map/ppermute | solution.py:58
  47.6 4.2 %collective-permute-start.13 = (bf16[304,2048]{1,0:T(8,128)(2,1)S(1)}, bf16[304,2048]{1,0:T(8,128)(2,1)S(1)}, u32[]{:S(2)}, u32[]{:S(2)}) collective-permute-start(bf16[304,2048]{1,0:T(8,128)(2,1)S(1)} %collective-permute-done.10.w1a), channel_id=1, source_target_pairs={{0,16},{1,17},{2,18},{3,19},{4,20},{5,21},{6,22},{7,23},{16,0},{17... | collective-permute-start | bytes 3735560 | tf_op jit(solution)/shard_map/ppermute | solution.py:58
  47.6 4.2 %collective-permute-start.12 = (bf16[208,2048]{1,0:T(8,128)(2,1)S(1)}, bf16[208,2048]{1,0:T(8,128)(2,1)S(1)}, u32[]{:S(2)}, u32[]{:S(2)}) collective-permute-start(bf16[208,2048]{1,0:T(8,128)(2,1)S(1)} %collective-permute-done.9.w0a), channel_id=1, source_target_pairs={{0,16},{1,17},{2,18},{3,19},{4,20},{5,21},{6,22},{7,23},{16,0},{17... | collective-permute-start | bytes 2555912 | tf_op jit(solution)/shard_map/ppermute | solution.py:58
  48.1 11.1 %collective-permute-start.21 = (bf16[256,512]{1,0:T(8,128)(2,1)S(1)}, bf16[256,512]{1,0:T(8,128)(2,1)S(1)}, u32[]{:S(2)}, u32[]{:S(2)}) collective-permute-start(bf16[256,512]{1,0:T(8,128)(2,1)S(1)} %attention.3.own_ref), channel_id=1, source_target_pairs={{0,8},{1,9},{2,10},{3,11},{4,12},{5,13},{6,14},{7,15},{16,24},{17,... | collective-permute-start | bytes 786440 | tf_op jit(solution)/shard_map/ppermute | solution.py:58
  53.2 16.5 %collective-permute-start.14 = (bf16[256,512]{1,0:T(8,128)(2,1)S(1)}, bf16[256,512]{1,0:T(8,128)(2,1)S(1)}, u32[]{:S(2)}, u32[]{:S(2)}) collective-permute-start(bf16[256,512]{1,0:T(8,128)(2,1)S(1)} %get-tuple-element.51), channel_id=1, source_target_pairs={{0,1},{1,2},{2,3},{3,4},{4,5},{5,6},{6,7},{7,0},{16,17},{17,18},{1... | collective-permute-start | bytes 786440 | tf_op jit(solution)/shard_map/ppermute | solution.py:58
  55.2 14.7 %collective-permute-start.18 = (bf16[256,512]{1,0:T(8,128)(2,1)S(1)}, bf16[256,512]{1,0:T(8,128)(2,1)S(1)}, u32[]{:S(2)}, u32[]{:S(2)}) collective-permute-start(bf16[256,512]{1,0:T(8,128)(2,1)S(1)} %get-tuple-element.55), channel_id=1, source_target_pairs={{0,7},{1,0},{2,1},{3,2},{4,3},{5,4},{6,5},{7,6},{16,23},{17,16},{1... | collective-permute-start | bytes 786440 | tf_op jit(solution)/shard_map/ppermute | solution.py:58
  60.7 12.6 %collective-permute-start.22 = (bf16[256,512]{1,0:T(8,128)(2,1)S(1)}, bf16[256,512]{1,0:T(8,128)(2,1)S(1)}, u32[]{:S(2)}, u32[]{:S(2)}) collective-permute-start(bf16[256,512]{1,0:T(8,128)(2,1)S(1)} %get-tuple-element.60), channel_id=1, source_target_pairs={{0,1},{1,2},{2,3},{3,4},{4,5},{5,6},{6,7},{7,0},{16,17},{17,18},{1... | collective-permute-start | bytes 786440 | tf_op jit(solution)/shard_map/ppermute | solution.py:58
  60.8 12.7 %collective-permute-start.25 = (bf16[256,512]{1,0:T(8,128)(2,1)S(1)}, bf16[256,512]{1,0:T(8,128)(2,1)S(1)}, u32[]{:S(2)}, u32[]{:S(2)}) collective-permute-start(bf16[256,512]{1,0:T(8,128)(2,1)S(1)} %get-tuple-element.63), channel_id=1, source_target_pairs={{0,7},{1,0},{2,1},{3,2},{4,3},{5,4},{6,5},{7,6},{16,23},{17,16},{1... | collective-permute-start | bytes 786440 | tf_op jit(solution)/shard_map/ppermute | solution.py:58
  69.8 10.5 %collective-permute-start.15 = (bf16[256,512]{1,0:T(8,128)(2,1)S(1)}, bf16[256,512]{1,0:T(8,128)(2,1)S(1)}, u32[]{:S(2)}, u32[]{:S(2)}) collective-permute-start(bf16[256,512]{1,0:T(8,128)(2,1)S(1)} %add_convert_fusion.11), channel_id=1, source_target_pairs={{0,1},{1,2},{2,3},{3,4},{4,5},{5,6},{6,7},{7,0},{16,17},{17,18},{1... | collective-permute-start | bytes 786440 | tf_op jit(solution)/shard_map/ppermute | solution.py:58
  70.0 10.7 %collective-permute-start.19 = (bf16[256,512]{1,0:T(8,128)(2,1)S(1)}, bf16[256,512]{1,0:T(8,128)(2,1)S(1)}, u32[]{:S(2)}, u32[]{:S(2)}) collective-permute-start(bf16[256,512]{1,0:T(8,128)(2,1)S(1)} %add_convert_fusion.8), channel_id=1, source_target_pairs={{0,7},{1,0},{2,1},{3,2},{4,3},{5,4},{6,5},{7,6},{16,23},{17,16},{1... | collective-permute-start | bytes 786440 | tf_op jit(solution)/shard_map/ppermute | solution.py:58
  73.3 16.6 %collective-permute-start.23 = (bf16[256,512]{1,0:T(8,128)(2,1)S(1)}, bf16[256,512]{1,0:T(8,128)(2,1)S(1)}, u32[]{:S(2)}, u32[]{:S(2)}) collective-permute-start(bf16[256,512]{1,0:T(8,128)(2,1)S(1)} %add_convert_fusion.5), channel_id=1, source_target_pairs={{0,1},{1,2},{2,3},{3,4},{4,5},{5,6},{6,7},{7,0},{16,17},{17,18},{1... | collective-permute-start | bytes 786440 | tf_op jit(solution)/shard_map/ppermute | solution.py:58
  73.5 12.1 %collective-permute-start.26 = (bf16[256,512]{1,0:T(8,128)(2,1)S(1)}, bf16[256,512]{1,0:T(8,128)(2,1)S(1)}, u32[]{:S(2)}, u32[]{:S(2)}) collective-permute-start(bf16[256,512]{1,0:T(8,128)(2,1)S(1)} %add_convert_fusion.3), channel_id=1, source_target_pairs={{0,7},{1,0},{2,1},{3,2},{4,3},{5,4},{6,5},{7,6},{16,23},{17,16},{1... | collective-permute-start | bytes 786440 | tf_op jit(solution)/shard_map/ppermute | solution.py:58
  80.4 9.4 %collective-permute-start.16 = (bf16[256,512]{1,0:T(8,128)(2,1)S(1)}, bf16[256,512]{1,0:T(8,128)(2,1)S(1)}, u32[]{:S(2)}, u32[]{:S(2)}) collective-permute-start(bf16[256,512]{1,0:T(8,128)(2,1)S(1)} %add_convert_fusion.10), channel_id=1, source_target_pairs={{0,1},{1,2},{2,3},{3,4},{4,5},{5,6},{6,7},{7,0},{16,17},{17,18},{1... | collective-permute-start | bytes 786440 | tf_op jit(solution)/shard_map/ppermute | solution.py:58
  80.8 17.9 %collective-permute-start.20 = (bf16[256,512]{1,0:T(8,128)(2,1)S(1)}, bf16[256,512]{1,0:T(8,128)(2,1)S(1)}, u32[]{:S(2)}, u32[]{:S(2)}) collective-permute-start(bf16[256,512]{1,0:T(8,128)(2,1)S(1)} %add_convert_fusion.7), channel_id=1, source_target_pairs={{0,7},{1,0},{2,1},{3,2},{4,3},{5,4},{6,5},{7,6},{16,23},{17,16},{1... | collective-permute-start | bytes 786440 | tf_op jit(solution)/shard_map/ppermute | solution.py:58
  85.7 9.1 %collective-permute-start.27 = (bf16[256,512]{1,0:T(8,128)(2,1)S(1)}, bf16[256,512]{1,0:T(8,128)(2,1)S(1)}, u32[]{:S(2)}, u32[]{:S(2)}) collective-permute-start(bf16[256,512]{1,0:T(8,128)(2,1)S(1)} %add_convert_fusion.2), channel_id=1, source_target_pairs={{0,7},{1,0},{2,1},{3,2},{4,3},{5,4},{6,5},{7,6},{16,23},{17,16},{1... | collective-permute-start | bytes 786440 | tf_op jit(solution)/shard_map/ppermute | solution.py:58
  89.9 10.5 %collective-permute-start.17 = (bf16[256,512]{1,0:T(8,128)(2,1)S(1)}, bf16[256,512]{1,0:T(8,128)(2,1)S(1)}, u32[]{:S(2)}, u32[]{:S(2)}) collective-permute-start(bf16[256,512]{1,0:T(8,128)(2,1)S(1)} %add_convert_fusion.9), channel_id=1, source_target_pairs={{0,1},{1,2},{2,3},{3,4},{4,5},{5,6},{6,7},{7,0},{16,17},{17,18},{1... | collective-permute-start | bytes 786440 | tf_op jit(solution)/shard_map/ppermute | solution.py:58
  90.1 13.3 %collective-permute-start.24 = (bf16[256,512]{1,0:T(8,128)(2,1)S(1)}, bf16[256,512]{1,0:T(8,128)(2,1)S(1)}, u32[]{:S(2)}, u32[]{:S(2)}) collective-permute-start(bf16[256,512]{1,0:T(8,128)(2,1)S(1)} %add_convert_fusion.4), channel_id=1, source_target_pairs={{0,1},{1,2},{2,3},{3,4},{4,5},{5,6},{6,7},{7,0},{16,17},{17,18},{1... | collective-permute-start | bytes 786440 | tf_op jit(solution)/shard_map/ppermute | solution.py:58
  94.9 8.4 %collective-permute-start.28 = (bf16[256,512]{1,0:T(8,128)(2,1)S(1)}, bf16[256,512]{1,0:T(8,128)(2,1)S(1)}, u32[]{:S(2)}, u32[]{:S(2)}) collective-permute-start(bf16[256,512]{1,0:T(8,128)(2,1)S(1)} %add_convert_fusion.1), channel_id=1, source_target_pairs={{0,7},{1,0},{2,1},{3,2},{4,3},{5,4},{6,5},{7,6},{16,23},{17,16},{1... | collective-permute-start | bytes 786440 | tf_op jit(solution)/shard_map/ppermute | solution.py:58
  (1 other events, 21.7 us)

commit v10 on v9

--- a/solution.py
+++ b/solution.py
@@ -316,7 +316,10 @@
         late = (*orders[0][1:], *orders[1][1:], 0)
         begun = project(coords, early, attended[k], near[k], out_weight, parts)
         moving.append([send(value, move) for value, move in zip(begun, moves)])
-        partial = dict(zip(late, project(coords, late, attended[k], near[k], out_weight, parts)))
+        held = near[k]
+        if k:
+            held, moving[0][0], moving[0][1] = barrier((held, moving[0][0], moving[0][1]))
+        partial = dict(zip(late, project(coords, late, attended[k], held, out_weight, parts)))
         ways.append((orders, partial))
 
     for step in range(1, 4):

time: 105 us -> 104 us (level)
  waiting for transfers between devices: 41.3 us -> 39.5 us
    ppermute x29, waiting for transfers between devices: 41.3 us -> 39.5 us  [send(): return lax.ppermute(array, AXES, MOVES[move])]
  transfers between devices with their start and end apart: 29 -> 29, of which waited for: 14 -> 14; matrix products, arithmetic and copies ran while one was open for 1% -> 1% of each run, Pallas kernels for 20% -> 21%
where the time goes in v10:
time: 104 us; the launch traced here: 103 us
  waiting for transfers between devices  39.5 us (38%)
  starting transfers between devices  38.9 us (37%)
  Pallas kernels  21.7 us (21%)
  other arithmetic  1.7 us (2%)
  local copies, waits for them, and re-layouts  1.18 us (1%)
    ppermute x29, waiting for transfers between devices, send(): return lax.ppermute(array, AXES, MOVES[move])  39.5 us
    ppermute x29, starting transfers between devices, send(): return lax.ppermute(array, AXES, MOVES[move])  38.9 us
    pallas_call x2, Pallas kernels, attention(): pl.pallas_call(functools.partial(attention_kernel, first_row, n_rows, slo...  10.5 us
    pallas_call x4, Pallas kernels, project(): pl.pallas_call(functools.partial(project_kernel, steps), out_shape=[jax.S...  8.59 us
    pallas_call x1, Pallas kernels, pick(): pl.pallas_call(pick_kernel, out_shape=parts, in_specs=[SMEM, HBM], out_sp...  2.38 us
  transfers between devices with their start and end apart: 29, of which 14 were waited for; matrix products, arithmetic and copies ran while one was open for 1% of the time, Pallas kernels for 21%

profile of v10, /device:TPU:6, one launch (start us, length us, event | category | flops | bytes accessed | tf_op | source)
XLA Modules:
  0.0 103.2 jit_solution(9079578644140569696)
XLA Ops:
  0.0 1.1 %constant_dynamic-slice_fusion = (bf16[2,512,128]{2,1,0:T(8,128)(2,1)S(1)}, bf16[2,512,128]{2,1,0:T(8,128)(2,1)S(1)}) fusion(bf16[2,512,1024]{2,1,0:T(8,128)(2,1)} %param.5, s32[]{:T(128)S(6)} %select_n.46, s32[]{:T(128)S(6)} %select_n.45), kind=kLoop, calls=%fused_computation.13 | loop fusion | bytes 1048584 | tf_op jit(solution)/shard_map/dynamic_slice | solution.py:281
  1.1 3.1 %collective-permute-start = (bf16[2,512,128]{2,1,0:T(8,128)(2,1)S(1)}, bf16[2,512,128]{2,1,0:T(8,128)(2,1)S(1)}, u32[]{:S(2)}, u32[]{:S(2)}) collective-permute-start(bf16[2,512,128]{2,1,0:T(8,128)(2,1)S(1)} %get-tuple-element.73), channel_id=1, source_target_pairs={{0,40},{1,41},{2,42},{3,43},{4,44},{5,45},{6,46},{7,47},{16,56},{1... | collective-permute-start | bytes 786440 | tf_op jit(solution)/shard_map/ppermute | solution.py:58
  4.2 0.8 collective-permute-start.2
  5.0 2.4 %collective-permute-start.1 = (bf16[2,512,128]{2,1,0:T(8,128)(2,1)S(1)}, bf16[2,512,128]{2,1,0:T(8,128)(2,1)S(1)}, u32[]{:S(2)}, u32[]{:S(2)}) collective-permute-start(bf16[2,512,128]{2,1,0:T(8,128)(2,1)S(1)} %get-tuple-element.74.refs_0_), channel_id=1, source_target_pairs={{0,64},{1,65},{2,66},{3,67},{4,68},{5,69},{6,70},{7,71},{16,80},{1... | collective-permute-start | bytes 786440 | tf_op jit(solution)/shard_map/ppermute | solution.py:58
  7.5 2.4 %pick.1 = (bf16[208,2048]{1,0:T(8,128)(2,1)S(1)}, bf16[304,2048]{1,0:T(8,128)(2,1)S(1)}) custom-call(s32[5]{0:T(128)S(1)} %stack.25.coords, bf16[512,8192]{1,0:T(8,128)(2,1)} %w_ref.9), custom_call_target="tpu_custom_call" | custom-call | tf_op jit(solution)/shard_map/pick/pallas_call | solution.py:84
  10.5 2.7 %collective-permute-done.2.refs_3_ = bf16[2,512,128]{2,1,0:T(8,128)(2,1)S(1)} collective-permute-done((bf16[2,512,128]{2,1,0:T(8,128)(2,1)S(1)}, bf16[2,512,128]{2,1,0:T(8,128)(2,1)S(1)}, u32[]{:S(2)}, u32[]{:S(2)}) %collective-permute-start.2) | collective-permute-done | bytes 262176 | tf_op jit(solution)/shard_map/ppermute | solution.py:58
  13.3 3.3 %collective-permute-start.4 = (bf16[2,2,512,128]{3,2,1,0:T(8,128)(2,1)S(1)}, bf16[2,2,512,128]{3,2,1,0:T(8,128)(2,1)S(1)}, u32[]{:S(2)}, u32[]{:S(2)}) collective-permute-start(bf16[2,2,512,128]{3,2,1,0:T(8,128)(2,1)S(1)} %get-tuple-element.45), channel_id=1, source_target_pairs={{0,64},{1,65},{2,66},{3,67},{4,68},{5,69},{6,70},{7,71},{16,80},{1... | collective-permute-start | bytes 1572872 | tf_op jit(solution)/shard_map/ppermute | solution.py:58
  17.0 4.3 %collective-permute-done.6.refs_0_ = bf16[2,512,128]{2,1,0:T(8,128)(2,1)S(1)} collective-permute-done((bf16[2,512,128]{2,1,0:T(8,128)(2,1)S(1)}, bf16[2,512,128]{2,1,0:T(8,128)(2,1)S(1)}, u32[]{:S(2)}, u32[]{:S(2)}) %collective-permute-start.6) | collective-permute-done | bytes 262176 | tf_op jit(solution)/shard_map/ppermute | solution.py:58
  21.4 7.4 %collective-permute-done.7.refs_1_ = bf16[2,512,128]{2,1,0:T(8,128)(2,1)S(1)} collective-permute-done((bf16[2,512,128]{2,1,0:T(8,128)(2,1)S(1)}, bf16[2,512,128]{2,1,0:T(8,128)(2,1)S(1)}, u32[]{:S(2)}, u32[]{:S(2)}) %collective-permute-start.7) | collective-permute-done | bytes 262176 | tf_op jit(solution)/shard_map/ppermute | solution.py:58
  29.4 1.4 %collective-permute-done.8.refs_5_ = bf16[2,2,512,128]{3,2,1,0:T(8,128)(2,1)S(1)} collective-permute-done((bf16[2,2,512,128]{3,2,1,0:T(8,128)(2,1)S(1)}, bf16[2,2,512,128]{3,2,1,0:T(8,128)(2,1)S(1)}, u32[]{:S(2)}, u32[]{:S(2)}) %collective-permute-start.8) | collective-permute-done | bytes 524320 | tf_op jit(solution)/shard_map/ppermute | solution.py:58
  31.6 6.3 %attention.2 = (bf16[256,512]{1,0:T(8,128)(2,1)S(1)}, bf16[2,8192,128]{2,1,0:T(8,128)(2,1)S(1)}) custom-call(s32[5]{0:T(128)S(1)} %stack.25.coords, s32[4,16]{1,0:T(4,128)S(1)} %copy-done.1, bf16[512,512]{1,0:T(8,128)(2,1)S(1)} %copy-done, bf16[4,2,512,128]{3,2,1,0:T(8,128)(2,1)S(1)} %get-tuple-element.44.refs_0_, ...), custom_call_target="tpu_custom_call" | custom-call | tf_op jit(solution)/shard_map/attention/pallas_call | solution.py:188
  38.2 4.2 %attention.3.own_ref = bf16[256,512]{1,0:T(8,128)(2,1)S(1)} custom-call(s32[5]{0:T(128)S(1)} %stack.25.coords, s32[4,16]{1,0:T(4,128)S(1)} %copy-done.1, bf16[512,512]{1,0:T(8,128)(2,1)S(1)} %copy-done, bf16[2,8192,128]{2,1,0:T(8,128)(2,1)S(1)} %get-tuple-element.49.refs_0_), custom_call_target="tpu_custom_call" | custom-call | tf_op jit(solution)/shard_map/attention/pallas_call | solution.py:188
  42.4 5.2 %collective-permute-done.10.w1a = bf16[304,2048]{1,0:T(8,128)(2,1)S(1)} collective-permute-done((bf16[304,2048]{1,0:T(8,128)(2,1)S(1)}, bf16[304,2048]{1,0:T(8,128)(2,1)S(1)}, u32[]{:S(2)}, u32[]{:S(2)}) %collective-permute-start.10) | collective-permute-done | bytes 1245216 | tf_op jit(solution)/shard_map/ppermute | solution.py:58
  48.1 3.6 %collective-permute-done.12.w0b = bf16[208,2048]{1,0:T(8,128)(2,1)S(1)} collective-permute-done((bf16[208,2048]{1,0:T(8,128)(2,1)S(1)}, bf16[208,2048]{1,0:T(8,128)(2,1)S(1)}, u32[]{:S(2)}, u32[]{:S(2)}) %collective-permute-start.12) | collective-permute-done | bytes 852000 | tf_op jit(solution)/shard_map/ppermute | solution.py:58
  51.8 1.4 %project.5 = (bf16[256,512]{1,0:T(8,128)(2,1)S(1)}, bf16[256,512]{1,0:T(8,128)(2,1)S(1)}) custom-call(s32[5]{0:T(128)S(1)} %stack.25.coords, bf16[256,512]{1,0:T(8,128)(2,1)S(1)} %get-tuple-element.46.own_ref, bf16[256,512]{1,0:T(8,128)(2,1)S(1)} %collective-permute-done.11.near_ref, bf16[512,8192]{1,0:T(8,128)(2,1)S(1)} %bitcast.6, ...), custom_call_target="tpu_custom_call" | custom-call | tf_op jit(solution)/shard_map/project/pallas_call | solution.py:261
  53.2 2.0 %collective-permute-start.15 = (bf16[256,512]{1,0:T(8,128)(2,1)S(1)}, bf16[256,512]{1,0:T(8,128)(2,1)S(1)}, u32[]{:S(2)}, u32[]{:S(2)}) collective-permute-start(bf16[256,512]{1,0:T(8,128)(2,1)S(1)} %get-tuple-element.55), channel_id=1, source_target_pairs={{0,1},{1,2},{2,3},{3,4},{4,5},{5,6},{6,7},{7,0},{16,17},{17,18},{1... | collective-permute-start | bytes 786440 | tf_op jit(solution)/shard_map/ppermute | solution.py:58
  55.2 4.0 %collective-permute-start.16 = (bf16[256,512]{1,0:T(8,128)(2,1)S(1)}, bf16[256,512]{1,0:T(8,128)(2,1)S(1)}, u32[]{:S(2)}, u32[]{:S(2)}) collective-permute-start(bf16[256,512]{1,0:T(8,128)(2,1)S(1)} %get-tuple-element.56), channel_id=1, source_target_pairs={{0,7},{1,0},{2,1},{3,2},{4,3},{5,4},{6,5},{7,6},{16,23},{17,16},{1... | collective-permute-start | bytes 786440 | tf_op jit(solution)/shard_map/ppermute | solution.py:58
  59.2 1.4 %project.7 = (bf16[256,512]{1,0:T(8,128)(2,1)S(1)}, bf16[256,512]{1,0:T(8,128)(2,1)S(1)}) custom-call(s32[5]{0:T(128)S(1)} %stack.25.coords, bf16[256,512]{1,0:T(8,128)(2,1)S(1)} %attention.3.own_ref, bf16[256,512]{1,0:T(8,128)(2,1)S(1)} %collective-permute-done.14.near_ref, bf16[512,8192]{1,0:T(8,128)(2,1)S(1)} %bitcast.6, ...), custom_call_target="tpu_custom_call" | custom-call | tf_op jit(solution)/shard_map/project/pallas_call | solution.py:261
  60.8 3.2 %collective-permute-start.25 = (bf16[256,512]{1,0:T(8,128)(2,1)S(1)}, bf16[256,512]{1,0:T(8,128)(2,1)S(1)}, u32[]{:S(2)}, u32[]{:S(2)}) collective-permute-start(bf16[256,512]{1,0:T(8,128)(2,1)S(1)} %get-tuple-element.69), channel_id=1, source_target_pairs={{0,7},{1,0},{2,1},{3,2},{4,3},{5,4},{6,5},{7,6},{16,23},{17,16},{1... | collective-permute-start | bytes 786440 | tf_op jit(solution)/shard_map/ppermute | solution.py:58
  64.0 2.9 %project.4 = (bf16[256,512]{1,0:T(8,128)(2,1)S(1)}, bf16[256,512]{1,0:T(8,128)(2,1)S(1)}, bf16[256,512]{1,0:T(8,128)(2,1)S(1)}, bf16[256,512]{1,0:T(8,128)(2,1)S...) custom-call(s32[5]{0:T(128)S(1)} %stack.25.coords, bf16[256,512]{1,0:T(8,128)(2,1)S(1)} %get-tuple-element.46.own_ref, ...), custom_call_target="tpu_custom_call" | custom-call | tf_op jit(solution)/shard_map/project/pallas_call | solution.py:261
  67.1 3.3 %collective-permute-start.20 = (bf16[256,512]{1,0:T(8,128)(2,1)S(1)}, bf16[256,512]{1,0:T(8,128)(2,1)S(1)}, u32[]{:S(2)}, u32[]{:S(2)}) collective-permute-start(bf16[256,512]{1,0:T(8,128)(2,1)S(1)} %add_convert_fusion.8), channel_id=1, source_target_pairs={{0,7},{1,0},{2,1},{3,2},{4,3},{5,4},{6,5},{7,6},{16,23},{17,16},{1... | collective-permute-start | bytes 786440 | tf_op jit(solution)/shard_map/ppermute | solution.py:58
  70.4 2.8 %project.6 = (bf16[256,512]{1,0:T(8,128)(2,1)S(1)}, bf16[256,512]{1,0:T(8,128)(2,1)S(1)}, bf16[256,512]{1,0:T(8,128)(2,1)S(1)}, bf16[256,512]{1,0:T(8,128)(2,1)S...) custom-call(s32[5]{0:T(128)S(1)} %stack.25.coords, bf16[256,512]{1,0:T(8,128)(2,1)S(1)} %attention.3.own_ref, ...), custom_call_target="tpu_custom_call" | custom-call | tf_op jit(solution)/shard_map/project/pallas_call | solution.py:261
  73.5 3.3 %collective-permute-start.26 = (bf16[256,512]{1,0:T(8,128)(2,1)S(1)}, bf16[256,512]{1,0:T(8,128)(2,1)S(1)}, u32[]{:S(2)}, u32[]{:S(2)}) collective-permute-start(bf16[256,512]{1,0:T(8,128)(2,1)S(1)} %add_convert_fusion.3), channel_id=1, source_target_pairs={{0,7},{1,0},{2,1},{3,2},{4,3},{5,4},{6,5},{7,6},{16,23},{17,16},{1... | collective-permute-start | bytes 786440 | tf_op jit(solution)/shard_map/ppermute | solution.py:58
  77.9 3.3 %collective-permute-start.21 = (bf16[256,512]{1,0:T(8,128)(2,1)S(1)}, bf16[256,512]{1,0:T(8,128)(2,1)S(1)}, u32[]{:S(2)}, u32[]{:S(2)}) collective-permute-start(bf16[256,512]{1,0:T(8,128)(2,1)S(1)} %add_convert_fusion.7), channel_id=1, source_target_pairs={{0,7},{1,0},{2,1},{3,2},{4,3},{5,4},{6,5},{7,6},{16,23},{17,16},{1... | collective-permute-start | bytes 786440 | tf_op jit(solution)/shard_map/ppermute | solution.py:58
  81.2 2.4 %collective-permute-done.26 = bf16[256,512]{1,0:T(8,128)(2,1)S(1)} collective-permute-done((bf16[256,512]{1,0:T(8,128)(2,1)S(1)}, bf16[256,512]{1,0:T(8,128)(2,1)S(1)}, u32[]{:S(2)}, u32[]{:S(2)}) %collective-permute-start.26) | collective-permute-done | bytes 262176 | tf_op jit(solution)/shard_map/ppermute | solution.py:58
  83.7 3.8 %collective-permute-start.27 = (bf16[256,512]{1,0:T(8,128)(2,1)S(1)}, bf16[256,512]{1,0:T(8,128)(2,1)S(1)}, u32[]{:S(2)}, u32[]{:S(2)}) collective-permute-start(bf16[256,512]{1,0:T(8,128)(2,1)S(1)} %add_convert_fusion.2), channel_id=1, source_target_pairs={{0,7},{1,0},{2,1},{3,2},{4,3},{5,4},{6,5},{7,6},{16,23},{17,16},{1... | collective-permute-start | bytes 786440 | tf_op jit(solution)/shard_map/ppermute | solution.py:58
  87.4 0.8 collective-permute-done.18
  88.6 4.6 %collective-permute-done.27 = bf16[256,512]{1,0:T(8,128)(2,1)S(1)} collective-permute-done((bf16[256,512]{1,0:T(8,128)(2,1)S(1)}, bf16[256,512]{1,0:T(8,128)(2,1)S(1)}, u32[]{:S(2)}, u32[]{:S(2)}) %collective-permute-start.27) | collective-permute-done | bytes 262176 | tf_op jit(solution)/shard_map/ppermute | solution.py:58
  93.3 3.8 %collective-permute-start.28 = (bf16[256,512]{1,0:T(8,128)(2,1)S(1)}, bf16[256,512]{1,0:T(8,128)(2,1)S(1)}, u32[]{:S(2)}, u32[]{:S(2)}) collective-permute-start(bf16[256,512]{1,0:T(8,128)(2,1)S(1)} %add_convert_fusion.1), channel_id=1, source_target_pairs={{0,7},{1,0},{2,1},{3,2},{4,3},{5,4},{6,5},{7,6},{16,23},{17,16},{1... | collective-permute-start | bytes 786440 | tf_op jit(solution)/shard_map/ppermute | solution.py:58
  97.0 1.8 %collective-permute-done.19 = bf16[256,512]{1,0:T(8,128)(2,1)S(1)} collective-permute-done((bf16[256,512]{1,0:T(8,128)(2,1)S(1)}, bf16[256,512]{1,0:T(8,128)(2,1)S(1)}, u32[]{:S(2)}, u32[]{:S(2)}) %collective-permute-start.19) | collective-permute-done | bytes 262176 | tf_op jit(solution)/shard_map/ppermute | solution.py:58
  98.9 3.3 %collective-permute-done.24 = bf16[256,512]{1,0:T(8,128)(2,1)S(1)} collective-permute-done((bf16[256,512]{1,0:T(8,128)(2,1)S(1)}, bf16[256,512]{1,0:T(8,128)(2,1)S(1)}, u32[]{:S(2)}, u32[]{:S(2)}) %collective-permute-start.24) | collective-permute-done | bytes 262176 | tf_op jit(solution)/shard_map/ppermute | solution.py:58
  102.3 0.8 pad_maximum_fusion
  (59 shorter events, 5.7 us)
Async XLA Ops:
  1.1 9.4 %collective-permute-start = (bf16[2,512,128]{2,1,0:T(8,128)(2,1)S(1)}, bf16[2,512,128]{2,1,0:T(8,128)(2,1)S(1)}, u32[]{:S(2)}, u32[]{:S(2)}) collective-permute-start(bf16[2,512,128]{2,1,0:T(8,128)(2,1)S(1)} %get-tuple-element.73), channel_id=1, source_target_pairs={{0,40},{1,41},{2,42},{3,43},{4,44},{5,45},{6,46},{7,47},{16,56},{1... | collective-permute-start | bytes 786440 | tf_op jit(solution)/shard_map/ppermute | solution.py:58
  4.2 9.0 %collective-permute-start.2 = (bf16[2,512,128]{2,1,0:T(8,128)(2,1)S(1)}, bf16[2,512,128]{2,1,0:T(8,128)(2,1)S(1)}, u32[]{:S(2)}, u32[]{:S(2)}) collective-permute-start(bf16[2,512,128]{2,1,0:T(8,128)(2,1)S(1)} %get-tuple-element.74.refs_0_), channel_id=1, source_target_pairs={{0,192},{1,193},{2,194},{3,195},{4,196},{5,197},{6,198},{7,199},{1... | collective-permute-start | bytes 786440 | tf_op jit(solution)/shard_map/ppermute | solution.py:58
  5.0 8.2 %collective-permute-start.1 = (bf16[2,512,128]{2,1,0:T(8,128)(2,1)S(1)}, bf16[2,512,128]{2,1,0:T(8,128)(2,1)S(1)}, u32[]{:S(2)}, u32[]{:S(2)}) collective-permute-start(bf16[2,512,128]{2,1,0:T(8,128)(2,1)S(1)} %get-tuple-element.74.refs_0_), channel_id=1, source_target_pairs={{0,64},{1,65},{2,66},{3,67},{4,68},{5,69},{6,70},{7,71},{16,80},{1... | collective-permute-start | bytes 786440 | tf_op jit(solution)/shard_map/ppermute | solution.py:58
  7.5 44.3 %slice-start = ((s8[8388608]{0:T(1024)(128)(4,1)}), s8[4194304]{0:T(1024)(128)(4,1)S(1)}, s32[]{:S(2)}) async-start(s8[8388608]{0:T(1024)(128)(4,1)} %bitcast.5), calls=%async_computation | async-start | bytes 8388608
  9.9 21.7 %copy-start = (bf16[512,512]{1,0:T(8,128)(2,1)S(1)}, bf16[512,512]{1,0:T(8,128)(2,1)}, u32[]{:S(2)}) copy-start(bf16[512,512]{1,0:T(8,128)(2,1)} %q_ref.3) | copy-start | bytes 1572868
  13.2 8.1 %collective-permute-start.6 = (bf16[2,512,128]{2,1,0:T(8,128)(2,1)S(1)}, bf16[2,512,128]{2,1,0:T(8,128)(2,1)S(1)}, u32[]{:S(2)}, u32[]{:S(2)}) collective-permute-start(bf16[2,512,128]{2,1,0:T(8,128)(2,1)S(1)} %collective-permute-done.refs_1_), channel_id=1, source_target_pairs={{0,192},{1,193},{2,194},{3,195},{4,196},{5,197},{6,198},{7,199},{1... | collective-permute-start | bytes 786440 | tf_op jit(solution)/shard_map/ppermute | solution.py:58
  13.3 15.7 %collective-permute-start.4 = (bf16[2,2,512,128]{3,2,1,0:T(8,128)(2,1)S(1)}, bf16[2,2,512,128]{3,2,1,0:T(8,128)(2,1)S(1)}, u32[]{:S(2)}, u32[]{:S(2)}) collective-permute-start(bf16[2,2,512,128]{3,2,1,0:T(8,128)(2,1)S(1)} %get-tuple-element.45), channel_id=1, source_target_pairs={{0,64},{1,65},{2,66},{3,67},{4,68},{5,69},{6,70},{7,71},{16,80},{1... | collective-permute-start | bytes 1572872 | tf_op jit(solution)/shard_map/ppermute | solution.py:58
  16.6 35.2 %slice-start.1 = ((s8[8388608]{0:T(1024)(128)(4,1)}), s8[4194304]{0:T(1024)(128)(4,1)S(1)}, s32[]{:S(2)}) async-start(s8[8388608]{0:T(1024)(128)(4,1)} %bitcast.5), calls=%async_computation.1 | async-start | bytes 8388608
  16.6 15.0 %collective-permute-start.3 = (bf16[4,2,512,128]{3,2,1,0:T(8,128)(2,1)S(1)}, bf16[4,2,512,128]{3,2,1,0:T(8,128)(2,1)S(1)}, u32[]{:S(2)}, u32[]{:S(2)}) collective-permute-start(bf16[4,2,512,128]{3,2,1,0:T(8,128)(2,1)S(1)} %get-tuple-element.44.refs_0_), channel_id=1, source_target_pairs={{0,16},{1,17},{2,18},{3,19},{4,20},{5,21},{6,22},{7,23},{16,0},{17... | collective-permute-start | bytes 3145736 | tf_op jit(solution)/shard_map/ppermute | solution.py:58
  16.6 31.0 %collective-permute-start.10 = (bf16[304,2048]{1,0:T(8,128)(2,1)S(1)}, bf16[304,2048]{1,0:T(8,128)(2,1)S(1)}, u32[]{:S(2)}, u32[]{:S(2)}) collective-permute-start(bf16[304,2048]{1,0:T(8,128)(2,1)S(1)} %get-tuple-element.48), channel_id=1, source_target_pairs={{0,40},{1,41},{2,42},{3,43},{4,44},{5,45},{6,46},{7,47},{16,56},{1... | collective-permute-start | bytes 3735560 | tf_op jit(solution)/shard_map/ppermute | solution.py:58
  21.2 7.6 %collective-permute-start.7 = (bf16[2,512,128]{2,1,0:T(8,128)(2,1)S(1)}, bf16[2,512,128]{2,1,0:T(8,128)(2,1)S(1)}, u32[]{:S(2)}, u32[]{:S(2)}) collective-permute-start(bf16[2,512,128]{2,1,0:T(8,128)(2,1)S(1)} %collective-permute-done.6.refs_0_), channel_id=1, source_target_pairs={{0,192},{1,193},{2,194},{3,195},{4,196},{5,197},{6,198},{7,199},{1... | collective-permute-start | bytes 786440 | tf_op jit(solution)/shard_map/ppermute | solution.py:58
  21.2 21.2 %collective-permute-start.9 = (bf16[208,2048]{1,0:T(8,128)(2,1)S(1)}, bf16[208,2048]{1,0:T(8,128)(2,1)S(1)}, u32[]{:S(2)}, u32[]{:S(2)}) collective-permute-start(bf16[208,2048]{1,0:T(8,128)(2,1)S(1)} %get-tuple-element.47), channel_id=1, source_target_pairs={{0,8},{1,9},{2,10},{3,11},{4,12},{5,13},{6,14},{7,15},{16,24},{17,... | collective-permute-start | bytes 2555912 | tf_op jit(solution)/shard_map/ppermute | solution.py:58
  28.8 2.0 %collective-permute-start.8 = (bf16[2,2,512,128]{3,2,1,0:T(8,128)(2,1)S(1)}, bf16[2,2,512,128]{3,2,1,0:T(8,128)(2,1)S(1)}, u32[]{:S(2)}, u32[]{:S(2)}) collective-permute-start(bf16[2,2,512,128]{3,2,1,0:T(8,128)(2,1)S(1)} %stack.27.refs_4_), channel_id=1, source_target_pairs={{0,16},{1,17},{2,18},{3,19},{4,20},{5,21},{6,22},{7,23},{16,0},{17... | collective-permute-start | bytes 1572872 | tf_op jit(solution)/shard_map/ppermute | solution.py:58
  29.0 2.6 %collective-permute-start.5 = (bf16[2,2,512,128]{3,2,1,0:T(8,128)(2,1)S(1)}, bf16[2,2,512,128]{3,2,1,0:T(8,128)(2,1)S(1)}, u32[]{:S(2)}, u32[]{:S(2)}) collective-permute-start(bf16[2,2,512,128]{3,2,1,0:T(8,128)(2,1)S(1)} %collective-permute-done.4.refs_2_), channel_id=1, source_target_pairs={{0,16},{1,17},{2,18},{3,19},{4,20},{5,21},{6,22},{7,23},{16,0},{17... | collective-permute-start | bytes 1572872 | tf_op jit(solution)/shard_map/ppermute | solution.py:58
  38.0 9.6 %collective-permute-start.11 = (bf16[256,512]{1,0:T(8,128)(2,1)S(1)}, bf16[256,512]{1,0:T(8,128)(2,1)S(1)}, u32[]{:S(2)}, u32[]{:S(2)}) collective-permute-start(bf16[256,512]{1,0:T(8,128)(2,1)S(1)} %get-tuple-element.46.own_ref), channel_id=1, source_target_pairs={{0,8},{1,9},{2,10},{3,11},{4,12},{5,13},{6,14},{7,15},{16,24},{17,... | collective-permute-start | bytes 786440 | tf_op jit(solution)/shard_map/ppermute | solution.py:58
  47.6 4.2 %collective-permute-start.13 = (bf16[304,2048]{1,0:T(8,128)(2,1)S(1)}, bf16[304,2048]{1,0:T(8,128)(2,1)S(1)}, u32[]{:S(2)}, u32[]{:S(2)}) collective-permute-start(bf16[304,2048]{1,0:T(8,128)(2,1)S(1)} %collective-permute-done.10.w1a), channel_id=1, source_target_pairs={{0,16},{1,17},{2,18},{3,19},{4,20},{5,21},{6,22},{7,23},{16,0},{17... | collective-permute-start | bytes 3735560 | tf_op jit(solution)/shard_map/ppermute | solution.py:58
  47.6 4.2 %collective-permute-start.12 = (bf16[208,2048]{1,0:T(8,128)(2,1)S(1)}, bf16[208,2048]{1,0:T(8,128)(2,1)S(1)}, u32[]{:S(2)}, u32[]{:S(2)}) collective-permute-start(bf16[208,2048]{1,0:T(8,128)(2,1)S(1)} %collective-permute-done.9.w0a), channel_id=1, source_target_pairs={{0,16},{1,17},{2,18},{3,19},{4,20},{5,21},{6,22},{7,23},{16,0},{17... | collective-permute-start | bytes 2555912 | tf_op jit(solution)/shard_map/ppermute | solution.py:58
  48.1 11.1 %collective-permute-start.14 = (bf16[256,512]{1,0:T(8,128)(2,1)S(1)}, bf16[256,512]{1,0:T(8,128)(2,1)S(1)}, u32[]{:S(2)}, u32[]{:S(2)}) collective-permute-start(bf16[256,512]{1,0:T(8,128)(2,1)S(1)} %attention.3.own_ref), channel_id=1, source_target_pairs={{0,8},{1,9},{2,10},{3,11},{4,12},{5,13},{6,14},{7,15},{16,24},{17,... | collective-permute-start | bytes 786440 | tf_op jit(solution)/shard_map/ppermute | solution.py:58
  53.2 13.7 %collective-permute-start.15 = (bf16[256,512]{1,0:T(8,128)(2,1)S(1)}, bf16[256,512]{1,0:T(8,128)(2,1)S(1)}, u32[]{:S(2)}, u32[]{:S(2)}) collective-permute-start(bf16[256,512]{1,0:T(8,128)(2,1)S(1)} %get-tuple-element.55), channel_id=1, source_target_pairs={{0,1},{1,2},{2,3},{3,4},{4,5},{5,6},{6,7},{7,0},{16,17},{17,18},{1... | collective-permute-start | bytes 786440 | tf_op jit(solution)/shard_map/ppermute | solution.py:58
  55.2 11.7 %collective-permute-start.16 = (bf16[256,512]{1,0:T(8,128)(2,1)S(1)}, bf16[256,512]{1,0:T(8,128)(2,1)S(1)}, u32[]{:S(2)}, u32[]{:S(2)}) collective-permute-start(bf16[256,512]{1,0:T(8,128)(2,1)S(1)} %get-tuple-element.56), channel_id=1, source_target_pairs={{0,7},{1,0},{2,1},{3,2},{4,3},{5,4},{6,5},{7,6},{16,23},{17,16},{1... | collective-permute-start | bytes 786440 | tf_op jit(solution)/shard_map/ppermute | solution.py:58
  60.7 12.6 %collective-permute-start.22 = (bf16[256,512]{1,0:T(8,128)(2,1)S(1)}, bf16[256,512]{1,0:T(8,128)(2,1)S(1)}, u32[]{:S(2)}, u32[]{:S(2)}) collective-permute-start(bf16[256,512]{1,0:T(8,128)(2,1)S(1)} %get-tuple-element.66), channel_id=1, source_target_pairs={{0,1},{1,2},{2,3},{3,4},{4,5},{5,6},{6,7},{7,0},{16,17},{17,18},{1... | collective-permute-start | bytes 786440 | tf_op jit(solution)/shard_map/ppermute | solution.py:58
  60.8 12.7 %collective-permute-start.25 = (bf16[256,512]{1,0:T(8,128)(2,1)S(1)}, bf16[256,512]{1,0:T(8,128)(2,1)S(1)}, u32[]{:S(2)}, u32[]{:S(2)}) collective-permute-start(bf16[256,512]{1,0:T(8,128)(2,1)S(1)} %get-tuple-element.69), channel_id=1, source_target_pairs={{0,7},{1,0},{2,1},{3,2},{4,3},{5,4},{6,5},{7,6},{16,23},{17,16},{1... | collective-permute-start | bytes 786440 | tf_op jit(solution)/shard_map/ppermute | solution.py:58
  67.0 10.5 %collective-permute-start.17 = (bf16[256,512]{1,0:T(8,128)(2,1)S(1)}, bf16[256,512]{1,0:T(8,128)(2,1)S(1)}, u32[]{:S(2)}, u32[]{:S(2)}) collective-permute-start(bf16[256,512]{1,0:T(8,128)(2,1)S(1)} %add_convert_fusion.11), channel_id=1, source_target_pairs={{0,1},{1,2},{2,3},{3,4},{4,5},{5,6},{6,7},{7,0},{16,17},{17,18},{1... | collective-permute-start | bytes 786440 | tf_op jit(solution)/shard_map/ppermute | solution.py:58
  67.1 10.7 %collective-permute-start.20 = (bf16[256,512]{1,0:T(8,128)(2,1)S(1)}, bf16[256,512]{1,0:T(8,128)(2,1)S(1)}, u32[]{:S(2)}, u32[]{:S(2)}) collective-permute-start(bf16[256,512]{1,0:T(8,128)(2,1)S(1)} %add_convert_fusion.8), channel_id=1, source_target_pairs={{0,7},{1,0},{2,1},{3,2},{4,3},{5,4},{6,5},{7,6},{16,23},{17,16},{1... | collective-permute-start | bytes 786440 | tf_op jit(solution)/shard_map/ppermute | solution.py:58
  73.4 15.0 %collective-permute-start.23 = (bf16[256,512]{1,0:T(8,128)(2,1)S(1)}, bf16[256,512]{1,0:T(8,128)(2,1)S(1)}, u32[]{:S(2)}, u32[]{:S(2)}) collective-permute-start(bf16[256,512]{1,0:T(8,128)(2,1)S(1)} %add_convert_fusion.5), channel_id=1, source_target_pairs={{0,1},{1,2},{2,3},{3,4},{4,5},{5,6},{6,7},{7,0},{16,17},{17,18},{1... | collective-permute-start | bytes 786440 | tf_op jit(solution)/shard_map/ppermute | solution.py:58
  73.5 10.1 %collective-permute-start.26 = (bf16[256,512]{1,0:T(8,128)(2,1)S(1)}, bf16[256,512]{1,0:T(8,128)(2,1)S(1)}, u32[]{:S(2)}, u32[]{:S(2)}) collective-permute-start(bf16[256,512]{1,0:T(8,128)(2,1)S(1)} %add_convert_fusion.3), channel_id=1, source_target_pairs={{0,7},{1,0},{2,1},{3,2},{4,3},{5,4},{6,5},{7,6},{16,23},{17,16},{1... | collective-permute-start | bytes 786440 | tf_op jit(solution)/shard_map/ppermute | solution.py:58
  77.5 10.7 %collective-permute-start.18 = (bf16[256,512]{1,0:T(8,128)(2,1)S(1)}, bf16[256,512]{1,0:T(8,128)(2,1)S(1)}, u32[]{:S(2)}, u32[]{:S(2)}) collective-permute-start(bf16[256,512]{1,0:T(8,128)(2,1)S(1)} %add_convert_fusion.10), channel_id=1, source_target_pairs={{0,1},{1,2},{2,3},{3,4},{4,5},{5,6},{6,7},{7,0},{16,17},{17,18},{1... | collective-permute-start | bytes 786440 | tf_op jit(solution)/shard_map/ppermute | solution.py:58
  77.9 19.1 %collective-permute-start.21 = (bf16[256,512]{1,0:T(8,128)(2,1)S(1)}, bf16[256,512]{1,0:T(8,128)(2,1)S(1)}, u32[]{:S(2)}, u32[]{:S(2)}) collective-permute-start(bf16[256,512]{1,0:T(8,128)(2,1)S(1)} %add_convert_fusion.7), channel_id=1, source_target_pairs={{0,7},{1,0},{2,1},{3,2},{4,3},{5,4},{6,5},{7,6},{16,23},{17,16},{1... | collective-permute-start | bytes 786440 | tf_op jit(solution)/shard_map/ppermute | solution.py:58
  83.7 9.5 %collective-permute-start.27 = (bf16[256,512]{1,0:T(8,128)(2,1)S(1)}, bf16[256,512]{1,0:T(8,128)(2,1)S(1)}, u32[]{:S(2)}, u32[]{:S(2)}) collective-permute-start(bf16[256,512]{1,0:T(8,128)(2,1)S(1)} %add_convert_fusion.2), channel_id=1, source_target_pairs={{0,7},{1,0},{2,1},{3,2},{4,3},{5,4},{6,5},{7,6},{16,23},{17,16},{1... | collective-permute-start | bytes 786440 | tf_op jit(solution)/shard_map/ppermute | solution.py:58
  88.3 10.5 %collective-permute-start.19 = (bf16[256,512]{1,0:T(8,128)(2,1)S(1)}, bf16[256,512]{1,0:T(8,128)(2,1)S(1)}, u32[]{:S(2)}, u32[]{:S(2)}) collective-permute-start(bf16[256,512]{1,0:T(8,128)(2,1)S(1)} %add_convert_fusion.9), channel_id=1, source_target_pairs={{0,1},{1,2},{2,3},{3,4},{4,5},{5,6},{6,7},{7,0},{16,17},{17,18},{1... | collective-permute-start | bytes 786440 | tf_op jit(solution)/shard_map/ppermute | solution.py:58
  88.5 13.8 %collective-permute-start.24 = (bf16[256,512]{1,0:T(8,128)(2,1)S(1)}, bf16[256,512]{1,0:T(8,128)(2,1)S(1)}, u32[]{:S(2)}, u32[]{:S(2)}) collective-permute-start(bf16[256,512]{1,0:T(8,128)(2,1)S(1)} %add_convert_fusion.4), channel_id=1, source_target_pairs={{0,1},{1,2},{2,3},{3,4},{4,5},{5,6},{6,7},{7,0},{16,17},{17,18},{1... | collective-permute-start | bytes 786440 | tf_op jit(solution)/shard_map/ppermute | solution.py:58
  93.3 9.0 %collective-permute-start.28 = (bf16[256,512]{1,0:T(8,128)(2,1)S(1)}, bf16[256,512]{1,0:T(8,128)(2,1)S(1)}, u32[]{:S(2)}, u32[]{:S(2)}) collective-permute-start(bf16[256,512]{1,0:T(8,128)(2,1)S(1)} %add_convert_fusion.1), channel_id=1, source_target_pairs={{0,7},{1,0},{2,1},{3,2},{4,3},{5,4},{6,5},{7,6},{16,23},{17,16},{1... | collective-permute-start | bytes 786440 | tf_op jit(solution)/shard_map/ppermute | solution.py:58
  (1 other events, 21.7 us)
